TPU v7x, 32 devices: a whole 2x2x4 slice. The times are simulated.
32 devices in a mesh: dp: 8 (over z, x), seq: 4 (over y, core).
Axes of the slice: x: 2, y: 2, z: 4, core: 2. Of those that a mesh axis runs over, the one named last changes fastest.
Arguments:
- tokens: bfloat16 [16, 1024, 1024], P('dp', 'seq'), may hold values from -6 to 6
- captions: bfloat16 [16, 128, 1024], P('dp'), may hold values from -6 to 6
- caption_lengths: int32 [16], P('dp'), may hold values from 1 to 128, as said below
- cotangent: bfloat16 [16, 1024, 1024], P('dp', 'seq'), may hold values from -6 to 6
- self_gain: bfloat16 [1024], P(('dp', 'seq')), may hold values from 0.5 to 1.5
- self_shift: bfloat16 [1024], P(('dp', 'seq')), may hold values from -3 to 3
- self_in_weight: bfloat16 [1024, 3072], P(('dp', 'seq')), may hold values from -0.1875 to 0.1875
- self_out_weight: bfloat16 [1024, 1024], P(('dp', 'seq')), may hold values from -0.5 to 0.5
- cross_gain: bfloat16 [1024], P(('dp', 'seq')), may hold values from 0.5 to 1.5
- cross_shift: bfloat16 [1024], P(('dp', 'seq')), may hold values from -3 to 3
- cross_query_weight: bfloat16 [1024, 1024], P(('dp', 'seq')), may hold values from -0.1875 to 0.1875
- cross_memory_weight: bfloat16 [1024, 2048], P(('dp', 'seq')), may hold values from -0.1875 to 0.1875
- cross_out_weight: bfloat16 [1024, 1024], P(('dp', 'seq')), may hold values from -0.375 to 0.375
- feed_gain: bfloat16 [1024], P(('dp', 'seq')), may hold values from 0.5 to 1.5
- feed_shift: bfloat16 [1024], P(('dp', 'seq')), may hold values from -3 to 3
- up_weight: bfloat16 [1024, 4096], P(('dp', 'seq')), may hold values from -0.1875 to 0.1875
- up_bias: bfloat16 [4096], P(('dp', 'seq')), may hold values from -3 to 3
- down_weight: bfloat16 [4096, 1024], P(('dp', 'seq')), may hold values from -0.09375 to 0.09375
- down_bias: bfloat16 [1024], P(('dp', 'seq')), may hold values from -3 to 3
Outputs:
- output: bfloat16 [16, 1024, 1024], P('dp', 'seq')
- grad_tokens: float32 [16, 1024, 1024], P('dp', 'seq')
- grad_captions: float32 [16, 128, 1024], P('dp')
- grad_self_gain: float32 [1024], P(('dp', 'seq'))
- grad_self_shift: float32 [1024], P(('dp', 'seq'))
- grad_self_in_weight: float32 [1024, 3072], P(('dp', 'seq'))
- grad_self_out_weight: float32 [1024, 1024], P(('dp', 'seq'))
- grad_cross_gain: float32 [1024], P(('dp', 'seq'))
- grad_cross_shift: float32 [1024], P(('dp', 'seq'))
- grad_cross_query_weight: float32 [1024, 1024], P(('dp', 'seq'))
- grad_cross_memory_weight: float32 [1024, 2048], P(('dp', 'seq'))
- grad_cross_out_weight: float32 [1024, 1024], P(('dp', 'seq'))
- grad_feed_gain: float32 [1024], P(('dp', 'seq'))
- grad_feed_shift: float32 [1024], P(('dp', 'seq'))
- grad_up_weight: float32 [1024, 4096], P(('dp', 'seq'))
- grad_up_bias: float32 [4096], P(('dp', 'seq'))
- grad_down_weight: float32 [4096, 1024], P(('dp', 'seq'))
- grad_down_bias: float32 [1024], P(('dp', 'seq'))
Inputs may be any that keep to these rules, and one draw needn't show every extreme that they name: `caption_lengths`: lengths are long-tailed, most of them short; in every draw some item has exactly 128.
All inputs are finite; a program needn't handle non-finite values.
Results may differ from a plain program's by a relative error of at most 0.017.
Values may be sent and summed in bfloat16 or wider, within the bound.
No kernel may reach another device: no remote copies, remote signals or barrier semaphores. Data moves between devices by JAX's collectives and lax.ppermute only.
A program may use at most 256 MiB of HBM per device.

v0:
```python
import jax
import jax.numpy as jnp
from jax import lax
from jax.sharding import PartitionSpec as P

HEADS = 16


epsilon = 1e-05
masked_score = -1e30


def normalize(inputs, norm_gain, norm_shift):
    average = jnp.mean(inputs, axis=-1, keepdims=True)
    centered = inputs - average
    inverse_spread = lax.rsqrt(jnp.mean(centered * centered, axis=-1, keepdims=True) + epsilon)
    return centered * inverse_spread * norm_gain + norm_shift


def norm_back(inputs, norm_gain, norm_shift, grad_normed):
    _, pullback = jax.vjp(normalize, inputs, norm_gain, norm_shift)
    return pullback(grad_normed)


def gelu_exact(inputs):
    return jax.nn.gelu(inputs, approximate=False)


def split_heads(tensor):
    return tensor.reshape(tensor.shape[0], tensor.shape[1], HEADS, tensor.shape[2] // HEADS)


def attend(queries, key_rows, value_rows, allowed):
    scaling = (queries.shape[2] // HEADS) ** (-0.5)
    scores = (
        jnp.einsum(
            "iqhd,ikhd->ihqk",
            split_heads(queries),
            split_heads(key_rows),
            preferred_element_type=jnp.float32,
        )
        * scaling
    )
    scores = jnp.where(allowed[:, None], scores, masked_score)
    softened = jax.nn.softmax(scores, axis=-1)
    attended = jnp.einsum(
        "ihqk,ikhd->iqhd",
        softened.astype(jnp.bfloat16),
        split_heads(value_rows),
        preferred_element_type=jnp.float32,
    )
    return (attended.reshape(queries.shape).astype(jnp.bfloat16), softened)


def attend_back(queries, key_rows, value_rows, softened, grad_attended):
    scaling = (queries.shape[2] // HEADS) ** (-0.5)
    grad_heads = split_heads(grad_attended)
    grad_soft = jnp.einsum(
        "iqhd,ikhd->ihqk", grad_heads, split_heads(value_rows), preferred_element_type=jnp.float32
    )
    grad_values = jnp.einsum(
        "ihqk,iqhd->ikhd",
        softened.astype(jnp.bfloat16),
        grad_heads,
        preferred_element_type=jnp.float32,
    ).reshape(value_rows.shape)
    grad_scores = (
        softened * (grad_soft - jnp.sum(softened * grad_soft, axis=-1, keepdims=True))
    ).astype(jnp.bfloat16)
    grad_queries = (
        jnp.einsum(
            "ihqk,ikhd->iqhd",
            grad_scores,
            split_heads(key_rows),
            preferred_element_type=jnp.float32,
        ).reshape(queries.shape)
        * scaling
    )
    grad_keys = (
        jnp.einsum(
            "ihqk,iqhd->ikhd", grad_scores, split_heads(queries), preferred_element_type=jnp.float32
        ).reshape(key_rows.shape)
        * scaling
    )
    return (grad_queries, grad_keys, grad_values)


def self_forward(inputs, self_gain, self_shift, self_in_weight, self_out_weight):
    norm_gain, norm_shift, in_weight, out_weight = (
        lax.all_gather(self_gain, ("dp", "seq"), axis=0, tiled=True),
        lax.all_gather(self_shift, ("dp", "seq"), axis=0, tiled=True),
        lax.all_gather(self_in_weight, ("dp", "seq"), axis=0, tiled=True),
        lax.all_gather(self_out_weight, ("dp", "seq"), axis=0, tiled=True),
    )
    features = inputs.shape[2]
    gain_wide = norm_gain.astype(jnp.float32)
    shift_wide = norm_shift.astype(jnp.float32)
    normed = normalize(inputs, gain_wide, shift_wide).astype(jnp.bfloat16)
    projected = jnp.dot(normed, in_weight, preferred_element_type=jnp.float32).astype(jnp.bfloat16)
    queries = projected[:, :, :features]
    key_rows = projected[:, :, features : 2 * features]
    value_rows = projected[:, :, 2 * features :]
    all_keys, all_values = (
        lax.all_gather(key_rows, "seq", axis=1, tiled=True),
        lax.all_gather(value_rows, "seq", axis=1, tiled=True),
    )
    row_count = inputs.shape[1]
    query_place = lax.axis_index("seq") * row_count + lax.iota(jnp.int32, row_count)
    key_place = lax.iota(jnp.int32, all_keys.shape[1])
    allowed = (key_place[None, :] <= query_place[:, None])[None]
    attended, softened = attend(queries, all_keys, all_values, allowed)
    residual = inputs + jnp.dot(attended, out_weight, preferred_element_type=jnp.float32)
    stored = (
        gain_wide,
        shift_wide,
        in_weight,
        out_weight,
        normed,
        queries,
        all_keys,
        all_values,
        attended,
        softened,
    )
    return (residual, stored)


def self_backward(inputs, stored, grad_residual):
    (
        gain_wide,
        shift_wide,
        in_weight,
        out_weight,
        normed,
        queries,
        all_keys,
        all_values,
        attended,
        softened,
    ) = stored
    grad_low = grad_residual.astype(jnp.bfloat16)
    grad_out_weight = jnp.einsum(
        "itd,ite->de", attended, grad_low, preferred_element_type=jnp.float32
    )
    grad_attended = jnp.einsum(
        "ite,de->itd", grad_low, out_weight, preferred_element_type=jnp.float32
    ).astype(jnp.bfloat16)
    grad_queries, grad_all_keys, grad_all_values = attend_back(
        queries, all_keys, all_values, softened, grad_attended
    )
    grad_keys, grad_values = (
        lax.psum_scatter(
            grad_all_keys.astype(jnp.bfloat16), "seq", scatter_dimension=1, tiled=True
        ).astype(jnp.float32),
        lax.psum_scatter(
            grad_all_values.astype(jnp.bfloat16), "seq", scatter_dimension=1, tiled=True
        ).astype(jnp.float32),
    )
    grad_projected = jnp.concatenate([grad_queries, grad_keys, grad_values], axis=-1).astype(
        jnp.bfloat16
    )
    grad_in_weight = jnp.einsum(
        "itd,ite->de", normed, grad_projected, preferred_element_type=jnp.float32
    )
    grad_normed = jnp.einsum(
        "ite,de->itd", grad_projected, in_weight, preferred_element_type=jnp.float32
    )
    grad_inputs, grad_gain, grad_shift = norm_back(inputs, gain_wide, shift_wide, grad_normed)
    shares = (
        lax.psum_scatter(grad_gain, ("dp", "seq"), scatter_dimension=0, tiled=True),
        lax.psum_scatter(grad_shift, ("dp", "seq"), scatter_dimension=0, tiled=True),
        lax.psum_scatter(grad_in_weight, ("dp", "seq"), scatter_dimension=0, tiled=True),
        lax.psum_scatter(grad_out_weight, ("dp", "seq"), scatter_dimension=0, tiled=True),
    )
    return (grad_residual + grad_inputs, shares)


def cross_forward(
    residual_in,
    captions,
    caption_lengths,
    cross_gain,
    cross_shift,
    cross_query_weight,
    cross_memory_weight,
    cross_out_weight,
):
    norm_gain, norm_shift, query_weight, memory_weight, out_weight = (
        lax.all_gather(cross_gain, ("dp", "seq"), axis=0, tiled=True),
        lax.all_gather(cross_shift, ("dp", "seq"), axis=0, tiled=True),
        lax.all_gather(cross_query_weight, ("dp", "seq"), axis=0, tiled=True),
        lax.all_gather(cross_memory_weight, ("dp", "seq"), axis=0, tiled=True),
        lax.all_gather(cross_out_weight, ("dp", "seq"), axis=0, tiled=True),
    )
    features = residual_in.shape[2]
    gain_wide = norm_gain.astype(jnp.float32)
    shift_wide = norm_shift.astype(jnp.float32)
    normed = normalize(residual_in, gain_wide, shift_wide).astype(jnp.bfloat16)
    queries = jnp.dot(normed, query_weight, preferred_element_type=jnp.float32).astype(jnp.bfloat16)
    memory = jnp.dot(captions, memory_weight, preferred_element_type=jnp.float32).astype(
        jnp.bfloat16
    )
    key_rows = memory[:, :, :features]
    value_rows = memory[:, :, features:]
    slot_index = lax.iota(jnp.int32, captions.shape[1])
    allowed = (slot_index[None, :] < caption_lengths[:, None])[:, None, :]
    attended, softened = attend(queries, key_rows, value_rows, allowed)
    residual = residual_in + jnp.dot(attended, out_weight, preferred_element_type=jnp.float32)
    stored = (
        gain_wide,
        shift_wide,
        query_weight,
        memory_weight,
        out_weight,
        normed,
        queries,
        key_rows,
        value_rows,
        attended,
        softened,
    )
    return (residual, stored)


def cross_backward(residual_in, captions, stored, grad_residual):
    (
        gain_wide,
        shift_wide,
        query_weight,
        memory_weight,
        out_weight,
        normed,
        queries,
        key_rows,
        value_rows,
        attended,
        softened,
    ) = stored
    grad_low = grad_residual.astype(jnp.bfloat16)
    grad_out_weight = jnp.einsum(
        "itd,ite->de", attended, grad_low, preferred_element_type=jnp.float32
    )
    grad_attended = jnp.einsum(
        "ite,de->itd", grad_low, out_weight, preferred_element_type=jnp.float32
    ).astype(jnp.bfloat16)
    grad_queries, grad_keys, grad_values = attend_back(
        queries, key_rows, value_rows, softened, grad_attended
    )
    grad_memory = lax.psum(
        jnp.concatenate([grad_keys, grad_values], axis=-1).astype(jnp.bfloat16), "seq"
    )
    grad_captions = jnp.einsum(
        "isf,df->isd", grad_memory, memory_weight, preferred_element_type=jnp.float32
    )
    slot_share = captions.shape[1] // lax.axis_size("seq")
    slot_first = lax.axis_index("seq") * slot_share
    caption_part = lax.dynamic_slice_in_dim(captions, slot_first, slot_share, 1)
    memory_part = lax.dynamic_slice_in_dim(grad_memory, slot_first, slot_share, 1)
    grad_memory_weight = jnp.einsum(
        "isd,isf->df", caption_part, memory_part, preferred_element_type=jnp.float32
    )
    query_low = grad_queries.astype(jnp.bfloat16)
    grad_query_weight = jnp.einsum(
        "itd,ite->de", normed, query_low, preferred_element_type=jnp.float32
    )
    grad_normed = jnp.einsum(
        "ite,de->itd", query_low, query_weight, preferred_element_type=jnp.float32
    )
    grad_inputs, grad_gain, grad_shift = norm_back(residual_in, gain_wide, shift_wide, grad_normed)
    shares = (
        lax.psum_scatter(grad_gain, ("dp", "seq"), scatter_dimension=0, tiled=True),
        lax.psum_scatter(grad_shift, ("dp", "seq"), scatter_dimension=0, tiled=True),
        lax.psum_scatter(grad_query_weight, ("dp", "seq"), scatter_dimension=0, tiled=True),
        lax.psum_scatter(grad_memory_weight, ("dp", "seq"), scatter_dimension=0, tiled=True),
        lax.psum_scatter(grad_out_weight, ("dp", "seq"), scatter_dimension=0, tiled=True),
    )
    return (grad_residual + grad_inputs, grad_captions, shares)


def feed_forward(residual_in, feed_gain, feed_shift, up_weight, up_bias, down_weight, down_bias):
    norm_gain, norm_shift, up_full, up_offset, down_full, down_offset = (
        lax.all_gather(feed_gain, ("dp", "seq"), axis=0, tiled=True),
        lax.all_gather(feed_shift, ("dp", "seq"), axis=0, tiled=True),
        lax.all_gather(up_weight, ("dp", "seq"), axis=0, tiled=True),
        lax.all_gather(up_bias, ("dp", "seq"), axis=0, tiled=True),
        lax.all_gather(down_weight, ("dp", "seq"), axis=0, tiled=True),
        lax.all_gather(down_bias, ("dp", "seq"), axis=0, tiled=True),
    )
    gain_wide = norm_gain.astype(jnp.float32)
    shift_wide = norm_shift.astype(jnp.float32)
    normed = normalize(residual_in, gain_wide, shift_wide).astype(jnp.bfloat16)
    before = jnp.dot(normed, up_full, preferred_element_type=jnp.float32) + up_offset.astype(
        jnp.float32
    )
    activated = gelu_exact(before).astype(jnp.bfloat16)
    final = (
        residual_in
        + jnp.dot(activated, down_full, preferred_element_type=jnp.float32)
        + down_offset.astype(jnp.float32)
    )
    stored = (gain_wide, shift_wide, up_full, down_full, normed, before, activated)
    return (final, stored)


def feed_backward(residual_in, stored, grad_final):
    gain_wide, shift_wide, up_full, down_full, normed, before, activated = stored
    grad_low = grad_final.astype(jnp.bfloat16)
    grad_down_weight = jnp.einsum(
        "itf,itd->fd", activated, grad_low, preferred_element_type=jnp.float32
    )
    grad_down_bias = jnp.sum(grad_low.astype(jnp.float32), axis=(0, 1))
    grad_activated = jnp.einsum(
        "itd,fd->itf", grad_low, down_full, preferred_element_type=jnp.float32
    )
    _, pullback = jax.vjp(gelu_exact, before)
    grad_before = pullback(grad_activated)[0].astype(jnp.bfloat16)
    grad_up_weight = jnp.einsum(
        "itd,itf->df", normed, grad_before, preferred_element_type=jnp.float32
    )
    grad_up_bias = jnp.sum(grad_before.astype(jnp.float32), axis=(0, 1))
    grad_normed = jnp.einsum(
        "itf,df->itd", grad_before, up_full, preferred_element_type=jnp.float32
    )
    grad_inputs, grad_gain, grad_shift = norm_back(residual_in, gain_wide, shift_wide, grad_normed)
    shares = (
        lax.psum_scatter(grad_gain, ("dp", "seq"), scatter_dimension=0, tiled=True),
        lax.psum_scatter(grad_shift, ("dp", "seq"), scatter_dimension=0, tiled=True),
        lax.psum_scatter(grad_up_weight, ("dp", "seq"), scatter_dimension=0, tiled=True),
        lax.psum_scatter(grad_up_bias, ("dp", "seq"), scatter_dimension=0, tiled=True),
        lax.psum_scatter(grad_down_weight, ("dp", "seq"), scatter_dimension=0, tiled=True),
        lax.psum_scatter(grad_down_bias, ("dp", "seq"), scatter_dimension=0, tiled=True),
    )
    return (grad_final + grad_inputs, shares)


def body(
    tokens,
    captions,
    caption_lengths,
    cotangent,
    self_gain,
    self_shift,
    self_in_weight,
    self_out_weight,
    cross_gain,
    cross_shift,
    cross_query_weight,
    cross_memory_weight,
    cross_out_weight,
    feed_gain,
    feed_shift,
    up_weight,
    up_bias,
    down_weight,
    down_bias,
):
    inputs = tokens.astype(jnp.float32)
    first_residual, kept_self = self_forward(
        inputs, self_gain, self_shift, self_in_weight, self_out_weight
    )
    second_residual, kept_cross = cross_forward(
        first_residual,
        captions,
        caption_lengths,
        cross_gain,
        cross_shift,
        cross_query_weight,
        cross_memory_weight,
        cross_out_weight,
    )
    final, kept_feed = feed_forward(
        second_residual, feed_gain, feed_shift, up_weight, up_bias, down_weight, down_bias
    )
    stored_feed = feed_forward(
        second_residual, feed_gain, feed_shift, up_weight, up_bias, down_weight, down_bias
    )[1]
    grad_second, feed_shares = feed_backward(
        second_residual, stored_feed, cotangent.astype(jnp.float32)
    )
    stored_cross = cross_forward(
        first_residual,
        captions,
        caption_lengths,
        cross_gain,
        cross_shift,
        cross_query_weight,
        cross_memory_weight,
        cross_out_weight,
    )[1]
    grad_first, grad_captions, cross_shares = cross_backward(
        first_residual, captions, stored_cross, grad_second
    )
    stored_self = self_forward(inputs, self_gain, self_shift, self_in_weight, self_out_weight)[1]
    grad_inputs, self_shares = self_backward(inputs, stored_self, grad_first)
    return (
        final.astype(jnp.bfloat16),
        grad_inputs,
        grad_captions,
        self_shares[0],
        self_shares[1],
        self_shares[2],
        self_shares[3],
        cross_shares[0],
        cross_shares[1],
        cross_shares[2],
        cross_shares[3],
        cross_shares[4],
        feed_shares[0],
        feed_shares[1],
        feed_shares[2],
        feed_shares[3],
        feed_shares[4],
        feed_shares[5],
    )


def solution(mesh):
    placed = (
        P("dp", "seq", None),
        P("dp", None, None),
        P("dp"),
        P("dp", "seq", None),
        P(("dp", "seq")),
        P(("dp", "seq")),
        P(("dp", "seq"), None),
        P(("dp", "seq"), None),
        P(("dp", "seq")),
        P(("dp", "seq")),
        P(("dp", "seq"), None),
        P(("dp", "seq"), None),
        P(("dp", "seq"), None),
        P(("dp", "seq")),
        P(("dp", "seq")),
        P(("dp", "seq"), None),
        P(("dp", "seq")),
        P(("dp", "seq"), None),
        P(("dp", "seq")),
    )
    return jax.shard_map(
        body,
        mesh=mesh,
        in_specs=placed,
        out_specs=(
            P("dp", "seq", None),
            P("dp", "seq", None),
            P("dp", None, None),
            P(("dp", "seq")),
            P(("dp", "seq")),
            P(("dp", "seq"), None),
            P(("dp", "seq"), None),
            P(("dp", "seq")),
            P(("dp", "seq")),
            P(("dp", "seq"), None),
            P(("dp", "seq"), None),
            P(("dp", "seq"), None),
            P(("dp", "seq")),
            P(("dp", "seq")),
            P(("dp", "seq"), None),
            P(("dp", "seq")),
            P(("dp", "seq"), None),
            P(("dp", "seq")),
        ),
        check_vma=False,
    )
```

profile of v0, /device:TPU:0, one launch (start us, length us, event | category | flops | bytes accessed | tf_op | source)
XLA Modules:
  0.0 1855.8 jit_solution(12212267961373239895)
XLA Ops:
  14.6 42.7 %all-reduce.16 = (bf16[1024]{0:T(1024)(128)(2,1)S(1)}, bf16[1024]{0:T(1024)(128)(2,1)S(1)}, bf16[1024]{0:T(1024)(128)(2,1)S(1)}, bf16[1024]{0:T(1024)(128)(2,1)S...) all-reduce(bf16[1024]{0:T(1024)(128)(2,1)S(1)} %dynamic-update-slic, ...), channel_id=1, replica_groups=mesh['dp'=8,'seq'=4] {'dp','seq'}, use_global_device_ids=true, to_apply=%add.1 | all-reduce | flops 7168 | bytes 28672
  61.4 22.0 %all-gather.11.cloned.1.call-done = bf16[1024,3072]{1,0:T(8,128)(2,1)} async-done(((bf16[32,3072]{1,0:T(8,128)(2,1)}), bf16[1024,3072]{1,0:T(8,128)(2,1)}) %all-gather.11.cloned.1.call-update) | async-done | bytes 6291472 | tf_op jit(solution)/shard_map/all_gather | solution.py:92
  83.4 6.7 fusion.30
  96.0 38.9 %all-gather = bf16[32,1,128]{2,1,0:T(2,128)(2,1)S(1)} all-gather(bf16[1,1,128]{2,1,0:T(2,128)(2,1)S(1)} %bitcast.183), channel_id=1, replica_groups=mesh['dp'=8,'seq'=4] {'dp','seq'}, dimensions={0}, use_global_device_ids=true | all-gather | bytes 8448 | tf_op jit(solution)/shard_map/all_gather | solution.py:285
  135.1 11.7 all-gather.19.cloned.1.call-done
  152.3 29.7 %all-gather.15.cloned.1.call-done = bf16[2,1024,1024]{2,1,0:T(8,128)(2,1)} async-done(((bf16[2,256,1024]{2,1,0:T(8,128)(2,1)}), bf16[2,1024,1024]{2,1,0:T(8,128)(2,1)}) %all-gather.15.cloned.1.call-update) | async-done | bytes 4194320 | tf_op jit(solution)/shard_map/all_gather | solution.py:104
  182.0 6.2 copy.97
  188.2 30.3 %all-gather.13.cloned.1.call-done = bf16[2,1024,1024]{2,1,0:T(8,128)(2,1)} async-done(((bf16[2,256,1024]{2,1,0:T(8,128)(2,1)}), bf16[2,1024,1024]{2,1,0:T(8,128)(2,1)}) %all-gather.13.cloned.1.call-update) | async-done | bytes 4194320 | tf_op jit(solution)/shard_map/all_gather | solution.py:105
  218.6 6.2 copy.95
  224.8 19.1 %fusion.123 = (f32[2,16,256]{2,1,0:T(8,128)S(1)}, f32[2,16,256,1024]{3,2,1,0:T(8,128)}) fusion(pred[256,1024]{1,0:T(8,128)(4,1)S(1)} %iota_compare_fusion, bf16[2,256,16,64]{1,3,2,0:T(8,128)(2,1)S(1)} %bitcast.158, bf16[2,1024,16,64]{1,3,2,0:T(8,128)(2,1)} %bitcast.156), kind=kOutput, calls=%fused_computation.171 | convolution fusion | flops 1107297280 | bytes 39092224 | tf_op jit(solution)/shard_map/sub | solution.py:45
  243.8 15.1 fusion.81
  259.0 18.7 %all-gather.17.cloned.1.call-done = bf16[1024,1024]{1,0:T(8,128)(2,1)} async-done(((bf16[32,1024]{1,0:T(8,128)(2,1)}), bf16[1024,1024]{1,0:T(8,128)(2,1)}) %all-gather.17.cloned.1.call-update) | async-done | bytes 2097168 | tf_op jit(solution)/shard_map/all_gather | solution.py:93
  282.3 53.4 %all-gather.21.cloned.1.call-done = bf16[1024,1024]{1,0:T(8,128)(2,1)} async-done(((bf16[32,1024]{1,0:T(8,128)(2,1)}), bf16[1024,1024]{1,0:T(8,128)(2,1)}) %all-gather.21.cloned.1.call-update) | async-done | bytes 2097168 | tf_op jit(solution)/shard_map/all_gather | solution.py:191
  347.7 46.2 %all-gather.23.cloned.1.call-done = bf16[1024,1024]{1,0:T(8,128)(2,1)} async-done(((bf16[32,1024]{1,0:T(8,128)(2,1)}), bf16[1024,1024]{1,0:T(8,128)(2,1)}) %all-gather.23.cloned.1.call-update) | async-done | bytes 2097168 | tf_op jit(solution)/shard_map/all_gather | solution.py:193
  398.8 74.3 %all-gather.25.cloned.1.call-done = bf16[1024,4096]{1,0:T(8,128)(2,1)} async-done(((bf16[32,4096]{1,0:T(8,128)(2,1)}), bf16[1024,4096]{1,0:T(8,128)(2,1)}) %all-gather.25.cloned.1.call-update) | async-done | bytes 8388624 | tf_op jit(solution)/shard_map/all_gather | solution.py:284
  473.2 11.1 fusion.72
  487.5 20.6 %multiply_convert_fusion.2 = (bf16[2,256,4096]{2,1,0:T(8,128)(2,1)}, f32[2,256,4096]{2,1,0:T(8,128)}) fusion(f32[2,256,4096]{2,1,0:T(8,128)S(1)} %get-tuple-element.65, f32[4096]{0:T(1024)S(1)} %bitcast.181, u8[256,4096]{1,0:T(8,128)(4,1)S(1)} %get-tuple-element.19, u8[256,4096]{1,0:T(8,128)(4,1)S(1)} %get-tuple-element.18), kind=kLoop, calls=%fused_computation.31 | loop fusion | flops 148897792 | bytes 23085056 | tf_op jit(solution)/shard_map/convert_element_type | solution.py:295
  508.2 44.0 %all-gather.27.cloned.1.call-done = bf16[4096,1024]{1,0:T(8,128)(2,1)} async-done(((bf16[128,1024]{1,0:T(8,128)(2,1)}), bf16[4096,1024]{1,0:T(8,128)(2,1)}) %all-gather.27.cloned.1.call-update) | async-done | bytes 8388624 | tf_op jit(solution)/shard_map/all_gather | solution.py:286
  552.2 14.7 convert_reduce_fusion
  566.9 9.5 multiply_reduce_fusion.2
  584.4 4.3 convolution_convert_fusion.1
  599.6 4.3 fusion.117
  613.0 15.3 fusion.44
  628.3 6.2 copy.109
  634.6 23.9 %multiply_reduce_fusion = (f32[2,16,256]{2,1,0:T(8,128)S(1)}, f32[2,16,256,1024]{3,2,1,0:T(8,128)}) fusion(f32[2,16,256,1024]{3,2,1,0:T(8,128)} %get-tuple-element.58, f32[2,16,256]{2,1,0:T(8,128)S(1)} %get-tuple-element.57, bf16[2,256,16,64]{1,3,2,0:T(8,128)(2,1)} %bitcast.172, bf16[2,1024,16,64]{1,3,2,0:T(8,128)(2,1)} %bitcast.163), kind=kOutput, calls=%fused_computation.3 | convolution fusion | flops 1098899456 | bytes 72417280 | tf_op jit(solution)/shard_map/iqhd,ikhd->ihqk/dot_general | solution.py:58
  658.5 27.8 %multiply_convert_fusion = bf16[2,16,256,1024]{3,2,1,0:T(8,128)(2,1)} fusion(f32[2,16,256,1024]{3,2,1,0:T(8,128)} %get-tuple-element.71, f32[2,16,256]{2,1,0:T(8,128)S(1)} %get-tuple-element.70, f32[2,16,256,1024]{3,2,1,0:T(8,128)} %get-tuple-element.58, f32[2,16,256]{2,1,0:T(8,128)S(1)} %get-tuple-element.57), kind=kLoop, calls=%fused_computation.2 | loop fusion | flops 33554432 | bytes 83951616 | tf_op jit(solution)/shard_map/convert_element_type | solution.py:69
  686.3 11.1 multiply_convert_fusion.1
  697.4 6.2 copy.108
  704.1 4.9 convolution_bitcast_fusion.4
  709.6 5.0 convolution_bitcast_fusion.5
  716.2 4.4 convolution_bitcast_fusion.6
  720.8 5.6 convolution_bitcast_fusion.3
  726.5 13.4 multiply_convert_fusion.4
  741.4 5.6 reduce-scatter.10.cloned.1.call-done
  747.0 9.7 convolution_bitcast_fusion.2
  757.4 13.3 convolution_bitcast_fusion.1
  770.8 12.9 convolution_bitcast_fusion
  784.3 10.8 add_convert_fusion.1
  797.4 6.6 fusion.118
  806.7 40.8 %all-reduce.15 = (f32[1024]{0:T(1024)S(1)}, f32[1024]{0:T(1024)S(1)}, f32[1024]{0:T(1024)S(1)}, f32[1024]{0:T(1024)S(1)}, f32[1024]{0:T(1024)S(1)}, /*index=5*/f...) all-reduce(f32[1024]{0:T(1024)S(1)} %get-tuple-element.24, ...), channel_id=4, replica_groups=mesh['dp'=8,'seq'=4] {'dp','seq'}, use_global_device_ids=true, to_apply=%region_22.23.clone | all-reduce | flops 11264 | bytes 90112
  852.2 4.2 add_add_fusion.3
  856.4 34.7 %reduce-scatter.22.cloned.1.call-done = f32[32,1024]{1,0:T(8,128)} async-done(((f32[1024,1024]{1,0:T(8,128)}), f32[32,1024]{1,0:T(8,128)}) %reduce-scatter.22.cloned.1.call-update) | async-done | bytes 131088 | tf_op jit(solution)/shard_map/reduce_scatter | solution.py:275
  891.1 139.5 %reduce-scatter.18.cloned.1.call-done = f32[32,1024]{1,0:T(8,128)} async-done(((f32[1024,1024]{1,0:T(8,128)}), f32[32,1024]{1,0:T(8,128)}) %reduce-scatter.18.cloned.1.call-update) | async-done | bytes 131088 | tf_op jit(solution)/shard_map/reduce_scatter | solution.py:273
  1030.6 139.7 %reduce-scatter.16.cloned.1.call-done = f32[32,1024]{1,0:T(8,128)} async-done(((f32[1024,1024]{1,0:T(8,128)}), f32[32,1024]{1,0:T(8,128)}) %reduce-scatter.16.cloned.1.call-update) | async-done | bytes 131088 | tf_op jit(solution)/shard_map/reduce_scatter | solution.py:173
  1170.3 147.5 %reduce-scatter.20.cloned.1.call-done = f32[32,2048]{1,0:T(8,128)} async-done(((f32[1024,2048]{1,0:T(8,128)}), f32[32,2048]{1,0:T(8,128)}) %reduce-scatter.20.cloned.1.call-update) | async-done | bytes 262160 | tf_op jit(solution)/shard_map/reduce_scatter | solution.py:274
  1317.8 158.9 %reduce-scatter.14.cloned.1.call-done = f32[32,3072]{1,0:T(8,128)} async-done(((f32[1024,3072]{1,0:T(8,128)}), f32[32,3072]{1,0:T(8,128)}) %reduce-scatter.14.cloned.1.call-update) | async-done | bytes 393232 | tf_op jit(solution)/shard_map/reduce_scatter | solution.py:172
  1476.7 184.9 %reduce-scatter.24.cloned.1.call-done = f32[32,4096]{1,0:T(8,128)} async-done(((f32[1024,4096]{1,0:T(8,128)}), f32[32,4096]{1,0:T(8,128)}) %reduce-scatter.24.cloned.1.call-update) | async-done | bytes 524304 | tf_op jit(solution)/shard_map/reduce_scatter | solution.py:328
  1661.6 187.5 %reduce-scatter.26.cloned.1.call-done = f32[128,1024]{1,0:T(8,128)} async-done(((f32[4096,1024]{1,0:T(8,128)}), f32[128,1024]{1,0:T(8,128)}) %reduce-scatter.26.cloned.1.call-update) | async-done | bytes 524304 | tf_op jit(solution)/shard_map/reduce_scatter | solution.py:330
  (237 shorter events, 90.7 us)
Async XLA Ops:
  7.2 139.6 %copy-start = (bf16[2,128,1024]{2,1,0:T(8,128)(2,1)S(1)}, bf16[2,128,1024]{2,1,0:T(8,128)(2,1)}, u32[]{:S(2)}) copy-start(bf16[2,128,1024]{2,1,0:T(8,128)(2,1)} %param.20) | copy-start | bytes 1572868
  7.2 76.2 %all-gather.11.cloned.1.call-start = ((), (), s32[]{:S(2)}) async-start(), calls=%async_computation.9 | async-start | bytes 6488064 | tf_op jit(solution)/shard_map/all_gather | solution.py:92
  7.9 138.9 %all-gather.19.cloned.1.call-start = ((), (), s32[]{:S(2)}) async-start(), calls=%async_computation.13 | async-start | bytes 4325376 | tf_op jit(solution)/shard_map/all_gather | solution.py:192
  8.7 173.4 %all-gather.15.cloned.1.call-start = ((), (), s32[]{:S(2)}) async-start(), calls=%async_computation.11 | async-start | bytes 5242880 | tf_op jit(solution)/shard_map/all_gather | solution.py:104
  57.4 32.7 %copy-start.28 = (f32[1024]{0:T(1024)}, f32[1024]{0:T(1024)S(1)}, u32[]{:S(2)}) copy-start(f32[1024]{0:T(1024)S(1)} %convert_element_type.157) | copy-start | bytes 12292
  57.4 32.7 %copy-start.26 = (f32[1024]{0:T(1024)}, f32[1024]{0:T(1024)S(1)}, u32[]{:S(2)}) copy-start(f32[1024]{0:T(1024)S(1)} %convert_element_type.156) | copy-start | bytes 12292
  58.8 31.2 %copy-start.30 = (f32[2,256]{1,0:T(2,128)}, f32[2,256]{1,0:T(2,128)S(1)}, u32[]{:S(2)}) copy-start(f32[2,256]{1,0:T(2,128)S(1)} %broadcast_multiply_fusion.2) | copy-start | bytes 6148
  61.4 28.7 %copy-start.32 = (f32[2,256]{1,0:T(2,128)}, f32[2,256]{1,0:T(2,128)S(1)}, u32[]{:S(2)}) copy-start(f32[2,256]{1,0:T(2,128)S(1)} %fusion.107) | copy-start | bytes 6148
  91.8 126.8 %all-gather.13.cloned.1.call-start = ((), (), s32[]{:S(2)}) async-start(), calls=%async_computation.10 | async-start | bytes 5242880 | tf_op jit(solution)/shard_map/all_gather | solution.py:105
  92.4 185.3 %all-gather.17.cloned.1.call-start = ((), (), s32[]{:S(2)}) async-start(), calls=%async_computation.12 | async-start | bytes 2162688 | tf_op jit(solution)/shard_map/all_gather | solution.py:93
  92.9 242.8 %all-gather.21.cloned.1.call-start = ((), (), s32[]{:S(2)}) async-start(), calls=%async_computation.14 | async-start | bytes 2162688 | tf_op jit(solution)/shard_map/all_gather | solution.py:191
  93.5 300.3 %all-gather.23.cloned.1.call-start = ((), (), s32[]{:S(2)}) async-start(), calls=%async_computation.15 | async-start | bytes 2162688 | tf_op jit(solution)/shard_map/all_gather | solution.py:193
  94.3 378.9 %all-gather.25.cloned.1.call-start = ((), (), s32[]{:S(2)}) async-start(), calls=%async_computation.16 | async-start | bytes 8650752 | tf_op jit(solution)/shard_map/all_gather | solution.py:284
  95.0 457.2 %all-gather.27.cloned.1.call-start = ((), (), s32[]{:S(2)}) async-start(), calls=%async_computation.17 | async-start | bytes 8650752 | tf_op jit(solution)/shard_map/all_gather | solution.py:286
  95.7 625.0 %all-reduce.19.cloned.1.call-start = ((), (), s32[]{:S(2)}) async-start(), calls=%async_computation.20 | async-start | bytes 2097152 | tf_op jit(solution)/shard_map/psum | solution.py:249
  95.9 480.6 %copy-start.41 = (f32[1024]{0:T(1024)}, f32[1024]{0:T(1024)S(1)}, u32[]{:S(2)}) copy-start(f32[1024]{0:T(1024)S(1)} %convert_element_type.173) | copy-start | bytes 12292
  95.9 239.8 %copy-start.48 = (f32[1024]{0:T(1024)}, f32[1024]{0:T(1024)S(1)}, u32[]{:S(2)}) copy-start(f32[1024]{0:T(1024)S(1)} %convert_element_type.166) | copy-start | bytes 12292
  95.9 377.2 %copy-start.46 = (f32[1024]{0:T(1024)}, f32[1024]{0:T(1024)S(1)}, u32[]{:S(2)}) copy-start(f32[1024]{0:T(1024)S(1)} %convert_element_type.174) | copy-start | bytes 12292
  152.3 72.4 %copy-start.13 = (bf16[2,256,1024]{1,2,0:T(8,128)(2,1)}, bf16[2,256,1024]{1,2,0:T(8,128)(2,1)S(1)}, u32[]{:S(2)}) copy-start(bf16[2,256,1024]{1,2,0:T(8,128)(2,1)S(1)} %copy.96) | copy-start | bytes 3145732
  243.8 33.9 %copy-start.1 = (bf16[2,256,1024]{2,1,0:T(8,128)(2,1)S(1)}, bf16[2,256,1024]{2,1,0:T(8,128)(2,1)}, u32[]{:S(2)}) copy-start(bf16[2,256,1024]{2,1,0:T(8,128)(2,1)} %param.19) | copy-start | bytes 3145732
  259.0 23.3 %copy-start.23 = (bf16[2,16,64,256]{3,2,1,0:T(8,128)(2,1)}, bf16[2,16,64,256]{3,2,1,0:T(8,128)(2,1)S(1)}, u32[]{:S(2)}) copy-start(bf16[2,16,64,256]{3,2,1,0:T(8,128)(2,1)S(1)} %fusion.81) | copy-start | bytes 3145732
  343.7 50.1 %copy-start.4 = (f32[2,256,1024]{2,1,0:T(8,128)S(1)}, f32[2,256,1024]{2,1,0:T(8,128)}, u32[]{:S(2)}) copy-start(f32[2,256,1024]{2,1,0:T(8,128)} %copy-done.3) | copy-start | bytes 6291460
  397.1 179.3 %copy-start.37 = (f32[2,256]{1,0:T(2,128)}, f32[2,256]{1,0:T(2,128)S(1)}, u32[]{:S(2)}) copy-start(f32[2,256]{1,0:T(2,128)S(1)} %broadcast_multiply_fusion) | copy-start | bytes 6148
  398.8 177.7 %copy-start.44 = (f32[2,256]{1,0:T(2,128)}, f32[2,256]{1,0:T(2,128)S(1)}, u32[]{:S(2)}) copy-start(f32[2,256]{1,0:T(2,128)S(1)} %fusion.109) | copy-start | bytes 6148
  552.2 14.7 copy-start.9
  566.9 9.5 copy-start.58
  599.3 142.1 %reduce-scatter.12.cloned.1.call-start = ((), (), s32[]{:S(2)}) async-start(), calls=%async_computation.19 | async-start | bytes 5242880 | tf_op jit(solution)/shard_map/reduce_scatter | solution.py:155
  634.5 112.5 %reduce-scatter.10.cloned.1.call-start = ((), (), s32[]{:S(2)}) async-start(), calls=%async_computation.18 | async-start | bytes 5242880 | tf_op jit(solution)/shard_map/reduce_scatter | solution.py:152
  703.6 187.5 %reduce-scatter.22.cloned.1.call-start = ((), (), s32[]{:S(2)}) async-start(), calls=%async_computation.25 | async-start | bytes 4325376 | tf_op jit(solution)/shard_map/reduce_scatter | solution.py:275
  709.0 321.7 %reduce-scatter.18.cloned.1.call-start = ((), (), s32[]{:S(2)}) async-start(), calls=%async_computation.23 | async-start | bytes 4325376 | tf_op jit(solution)/shard_map/reduce_scatter | solution.py:273
  714.7 455.6 %reduce-scatter.16.cloned.1.call-start = ((), (), s32[]{:S(2)}) async-start(), calls=%async_computation.22 | async-start | bytes 4325376 | tf_op jit(solution)/shard_map/reduce_scatter | solution.py:173
  720.7 597.1 %reduce-scatter.20.cloned.1.call-start = ((), (), s32[]{:S(2)}) async-start(), calls=%async_computation.24 | async-start | bytes 8650752 | tf_op jit(solution)/shard_map/reduce_scatter | solution.py:274
  726.4 20.6 %copy-start.2 = (bf16[2,256,1024]{2,1,0:T(8,128)(2,1)S(1)}, bf16[2,256,1024]{2,1,0:T(8,128)(2,1)}, u32[]{:S(2)}) copy-start(bf16[2,256,1024]{2,1,0:T(8,128)(2,1)} %param.19) | copy-start | bytes 3145732
  726.4 20.6 %copy-start.27 = (f32[1024]{0:T(1024)S(1)}, f32[1024]{0:T(1024)}, u32[]{:S(2)}) copy-start(f32[1024]{0:T(1024)} %copy-done.26) | copy-start | bytes 12292
  726.4 20.6 %copy-start.29 = (f32[1024]{0:T(1024)S(1)}, f32[1024]{0:T(1024)}, u32[]{:S(2)}) copy-start(f32[1024]{0:T(1024)} %copy-done.28) | copy-start | bytes 12292
  726.4 20.6 %copy-start.31 = (f32[2,256]{1,0:T(2,128)S(1)}, f32[2,256]{1,0:T(2,128)}, u32[]{:S(2)}) copy-start(f32[2,256]{1,0:T(2,128)} %copy-done.30) | copy-start | bytes 6148
  726.5 20.6 %copy-start.33 = (f32[2,256]{1,0:T(2,128)S(1)}, f32[2,256]{1,0:T(2,128)}, u32[]{:S(2)}) copy-start(f32[2,256]{1,0:T(2,128)} %copy-done.32) | copy-start | bytes 6148
  726.5 750.2 %reduce-scatter.14.cloned.1.call-start = ((), (), s32[]{:S(2)}) async-start(), calls=%async_computation.21 | async-start | bytes 12976128 | tf_op jit(solution)/shard_map/reduce_scatter | solution.py:172
  756.7 904.8 %reduce-scatter.24.cloned.1.call-start = ((), (), s32[]{:S(2)}) async-start(), calls=%async_computation.26 | async-start | bytes 17301504 | tf_op jit(solution)/shard_map/reduce_scatter | solution.py:328
  770.7 1078.3 %reduce-scatter.26.cloned.1.call-start = ((), (), s32[]{:S(2)}) async-start(), calls=%async_computation.27 | async-start | bytes 17301504 | tf_op jit(solution)/shard_map/reduce_scatter | solution.py:330
  784.3 10.8 copy-start.34
  784.3 10.8 copy-start.55
  797.4 9.3 copy-start.39
  797.4 9.3 copy-start.40
  797.4 9.3 copy-start.43
  797.4 9.3 copy-start.50
  797.4 9.3 copy-start.51
  797.4 9.3 copy-start.52
  (30 other events, 77.8 us)
Sparse Core Ops, SparseCore 0:
  10.9 72.4 all-gather.10
  86.2 60.5 all-gather.18
  149.0 33.0 all-gather.14
  184.0 34.4 all-gather.12
  221.3 56.3 all-gather.16
  280.4 55.2 all-gather.20
  338.6 55.2 all-gather.22
  396.7 76.4 all-gather.24
  476.0 76.1 all-gather.26
  599.5 34.6 all-reduce.18
  636.8 44.8 reduce-scatter.11
  703.8 43.2 reduce-scatter.9
  750.0 141.0 reduce-scatter.21
  893.9 136.6 reduce-scatter.17
  1033.4 136.8 reduce-scatter.15
  1173.1 144.5 reduce-scatter.19
  1325.3 151.3 reduce-scatter.13
  1479.4 182.1 reduce-scatter.23
  1664.4 184.5 reduce-scatter.25
where the time goes:
time: 1860 us
  waiting for transfers between devices  1330 us (72%)
  matrix products  253 us (14%)
  blocking collectives  122 us (7%)
  other arithmetic  66 us (4%)
  local copies, waits for them, and re-layouts  63.9 us (3%)
    reduce_scatter x1, waiting for transfers between devices, feed_backward(): lax.psum_scatter(grad_down_weight, ('dp', 'seq'), scatter_dimension=0, ti...  187 us
    reduce_scatter x1, waiting for transfers between devices, feed_backward(): lax.psum_scatter(grad_up_weight, ('dp', 'seq'), scatter_dimension=0, tile...  185 us
    reduce_scatter x1, waiting for transfers between devices, self_backward(): lax.psum_scatter(grad_in_weight, ('dp', 'seq'), scatter_dimension=0, tile...  159 us
    reduce_scatter x1, waiting for transfers between devices, cross_backward(): lax.psum_scatter(grad_memory_weight, ('dp', 'seq'), scatter_dimension=0,...  147 us
    reduce_scatter x1, waiting for transfers between devices, self_backward(): lax.psum_scatter(grad_out_weight, ('dp', 'seq'), scatter_dimension=0, til...  140 us
    reduce_scatter x1, waiting for transfers between devices, cross_backward(): lax.psum_scatter(grad_query_weight, ('dp', 'seq'), scatter_dimension=0, t...  140 us
    unnamed x2, blocking collectives  83.5 us
    all_gather x1, waiting for transfers between devices, feed_forward(): lax.all_gather(up_weight, ('dp', 'seq'), axis=0, tiled=True)  74.3 us
  transfers between devices with their start and end apart: 19, of which 17 were waited for; matrix products, arithmetic and copies ran while one was open for 17% of the time, Pallas kernels for 0%

commit v1 on v0

v1 whole, which is shorter than its diff:
```python
import functools

import jax
import jax.numpy as jnp
from jax import lax
from jax.experimental import pallas as pl
from jax.experimental.pallas import tpu as pltpu
from jax.sharding import PartitionSpec as P

HEADS = 16
AXES = ("dp", "seq")
BF = jnp.bfloat16
F32 = jnp.float32
epsilon = 1e-05
masked_score = -1e30
VMEM_LIMIT = 56 * 1024 * 1024


def device_count():
    return lax.axis_size("dp") * lax.axis_size("seq")


def place():
    index = lax.axis_index("dp") * lax.axis_size("seq") + lax.axis_index("seq")
    return index


def spots(core):
    index = place()
    c = index % 2
    half = c if core == "own" else 1 - c
    return jnp.stack(
        [half, (index // 4) % 2, (index // 2) % 2, (index // 8) % 2, index // 16]
    ).astype(jnp.int32)


def hop(values, change):
    count = device_count()
    pairs = [(i, change(i)) for i in range(count)]
    return lax.ppermute(values, AXES, pairs)


def hop_core(values):
    return hop(values, lambda i: i ^ 1)


def hop_first(values):
    return hop(values, lambda i: i ^ 4 if i % 2 == 0 else i ^ 2)


def hop_second(values):
    return hop(values, lambda i: i ^ 2 if i % 2 == 0 else i ^ 4)


def hop_z0(values):
    return hop(values, lambda i: i ^ 8)


def hop_z1(values, step):
    return hop(values, lambda i: i ^ (16 * step))


def far_count():
    return device_count() // 16


def column_half(values, half):
    width = values.shape[-1] // 2
    return lax.dynamic_slice_in_dim(values, half * width, width, values.ndim - 1)


def chip_rows(shards):
    c = place() % 2
    own = jnp.concatenate([column_half(s, c) for s in shards], axis=1)
    other = jnp.concatenate([column_half(s, 1 - c) for s in shards], axis=1)
    came = hop_core(other)
    return jnp.where(
        c == 0, jnp.concatenate([own, came], 0), jnp.concatenate([came, own], 0)
    )


def gather_chips(block):
    far = far_count()
    one = jnp.stack([block] + [hop_z1(block, k) for k in range(1, far)])
    two = jnp.stack([one, hop_first(one)])
    three = jnp.stack([two, hop_z0(two)])
    four = hop_second(three)
    return three, four, hop_core(three), hop_core(four)


def assemble_kernel(widths, far, rows, spot_ref, *refs):
    near_own, far_own, near_other, far_other = refs[:4]
    outs = refs[4 : 4 + len(widths)]
    sem = refs[-1]
    c, mx, my, mz0, mz1 = (spot_ref[i] for i in range(5))
    copies = []
    for side, pieces in (("own", (near_own, far_own)), ("other", (near_other, far_other))):
        half = c if side == "own" else 1 - c
        for d4 in range(2):
            for dz0 in range(2):
                for d2 in range(2):
                    for dz1 in range(far):
                        x = jnp.where(half == 0, d2, d4) ^ mx
                        y = jnp.where(half == 0, d4, d2) ^ my
                        z = (dz1 ^ mz1) * 2 + (dz0 ^ mz0)
                        row = pl.multiple_of(((z * 2 + x) * 2 + y) * rows, rows)
                        start = 0
                        for out, width in zip(outs, widths):
                            column = pl.multiple_of(half * width, 128)
                            copies.append(
                                pltpu.make_async_copy(
                                    pieces[d4].at[dz0, d2, dz1, :, pl.ds(start, width)],
                                    out.at[pl.ds(row, rows), pl.ds(column, width)],
                                    sem,
                                )
                            )
                            start += width
    for copy in copies:
        copy.start()
    for copy in copies:
        copy.wait()


def assemble(pieces, widths):
    far, rows = pieces[0].shape[2], pieces[0].shape[3]
    total = rows * 8 * far
    return pl.pallas_call(
        functools.partial(assemble_kernel, widths, far, rows),
        out_shape=[jax.ShapeDtypeStruct((total, 2 * w), BF) for w in widths],
        in_specs=[pl.BlockSpec(memory_space=pltpu.SMEM)]
        + [pl.BlockSpec(memory_space=pl.ANY)] * 4,
        out_specs=[pl.BlockSpec(memory_space=pltpu.VMEM)] * len(widths),
        scratch_shapes=[pltpu.SemaphoreType.DMA],
        compiler_params=pltpu.CompilerParams(vmem_limit_bytes=VMEM_LIMIT),
        name="assemble",
    )(spots("own"), *pieces)


def wgrad_kernel(kinds, rows, spot_ref, *refs):
    half, mx, my, mz0 = (spot_ref[i] for i in range(4))
    out = refs[-1]
    at, start = 0, 0
    for kind in kinds:
        if kind == "dot":
            left, right = refs[at], refs[at + 1]
            at += 2
            block = lax.dot_general(
                left[...], right[...], (((0,), (0,)), ((), ())), preferred_element_type=F32
            ).astype(BF)
        else:
            block = refs[at][...].astype(BF)
            at += 1
        width = block.shape[1]
        for j in range(8):
            z0 = (j // 4) ^ mz0
            x = (j // 2 % 2) ^ mx
            y = (j % 2) ^ my
            d4 = jnp.where(half == 0, y, x)
            d2 = jnp.where(half == 0, x, y)
            out[d4, z0, d2, 0, :, start : start + width] = block[j * rows : (j + 1) * rows]
        start += width


def wgrad(terms, core):
    far = far_count()
    kinds = tuple("dot" if len(t) == 2 else "raw" for t in terms)
    height = terms[0][0].shape[1] if kinds[0] == "dot" else terms[0][0].shape[0]
    rows = height // (8 * far)
    specs, args, total, flops, moved = [], [], 0, 0, 0
    for term in terms:
        right = term[-1]
        width = right.shape[1] // 2
        if len(term) == 2:
            left = term[0]
            specs.append(pl.BlockSpec((left.shape[0], 8 * rows), lambda z, s: (0, z)))
            specs.append(pl.BlockSpec((right.shape[0], width), lambda z, s: (0, s[0])))
            flops += 2 * left.shape[0] * height * width
            moved += left.size * 2 + right.size
        else:
            specs.append(pl.BlockSpec((8 * rows, width), lambda z, s: (z, s[0])))
        args += list(term)
        total += width
    return pl.pallas_call(
        functools.partial(wgrad_kernel, kinds, rows),
        out_shape=jax.ShapeDtypeStruct((2, 2, 2, far, rows, total), BF),
        grid_spec=pltpu.PrefetchScalarGridSpec(
            num_scalar_prefetch=1,
            grid=(far,),
            in_specs=specs,
            out_specs=pl.BlockSpec(
                (2, 2, 2, 1, rows, total),
                lambda z, s: (0, 0, 0, z ^ s[4], 0, 0),
            ),
        ),
        compiler_params=pltpu.CompilerParams(vmem_limit_bytes=VMEM_LIMIT),
        cost_estimate=pl.CostEstimate(
            flops=flops, bytes_accessed=moved + 2 * height * total, transcendentals=0
        ),
        name="wgrad",
    )(spots(core), *args)


def wide(values):
    return values.astype(F32)


def scatter_chips(terms):
    far = far_count()
    other = wgrad(terms, "other")
    came0 = hop_core(other)
    own = wgrad(terms, "own")
    came1 = hop_second((wide(own[1]) + wide(came0[1])).astype(BF))
    came2 = hop_z0((wide(own[0, 1]) + wide(came0[0, 1]) + wide(came1[1])).astype(BF))
    came3 = hop_first(
        (wide(own[0, 0, 1]) + wide(came0[0, 0, 1]) + wide(came1[0, 1]) + wide(came2[1])).astype(BF)
    )
    kept = (
        wide(own[0, 0, 0])
        + wide(came0[0, 0, 0])
        + wide(came1[0, 0])
        + wide(came2[0])
        + wide(came3)
    )
    low = kept.astype(BF)
    total = kept[0]
    for k in range(1, far):
        total = total + wide(hop_z1(low[k], k))
    c = place() % 2
    rows = total.shape[0] // 2
    mine = lax.dynamic_slice_in_dim(total, c * rows, rows, 0)
    came = hop_core(lax.dynamic_slice_in_dim(total, (1 - c) * rows, rows, 0))
    left = jnp.where(c == 0, mine, came)
    right = jnp.where(c == 0, came, mine)
    results, start = [], 0
    for term in terms:
        width = term[-1].shape[1] // 2
        results.append(
            jnp.concatenate(
                [left[:, start : start + width], right[:, start : start + width]], axis=1
            )
        )
        start += width
    return results


def pack_small(vectors, bias):
    r = vectors[0].shape[0]
    left = jnp.pad(jnp.stack(vectors, 1), ((0, 0), (0, 128 - len(vectors))))
    k = bias.shape[0] // r
    right = jnp.pad(bias.reshape(k, r).T, ((0, 0), (0, 128 - k)))
    return jnp.concatenate([left, right], axis=1)


def unpack_small(packed, count, k):
    n = device_count()
    d = packed.shape[0]
    flat = packed.T
    vectors = [flat[i] for i in range(count)]
    bias = flat[128 : 128 + k].reshape(k, n, d // n).transpose(1, 0, 2).reshape(k * d)
    return vectors, bias


def pack_small_grads(vectors, bias):
    n = device_count()
    d = vectors[0].shape[0]
    k = bias.shape[0] // d
    rows = bias.reshape(n, k, d // n).transpose(1, 0, 2).reshape(k, d)
    block = jnp.concatenate(
        [
            jnp.stack(vectors),
            jnp.zeros((128 - len(vectors), d), F32),
            rows,
            jnp.zeros((128 - k, d), F32),
        ]
    )
    return block.T


def normalize(inputs, norm_gain, norm_shift):
    average = jnp.mean(inputs, axis=-1, keepdims=True)
    centered = inputs - average
    inverse_spread = lax.rsqrt(jnp.mean(centered * centered, axis=-1, keepdims=True) + epsilon)
    return centered * inverse_spread * norm_gain + norm_shift


def norm_back(inputs, gain, grad_normed):
    average = jnp.mean(inputs, axis=-1, keepdims=True)
    centered = inputs - average
    inverse_spread = lax.rsqrt(jnp.mean(centered * centered, axis=-1, keepdims=True) + epsilon)
    unit = centered * inverse_spread
    grad_unit = grad_normed * gain
    grad_inputs = inverse_spread * (
        grad_unit
        - jnp.mean(grad_unit, axis=-1, keepdims=True)
        - unit * jnp.mean(grad_unit * unit, axis=-1, keepdims=True)
    )
    return grad_inputs, jnp.sum(grad_normed * unit, axis=(0, 1)), jnp.sum(grad_normed, axis=(0, 1))


def gelu_exact(inputs):
    return jax.nn.gelu(inputs, approximate=False)


def split_heads(tensor):
    return tensor.reshape(tensor.shape[0], tensor.shape[1], HEADS, tensor.shape[2] // HEADS)


def attend(queries, key_rows, value_rows, allowed):
    scaling = (queries.shape[2] // HEADS) ** (-0.5)
    scores = (
        jnp.einsum(
            "iqhd,ikhd->ihqk",
            split_heads(queries),
            split_heads(key_rows),
            preferred_element_type=F32,
        )
        * scaling
    )
    scores = jnp.where(allowed[:, None], scores, masked_score)
    softened = jax.nn.softmax(scores, axis=-1)
    attended = jnp.einsum(
        "ihqk,ikhd->iqhd",
        softened.astype(BF),
        split_heads(value_rows),
        preferred_element_type=F32,
    )
    return (attended.reshape(queries.shape).astype(BF), softened)


def attend_back(queries, key_rows, value_rows, softened, grad_attended):
    scaling = (queries.shape[2] // HEADS) ** (-0.5)
    grad_heads = split_heads(grad_attended)
    grad_soft = jnp.einsum(
        "iqhd,ikhd->ihqk", grad_heads, split_heads(value_rows), preferred_element_type=F32
    )
    grad_values = jnp.einsum(
        "ihqk,iqhd->ikhd", softened.astype(BF), grad_heads, preferred_element_type=F32
    ).reshape(value_rows.shape)
    grad_scores = (
        softened * (grad_soft - jnp.sum(softened * grad_soft, axis=-1, keepdims=True))
    ).astype(BF)
    grad_queries = (
        jnp.einsum(
            "ihqk,ikhd->iqhd", grad_scores, split_heads(key_rows), preferred_element_type=F32
        ).reshape(queries.shape)
        * scaling
    )
    grad_keys = (
        jnp.einsum(
            "ihqk,iqhd->ikhd", grad_scores, split_heads(queries), preferred_element_type=F32
        ).reshape(key_rows.shape)
        * scaling
    )
    return (grad_queries, grad_keys, grad_values)


def flat(tensor):
    return tensor.reshape(-1, tensor.shape[-1])


def dot(left, right):
    return jnp.dot(left, right, preferred_element_type=F32)


def dot_t(left, right):
    return lax.dot_general(
        left, right, (((left.ndim - 1,), (1,)), ((), ())), preferred_element_type=F32
    )


def sum_seq(values):
    size = lax.axis_size("seq")
    dp = lax.axis_size("dp")
    step = 1
    total = values.astype(BF)
    while step < size:
        pairs = [
            (d * size + s, d * size + (s ^ step)) for d in range(dp) for s in range(size)
        ]
        came = lax.ppermute(total, AXES, pairs)
        total = wide(total) + wide(came)
        step *= 2
        if step < size:
            total = total.astype(BF)
    return total


def body(
    tokens,
    captions,
    caption_lengths,
    cotangent,
    self_gain,
    self_shift,
    self_in_weight,
    self_out_weight,
    cross_gain,
    cross_shift,
    cross_query_weight,
    cross_memory_weight,
    cross_out_weight,
    feed_gain,
    feed_shift,
    up_weight,
    up_bias,
    down_weight,
    down_bias,
):
    features = tokens.shape[2]
    k_bias = up_weight.shape[1] // features
    small = pack_small(
        [self_gain, self_shift, cross_gain, cross_shift, feed_gain, feed_shift, down_bias], up_bias
    )
    groups = (
        (self_in_weight, self_out_weight, small),
        (cross_query_weight, cross_memory_weight, cross_out_weight),
        (up_weight,),
    )
    shards = [s for g in groups for s in g]
    rows = chip_rows(shards)
    blocks, start = [], 0
    for group in groups:
        widths = tuple(s.shape[1] // 2 for s in group)
        blocks.append((rows[:, start : start + sum(widths)], widths))
        start += sum(widths)
    blocks.append((chip_rows([down_weight]), (down_weight.shape[1] // 2,)))
    gathered = [assemble(gather_chips(b), w) for b, w in blocks]
    (self_in, self_out, small_full), (cross_query, cross_memory, cross_out), (up,), (down,) = (
        gathered
    )
    vectors, up_offset = unpack_small(small_full, 7, k_bias)
    self_gain, self_shift, cross_gain, cross_shift, feed_gain, feed_shift, down_offset = (
        wide(v) for v in vectors
    )
    up_offset = wide(up_offset)

    inputs = wide(tokens)
    normed1 = normalize(inputs, self_gain, self_shift).astype(BF)
    projected = dot(normed1, self_in).astype(BF)
    queries = projected[:, :, :features]
    key_rows = projected[:, :, features : 2 * features]
    value_rows = projected[:, :, 2 * features :]
    all_keys = lax.all_gather(key_rows, "seq", axis=1, tiled=True)
    all_values = lax.all_gather(value_rows, "seq", axis=1, tiled=True)
    row_count = inputs.shape[1]
    query_place = lax.axis_index("seq") * row_count + lax.iota(jnp.int32, row_count)
    key_place = lax.iota(jnp.int32, all_keys.shape[1])
    allowed = (key_place[None, :] <= query_place[:, None])[None]
    attended1, softened1 = attend(queries, all_keys, all_values, allowed)
    residual1 = inputs + dot(attended1, self_out)

    normed2 = normalize(residual1, cross_gain, cross_shift).astype(BF)
    cross_queries = dot(normed2, cross_query).astype(BF)
    memory = dot(captions, cross_memory).astype(BF)
    memory_keys, memory_values = memory[:, :, :features], memory[:, :, features:]
    slot_index = lax.iota(jnp.int32, captions.shape[1])
    visible = (slot_index[None, :] < caption_lengths[:, None])[:, None, :]
    attended2, softened2 = attend(cross_queries, memory_keys, memory_values, visible)
    residual2 = residual1 + dot(attended2, cross_out)

    normed3 = normalize(residual2, feed_gain, feed_shift).astype(BF)
    before = dot(normed3, up) + up_offset
    activated = gelu_exact(before).astype(BF)
    final = residual2 + dot(activated, down) + down_offset

    grad_final = wide(cotangent)
    grad_activated = dot_t(cotangent, down)
    _, pullback = jax.vjp(gelu_exact, before)
    grad_before = pullback(grad_activated)[0].astype(BF)
    grad_normed3 = dot_t(grad_before, up)
    grad_in3, grad_feed_gain, grad_feed_shift = norm_back(residual2, feed_gain, grad_normed3)
    grad_up_bias = jnp.sum(wide(grad_before), axis=(0, 1))
    grad_down_bias = jnp.sum(grad_final, axis=(0, 1))
    (grad_down,) = scatter_chips([(flat(activated), flat(cotangent))])
    (grad_up,) = scatter_chips([(flat(normed3), flat(grad_before))])
    grad_second = grad_final + grad_in3

    low2 = grad_second.astype(BF)
    grad_attended2 = dot_t(low2, cross_out).astype(BF)
    grad_cq, grad_mk, grad_mv = attend_back(
        cross_queries, memory_keys, memory_values, softened2, grad_attended2
    )
    grad_memory = jnp.concatenate([grad_mk, grad_mv], axis=-1).astype(BF)
    grad_captions = sum_seq(dot_t(grad_memory, cross_memory))
    low_cq = grad_cq.astype(BF)
    grad_normed2 = dot_t(low_cq, cross_query)
    grad_in2, grad_cross_gain, grad_cross_shift = norm_back(residual1, cross_gain, grad_normed2)
    grad_first = grad_second + grad_in2

    low1 = grad_first.astype(BF)
    grad_cross_query, grad_cross_memory, grad_cross_out, grad_self_out = scatter_chips(
        [
            (flat(normed2), flat(low_cq)),
            (flat(captions), flat(grad_memory)),
            (flat(attended2), flat(low2)),
            (flat(attended1), flat(low1)),
        ]
    )
    grad_attended1 = dot_t(low1, self_out).astype(BF)
    grad_q, grad_all_keys, grad_all_values = attend_back(
        queries, all_keys, all_values, softened1, grad_attended1
    )
    grad_keys = lax.psum_scatter(
        grad_all_keys.astype(BF), "seq", scatter_dimension=1, tiled=True
    ).astype(BF)
    grad_values = lax.psum_scatter(
        grad_all_values.astype(BF), "seq", scatter_dimension=1, tiled=True
    ).astype(BF)
    grad_projected = jnp.concatenate([grad_q.astype(BF), grad_keys, grad_values], axis=-1)
    grad_normed1 = dot_t(grad_projected, self_in)
    grad_in1, grad_self_gain, grad_self_shift = norm_back(inputs, self_gain, grad_normed1)
    small_grads = pack_small_grads(
        [
            grad_self_gain,
            grad_self_shift,
            grad_cross_gain,
            grad_cross_shift,
            grad_feed_gain,
            grad_feed_shift,
            grad_down_bias,
        ],
        grad_up_bias,
    )
    grad_self_in, small_out = scatter_chips(
        [(flat(normed1), flat(grad_projected)), (small_grads,)]
    )
    small_columns = small_out.T
    return (
        final.astype(BF),
        grad_first + grad_in1,
        grad_captions,
        small_columns[0],
        small_columns[1],
        grad_self_in,
        grad_self_out,
        small_columns[2],
        small_columns[3],
        grad_cross_query,
        grad_cross_memory,
        grad_cross_out,
        small_columns[4],
        small_columns[5],
        grad_up,
        small_columns[128 : 128 + k_bias].reshape(-1),
        grad_down,
        small_columns[6],
    )


def solution(mesh):
    tokens_spec = P("dp", "seq", None)
    rows1, rows2 = P(AXES), P(AXES, None)
    return jax.shard_map(
        body,
        mesh=mesh,
        in_specs=(
            tokens_spec, P("dp", None, None), P("dp"), tokens_spec,
            rows1, rows1, rows2, rows2, rows1, rows1, rows2, rows2, rows2,
            rows1, rows1, rows2, rows1, rows2, rows1,
        ),
        out_specs=(
            tokens_spec, tokens_spec, P("dp", None, None),
            rows1, rows1, rows2, rows2, rows1, rows1, rows2, rows2, rows2,
            rows1, rows1, rows2, rows1, rows2, rows1,
        ),
        check_vma=False,
    )
```

time: 1860 us -> 874 us (0.47)
  waiting for transfers between devices: 1330 us -> 314 us
  blocking collectives: 122 us -> 0 us
  Pallas kernels: 0 us -> 83.3 us
  matrix products: 253 us -> 191 us
  starting transfers between devices: 1.51 us -> 55.7 us
  other arithmetic: 66 us -> 109 us
  local copies, waits for them, and re-layouts: 63.9 us -> 95.6 us
    reduce_scatter x9 -> x2, waiting for transfers between devices: 998 us -> 0.02 us  [the longest x1 0.01 us: body(): lax.psum_scatter(grad_all_keys.astype(BF), 'seq', scatter_dimension=1, ti...]
    all_gather x9 -> x2, waiting for transfers between devices: 330 us -> 0.02 us  [the longest x1 0.02 us: body(): all_keys = lax.all_gather(key_rows, 'seq', axis=1, tiled=True)]
    ppermute x0 -> x52, waiting for transfers between devices: none -> 314 us  [the longest x50 314 us: hop(): return lax.ppermute(values, AXES, pairs)]
    unnamed x2 -> x0, blocking collectives: 83.5 us -> none
    pallas_call x0 -> x12, Pallas kernels: none -> 83.3 us  [the longest x8 53.2 us: wgrad(): pl.pallas_call(functools.partial(wgrad_kernel, kinds, rows), out_shape=ja...]
    dot_general x25 -> x18, matrix products: 178 us -> 115 us  [the longest x7 40.4 us: dot_t(): lax.dot_general(left, right, (((left.ndim - 1,), (1,)), ((), ())), prefer...]
    ppermute x0 -> x52, starting transfers between devices: none -> 55.5 us  [the longest x50 53.4 us: hop(): return lax.ppermute(values, AXES, pairs)]
    all_gather x1 -> x0, blocking collectives: 38.9 us -> none  [feed_forward(): lax.all_gather(up_bias, ('dp', 'seq'), axis=0, tiled=True)]
  transfers between devices with their start and end apart: 19 -> 56, of which waited for: 17 -> 29; matrix products, arithmetic and copies ran while one was open for 17% -> 23% of each run, Pallas kernels for 0% -> 9%
where the time goes in v1:
time: 874 us; the launch traced here: 864 us
  waiting for transfers between devices  314 us (36%)
  matrix products  191 us (22%)
  other arithmetic  109 us (12%)
  local copies, waits for them, and re-layouts  95.6 us (11%)
  Pallas kernels  83.3 us (10%)
  starting transfers between devices  55.7 us (6%)
  between operations  15.8 us (2%)
    ppermute x50, waiting for transfers between devices, hop(): return lax.ppermute(values, AXES, pairs)  314 us
    ppermute x50, starting transfers between devices, hop(): return lax.ppermute(values, AXES, pairs)  53.4 us
    pallas_call x8, Pallas kernels, wgrad(): pl.pallas_call(functools.partial(wgrad_kernel, kinds, rows), out_shape=ja...  53.2 us
    dot_general x7, matrix products, dot_t(): lax.dot_general(left, right, (((left.ndim - 1,), (1,)), ((), ())), prefer...  40.4 us
    dot_general x7, matrix products, dot(): return jnp.dot(left, right, preferred_element_type=F32)  38.7 us
    pallas_call x4, Pallas kernels, assemble(): pl.pallas_call(functools.partial(assemble_kernel, widths, far, rows), out...  30.1 us
    convert_element_type x2, other arithmetic, attend_back(): grad_scores = (softened * (grad_soft - jnp.sum(softened * grad_soft, axis...  28.9 us
    dot_general x2, matrix products, attend_back(): jnp.einsum('iqhd,ikhd->ihqk', grad_heads, split_heads(value_rows), prefer...  26.6 us
  transfers between devices with their start and end apart: 56, of which 29 were waited for; matrix products, arithmetic and copies ran while one was open for 23% of the time, Pallas kernels for 9%

profile of v1, /device:TPU:0, one launch (start us, length us, event | category | flops | bytes accessed | tf_op | source)
XLA Modules:
  0.0 864.1 jit_solution(7670798734974195393)
XLA Ops:
  20.3 12.9 %collective-permute-done.1 = bf16[64,2176]{1,0:T(8,128)(2,1)S(1)} collective-permute-done((bf16[64,2176]{1,0:T(8,128)(2,1)S(1)}, bf16[64,2176]{1,0:T(8,128)(2,1)S(1)}, u32[]{:S(2)}, u32[]{:S(2)}) %collective-permute-start.1) | collective-permute-done | bytes 278560 | tf_op jit(solution)/shard_map/ppermute | solution.py:40
  34.9 8.0 collective-permute-done.2
  43.9 24.5 %collective-permute-done.3 = bf16[2,2,64,2176]{3,2,1,0:T(8,128)(2,1)S(1)} collective-permute-done((bf16[2,2,64,2176]{3,2,1,0:T(8,128)(2,1)S(1)}, bf16[2,2,64,2176]{3,2,1,0:T(8,128)(2,1)S(1)}, u32[]{:S(2)}, u32[]{:S(2)}) %collective-permute-start.3) | collective-permute-done | bytes 1114144 | tf_op jit(solution)/shard_map/ppermute | solution.py:40
  70.0 26.3 %collective-permute-done.4.refs_1_ = bf16[2,2,2,64,2176]{4,3,2,1,0:T(8,128)(2,1)} collective-permute-done((bf16[2,2,2,64,2176]{4,3,2,1,0:T(8,128)(2,1)S(1)}, bf16[2,2,2,64,2176]{4,3,2,1,0:T(8,128)(2,1)}, u32[]{:S(2)}, u32[]{:S(2)}) %collective-permute-start.4) | collective-permute-done | bytes 2228256 | tf_op jit(solution)/shard_map/ppermute | solution.py:40
  100.9 7.9 assemble.4
  113.0 6.8 fusion.37
  126.4 18.1 %collective-permute-done.20 = bf16[256,512]{1,0:T(8,128)(2,1)S(1)} collective-permute-done((bf16[256,512]{1,0:T(8,128)(2,1)S(1)}, bf16[256,512]{1,0:T(8,128)(2,1)S(1)}, u32[]{:S(2)}, u32[]{:S(2)}) %collective-permute-start.20) | collective-permute-done | bytes 262176 | tf_op jit(solution)/shard_map/ppermute | solution.py:40
  146.0 9.8 %collective-permute-done.7 = bf16[64,2048]{1,0:T(8,128)(2,1)S(1)} collective-permute-done((bf16[64,2048]{1,0:T(8,128)(2,1)S(1)}, bf16[64,2048]{1,0:T(8,128)(2,1)S(1)}, u32[]{:S(2)}, u32[]{:S(2)}) %collective-permute-start.7) | collective-permute-done | bytes 262176 | tf_op jit(solution)/shard_map/ppermute | solution.py:40
  165.4 5.3 collective-permute-done.14
  171.0 17.6 %collective-permute-done.22 = bf16[2,2,256,512]{3,2,1,0:T(8,128)(2,1)S(1)} collective-permute-done((bf16[2,2,256,512]{3,2,1,0:T(8,128)(2,1)S(1)}, bf16[2,2,256,512]{3,2,1,0:T(8,128)(2,1)S(1)}, u32[]{:S(2)}, u32[]{:S(2)}) %collective-permute-start.22) | collective-permute-done | bytes 1048608 | tf_op jit(solution)/shard_map/ppermute | solution.py:40
  190.5 20.6 %collective-permute-done.9 = bf16[2,2,64,2048]{3,2,1,0:T(8,128)(2,1)S(1)} collective-permute-done((bf16[2,2,64,2048]{3,2,1,0:T(8,128)(2,1)S(1)}, bf16[2,2,64,2048]{3,2,1,0:T(8,128)(2,1)S(1)}, u32[]{:S(2)}, u32[]{:S(2)}) %collective-permute-start.9) | collective-permute-done | bytes 1048608 | tf_op jit(solution)/shard_map/ppermute | solution.py:40
  214.2 18.0 %collective-permute-done.15 = bf16[2,2,64,2048]{3,2,1,0:T(8,128)(2,1)S(1)} collective-permute-done((bf16[2,2,64,2048]{3,2,1,0:T(8,128)(2,1)S(1)}, bf16[2,2,64,2048]{3,2,1,0:T(8,128)(2,1)S(1)}, u32[]{:S(2)}, u32[]{:S(2)}) %collective-permute-start.15) | collective-permute-done | bytes 1048608 | tf_op jit(solution)/shard_map/ppermute | solution.py:40
  239.5 44.4 %collective-permute-done.16.refs_1_ = bf16[2,2,2,64,2048]{4,3,2,1,0:T(8,128)(2,1)} collective-permute-done((bf16[2,2,2,64,2048]{4,3,2,1,0:T(8,128)(2,1)}, bf16[2,2,2,64,2048]{4,3,2,1,0:T(8,128)(2,1)}, u32[]{:S(2)}, u32[]{:S(2)}) %collective-permute-start.16) | collective-permute-done | bytes 2097184 | tf_op jit(solution)/shard_map/ppermute | solution.py:40
  284.8 7.4 assemble.7
  292.2 7.4 assemble.5
  301.0 7.4 assemble.6
  312.2 6.6 copy.130
  318.8 19.1 %fusion.164 = (f32[2,16,256]{2,1,0:T(8,128)S(1)}, f32[2,16,256,1024]{3,2,1,0:T(8,128)}) fusion(pred[256,1024]{1,0:T(8,128)(4,1)S(1)} %iota_compare_fusion, bf16[2,256,16,64]{1,3,2,0:T(8,128)(2,1)S(1)} %bitcast.432, bf16[2,1024,16,64]{1,3,2,0:T(8,128)(2,1)} %bitcast.414), kind=kOutput, calls=%fused_computation.330 | convolution fusion | flops 1107297280 | bytes 39092224 | tf_op jit(solution)/shard_map/sub | solution.py:320
  337.9 6.2 copy.128
  344.2 15.0 %fusion.102 = bf16[2,16,64,256]{3,2,1,0:T(8,128)(2,1)S(1)} fusion(bf16[2,1024,16,64]{1,3,2,0:T(8,128)(2,1)} %bitcast.440, f32[2,16,256,1024]{3,2,1,0:T(8,128)} %get-tuple-element.121, f32[2,16,256]{2,1,0:T(8,128)S(1)} %get-tuple-element.120), kind=kOutput, calls=%fused_computation.148 | convolution fusion | flops 1091043328 | bytes 38830080 | tf_op jit(solution)/shard_map/ihqk,ikhd->iqhd/dot_general | solution.py:321
  376.8 14.4 %fusion.91 = (u8[256,4096]{1,0:T(8,128)(4,1)S(1)}, u8[256,4096]{1,0:T(8,128)(4,1)S(1)}, f32[2,256,4096]{2,1,0:T(8,128)}) fusion(f32[4096]{0:T(1024)S(1)} %reshape.496, bf16[2,256,1024]{2,1,0:T(8,128)(2,1)S(1)} %add_convert_fusion.5, bf16[1024,4096]{1,0:T(8,128)(2,1)} %assemble.6), kind=kOutput, calls=%fused_computation.137 | convolution fusion | flops 4322230272 | bytes 19939328 | tf_op jit(solution)/shard_map/dot_general | solution.py:362
  391.3 22.0 %multiply_convert_fusion.2 = (bf16[2,256,4096]{2,1,0:T(8,128)(2,1)}, f32[2,256,4096]{2,1,0:T(8,128)}) fusion(f32[2,256,4096]{2,1,0:T(8,128)} %get-tuple-element.128, f32[4096]{0:T(1024)S(1)} %reshape.496, u8[256,4096]{1,0:T(8,128)(4,1)S(1)} %get-tuple-element.31, u8[256,4096]{1,0:T(8,128)(4,1)S(1)} %get-tuple-element.30), kind=kLoop, calls=%fused_computation.37 | loop fusion | flops 148897792 | bytes 23085056 | tf_op jit(solution)/shard_map/convert_element_type | solution.py:463
  413.3 11.8 %convert_reduce_fusion = (f32[4096]{0:T(1024)}, bf16[2,256,4096]{2,1,0:T(8,128)(2,1)S(1)}) fusion(f32[2,256,4096]{2,1,0:T(8,128)} %get-tuple-element.61, bf16[2,256,1024]{2,1,0:T(8,128)(2,1)S(1)} %copy-done.14, bf16[4096,1024]{1,0:T(8,128)(2,1)S(1)} %bitcast.429, f32[2,256,4096]{2,1,0:T(8,128)} %get-tuple-element.128, f32[4096]{0:T(1024)S(1)} %reshape.496), kind=kOutput, calls=%fused_computation.35 | convolution fusion | flops 4330614784 | bytes 30441472 | tf_op jit(solution)/shard_map/dot_general | solution.py:366
  425.1 9.6 %multiply_reduce_fusion.2 = (f32[1024]{0:T(1024)}, f32[2,256]{1,0:T(2,128)S(1)}, f32[2,256]{1,0:T(2,128)S(1)}, f32[1024]{0:T(1024)}, f32[2,256,1024]{2,1,0:T(8,128)S(1)}) fusion(f32[2,256,1024]{2,1,0:T(8,128)S(1)} %get-tuple-element.127, f32[2,256]{1,0:T(2,128)S(1)} %add_rsqrt_fusion, f32[2,256]{1,0:T(2,128)S(1)} %broadcast_multiply_fusion.6, ...), kind=kOutput, calls=%fused_computation.121 | convolution fusion | flops 4299682816 | bytes 16797696 | tf_op jit(solution)/shard_map/dot_general | solution.py:366
  459.3 14.6 %fusion.47 = bf16[2,16,64,1024]{3,2,1,0:T(8,128)(2,1)} fusion(bf16[2,256,16,64]{1,3,2,0:T(8,128)(2,1)S(1)} %bitcast.460, f32[2,16,256,1024]{3,2,1,0:T(8,128)} %get-tuple-element.121, f32[2,16,256]{2,1,0:T(8,128)S(1)} %get-tuple-element.120), kind=kOutput, calls=%fused_computation.77 | convolution fusion | flops 1092616192 | bytes 38830080 | tf_op jit(solution)/shard_map/ihqk,iqhd->ikhd/dot_general | solution.py:336
  473.9 23.0 %multiply_reduce_fusion = (f32[2,16,256]{2,1,0:T(8,128)S(1)}, f32[2,16,256,1024]{3,2,1,0:T(8,128)}) fusion(f32[2,16,256,1024]{3,2,1,0:T(8,128)} %get-tuple-element.121, f32[2,16,256]{2,1,0:T(8,128)S(1)} %get-tuple-element.120, bf16[2,256,16,64]{1,3,2,0:T(8,128)(2,1)S(1)} %bitcast.461, bf16[2,1024,16,64]{1,3,2,0:T(8,128)(2,1)} %bitcast.441), kind=kOutput, calls=%fused_computation.3 | convolution fusion | flops 1098899456 | bytes 72417280 | tf_op jit(solution)/shard_map/iqhd,ikhd->ihqk/dot_general | solution.py:333
  496.9 6.2 copy.142
  539.4 6.4 wgrad.13
  545.9 6.6 wgrad.15
  554.1 7.0 wgrad.11
  561.1 27.6 %multiply_convert_fusion = bf16[2,16,256,1024]{3,2,1,0:T(8,128)(2,1)} fusion(f32[2,16,256,1024]{3,2,1,0:T(8,128)} %get-tuple-element.134, f32[2,16,256]{2,1,0:T(8,128)S(1)} %get-tuple-element.133, f32[2,16,256,1024]{3,2,1,0:T(8,128)} %get-tuple-element.121, f32[2,16,256]{2,1,0:T(8,128)S(1)} %get-tuple-element.120), kind=kLoop, calls=%fused_computation.2 | loop fusion | flops 33554432 | bytes 83951616 | tf_op jit(solution)/shard_map/convert_element_type | solution.py:341
  588.8 10.8 %multiply_convert_fusion.1 = bf16[2,16,64,1024]{3,2,1,0:T(8,128)(2,1)} fusion(bf16[2,256,16,64]{1,3,2,0:T(8,128)(2,1)S(1)} %bitcast.433, bf16[2,16,256,1024]{3,2,1,0:T(8,128)(2,1)} %multiply_convert_fusion), kind=kOutput, calls=%fused_computation.36 | convolution fusion | flops 1077936128 | bytes 22020096 | tf_op jit(solution)/shard_map/ihqk,iqhd->ikhd/dot_general | solution.py:349
  599.5 6.2 copy.141
  605.8 7.0 wgrad.12
  612.8 10.2 %add_convert_fusion.4 = bf16[2,256,1024]{2,1,0:T(8,128)(2,1)} fusion(f32[2,256,1024]{2,1,0:T(8,128)S(1)} %copy-done.2, bf16[2,256,4096]{2,1,0:T(8,128)(2,1)S(1)} %copy-done, bf16[4096,1024]{1,0:T(8,128)(2,1)} %assemble.7, f32[1024]{0:T(1024)S(1)} %copy-done.64), kind=kOutput, calls=%fused_computation.128 | convolution fusion | flops 4296540160 | bytes 15732736 | tf_op jit(solution)/shard_map/dot_general | solution.py:362
  628.3 6.5 wgrad.14
  639.6 12.3 %multiply_convert_fusion.4 = bf16[2,16,64,256]{3,2,1,0:T(8,128)(2,1)S(1)} fusion(bf16[2,1024,16,64]{1,3,2,0:T(8,128)(2,1)} %bitcast.415, bf16[2,16,256,1024]{3,2,1,0:T(8,128)(2,1)} %multiply_convert_fusion), kind=kOutput, calls=%fused_computation.123 | convolution fusion | flops 1074790400 | bytes 22020096 | tf_op jit(solution)/shard_map/ihqk,ikhd->iqhd/dot_general | solution.py:343
  658.9 7.9 wgrad.10
  677.9 25.1 %collective-permute-done.47 = bf16[2,2,2,256,512]{4,3,2,1,0:T(8,128)(2,1)} collective-permute-done((bf16[2,2,2,256,512]{4,3,2,1,0:T(8,128)(2,1)}, bf16[2,2,2,256,512]{4,3,2,1,0:T(8,128)(2,1)}, u32[]{:S(2)}, u32[]{:S(2)}) %collective-permute-start.47) | collective-permute-done | bytes 2097184 | tf_op jit(solution)/shard_map/ppermute | solution.py:40
  716.7 7.5 collective-permute-done.48
  740.5 5.7 collective-permute-done.35
  752.2 8.7 %fusion.70 = (f32[1024]{0:T(1024)S(1)}, f32[2,256]{1,0:T(2,128)S(1)}, f32[2,256]{1,0:T(2,128)S(1)}, f32[1024]{0:T(1024)S(1)}, f32[2,256,1024]{2,1,0:T(8,128)}) fusion(bf16[2,256,1024]{2,1,0:T(8,128)(2,1)S(1)} %copy-done.7, f32[2,256]{1,0:T(2,128)S(1)} %copy-done.61, f32[2,256]{1,0:T(2,128)S(1)} %copy-done.59, f32[1024]{0:T(1024)S(1)} %copy-done.57, ...), kind=kOutput, calls=%fused_computation.98 | convolution fusion | flops 3235902464 | bytes 12603392 | tf_op jit(solution)/shard_map/dot_general | solution.py:366
  769.4 5.7 wgrad.9
  782.5 6.1 wgrad.8
  796.8 14.1 %collective-permute-done.38 = bf16[64,2560]{1,0:T(8,128)(2,1)S(1)} collective-permute-done((bf16[64,2560]{1,0:T(8,128)(2,1)S(1)}, bf16[64,2560]{1,0:T(8,128)(2,1)S(1)}, u32[]{:S(2)}, u32[]{:S(2)}) %collective-permute-start.38) | collective-permute-done | bytes 327712 | tf_op jit(solution)/shard_map/ppermute | solution.py:40
  817.0 17.4 %collective-permute-done.30 = bf16[2,2,64,1664]{3,2,1,0:T(8,128)(2,1)S(1)} collective-permute-done((bf16[2,2,64,1664]{3,2,1,0:T(8,128)(2,1)S(1)}, bf16[2,2,64,1664]{3,2,1,0:T(8,128)(2,1)S(1)}, u32[]{:S(2)}, u32[]{:S(2)}) %collective-permute-start.30) | collective-permute-done | bytes 852000 | tf_op jit(solution)/shard_map/ppermute | solution.py:40
  836.5 6.2 collective-permute-done.31
  847.0 6.0 collective-permute-done.32
  (419 shorter events, 246.3 us)
Async XLA Ops:
  7.2 305.0 %all-gather.5.cloned.1.call-start = ((), (), s32[]{:S(2)}) async-start(), calls=%async_computation.3 | async-start | bytes 5242880 | tf_op jit(solution)/shard_map/all_gather | solution.py:443
  16.3 16.9 %collective-permute-start.1 = (bf16[64,2176]{1,0:T(8,128)(2,1)S(1)}, bf16[64,2176]{1,0:T(8,128)(2,1)S(1)}, u32[]{:S(2)}, u32[]{:S(2)}) collective-permute-start(bf16[64,2176]{1,0:T(8,128)(2,1)S(1)} %get-tuple-element.83), channel_id=1, source_target_pairs={{0,16},{1,17},{2,18},{3,19},{4,20},{5,21},{6,22},{7,23},{8,24},{9,... | collective-permute-start | bytes 835592 | tf_op jit(solution)/shard_map/ppermute | solution.py:40
  43.1 25.3 %collective-permute-start.3 = (bf16[2,2,64,2176]{3,2,1,0:T(8,128)(2,1)S(1)}, bf16[2,2,64,2176]{3,2,1,0:T(8,128)(2,1)S(1)}, u32[]{:S(2)}, u32[]{:S(2)}) collective-permute-start(bf16[2,2,64,2176]{3,2,1,0:T(8,128)(2,1)S(1)} %get-tuple-element.66), channel_id=1, source_target_pairs={{0,8},{1,9},{2,10},{3,11},{4,12},{5,13},{6,14},{7,15},{8,0},{9,1},... | collective-permute-start | bytes 3342344 | tf_op jit(solution)/shard_map/ppermute | solution.py:40
  68.6 27.6 %collective-permute-start.4 = (bf16[2,2,2,64,2176]{4,3,2,1,0:T(8,128)(2,1)S(1)}, bf16[2,2,2,64,2176]{4,3,2,1,0:T(8,128)(2,1)}, u32[]{:S(2)}, u32[]{:S(2)}) collective-permute-start(bf16[2,2,2,64,2176]{4,3,2,1,0:T(8,128)(2,1)S(1)} %pad_maximum_fusion.1.refs_0_), channel_id=1, source_target_pairs={{0,2},{1,5},{2,0},{3,7},{4,6},{5,1},{6,4},{7,3},{8,10},{9,13},{10,... | collective-permute-start | bytes 6684680 | tf_op jit(solution)/shard_map/ppermute | solution.py:40
  70.0 27.6 %collective-permute-start.5 = (bf16[2,2,2,64,2176]{4,3,2,1,0:T(8,128)(2,1)S(1)}, bf16[2,2,2,64,2176]{4,3,2,1,0:T(8,128)(2,1)}, u32[]{:S(2)}, u32[]{:S(2)}) collective-permute-start(bf16[2,2,2,64,2176]{4,3,2,1,0:T(8,128)(2,1)S(1)} %pad_maximum_fusion.1.refs_0_), channel_id=1, source_target_pairs={{0,1},{1,0},{2,3},{3,2},{4,5},{5,4},{6,7},{7,6},{8,9},{9,8},{10,11... | collective-permute-start | bytes 6684680 | tf_op jit(solution)/shard_map/ppermute | solution.py:40
  121.6 216.3 %all-gather.3.cloned.1.call-start = ((), (), s32[]{:S(2)}) async-start(), calls=%async_computation.2 | async-start | bytes 5242880 | tf_op jit(solution)/shard_map/all_gather | solution.py:444
  123.2 21.3 %collective-permute-start.20 = (bf16[256,512]{1,0:T(8,128)(2,1)S(1)}, bf16[256,512]{1,0:T(8,128)(2,1)S(1)}, u32[]{:S(2)}, u32[]{:S(2)}) collective-permute-start(bf16[256,512]{1,0:T(8,128)(2,1)S(1)} %maximum_select_fusion.2), channel_id=1, source_target_pairs={{0,16},{1,17},{2,18},{3,19},{4,20},{5,21},{6,22},{7,23},{8,24},{9,... | collective-permute-start | bytes 786440 | tf_op jit(solution)/shard_map/ppermute | solution.py:40
  126.1 29.7 %collective-permute-start.7 = (bf16[64,2048]{1,0:T(8,128)(2,1)S(1)}, bf16[64,2048]{1,0:T(8,128)(2,1)S(1)}, u32[]{:S(2)}, u32[]{:S(2)}) collective-permute-start(bf16[64,2048]{1,0:T(8,128)(2,1)S(1)} %get-tuple-element.81), channel_id=1, source_target_pairs={{0,16},{1,17},{2,18},{3,19},{4,20},{5,21},{6,22},{7,23},{8,24},{9,... | collective-permute-start | bytes 786440 | tf_op jit(solution)/shard_map/ppermute | solution.py:40
  144.6 17.8 %collective-permute-start.21 = (bf16[2,256,512]{2,1,0:T(8,128)(2,1)S(1)}, bf16[2,256,512]{2,1,0:T(8,128)(2,1)S(1)}, u32[]{:S(2)}, u32[]{:S(2)}) collective-permute-start(bf16[2,256,512]{2,1,0:T(8,128)(2,1)S(1)} %get-tuple-element.93), channel_id=1, source_target_pairs={{0,4},{1,3},{2,6},{3,1},{4,0},{5,7},{6,2},{7,5},{8,12},{9,11},{10,... | collective-permute-start | bytes 1572872 | tf_op jit(solution)/shard_map/ppermute | solution.py:40
  146.0 14.8 %collective-permute-start.13 = (bf16[64,2048]{1,0:T(8,128)(2,1)S(1)}, bf16[64,2048]{1,0:T(8,128)(2,1)S(1)}, u32[]{:S(2)}, u32[]{:S(2)}) collective-permute-start(bf16[64,2048]{1,0:T(8,128)(2,1)S(1)} %get-tuple-element.80), channel_id=1, source_target_pairs={{0,16},{1,17},{2,18},{3,19},{4,20},{5,21},{6,22},{7,23},{8,24},{9,... | collective-permute-start | bytes 786440 | tf_op jit(solution)/shard_map/ppermute | solution.py:40
  160.8 9.9 %collective-permute-start.14 = (bf16[2,64,2048]{2,1,0:T(8,128)(2,1)S(1)}, bf16[2,64,2048]{2,1,0:T(8,128)(2,1)S(1)}, u32[]{:S(2)}, u32[]{:S(2)}) collective-permute-start(bf16[2,64,2048]{2,1,0:T(8,128)(2,1)S(1)} %get-tuple-element.95), channel_id=1, source_target_pairs={{0,4},{1,3},{2,6},{3,1},{4,0},{5,7},{6,2},{7,5},{8,12},{9,11},{10,... | collective-permute-start | bytes 1572872 | tf_op jit(solution)/shard_map/ppermute | solution.py:40
  162.5 26.1 %collective-permute-start.22 = (bf16[2,2,256,512]{3,2,1,0:T(8,128)(2,1)S(1)}, bf16[2,2,256,512]{3,2,1,0:T(8,128)(2,1)S(1)}, u32[]{:S(2)}, u32[]{:S(2)}) collective-permute-start(bf16[2,2,256,512]{3,2,1,0:T(8,128)(2,1)S(1)} %get-tuple-element.69), channel_id=1, source_target_pairs={{0,8},{1,9},{2,10},{3,11},{4,12},{5,13},{6,14},{7,15},{8,0},{9,1},... | collective-permute-start | bytes 3145736 | tf_op jit(solution)/shard_map/ppermute | solution.py:40
  165.2 45.9 %collective-permute-start.9 = (bf16[2,2,64,2048]{3,2,1,0:T(8,128)(2,1)S(1)}, bf16[2,2,64,2048]{3,2,1,0:T(8,128)(2,1)S(1)}, u32[]{:S(2)}, u32[]{:S(2)}) collective-permute-start(bf16[2,2,64,2048]{3,2,1,0:T(8,128)(2,1)S(1)} %get-tuple-element.75), channel_id=1, source_target_pairs={{0,8},{1,9},{2,10},{3,11},{4,12},{5,13},{6,14},{7,15},{8,0},{9,1},... | collective-permute-start | bytes 3145736 | tf_op jit(solution)/shard_map/ppermute | solution.py:40
  170.8 61.3 %collective-permute-start.15 = (bf16[2,2,64,2048]{3,2,1,0:T(8,128)(2,1)S(1)}, bf16[2,2,64,2048]{3,2,1,0:T(8,128)(2,1)S(1)}, u32[]{:S(2)}, u32[]{:S(2)}) collective-permute-start(bf16[2,2,64,2048]{3,2,1,0:T(8,128)(2,1)S(1)} %get-tuple-element.71), channel_id=1, source_target_pairs={{0,8},{1,9},{2,10},{3,11},{4,12},{5,13},{6,14},{7,15},{8,0},{9,1},... | collective-permute-start | bytes 3145736 | tf_op jit(solution)/shard_map/ppermute | solution.py:40
  188.9 50.1 %collective-permute-start.24 = (bf16[2,2,2,256,512]{4,3,2,1,0:T(8,128)(2,1)S(1)}, bf16[2,2,2,256,512]{4,3,2,1,0:T(8,128)(2,1)}, u32[]{:S(2)}, u32[]{:S(2)}) collective-permute-start(bf16[2,2,2,256,512]{4,3,2,1,0:T(8,128)(2,1)S(1)} %pad_maximum_fusion.4.refs_0_), channel_id=1, source_target_pairs={{0,1},{1,0},{2,3},{3,2},{4,5},{5,4},{6,7},{7,6},{8,9},{9,8},{10,11... | collective-permute-start | bytes 6291464 | tf_op jit(solution)/shard_map/ppermute | solution.py:40
  188.9 46.0 %collective-permute-start.23 = (bf16[2,2,2,256,512]{4,3,2,1,0:T(8,128)(2,1)S(1)}, bf16[2,2,2,256,512]{4,3,2,1,0:T(8,128)(2,1)}, u32[]{:S(2)}, u32[]{:S(2)}) collective-permute-start(bf16[2,2,2,256,512]{4,3,2,1,0:T(8,128)(2,1)S(1)} %pad_maximum_fusion.4.refs_0_), channel_id=1, source_target_pairs={{0,2},{1,5},{2,0},{3,7},{4,6},{5,1},{6,4},{7,3},{8,10},{9,13},{10,... | collective-permute-start | bytes 6291464 | tf_op jit(solution)/shard_map/ppermute | solution.py:40
  212.6 26.4 %collective-permute-start.10 = (bf16[2,2,2,64,2048]{4,3,2,1,0:T(8,128)(2,1)}, bf16[2,2,2,64,2048]{4,3,2,1,0:T(8,128)(2,1)}, u32[]{:S(2)}, u32[]{:S(2)}) collective-permute-start(bf16[2,2,2,64,2048]{4,3,2,1,0:T(8,128)(2,1)} %pad_maximum_fusion.2.refs_0_), channel_id=1, source_target_pairs={{0,2},{1,5},{2,0},{3,7},{4,6},{5,1},{6,4},{7,3},{8,10},{9,13},{10,... | collective-permute-start | bytes 6291464 | tf_op jit(solution)/shard_map/ppermute | solution.py:40
  233.7 50.2 %collective-permute-start.16 = (bf16[2,2,2,64,2048]{4,3,2,1,0:T(8,128)(2,1)}, bf16[2,2,2,64,2048]{4,3,2,1,0:T(8,128)(2,1)}, u32[]{:S(2)}, u32[]{:S(2)}) collective-permute-start(bf16[2,2,2,64,2048]{4,3,2,1,0:T(8,128)(2,1)} %pad_maximum_fusion.3.refs_0_), channel_id=1, source_target_pairs={{0,2},{1,5},{2,0},{3,7},{4,6},{5,1},{6,4},{7,3},{8,10},{9,13},{10,... | collective-permute-start | bytes 6291464 | tf_op jit(solution)/shard_map/ppermute | solution.py:40
  234.0 518.1 %reduce-scatter.5.cloned.1.call-start = ((), (), s32[]{:S(2)}) async-start(), calls=%async_computation.5 | async-start | bytes 5242880 | tf_op jit(solution)/shard_map/reduce_scatter | solution.py:506
  234.1 58.1 %collective-permute-start.11 = (bf16[2,2,2,64,2048]{4,3,2,1,0:T(8,128)(2,1)}, bf16[2,2,2,64,2048]{4,3,2,1,0:T(8,128)(2,1)}, u32[]{:S(2)}, u32[]{:S(2)}) collective-permute-start(bf16[2,2,2,64,2048]{4,3,2,1,0:T(8,128)(2,1)} %pad_maximum_fusion.2.refs_0_), channel_id=1, source_target_pairs={{0,1},{1,0},{2,3},{3,2},{4,5},{5,4},{6,7},{7,6},{8,9},{9,8},{10,11... | collective-permute-start | bytes 6291464 | tf_op jit(solution)/shard_map/ppermute | solution.py:40
  234.9 49.9 %collective-permute-start.25 = (bf16[2,2,2,256,512]{4,3,2,1,0:T(8,128)(2,1)}, bf16[2,2,2,256,512]{4,3,2,1,0:T(8,128)(2,1)}, u32[]{:S(2)}, u32[]{:S(2)}) collective-permute-start(bf16[2,2,2,256,512]{4,3,2,1,0:T(8,128)(2,1)} %collective-permute-done.23.refs_1_), channel_id=1, source_target_pairs={{0,1},{1,0},{2,3},{3,2},{4,5},{5,4},{6,7},{7,6},{8,9},{9,8},{10,11... | collective-permute-start | bytes 6291464 | tf_op jit(solution)/shard_map/ppermute | solution.py:40
  239.0 53.2 %collective-permute-start.12 = (bf16[2,2,2,64,2048]{4,3,2,1,0:T(8,128)(2,1)}, bf16[2,2,2,64,2048]{4,3,2,1,0:T(8,128)(2,1)}, u32[]{:S(2)}, u32[]{:S(2)}) collective-permute-start(bf16[2,2,2,64,2048]{4,3,2,1,0:T(8,128)(2,1)} %collective-permute-done.10.refs_1_), channel_id=1, source_target_pairs={{0,1},{1,0},{2,3},{3,2},{4,5},{5,4},{6,7},{7,6},{8,9},{9,8},{10,11... | collective-permute-start | bytes 6291464 | tf_op jit(solution)/shard_map/ppermute | solution.py:40
  239.0 60.7 %collective-permute-start.17 = (bf16[2,2,2,64,2048]{4,3,2,1,0:T(8,128)(2,1)}, bf16[2,2,2,64,2048]{4,3,2,1,0:T(8,128)(2,1)S(1)}, u32[]{:S(2)}, u32[]{:S(2)}) collective-permute-start(bf16[2,2,2,64,2048]{4,3,2,1,0:T(8,128)(2,1)} %pad_maximum_fusion.3.refs_0_), channel_id=1, source_target_pairs={{0,1},{1,0},{2,3},{3,2},{4,5},{5,4},{6,7},{7,6},{8,9},{9,8},{10,11... | collective-permute-start | bytes 6291464 | tf_op jit(solution)/shard_map/ppermute | solution.py:40
  283.9 15.8 %collective-permute-start.18 = (bf16[2,2,2,64,2048]{4,3,2,1,0:T(8,128)(2,1)}, bf16[2,2,2,64,2048]{4,3,2,1,0:T(8,128)(2,1)}, u32[]{:S(2)}, u32[]{:S(2)}) collective-permute-start(bf16[2,2,2,64,2048]{4,3,2,1,0:T(8,128)(2,1)} %collective-permute-done.16.refs_1_), channel_id=1, source_target_pairs={{0,1},{1,0},{2,3},{3,2},{4,5},{5,4},{6,7},{7,6},{8,9},{9,8},{10,11... | collective-permute-start | bytes 6291464 | tf_op jit(solution)/shard_map/ppermute | solution.py:40
  503.2 249.0 %reduce-scatter.3.cloned.1.call-start = ((), (), s32[]{:S(2)}) async-start(), calls=%async_computation.4 | async-start | bytes 5242880 | tf_op jit(solution)/shard_map/reduce_scatter | solution.py:503
  532.1 134.6 %collective-permute-start.26 = (bf16[2,128,1024]{2,1,0:T(8,128)(2,1)}, bf16[2,128,1024]{2,1,0:T(8,128)(2,1)}, u32[]{:S(2)}, u32[]{:S(2)}) collective-permute-start(bf16[2,128,1024]{2,1,0:T(8,128)(2,1)} %fusion.117), channel_id=1, source_target_pairs={{0,1},{1,0},{2,3},{3,2},{4,5},{5,4},{6,7},{7,6},{8,9},{9,8},{10,11... | collective-permute-start | bytes 1572872 | tf_op jit(solution)/shard_map/ppermute | solution.py:380
  545.8 77.2 %collective-permute-start.40 = (bf16[2,2,2,2,64,2048]{5,4,3,2,1,0:T(8,128)(2,1)}, bf16[2,2,2,2,64,2048]{5,4,3,2,1,0:T(8,128)(2,1)}, u32[]{:S(2)}, u32[]{:S(2)}) collective-permute-start(bf16[2,2,2,2,64,2048]{5,4,3,2,1,0:T(8,128)(2,1)} %wgrad.13), channel_id=1, source_target_pairs={{0,1},{1,0},{2,3},{3,2},{4,5},{5,4},{6,7},{7,6},{8,9},{9,8},{10,11... | collective-permute-start | bytes 12582920 | tf_op jit(solution)/shard_map/ppermute | solution.py:40
  552.5 82.3 %collective-permute-start.46 = (bf16[2,2,2,2,256,512]{5,4,3,2,1,0:T(8,128)(2,1)}, bf16[2,2,2,2,256,512]{5,4,3,2,1,0:T(8,128)(2,1)}, u32[]{:S(2)}, u32[]{:S(2)}) collective-permute-start(bf16[2,2,2,2,256,512]{5,4,3,2,1,0:T(8,128)(2,1)} %wgrad.15), channel_id=1, source_target_pairs={{0,1},{1,0},{2,3},{3,2},{4,5},{5,4},{6,7},{7,6},{8,9},{9,8},{10,11... | collective-permute-start | bytes 12582920 | tf_op jit(solution)/shard_map/ppermute | solution.py:40
  561.1 147.5 %collective-permute-start.34 = (bf16[2,2,2,2,64,2560]{5,4,3,2,1,0:T(8,128)(2,1)}, bf16[2,2,2,2,64,2560]{5,4,3,2,1,0:T(8,128)(2,1)}, u32[]{:S(2)}, u32[]{:S(2)}) collective-permute-start(bf16[2,2,2,2,64,2560]{5,4,3,2,1,0:T(8,128)(2,1)} %wgrad.11), channel_id=1, source_target_pairs={{0,1},{1,0},{2,3},{3,2},{4,5},{5,4},{6,7},{7,6},{8,9},{9,8},{10,11... | collective-permute-start | bytes 15728648 | tf_op jit(solution)/shard_map/ppermute | solution.py:40
  626.7 46.5 %collective-permute-start.41 = (bf16[2,2,2,64,2048]{4,3,2,1,0:T(8,128)(2,1)}, bf16[2,2,2,64,2048]{4,3,2,1,0:T(8,128)(2,1)}, u32[]{:S(2)}, u32[]{:S(2)}) collective-permute-start(bf16[2,2,2,64,2048]{4,3,2,1,0:T(8,128)(2,1)} %fusion.72), channel_id=1, source_target_pairs={{0,2},{1,5},{2,0},{3,7},{4,6},{5,1},{6,4},{7,3},{8,10},{9,13},{10,... | collective-permute-start | bytes 6291464 | tf_op jit(solution)/shard_map/ppermute | solution.py:40
  639.1 63.9 %collective-permute-start.47 = (bf16[2,2,2,256,512]{4,3,2,1,0:T(8,128)(2,1)}, bf16[2,2,2,256,512]{4,3,2,1,0:T(8,128)(2,1)}, u32[]{:S(2)}, u32[]{:S(2)}) collective-permute-start(bf16[2,2,2,256,512]{4,3,2,1,0:T(8,128)(2,1)} %fusion.73), channel_id=1, source_target_pairs={{0,2},{1,5},{2,0},{3,7},{4,6},{5,1},{6,4},{7,3},{8,10},{9,13},{10,... | collective-permute-start | bytes 6291464 | tf_op jit(solution)/shard_map/ppermute | solution.py:40
  668.3 47.2 %collective-permute-start.27 = (bf16[2,128,1024]{2,1,0:T(8,128)(2,1)S(1)}, bf16[2,128,1024]{2,1,0:T(8,128)(2,1)S(1)}, u32[]{:S(2)}, u32[]{:S(2)}) collective-permute-start(bf16[2,128,1024]{2,1,0:T(8,128)(2,1)S(1)} %add_convert_fusion.7), channel_id=1, source_target_pairs={{0,2},{1,3},{2,0},{3,1},{4,6},{5,7},{6,4},{7,5},{8,10},{9,11},{10,... | collective-permute-start | bytes 1572872 | tf_op jit(solution)/shard_map/ppermute | solution.py:380
  675.3 35.8 %collective-permute-start.42 = (bf16[2,2,64,2048]{3,2,1,0:T(8,128)(2,1)S(1)}, bf16[2,2,64,2048]{3,2,1,0:T(8,128)(2,1)S(1)}, u32[]{:S(2)}, u32[]{:S(2)}) collective-permute-start(bf16[2,2,64,2048]{3,2,1,0:T(8,128)(2,1)S(1)} %fusion.75), channel_id=1, source_target_pairs={{0,8},{1,9},{2,10},{3,11},{4,12},{5,13},{6,14},{7,15},{8,0},{9,1},... | collective-permute-start | bytes 3145736 | tf_op jit(solution)/shard_map/ppermute | solution.py:40
  705.0 19.2 %collective-permute-start.48 = (bf16[2,2,256,512]{3,2,1,0:T(8,128)(2,1)S(1)}, bf16[2,2,256,512]{3,2,1,0:T(8,128)(2,1)S(1)}, u32[]{:S(2)}, u32[]{:S(2)}) collective-permute-start(bf16[2,2,256,512]{3,2,1,0:T(8,128)(2,1)S(1)} %fusion.74), channel_id=1, source_target_pairs={{0,8},{1,9},{2,10},{3,11},{4,12},{5,13},{6,14},{7,15},{8,0},{9,1},... | collective-permute-start | bytes 3145736 | tf_op jit(solution)/shard_map/ppermute | solution.py:40
  711.1 35.1 %collective-permute-start.35 = (bf16[2,2,2,64,2560]{4,3,2,1,0:T(8,128)(2,1)S(1)}, bf16[2,2,2,64,2560]{4,3,2,1,0:T(8,128)(2,1)S(1)}, u32[]{:S(2)}, u32[]{:S(2)}) collective-permute-start(bf16[2,2,2,64,2560]{4,3,2,1,0:T(8,128)(2,1)S(1)} %fusion.50), channel_id=1, source_target_pairs={{0,2},{1,5},{2,0},{3,7},{4,6},{5,1},{6,4},{7,3},{8,10},{9,13},{10,... | collective-permute-start | bytes 7864328 | tf_op jit(solution)/shard_map/ppermute | solution.py:40
  712.7 15.9 %collective-permute-start.43 = (bf16[2,64,2048]{2,1,0:T(8,128)(2,1)S(1)}, bf16[2,64,2048]{2,1,0:T(8,128)(2,1)S(1)}, u32[]{:S(2)}, u32[]{:S(2)}) collective-permute-start(bf16[2,64,2048]{2,1,0:T(8,128)(2,1)S(1)} %fusion.125), channel_id=1, source_target_pairs={{0,4},{1,3},{2,6},{3,1},{4,0},{5,7},{6,2},{7,5},{8,12},{9,11},{10,... | collective-permute-start | bytes 1572872 | tf_op jit(solution)/shard_map/ppermute | solution.py:40
  725.7 10.1 %collective-permute-start.49 = (bf16[2,256,512]{2,1,0:T(8,128)(2,1)S(1)}, bf16[2,256,512]{2,1,0:T(8,128)(2,1)S(1)}, u32[]{:S(2)}, u32[]{:S(2)}) collective-permute-start(bf16[2,256,512]{2,1,0:T(8,128)(2,1)S(1)} %fusion.123), channel_id=1, source_target_pairs={{0,4},{1,3},{2,6},{3,1},{4,0},{5,7},{6,2},{7,5},{8,12},{9,11},{10,... | collective-permute-start | bytes 1572872 | tf_op jit(solution)/shard_map/ppermute | solution.py:40
  730.2 20.3 %collective-permute-start.44 = (bf16[64,2048]{1,0:T(8,128)(2,1)S(1)}, bf16[64,2048]{1,0:T(8,128)(2,1)S(1)}, u32[]{:S(2)}, u32[]{:S(2)}) collective-permute-start(bf16[64,2048]{1,0:T(8,128)(2,1)S(1)} %fusion.138), channel_id=1, source_target_pairs={{0,16},{1,17},{2,18},{3,19},{4,20},{5,21},{6,22},{7,23},{8,24},{9,... | collective-permute-start | bytes 786440 | tf_op jit(solution)/shard_map/ppermute | solution.py:40
  738.0 37.6 %collective-permute-start.50 = (bf16[256,512]{1,0:T(8,128)(2,1)}, bf16[256,512]{1,0:T(8,128)(2,1)}, u32[]{:S(2)}, u32[]{:S(2)}) collective-permute-start(bf16[256,512]{1,0:T(8,128)(2,1)} %fusion.139), channel_id=1, source_target_pairs={{0,16},{1,17},{2,18},{3,19},{4,20},{5,21},{6,22},{7,23},{8,24},{9,... | collective-permute-start | bytes 786440 | tf_op jit(solution)/shard_map/ppermute | solution.py:40
  750.0 27.0 %collective-permute-start.36 = (bf16[2,2,64,2560]{3,2,1,0:T(8,128)(2,1)}, bf16[2,2,64,2560]{3,2,1,0:T(8,128)(2,1)}, u32[]{:S(2)}, u32[]{:S(2)}) collective-permute-start(bf16[2,2,64,2560]{3,2,1,0:T(8,128)(2,1)} %fusion.51), channel_id=1, source_target_pairs={{0,8},{1,9},{2,10},{3,11},{4,12},{5,13},{6,14},{7,15},{8,0},{9,1},... | collective-permute-start | bytes 3932168 | tf_op jit(solution)/shard_map/ppermute | solution.py:40
  752.1 36.5 %collective-permute-start.45 = (f32[32,2048]{1,0:T(8,128)}, f32[32,2048]{1,0:T(8,128)S(1)}, u32[]{:S(2)}, u32[]{:S(2)}) collective-permute-start(f32[32,2048]{1,0:T(8,128)} %constant_dynamic-slice_fusion.1), channel_id=1, source_target_pairs={{0,1},{1,0},{2,3},{3,2},{4,5},{5,4},{6,7},{7,6},{8,9},{9,8},{10,11... | collective-permute-start | bytes 786440 | tf_op jit(solution)/shard_map/ppermute | solution.py:40
  775.1 16.6 %collective-permute-start.28 = (bf16[2,2,2,2,64,1664]{5,4,3,2,1,0:T(8,128)(2,1)}, bf16[2,2,2,2,64,1664]{5,4,3,2,1,0:T(8,128)(2,1)S(1)}, u32[]{:S(2)}, u32[]{:S(2)}) collective-permute-start(bf16[2,2,2,2,64,1664]{5,4,3,2,1,0:T(8,128)(2,1)} %wgrad.9), channel_id=1, source_target_pairs={{0,1},{1,0},{2,3},{3,2},{4,5},{5,4},{6,7},{7,6},{8,9},{9,8},{10,11... | collective-permute-start | bytes 10223624 | tf_op jit(solution)/shard_map/ppermute | solution.py:40
  776.9 39.1 %collective-permute-start.51 = (f32[128,512]{1,0:T(8,128)S(1)}, f32[128,512]{1,0:T(8,128)S(1)}, u32[]{:S(2)}, u32[]{:S(2)}) collective-permute-start(f32[128,512]{1,0:T(8,128)S(1)} %constant_dynamic-slice_fusion), channel_id=1, source_target_pairs={{0,1},{1,0},{2,3},{3,2},{4,5},{5,4},{6,7},{7,6},{8,9},{9,8},{10,11... | collective-permute-start | bytes 786440 | tf_op jit(solution)/shard_map/ppermute | solution.py:40
  779.0 10.7 %collective-permute-start.37 = (bf16[2,64,2560]{2,1,0:T(8,128)(2,1)S(1)}, bf16[2,64,2560]{2,1,0:T(8,128)(2,1)S(1)}, u32[]{:S(2)}, u32[]{:S(2)}) collective-permute-start(bf16[2,64,2560]{2,1,0:T(8,128)(2,1)S(1)} %fusion.114), channel_id=1, source_target_pairs={{0,4},{1,3},{2,6},{3,1},{4,0},{5,7},{6,2},{7,5},{8,12},{9,11},{10,... | collective-permute-start | bytes 1966088 | tf_op jit(solution)/shard_map/ppermute | solution.py:40
  792.2 21.9 %collective-permute-start.29 = (bf16[2,2,2,64,1664]{4,3,2,1,0:T(8,128)(2,1)S(1)}, bf16[2,2,2,64,1664]{4,3,2,1,0:T(8,128)(2,1)S(1)}, u32[]{:S(2)}, u32[]{:S(2)}) collective-permute-start(bf16[2,2,2,64,1664]{4,3,2,1,0:T(8,128)(2,1)S(1)} %fusion.93), channel_id=1, source_target_pairs={{0,2},{1,5},{2,0},{3,7},{4,6},{5,1},{6,4},{7,3},{8,10},{9,13},{10,... | collective-permute-start | bytes 5111816 | tf_op jit(solution)/shard_map/ppermute | solution.py:40
  793.4 17.4 %collective-permute-start.38 = (bf16[64,2560]{1,0:T(8,128)(2,1)S(1)}, bf16[64,2560]{1,0:T(8,128)(2,1)S(1)}, u32[]{:S(2)}, u32[]{:S(2)}) collective-permute-start(bf16[64,2560]{1,0:T(8,128)(2,1)S(1)} %fusion.135), channel_id=1, source_target_pairs={{0,16},{1,17},{2,18},{3,19},{4,20},{5,21},{6,22},{7,23},{8,24},{9,... | collective-permute-start | bytes 983048 | tf_op jit(solution)/shard_map/ppermute | solution.py:40
  814.4 19.9 %collective-permute-start.30 = (bf16[2,2,64,1664]{3,2,1,0:T(8,128)(2,1)S(1)}, bf16[2,2,64,1664]{3,2,1,0:T(8,128)(2,1)S(1)}, u32[]{:S(2)}, u32[]{:S(2)}) collective-permute-start(bf16[2,2,64,1664]{3,2,1,0:T(8,128)(2,1)S(1)} %fusion.94), channel_id=1, source_target_pairs={{0,8},{1,9},{2,10},{3,11},{4,12},{5,13},{6,14},{7,15},{8,0},{9,1},... | collective-permute-start | bytes 2555912 | tf_op jit(solution)/shard_map/ppermute | solution.py:40
  843.1 9.9 %collective-permute-start.32 = (bf16[64,1664]{1,0:T(8,128)(2,1)S(1)}, bf16[64,1664]{1,0:T(8,128)(2,1)S(1)}, u32[]{:S(2)}, u32[]{:S(2)}) collective-permute-start(bf16[64,1664]{1,0:T(8,128)(2,1)S(1)} %fusion.140), channel_id=1, source_target_pairs={{0,16},{1,17},{2,18},{3,19},{4,20},{5,21},{6,22},{7,23},{8,24},{9,... | collective-permute-start | bytes 638984 | tf_op jit(solution)/shard_map/ppermute | solution.py:40
  (86 other events, 1053.4 us)
Sparse Core Ops, SparseCore 0:
  121.7 41.2 all-gather.4
  234.2 47.3 all-gather.2
  503.3 44.9 reduce-scatter.4
  605.9 54.7 reduce-scatter.2

commit v2 on v1

--- a/solution.py
+++ b/solution.py
@@ -79,17 +79,53 @@
     )
 
 
-def gather_chips(block):
-    far = far_count()
-    one = jnp.stack([block] + [hop_z1(block, k) for k in range(1, far)])
-    two = jnp.stack([one, hop_first(one)])
-    three = jnp.stack([two, hop_z0(two)])
-    four = hop_second(three)
-    return three, four, hop_core(three), hop_core(four)
+def after(value, *others):
+    return lax.optimization_barrier((value, *others))[0]
+
+
+class Line:
+    def __init__(self):
+        self.last = ()
+
+    def __call__(self, function, first, *rest):
+        if self.last:
+            first = after(first, *self.last)
+        result = function(first, *rest)
+        self.last = jax.tree.leaves(result)[:1]
+        return result
+
+
+class Gather:
+    def __init__(self, block):
+        self.sent = block
+
+    def far(self, line):
+        self.sent = line(lambda v: v + 0 if line.last else v, self.sent)
+        self.came = [hop_z1(self.sent, k) for k in range(1, far_count())]
+
+    def first(self, line):
+        self.sent = line(lambda c, s, *o: jnp.stack([s, *o, c]), self.came[-1], self.sent, *self.came[:-1])
+        self.came = hop_first(self.sent)
+
+    def near(self, line):
+        self.sent = line(lambda c, s: jnp.stack([s, c]), self.came, self.sent)
+        self.came = hop_z0(self.sent)
+
+    def second(self, line):
+        self.sent = line(lambda c, s: jnp.stack([s, c]), self.came, self.sent)
+        self.came = hop_second(self.sent)
+        self.sent_other = hop_core(self.sent)
+
+    def pair(self, line):
+        self.came = after(self.came, *line.last)
+        self.came_other = hop_core(self.came)
+
+    def pieces(self):
+        return self.came_other, self.sent, self.came, self.sent_other
 
 
 def assemble_kernel(widths, far, rows, spot_ref, *refs):
-    near_own, far_own, near_other, far_other = refs[:4]
+    far_other, near_own, far_own, near_other = refs[:4]
     outs = refs[4 : 4 + len(widths)]
     sem = refs[-1]
     c, mx, my, mz0, mz1 = (spot_ref[i] for i in range(5))
@@ -204,43 +240,61 @@
     return values.astype(F32)
 
 
-def scatter_chips(terms):
-    far = far_count()
-    other = wgrad(terms, "other")
-    came0 = hop_core(other)
-    own = wgrad(terms, "own")
-    came1 = hop_second((wide(own[1]) + wide(came0[1])).astype(BF))
-    came2 = hop_z0((wide(own[0, 1]) + wide(came0[0, 1]) + wide(came1[1])).astype(BF))
-    came3 = hop_first(
-        (wide(own[0, 0, 1]) + wide(came0[0, 0, 1]) + wide(came1[0, 1]) + wide(came2[1])).astype(BF)
-    )
-    kept = (
-        wide(own[0, 0, 0])
-        + wide(came0[0, 0, 0])
-        + wide(came1[0, 0])
-        + wide(came2[0])
-        + wide(came3)
-    )
-    low = kept.astype(BF)
-    total = kept[0]
-    for k in range(1, far):
-        total = total + wide(hop_z1(low[k], k))
-    c = place() % 2
-    rows = total.shape[0] // 2
-    mine = lax.dynamic_slice_in_dim(total, c * rows, rows, 0)
-    came = hop_core(lax.dynamic_slice_in_dim(total, (1 - c) * rows, rows, 0))
-    left = jnp.where(c == 0, mine, came)
-    right = jnp.where(c == 0, came, mine)
-    results, start = [], 0
-    for term in terms:
-        width = term[-1].shape[1] // 2
-        results.append(
-            jnp.concatenate(
-                [left[:, start : start + width], right[:, start : start + width]], axis=1
-            )
-        )
-        start += width
-    return results
+class Scatter:
+    def __init__(self, line, terms):
+        self.widths = [t[-1].shape[1] // 2 for t in terms]
+
+        def run(core):
+            return line(lambda f: wgrad([(f, *terms[0][1:]), *terms[1:]], core), terms[0][0])
+
+        self.came0 = hop_core(run("other"))
+        self.own = run("own")
+
+    def second(self, line):
+        sent = line(lambda c, o: (wide(o[1]) + wide(c[1])).astype(BF), self.came0, self.own)
+        self.came1 = hop_second(sent)
+
+    def near(self, line):
+        def add(c1, c0, o):
+            return (wide(o[0, 1]) + wide(c0[0, 1]) + wide(c1[1])).astype(BF)
+
+        self.came2 = hop_z0(line(add, self.came1, self.came0, self.own))
+
+    def first(self, line):
+        def add(c2, c1, c0, o):
+            return (wide(o[0, 0, 1]) + wide(c0[0, 0, 1]) + wide(c1[0, 1]) + wide(c2[1])).astype(BF)
+
+        self.came3 = hop_first(line(add, self.came2, self.came1, self.came0, self.own))
+
+    def far(self, line):
+        def add(c3, c2, c1, c0, o):
+            kept = wide(o[0, 0, 0]) + wide(c0[0, 0, 0]) + wide(c1[0, 0]) + wide(c2[0]) + wide(c3)
+            return kept.astype(BF), kept[0]
+
+        low, self.kept = line(add, self.came3, self.came2, self.came1, self.came0, self.own)
+        self.came4 = [hop_z1(low[k], k) for k in range(1, far_count())]
+
+    def close(self, line):
+        total = line(lambda c, t, *o: sum(map(wide, o), t + wide(c)), self.came4[-1], self.kept, *self.came4[:-1])
+        rows = total.shape[0] // 2
+        c = place() % 2
+        self.mine = lax.dynamic_slice_in_dim(total, c * rows, rows, 0)
+        self.theirs = hop_core(lax.dynamic_slice_in_dim(total, (1 - c) * rows, rows, 0))
+
+    def result(self, line):
+        c = place() % 2
+
+        def join(came, mine):
+            left = jnp.where(c == 0, mine, came)
+            right = jnp.where(c == 0, came, mine)
+            results, start = [], 0
+            for width in self.widths:
+                at = slice(start, start + width)
+                results.append(jnp.concatenate([left[:, at], right[:, at]], axis=1))
+                start += width
+            return results
+
+        return line(join, self.theirs, self.mine)
 
 
 def pack_small(vectors, bias):
@@ -297,65 +351,170 @@
     return grad_inputs, jnp.sum(grad_normed * unit, axis=(0, 1)), jnp.sum(grad_normed, axis=(0, 1))
 
 
-def gelu_exact(inputs):
-    return jax.nn.gelu(inputs, approximate=False)
-
-
-def split_heads(tensor):
-    return tensor.reshape(tensor.shape[0], tensor.shape[1], HEADS, tensor.shape[2] // HEADS)
-
-
-def attend(queries, key_rows, value_rows, allowed):
-    scaling = (queries.shape[2] // HEADS) ** (-0.5)
-    scores = (
-        jnp.einsum(
-            "iqhd,ikhd->ihqk",
-            split_heads(queries),
-            split_heads(key_rows),
-            preferred_element_type=F32,
-        )
-        * scaling
-    )
-    scores = jnp.where(allowed[:, None], scores, masked_score)
-    softened = jax.nn.softmax(scores, axis=-1)
-    attended = jnp.einsum(
-        "ihqk,ikhd->iqhd",
-        softened.astype(BF),
-        split_heads(value_rows),
-        preferred_element_type=F32,
-    )
-    return (attended.reshape(queries.shape).astype(BF), softened)
-
-
-def attend_back(queries, key_rows, value_rows, softened, grad_attended):
-    scaling = (queries.shape[2] // HEADS) ** (-0.5)
-    grad_heads = split_heads(grad_attended)
-    grad_soft = jnp.einsum(
-        "iqhd,ikhd->ihqk", grad_heads, split_heads(value_rows), preferred_element_type=F32
-    )
-    grad_values = jnp.einsum(
-        "ihqk,iqhd->ikhd", softened.astype(BF), grad_heads, preferred_element_type=F32
-    ).reshape(value_rows.shape)
-    grad_scores = (
-        softened * (grad_soft - jnp.sum(softened * grad_soft, axis=-1, keepdims=True))
-    ).astype(BF)
-    grad_queries = (
-        jnp.einsum(
-            "ihqk,ikhd->iqhd", grad_scores, split_heads(key_rows), preferred_element_type=F32
-        ).reshape(queries.shape)
-        * scaling
-    )
-    grad_keys = (
-        jnp.einsum(
-            "ihqk,iqhd->ikhd", grad_scores, split_heads(queries), preferred_element_type=F32
-        ).reshape(key_rows.shape)
-        * scaling
-    )
-    return (grad_queries, grad_keys, grad_values)
+def shifts(info_ref, kind, block):
+    if kind == "length" or block == 0:
+        return None
+    me = info_ref[0]
+    return jnp.where((me ^ block) < me, 0.0, -masked_score).astype(F32)
+
+def allowed_keys(info_ref, kind, item, span, count):
+    shape = (span, count)
+    row = lax.broadcasted_iota(jnp.int32, shape, 0)
+    if kind == "length":
+        return row < info_ref[item]
+    return row <= lax.broadcasted_iota(jnp.int32, shape, 1)
+
+def attend_kernel(kind, info_ref, q_ref, k_ref, v_ref, o_ref, lse_ref):
+    blocks, _, span, wide_lanes = k_ref.shape
+    count = q_ref.shape[2]
+    lanes = 128
+    head = lanes // 2
+    low_lane = lax.broadcasted_iota(jnp.int32, (count, lanes), 1) < head
+    allowed = allowed_keys(info_ref, kind, pl.program_id(0), span, count)
+    outside = [shifts(info_ref, kind, j) for j in range(blocks)]
+    for pair in range(wide_lanes // lanes):
+        at = slice(pair * lanes, (pair + 1) * lanes)
+        values_t = v_ref[:, :, :, at].reshape(blocks * span, lanes).T
+        queries = q_ref[0, 0, :, at] * (head ** -0.5)
+        outs = []
+        for h in range(2):
+            mine = jnp.where(low_lane if h == 0 else ~low_lane, queries, 0).astype(BF)
+            scores = [
+                lax.dot_general(k_ref[j, 0, :, at], mine, (((1,), (1,)), ((), ())), preferred_element_type=F32)
+                for j in range(blocks)
+            ]
+            scores[0] = jnp.where(allowed, scores[0], masked_score)
+            top = jnp.max(scores[0], axis=0, keepdims=True)
+            for j in range(1, blocks):
+                top = jnp.maximum(top, jnp.max(scores[j], axis=0, keepdims=True) - outside[j])
+            soft = [jnp.exp(scores[0] - top)]
+            soft += [jnp.exp(scores[j] - (top + outside[j])) for j in range(1, blocks)]
+            total = sum(jnp.sum(s, axis=0, keepdims=True) for s in soft)
+            lse_ref[0, pair, h : h + 1, :] = top + jnp.log(total)
+            low = jnp.concatenate([s.astype(BF) for s in soft], axis=0)
+            out = jnp.dot(values_t[h * head : (h + 1) * head], low, preferred_element_type=F32)
+            outs.append(out / total)
+        o_ref[0, :, at] = jnp.concatenate(outs, axis=0).T.astype(BF)
+
+def attend(kind, info, queries, q_at, keyed, k_at, valued, v_at, group=1):
+    blocks, items, span, _ = keyed.shape
+    count = queries.shape[2]
+    pairs = HEADS // 2
+    lanes = 128 * group
+    width = pairs * 128
+    return pl.pallas_call(
+        functools.partial(attend_kernel, kind),
+        out_shape=[jax.ShapeDtypeStruct((items, count, width), BF), jax.ShapeDtypeStruct((items, pairs, 2, count), F32)],
+        grid_spec=pltpu.PrefetchScalarGridSpec(
+            num_scalar_prefetch=1, grid=(items, pairs // group),
+            in_specs=[
+                pl.BlockSpec((1, 1, count, lanes), lambda i, p, s: (0, i, 0, p + q_at // lanes)),
+                pl.BlockSpec((blocks, 1, span, lanes), lambda i, p, s: (0, i, 0, p + k_at // lanes)),
+                pl.BlockSpec((blocks, 1, span, lanes), lambda i, p, s: (0, i, 0, p + v_at // lanes)),
+            ],
+            out_specs=[
+                pl.BlockSpec((1, count, lanes), lambda i, p, s: (i, 0, p)),
+                pl.BlockSpec((1, group, 2, count), lambda i, p, s: (i, p, 0, 0)),
+            ]),
+        compiler_params=pltpu.CompilerParams(vmem_limit_bytes=VMEM_LIMIT),
+        cost_estimate=pl.CostEstimate(flops=8*items*count*blocks*span*width, bytes_accessed=2*(2*items*count*width+2*items*blocks*span*width), transcendentals=items*HEADS*count*blocks*span),
+        name="attend",
+    )(info, queries, keyed, valued)
+
+def attend_back_kernel(kind, info_ref, q_ref, k_ref, v_ref, o_ref, lse_ref, do_ref, dq_ref, dk_ref, dv_ref):
+    blocks, _, span, wide_lanes = k_ref.shape
+    count = q_ref.shape[2]
+    lanes = 128
+    head = lanes // 2
+    scaling = head ** -0.5
+    low_lane = lax.broadcasted_iota(jnp.int32, (count, lanes), 1) < head
+    allowed = allowed_keys(info_ref, kind, pl.program_id(0), span, count)
+    outside = [shifts(info_ref, kind, j) for j in range(blocks)]
+    for pair in range(wide_lanes // lanes):
+        at = slice(pair * lanes, (pair + 1) * lanes)
+        keys_t = k_ref[:, :, :, at].reshape(blocks * span, lanes).T
+        queries = q_ref[0, 0, :, at] * scaling
+        grad = do_ref[0, :, at]
+        product_t = (grad.astype(F32) * o_ref[0, :, at].astype(F32)).T
+        grad_q, dk, dv = [], [0.0] * blocks, [0.0] * blocks
+        for h in range(2):
+            lane = low_lane if h == 0 else ~low_lane
+            mine = jnp.where(lane, queries, 0).astype(BF)
+            grad_mine = jnp.where(lane, grad, 0).astype(BF)
+            lse = lse_ref[0, pair, h : h + 1, :]
+            delta = jnp.sum(product_t[h * head : (h + 1) * head], axis=0, keepdims=True)
+            grads = []
+            for j in range(blocks):
+                scores = lax.dot_general(k_ref[j, 0, :, at], mine, (((1,), (1,)), ((), ())), preferred_element_type=F32)
+                if j == 0:
+                    soft = jnp.where(allowed, jnp.exp(scores - lse), 0.0)
+                else:
+                    soft = jnp.exp(scores - (lse + outside[j]))
+                grad_soft = lax.dot_general(v_ref[j, 0, :, at], grad_mine, (((1,), (1,)), ((), ())), preferred_element_type=F32)
+                grads.append((soft * (grad_soft - delta)).astype(BF))
+                dv[j] += jnp.dot(soft.astype(BF), grad_mine, preferred_element_type=F32)
+                dk[j] += jnp.dot(grads[j], mine, preferred_element_type=F32)
+            grad_scores = jnp.concatenate(grads, axis=0)
+            grad_q.append(jnp.dot(keys_t[h * head : (h + 1) * head], grad_scores, preferred_element_type=F32))
+        dq_ref[0, :, at] = (jnp.concatenate(grad_q, axis=0) * scaling).T.astype(BF)
+        for j in range(blocks):
+            dk_ref[j, 0, :, at] = dk[j].astype(BF)
+            dv_ref[j, 0, :, at] = dv[j].astype(BF)
+
+def attend_back(kind, info, queries, q_at, keyed, k_at, valued, v_at, attended, lse, grad, group=1):
+    blocks, items, span, _ = keyed.shape
+    count = queries.shape[2]
+    pairs = HEADS // 2
+    lanes = 128 * group
+    width = pairs * 128
+    row = pl.BlockSpec((1, count, lanes), lambda i, p, s: (i, 0, p))
+    key = pl.BlockSpec((blocks, 1, span, lanes), lambda i, p, s: (0, i, 0, p))
+    return pl.pallas_call(
+        functools.partial(attend_back_kernel, kind),
+        out_shape=[jax.ShapeDtypeStruct((items, count, width), BF)] + [jax.ShapeDtypeStruct((blocks, items, span, width), BF)]*2,
+        grid_spec=pltpu.PrefetchScalarGridSpec(
+            num_scalar_prefetch=1, grid=(items, pairs // group),
+            in_specs=[
+                pl.BlockSpec((1, 1, count, lanes), lambda i, p, s: (0, i, 0, p + q_at // lanes)),
+                pl.BlockSpec((blocks, 1, span, lanes), lambda i, p, s: (0, i, 0, p + k_at // lanes)),
+                pl.BlockSpec((blocks, 1, span, lanes), lambda i, p, s: (0, i, 0, p + v_at // lanes)),
+                row,
+                pl.BlockSpec((1, group, 2, count), lambda i, p, s: (i, p, 0, 0)),
+                row,
+            ],
+            out_specs=[row, key, key]),
+        compiler_params=pltpu.CompilerParams(vmem_limit_bytes=VMEM_LIMIT),
+        cost_estimate=pl.CostEstimate(flops=20*items*count*blocks*span*width, bytes_accessed=2*(4*items*count*width+4*items*blocks*span*width), transcendentals=items*HEADS*count*blocks*span),
+        name="attend_back",
+    )(info, queries, keyed, valued, attended, lse, grad)
+
+def up_kernel(x_ref, w_ref, b_ref, act_ref, slope_ref):
+    before = jnp.dot(x_ref[...], w_ref[...], preferred_element_type=F32) + b_ref[...]
+    phi = 0.5 + 0.5 * lax.erf(before * (0.5 ** 0.5))
+    act_ref[...] = (before * phi).astype(BF)
+    slope_ref[...] = (phi + before * (jnp.exp(-0.5 * before * before) * 0.3989422804014327)).astype(BF)
+
+def up_gelu(x, w, bias, block=512):
+    rows, depth = x.shape
+    hidden = w.shape[1]
+    return pl.pallas_call(
+        up_kernel,
+        out_shape=[jax.ShapeDtypeStruct((rows, hidden), BF)] * 2,
+        grid=(hidden // block,),
+        in_specs=[pl.BlockSpec((rows, depth), lambda n: (0, 0)), pl.BlockSpec((depth, block), lambda n: (0, n)), pl.BlockSpec((1, block), lambda n: (0, n))],
+        out_specs=[pl.BlockSpec((rows, block), lambda n: (0, n))]*2,
+        compiler_params=pltpu.CompilerParams(vmem_limit_bytes=VMEM_LIMIT),
+        cost_estimate=pl.CostEstimate(flops=2*rows*depth*hidden, bytes_accessed=2*(rows*depth+depth*hidden+2*rows*hidden), transcendentals=2*rows*hidden),
+        name="up_gelu",
+    )(x, w, bias)
 
 
 def flat(tensor):
     return tensor.reshape(-1, tensor.shape[-1])
+
+
+def flat_blocks(tensor):
+    return tensor.reshape(-1, *tensor.shape[2:])
 
 
 def dot(left, right):
@@ -368,21 +527,44 @@
     )
 
 
+def hop_seq(values, step):
+    size = lax.axis_size("seq")
+    return hop(values, lambda i: i // size * size + (i % size ^ step))
+
+
 def sum_seq(values):
     size = lax.axis_size("seq")
-    dp = lax.axis_size("dp")
     step = 1
     total = values.astype(BF)
     while step < size:
-        pairs = [
-            (d * size + s, d * size + (s ^ step)) for d in range(dp) for s in range(size)
-        ]
-        came = lax.ppermute(total, AXES, pairs)
-        total = wide(total) + wide(came)
+        total = wide(total) + wide(hop_seq(total, step))
         step *= 2
         if step < size:
             total = total.astype(BF)
     return total
+
+
+def gather_seq(values):
+    step = lax.axis_size("seq") // 2
+    blocks = {0: values}
+    while step:
+        blocks.update({j ^ step: hop_seq(b, step) for j, b in list(blocks.items())})
+        step //= 2
+    return jnp.stack([blocks[j] for j in range(len(blocks))])
+
+
+def scatter_seq(blocks):
+    size = lax.axis_size("seq")
+    blocks = {j: blocks[j] for j in range(size)}
+    step = 1
+    while step < size:
+        blocks = {
+            j: b + wide(hop_seq(blocks[j ^ step].astype(BF), step))
+            for j, b in blocks.items()
+            if not j & step
+        }
+        step *= 2
+    return blocks[0]
 
 
 def body(
@@ -412,103 +594,181 @@
         [self_gain, self_shift, cross_gain, cross_shift, feed_gain, feed_shift, down_bias], up_bias
     )
     groups = (
-        (self_in_weight, self_out_weight, small),
+        (
+            self_in_weight[:, :features],
+            self_in_weight[:, features : 2 * features],
+            self_in_weight[:, 2 * features :],
+            self_out_weight,
+            small,
+        ),
         (cross_query_weight, cross_memory_weight, cross_out_weight),
         (up_weight,),
     )
     shards = [s for g in groups for s in g]
     rows = chip_rows(shards)
-    blocks, start = [], 0
+    blocks, widths, start = [], [], 0
     for group in groups:
-        widths = tuple(s.shape[1] // 2 for s in group)
-        blocks.append((rows[:, start : start + sum(widths)], widths))
-        start += sum(widths)
-    blocks.append((chip_rows([down_weight]), (down_weight.shape[1] // 2,)))
-    gathered = [assemble(gather_chips(b), w) for b, w in blocks]
-    (self_in, self_out, small_full), (cross_query, cross_memory, cross_out), (up,), (down,) = (
-        gathered
+        widths.append(tuple(s.shape[1] // 2 for s in group))
+        blocks.append(rows[:, start : start + sum(widths[-1])])
+        start += sum(widths[-1])
+    blocks.append(chip_rows([down_weight]))
+    widths.append((down_weight.shape[1] // 2,))
+    ga, gb, gc, gd = (Gather(b) for b in blocks)
+    size = lax.axis_size("seq")
+    line = Line()
+    tokens_y = hop_seq(tokens, 2)
+    ga.far(line)
+    tokens_1 = hop_seq(tokens, 1)
+    ga.first(line)
+    gb.far(line)
+    ga.near(line)
+    gb.first(line)
+    gc.far(line)
+    tokens_y = after(tokens_y, *line.last)
+    tokens_3 = hop_seq(tokens_y, 1)
+    gd.far(line)
+    ga.second(line)
+    gc.first(line)
+    all_tokens = line(lambda a, b, c, d: jnp.stack([d, b, c, a]), tokens_3, tokens_1, tokens_y, tokens)
+    gb.near(line)
+    ga.pair(line)
+    gb.second(line)
+    gc.near(line)
+    (self_q, self_k, self_v, self_out, small_full) = line(
+        lambda *p: assemble(p, widths[0]), *ga.pieces()
     )
     vectors, up_offset = unpack_small(small_full, 7, k_bias)
     self_gain, self_shift, cross_gain, cross_shift, feed_gain, feed_shift, down_offset = (
         wide(v) for v in vectors
     )
     up_offset = wide(up_offset)
+    seq_place = lax.axis_index("seq").astype(jnp.int32)[None]
 
     inputs = wide(tokens)
-    normed1 = normalize(inputs, self_gain, self_shift).astype(BF)
-    projected = dot(normed1, self_in).astype(BF)
-    queries = projected[:, :, :features]
-    key_rows = projected[:, :, features : 2 * features]
-    value_rows = projected[:, :, 2 * features :]
-    all_keys = lax.all_gather(key_rows, "seq", axis=1, tiled=True)
-    all_values = lax.all_gather(value_rows, "seq", axis=1, tiled=True)
-    row_count = inputs.shape[1]
-    query_place = lax.axis_index("seq") * row_count + lax.iota(jnp.int32, row_count)
-    key_place = lax.iota(jnp.int32, all_keys.shape[1])
-    allowed = (key_place[None, :] <= query_place[:, None])[None]
-    attended1, softened1 = attend(queries, all_keys, all_values, allowed)
-    residual1 = inputs + dot(attended1, self_out)
-
-    normed2 = normalize(residual1, cross_gain, cross_shift).astype(BF)
-    cross_queries = dot(normed2, cross_query).astype(BF)
-    memory = dot(captions, cross_memory).astype(BF)
-    memory_keys, memory_values = memory[:, :, :features], memory[:, :, features:]
-    slot_index = lax.iota(jnp.int32, captions.shape[1])
-    visible = (slot_index[None, :] < caption_lengths[:, None])[:, None, :]
-    attended2, softened2 = attend(cross_queries, memory_keys, memory_values, visible)
-    residual2 = residual1 + dot(attended2, cross_out)
-
-    normed3 = normalize(residual2, feed_gain, feed_shift).astype(BF)
-    before = dot(normed3, up) + up_offset
-    activated = gelu_exact(before).astype(BF)
-    final = residual2 + dot(activated, down) + down_offset
-
-    grad_final = wide(cotangent)
-    grad_activated = dot_t(cotangent, down)
-    _, pullback = jax.vjp(gelu_exact, before)
-    grad_before = pullback(grad_activated)[0].astype(BF)
-    grad_normed3 = dot_t(grad_before, up)
-    grad_in3, grad_feed_gain, grad_feed_shift = norm_back(residual2, feed_gain, grad_normed3)
-    grad_up_bias = jnp.sum(wide(grad_before), axis=(0, 1))
-    grad_down_bias = jnp.sum(grad_final, axis=(0, 1))
-    (grad_down,) = scatter_chips([(flat(activated), flat(cotangent))])
-    (grad_up,) = scatter_chips([(flat(normed3), flat(grad_before))])
-    grad_second = grad_final + grad_in3
-
-    low2 = grad_second.astype(BF)
-    grad_attended2 = dot_t(low2, cross_out).astype(BF)
-    grad_cq, grad_mk, grad_mv = attend_back(
-        cross_queries, memory_keys, memory_values, softened2, grad_attended2
-    )
-    grad_memory = jnp.concatenate([grad_mk, grad_mv], axis=-1).astype(BF)
-    grad_captions = sum_seq(dot_t(grad_memory, cross_memory))
-    low_cq = grad_cq.astype(BF)
-    grad_normed2 = dot_t(low_cq, cross_query)
-    grad_in2, grad_cross_gain, grad_cross_shift = norm_back(residual1, cross_gain, grad_normed2)
-    grad_first = grad_second + grad_in2
-
-    low1 = grad_first.astype(BF)
-    grad_cross_query, grad_cross_memory, grad_cross_out, grad_self_out = scatter_chips(
+    normed1 = line(
+        lambda g, t, s: normalize(wide(t), g, s).astype(BF), self_gain, all_tokens, self_shift
+    )
+    normed1 = lax.optimization_barrier(normed1)
+    queries = line(lambda a, w: dot(a[0], w).astype(BF)[None], normed1, self_q)
+    key_rows = line(lambda a, w: dot(a, w).astype(BF), normed1, self_k)
+    value_rows = line(lambda a, w: dot(a, w).astype(BF), normed1, self_v)
+    gd.first(line)
+    gb.pair(line)
+    gc.second(line)
+    gd.near(line)
+    attended1, lse1 = line(
+        lambda q: attend("causal", seq_place, q, 0, key_rows, 0, value_rows, 0, 2), queries
+    )
+    gc.pair(line)
+    gd.second(line)
+    cross_query, cross_memory, cross_out = line(lambda *p: assemble(p, widths[1]), *gb.pieces())
+    residual1 = line(lambda a: inputs + dot(a, self_out), attended1)
+
+    normed2 = line(lambda r: normalize(r, cross_gain, cross_shift).astype(BF), residual1)
+    normed2 = lax.optimization_barrier(normed2)
+    cross_queries = line(lambda a: dot(a, cross_query).astype(BF)[None], normed2)
+    memory = line(lambda a: dot(a, cross_memory).astype(BF)[None], captions)
+    attended2, lse2 = line(
+        lambda q: attend("length", caption_lengths, q, 0, memory, 0, memory, features, 8),
+        cross_queries,
+    )
+    gd.pair(line)
+    residual2 = line(lambda a: residual1 + dot(a, cross_out), attended2)
+
+    normed3 = line(lambda r: normalize(r, feed_gain, feed_shift).astype(BF), residual2)
+    normed3 = lax.optimization_barrier(normed3)
+    (up,) = line(lambda *p: assemble(p, widths[2]), *gc.pieces())
+    activated, slope = line(lambda a: up_gelu(flat(a), up, up_offset[None]), normed3)
+    low3 = flat(cotangent)
+    s1 = Scatter(line, [(activated, low3)])
+    (down,) = line(lambda *p: assemble(p, widths[3]), *gd.pieces())
+    s1.second(line)
+
+    grad_before = line(lambda g: (dot_t(g, down) * wide(slope)).astype(BF), low3)
+    s2 = Scatter(line, [(flat(normed3), grad_before)])
+    s2.second(line)
+
+    def back3(g):
+        d = dot_t(g, up).reshape(inputs.shape)
+        grad_in, gain, shift = norm_back(residual2, feed_gain, d)
+        out = wide(cotangent) + grad_in
+        return out, out.astype(BF), gain, shift
+
+    grad_second, low2, grad_feed_gain, grad_feed_shift = line(back3, grad_before)
+
+    s1.near(line)
+    grad_attended2 = line(lambda g: dot_t(g, cross_out).astype(BF), low2)
+    grad_cq, grad_mk, grad_mv = line(
+        lambda g: attend_back(
+            "length", caption_lengths, cross_queries, 0, memory, 0, memory, features,
+            attended2, lse2, g, 8,
+        ),
+        grad_attended2,
+    )
+    grad_memory = line(lambda k, v: jnp.concatenate([k[0], v[0]], axis=-1), grad_mk, grad_mv)
+
+    def back2(g):
+        grad_in, gain, shift = norm_back(residual1, cross_gain, dot_t(g, cross_query))
+        out = grad_second + grad_in
+        return out, out.astype(BF), gain, shift
+
+    grad_first, low1, grad_cross_gain, grad_cross_shift = line(back2, grad_cq)
+    s1.first(line)
+    s2.near(line)
+    s3 = Scatter(
+        line,
         [
-            (flat(normed2), flat(low_cq)),
+            (flat(normed2), flat(grad_cq)),
             (flat(captions), flat(grad_memory)),
             (flat(attended2), flat(low2)),
             (flat(attended1), flat(low1)),
-        ]
-    )
-    grad_attended1 = dot_t(low1, self_out).astype(BF)
-    grad_q, grad_all_keys, grad_all_values = attend_back(
-        queries, all_keys, all_values, softened1, grad_attended1
-    )
-    grad_keys = lax.psum_scatter(
-        grad_all_keys.astype(BF), "seq", scatter_dimension=1, tiled=True
-    ).astype(BF)
-    grad_values = lax.psum_scatter(
-        grad_all_values.astype(BF), "seq", scatter_dimension=1, tiled=True
-    ).astype(BF)
-    grad_projected = jnp.concatenate([grad_q.astype(BF), grad_keys, grad_values], axis=-1)
-    grad_normed1 = dot_t(grad_projected, self_in)
-    grad_in1, grad_self_gain, grad_self_shift = norm_back(inputs, self_gain, grad_normed1)
+        ],
+    )
+    s1.far(line)
+    s3.second(line)
+    grad_attended1 = line(lambda g: dot_t(g, self_out).astype(BF), low1)
+    s2.first(line)
+    grad_q, grad_keys, grad_values = line(
+        lambda g: attend_back(
+            "causal", seq_place, queries, 0, key_rows, 0, value_rows, 0, attended1, lse1, g, 2
+        ),
+        grad_attended1,
+    )
+    s1.close(line)
+    s2.far(line)
+    s3.near(line)
+    s4 = Scatter(
+        line,
+        [
+            (flat(normed1[0]), flat(grad_q)),
+            (flat(normed1), flat(grad_keys)),
+            (flat(normed1), flat(grad_values)),
+        ],
+    )
+    s4.second(line)
+    grad_blocks = line(
+        lambda k: dot_t(k, self_k) + dot_t(grad_values, self_v), grad_keys
+    )
+    grad_blocks = jnp.concatenate([grad_blocks[:1] + dot_t(grad_q, self_q)[None], grad_blocks[1:]])
+    s3.first(line)
+    _, grad_self_gain, grad_self_shift = norm_back(
+        wide(flat_blocks(all_tokens)), self_gain, flat_blocks(grad_blocks)
+    )
+    (grad_down,) = s1.result(line)
+    s4.near(line)
+    s3.far(line)
+    (final, grad_captions) = line(
+        lambda a: (
+            (residual2 + dot(a, down).reshape(inputs.shape) + down_offset).astype(BF),
+            None,
+        ),
+        activated,
+    )
+    grad_captions = sum_seq(line(lambda a: dot_t(a, cross_memory), grad_memory))
+    s2.close(line)
+    grad_in1, _, _ = norm_back(inputs, self_gain, scatter_seq(grad_blocks))
+    grad_up_bias = jnp.sum(wide(grad_before), axis=0)
+    grad_down_bias = jnp.sum(wide(cotangent), axis=(0, 1))
     small_grads = pack_small_grads(
         [
             grad_self_gain,
@@ -521,17 +781,28 @@
         ],
         grad_up_bias,
     )
-    grad_self_in, small_out = scatter_chips(
-        [(flat(normed1), flat(grad_projected)), (small_grads,)]
-    )
+    s5 = Scatter(line, [(small_grads,)])
+    s4.first(line)
+    s5.second(line)
+    (grad_up,) = s2.result(line)
+    s3.close(line)
+    s5.near(line)
+    s4.far(line)
+    s5.first(line)
+    s5.far(line)
+    grad_cross_query, grad_cross_memory, grad_cross_out, grad_self_out = s3.result(line)
+    s4.close(line)
+    s5.close(line)
+    grad_self_q, grad_self_k, grad_self_v = s4.result(line)
+    (small_out,) = s5.result(line)
     small_columns = small_out.T
     return (
-        final.astype(BF),
+        final,
         grad_first + grad_in1,
         grad_captions,
         small_columns[0],
         small_columns[1],
-        grad_self_in,
+        jnp.concatenate([grad_self_q, grad_self_k, grad_self_v], axis=1),
         grad_self_out,
         small_columns[2],
         small_columns[3],

time: 874 us -> 624 us (0.71)
  waiting for transfers between devices: 314 us -> 131 us
  matrix products: 191 us -> 81.4 us
  Pallas kernels: 83.3 us -> 181 us
  local copies, waits for them, and re-layouts: 95.6 us -> 40.6 us
  other arithmetic: 109 us -> 123 us
  between operations: 15.8 us -> 2.04 us
    ppermute x50 -> x64, waiting for transfers between devices: 314 us -> 131 us  [hop(): return lax.ppermute(values, AXES, pairs)]
    dot_general x10 -> x0, matrix products: 88.5 us -> none  [the longest x2 26.6 us: attend_back(): jnp.einsum('iqhd,ikhd->ihqk', grad_heads, split_heads(value_rows), prefer...]
    pallas_call x0 -> x5, Pallas kernels: none -> 82.2 us  [the longest x2 39.1 us: attend_back(): pl.pallas_call(functools.partial(attend_back_kernel, kind), out_shape=[ja...]
    convert_element_type x12 -> x1, local copies, waits for them, and re-layouts: 34.9 us -> 1.56 us  [scatter_seq(): blocks[j ^ step].astype(BF)]
    sub x2 -> x0, matrix products: 22.9 us -> none  [attend(): softened = jax.nn.softmax(scores, axis=-1)]
    reduce_sum x0 -> x9, other arithmetic: none -> 16 us  [the longest x2 8.4 us: norm_back(): jnp.sum(grad_normed * unit, axis=(0, 1))]
    pallas_call x8 -> x10, Pallas kernels: 53.2 us -> 68.2 us  [wgrad(): pl.pallas_call(functools.partial(wgrad_kernel, kinds, rows), out_shape=ja...]
    convert_element_type x20 -> x27, other arithmetic: 80.6 us -> 65.6 us  [the longest x5 18.4 us: second(): (wide(o[1]) + wide(c[1])).astype(BF)]
  transfers between devices with their start and end apart: 56 -> 64, of which waited for: 29 -> 21; matrix products, arithmetic and copies ran while one was open for 23% -> 34% of each run, Pallas kernels for 9% -> 25%
where the time goes in v2:
time: 624 us; the launch traced here: 619 us
  Pallas kernels  181 us (29%)
  waiting for transfers between devices  131 us (21%)
  other arithmetic  123 us (20%)
  matrix products  81.4 us (13%)
  starting transfers between devices  60.2 us (10%)
  local copies, waits for them, and re-layouts  40.6 us (7%)
    ppermute x64, waiting for transfers between devices, hop(): return lax.ppermute(values, AXES, pairs)  131 us
    pallas_call x10, Pallas kernels, wgrad(): pl.pallas_call(functools.partial(wgrad_kernel, kinds, rows), out_shape=ja...  68.2 us
    ppermute x64, starting transfers between devices, hop(): return lax.ppermute(values, AXES, pairs)  60.2 us
    dot_general x9, matrix products, dot_t(): lax.dot_general(left, right, (((left.ndim - 1,), (1,)), ((), ())), prefer...  51.8 us
    pallas_call x2, Pallas kernels, attend_back(): pl.pallas_call(functools.partial(attend_back_kernel, kind), out_shape=[ja...  39.1 us
    pallas_call x4, Pallas kernels, assemble(): pl.pallas_call(functools.partial(assemble_kernel, widths, far, rows), out...  30.4 us
    pallas_call x2, Pallas kernels, attend(): pl.pallas_call(functools.partial(attend_kernel, kind), out_shape=[jax.Sha...  30 us
    dot_general x8, matrix products, dot(): return jnp.dot(left, right, preferred_element_type=F32)  29.7 us
  transfers between devices with their start and end apart: 64, of which 21 were waited for; matrix products, arithmetic and copies ran while one was open for 34% of the time, Pallas kernels for 25%

profile of v2, /device:TPU:0, one launch (start us, length us, event | category | flops | bytes accessed | tf_op | source)
XLA Modules:
  0.0 619.4 jit_solution(11390687153349795016)
XLA Ops:
  9.8 4.0 collective-permute-start.3
  13.8 12.9 %collective-permute-done.3 = bf16[64,2176]{1,0:T(8,128)(2,1)S(1)} collective-permute-done((bf16[64,2176]{1,0:T(8,128)(2,1)S(1)}, bf16[64,2176]{1,0:T(8,128)(2,1)S(1)}, u32[]{:S(2)}, u32[]{:S(2)}) %collective-permute-start.3) | collective-permute-done | bytes 278560 | tf_op jit(solution)/shard_map/ppermute | solution.py:40
  28.5 7.9 %collective-permute-done.5 = bf16[2,64,2176]{2,1,0:T(8,128)(2,1)S(1)} collective-permute-done((bf16[2,64,2176]{2,1,0:T(8,128)(2,1)S(1)}, bf16[2,64,2176]{2,1,0:T(8,128)(2,1)S(1)}, u32[]{:S(2)}, u32[]{:S(2)}) %collective-permute-start.5) | collective-permute-done | bytes 557088 | tf_op jit(solution)/shard_map/ppermute | solution.py:40
  37.4 3.4 collective-permute-start.4
  42.5 23.6 %collective-permute-done.4 = bf16[64,2048]{1,0:T(8,128)(2,1)S(1)} collective-permute-done((bf16[64,2048]{1,0:T(8,128)(2,1)S(1)}, bf16[64,2048]{1,0:T(8,128)(2,1)S(1)}, u32[]{:S(2)}, u32[]{:S(2)}) %collective-permute-start.4) | collective-permute-done | bytes 262176 | tf_op jit(solution)/shard_map/ppermute | solution.py:40
  73.4 10.9 %collective-permute-done.7 = bf16[64,2048]{1,0:T(8,128)(2,1)S(1)} collective-permute-done((bf16[64,2048]{1,0:T(8,128)(2,1)S(1)}, bf16[64,2048]{1,0:T(8,128)(2,1)S(1)}, u32[]{:S(2)}, u32[]{:S(2)}) %collective-permute-start.7) | collective-permute-done | bytes 262176 | tf_op jit(solution)/shard_map/ppermute | solution.py:40
  89.4 11.5 %collective-permute-done.10.refs_2_ = bf16[2,2,2,64,2176]{4,3,2,1,0:T(8,128)(2,1)} collective-permute-done((bf16[2,2,2,64,2176]{4,3,2,1,0:T(8,128)(2,1)S(1)}, bf16[2,2,2,64,2176]{4,3,2,1,0:T(8,128)(2,1)}, u32[]{:S(2)}, u32[]{:S(2)}) %collective-permute-start.10) | collective-permute-done | bytes 2228256 | tf_op jit(solution)/shard_map/ppermute | solution.py:40
  111.2 22.4 %collective-permute-done.14 = bf16[2,2,64,2048]{3,2,1,0:T(8,128)(2,1)} collective-permute-done((bf16[2,2,64,2048]{3,2,1,0:T(8,128)(2,1)}, bf16[2,2,64,2048]{3,2,1,0:T(8,128)(2,1)}, u32[]{:S(2)}, u32[]{:S(2)}) %collective-permute-start.14) | collective-permute-done | bytes 1048608 | tf_op jit(solution)/shard_map/ppermute | solution.py:40
  139.4 8.3 %assemble.4 = (bf16[1024,1024]{1,0:T(8,128)(2,1)}, bf16[1024,1024]{1,0:T(8,128)(2,1)}, bf16[1024,1024]{1,0:T(8,128)(2,1)}, bf16[1024,1024]{1,0:T(8,128)(2,1)}, bf16[1024,256]{1,0:T(8,128)(2,1)}) custom-call(s32[5]{0:T(128)} %stack.299.spot_ref, bf16[2,2,2,64,2176]{4,3,2,1,0:T(8,128)(2,1)} %collective-permute-done.12.refs_0_, ...), custom_call_target="tpu_custom_call" | custom-call | tf_op jit(solution)/shard_map/assemble/pallas_call | solution.py:163
  147.6 3.9 convert_reduce_fusion.4
  156.4 6.1 convolution_convert_fusion.1.k_ref
  162.5 6.1 convolution_convert_fusion.v_ref
  173.4 5.0 collective-permute-done.17
  183.7 22.1 %attend.2 = (bf16[2,256,1024]{2,1,0:T(8,128)(2,1)}, f32[2,8,2,256]{3,2,1,0:T(2,128)}) custom-call(s32[1]{0:T(128)} %bitcast.info_ref, bf16[1,2,256,1024]{3,2,1,0:T(8,128)(2,1)} %fusion.82.q_ref, bf16[4,2,256,1024]{3,2,1,0:T(8,128)(2,1)} %convolution_convert_fusion.1.k_ref, bf16[4,2,256,1024]{3,2,1,0:T(8,128)(2,1)} %convolution_convert_fusion.v_ref), custom_call_target="tpu_custom_call" | custom-call | flops 4294967296 | bytes 10485760 | tf_op jit(solution)/shard_map/attend/pallas_call | solution.py:405
  210.0 7.4 %assemble.5 = (bf16[1024,1024]{1,0:T(8,128)(2,1)}, bf16[1024,2048]{1,0:T(8,128)(2,1)}, bf16[1024,1024]{1,0:T(8,128)(2,1)}) custom-call(s32[5]{0:T(128)} %stack.299.spot_ref, bf16[2,2,2,64,2048]{4,3,2,1,0:T(8,128)(2,1)} %collective-permute-done.20.refs_0_, bf16[2,2,2,64,2048]{4,3,2,1,0:T(8,128)(2,1)} %pad_maximum_fusion.2.refs_1_, ...), custom_call_target="tpu_custom_call" | custom-call | tf_op jit(solution)/shard_map/assemble/pallas_call | solution.py:163
  225.7 7.9 %attend.3 = (bf16[2,256,1024]{2,1,0:T(8,128)(2,1)}, f32[2,8,2,256]{3,2,1,0:T(2,128)}) custom-call(s32[2]{0:T(128)} %info_ref.3, bf16[1,2,256,1024]{3,2,1,0:T(8,128)(2,1)} %fusion.79.q_ref, bf16[1,2,128,2048]{3,2,1,0:T(8,128)(2,1)} %fusion.19.k_ref.v_ref, bf16[1,2,128,2048]{3,2,1,0:T(8,128)(2,1)} %fusion.19.k_ref.v_ref), custom_call_target="tpu_custom_call" | custom-call | flops 536870912 | bytes 3145728 | tf_op jit(solution)/shard_map/attend/pallas_call | solution.py:405
  238.2 7.4 %assemble.6.w_ref = bf16[1024,4096]{1,0:T(8,128)(2,1)} custom-call(s32[5]{0:T(128)} %stack.299.spot_ref, bf16[2,2,2,64,2048]{4,3,2,1,0:T(8,128)(2,1)} %collective-permute-done.24.refs_0_, bf16[2,2,2,64,2048]{4,3,2,1,0:T(8,128)(2,1)} %pad_maximum_fusion.3.refs_1_, bf16[2,2,2,64,2048]{4,3,2,1,0:T(8,128)(2,1)} %collective-permute-done.23.refs_2_, ...), custom_call_target="tpu_custom_call" | custom-call | tf_op jit(solution)/shard_map/assemble/pallas_call | solution.py:163
  245.5 13.0 %up_gelu.1 = (bf16[512,4096]{1,0:T(8,128)(2,1)}, bf16[512,4096]{1,0:T(8,128)(2,1)}) custom-call(bf16[512,1024]{1,0:T(8,128)(2,1)} %bitcast.416, bf16[1024,4096]{1,0:T(8,128)(2,1)} %assemble.6.w_ref, f32[1,4096]{1,0:T(1,128)} %reshape.448.b_ref), custom_call_target="tpu_custom_call" | custom-call | flops 4294967296 | bytes 17825792 | tf_op jit(solution)/shard_map/up_gelu/pallas_call | solution.py:500
  258.6 6.6 %wgrad.10 = bf16[2,2,2,2,256,512]{5,4,3,2,1,0:T(8,128)(2,1)} custom-call(s32[5]{0:T(128)} %stack.322.spot_ref, bf16[512,4096]{1,0:T(8,128)(2,1)} %get-tuple-element.215.refs_0_, bf16[512,1024]{1,0:T(8,128)(2,1)} %bitcast.421), custom_call_target="tpu_custom_call" | custom-call | flops 2147483648 | bytes 8912896 | tf_op jit(solution)/shard_map/wgrad/pallas_call | solution.py:219
  265.9 6.4 %wgrad.11 = bf16[2,2,2,2,256,512]{5,4,3,2,1,0:T(8,128)(2,1)} custom-call(s32[5]{0:T(128)} %stack.299.spot_ref, bf16[512,4096]{1,0:T(8,128)(2,1)} %get-tuple-element.215.refs_0_, bf16[512,1024]{1,0:T(8,128)(2,1)} %bitcast.422), custom_call_target="tpu_custom_call" | custom-call | flops 2147483648 | bytes 8912896 | tf_op jit(solution)/shard_map/wgrad/pallas_call | solution.py:219
  272.2 3.4 collective-permute-done.28.refs_0_
  278.7 7.3 %assemble.7 = bf16[4096,1024]{1,0:T(8,128)(2,1)} custom-call(s32[5]{0:T(128)} %stack.299.spot_ref, bf16[2,2,2,256,512]{4,3,2,1,0:T(8,128)(2,1)} %collective-permute-done.28.refs_0_, bf16[2,2,2,256,512]{4,3,2,1,0:T(8,128)(2,1)} %pad_maximum_fusion.4.refs_1_, bf16[2,2,2,256,512]{4,3,2,1,0:T(8,128)(2,1)} %collective-permute-done.27.refs_2_, ...), custom_call_target="tpu_custom_call" | custom-call | tf_op jit(solution)/shard_map/assemble/pallas_call | solution.py:163
  286.0 3.7 fusion.29
  289.7 10.2 %convert_reduce_fusion.1 = (f32[4096]{0:T(1024)S(1)}, bf16[512,4096]{1,0:T(8,128)(2,1)}) fusion(bf16[512,4096]{1,0:T(8,128)(2,1)} %get-tuple-element.178, bf16[512,1024]{1,0:T(8,128)(2,1)S(1)} %bitcast.423, bf16[4096,1024]{1,0:T(8,128)(2,1)} %assemble.7), kind=kOutput, calls=%fused_computation.10 | convolution fusion | flops 4305448960 | bytes 17842176 | tf_op jit(solution)/shard_map/dot_general | solution.py:525
  299.9 6.5 %wgrad.12 = bf16[2,2,2,2,64,2048]{5,4,3,2,1,0:T(8,128)(2,1)} custom-call(s32[5]{0:T(128)} %stack.322.spot_ref, bf16[512,1024]{1,0:T(8,128)(2,1)} %bitcast.417, bf16[512,4096]{1,0:T(8,128)(2,1)} %get-tuple-element.182.refs_1_), custom_call_target="tpu_custom_call" | custom-call | flops 2147483648 | bytes 7340032 | tf_op jit(solution)/shard_map/wgrad/pallas_call | solution.py:219
  309.7 6.7 %wgrad.13 = bf16[2,2,2,2,64,2048]{5,4,3,2,1,0:T(8,128)(2,1)} custom-call(s32[5]{0:T(128)} %stack.299.spot_ref, bf16[512,1024]{1,0:T(8,128)(2,1)} %bitcast.418, bf16[512,4096]{1,0:T(8,128)(2,1)} %get-tuple-element.182.refs_1_), custom_call_target="tpu_custom_call" | custom-call | flops 2147483648 | bytes 7340032 | tf_op jit(solution)/shard_map/wgrad/pallas_call | solution.py:219
  316.4 5.4 fusion.30
  322.6 9.2 %fusion.115 = (f32[1024]{0:T(1024)S(1)}, f32[512]{0:T(512)S(1)}, f32[512,1024]{1,0:T(8,128)}) fusion(f32[1024]{0:T(1024)S(1)} %get-tuple-element.244, bf16[512,4096]{1,0:T(8,128)(2,1)S(1)} %copy-done.9, bf16[1024,4096]{1,0:T(8,128)(2,1)} %assemble.6.w_ref), kind=kOutput, calls=%fused_computation.284 | convolution fusion | flops 4296538624 | bytes 14690304 | tf_op jit(solution)/shard_map/dot_general | solution.py:525
  337.2 3.7 fusion.34
  343.2 10.6 %attend_back.2 = (bf16[2,256,1024]{2,1,0:T(8,128)(2,1)}, bf16[1,2,128,1024]{3,2,1,0:T(8,128)(2,1)}, bf16[1,2,128,1024]{3,2,1,0:T(8,128)(2,1)}) custom-call(s32[2]{0:T(128)} %info_ref.3, bf16[1,2,256,1024]{3,2,1,0:T(8,128)(2,1)} %fusion.79.q_ref, bf16[1,2,128,2048]{3,2,1,0:T(8,128)(2,1)} %fusion.19.k_ref.v_ref, bf16[1,2,128,2048]{3,2,1,0:T(8,128)(2,1)} %fusion.19.k_ref.v_ref, ...), custom_call_target="tpu_custom_call" | custom-call | flops 1342177280 | bytes 6291456 | tf_op jit(solution)/shard_map/attend_back/pallas_call | solution.py:472
  370.8 7.0 %wgrad.14 = bf16[2,2,2,2,64,2560]{5,4,3,2,1,0:T(8,128)(2,1)} custom-call(s32[5]{0:T(128)} %stack.322.spot_ref, bf16[512,1024]{1,0:T(8,128)(2,1)} %bitcast.412, bf16[512,1024]{1,0:T(8,128)(2,1)} %bitcast.434, bf16[256,1024]{1,0:T(8,128)(2,1)} %bitcast.436, bf16[256,2048]{1,0:T(8,128)(2,1)} %pad_maximum_fusion.10.refs_3_, bf16[512,1024]{1,0:T(8,128)(2,1)} %bitcast.419, ...), custom_call_target="tpu_custom_call" | custom-call | flops 2147483648 | bytes 11010048 | tf_op jit(solution)/shard_map/wgrad/pallas_call | solution.py:219
  381.9 7.0 %wgrad.15 = bf16[2,2,2,2,64,2560]{5,4,3,2,1,0:T(8,128)(2,1)} custom-call(s32[5]{0:T(128)} %stack.299.spot_ref, bf16[512,1024]{1,0:T(8,128)(2,1)} %bitcast.413, bf16[512,1024]{1,0:T(8,128)(2,1)} %bitcast.435, bf16[256,1024]{1,0:T(8,128)(2,1)} %bitcast.437, bf16[256,2048]{1,0:T(8,128)(2,1)} %pad_maximum_fusion.10.refs_3_, bf16[512,1024]{1,0:T(8,128)(2,1)} %bitcast.420, ...), custom_call_target="tpu_custom_call" | custom-call | flops 2147483648 | bytes 11010048 | tf_op jit(solution)/shard_map/wgrad/pallas_call | solution.py:219
  395.8 4.7 fusion.12
  403.5 9.3 %collective-permute-done.37 = bf16[2,2,64,2048]{3,2,1,0:T(8,128)(2,1)} collective-permute-done((bf16[2,2,64,2048]{3,2,1,0:T(8,128)(2,1)}, bf16[2,2,64,2048]{3,2,1,0:T(8,128)(2,1)}, u32[]{:S(2)}, u32[]{:S(2)}) %collective-permute-start.37) | collective-permute-done | bytes 1048608 | tf_op jit(solution)/shard_map/ppermute | solution.py:40
  415.3 28.5 %attend_back.3 = (bf16[2,256,1024]{2,1,0:T(8,128)(2,1)}, bf16[4,2,256,1024]{3,2,1,0:T(8,128)(2,1)}, bf16[4,2,256,1024]{3,2,1,0:T(8,128)(2,1)}) custom-call(s32[1]{0:T(128)} %bitcast.info_ref, bf16[1,2,256,1024]{3,2,1,0:T(8,128)(2,1)} %fusion.82.q_ref, bf16[4,2,256,1024]{3,2,1,0:T(8,128)(2,1)} %convolution_convert_fusion.1.k_ref, ...), custom_call_target="tpu_custom_call" | custom-call | flops 10737418240 | bytes 20971520 | tf_op jit(solution)/shard_map/attend_back/pallas_call | solution.py:472
  448.9 3.7 fusion.13
  452.5 11.6 %wgrad.16 = bf16[2,2,2,2,64,1536]{5,4,3,2,1,0:T(8,128)(2,1)} custom-call(s32[5]{0:T(128)} %stack.322.spot_ref, bf16[512,1024]{1,0:T(8,128)(2,1)} %bitcast.414, bf16[512,1024]{1,0:T(8,128)(2,1)} %bitcast.432, bf16[2048,1024]{1,0:T(8,128)(2,1)} %bitcast.400, bf16[2048,1024]{1,0:T(8,128)(2,1)} %bitcast.406, bf16[2048,1024]{1,0:T(8,128)(2,1)} %bitcast.401, ...), custom_call_target="tpu_custom_call" | custom-call | flops 4831838208 | bytes 17301504 | tf_op jit(solution)/shard_map/wgrad/pallas_call | solution.py:219
  472.7 10.8 %fusion.37 = f32[4,2,256,1024]{3,2,1,0:T(8,128)} fusion(bf16[4,2,256,1024]{3,2,1,0:T(8,128)(2,1)} %get-tuple-element.207, bf16[1024,1024]{1,0:T(8,128)(2,1)} %get-tuple-element.147), kind=kOutput, calls=%fused_computation.60 | convolution fusion | flops 4294967296 | bytes 14680064 | tf_op jit(solution)/shard_map/dot_general | solution.py:525
  487.5 11.5 %wgrad.17 = bf16[2,2,2,2,64,1536]{5,4,3,2,1,0:T(8,128)(2,1)} custom-call(s32[5]{0:T(128)} %stack.299.spot_ref, bf16[512,1024]{1,0:T(8,128)(2,1)} %bitcast.415, bf16[512,1024]{1,0:T(8,128)(2,1)} %bitcast.433, bf16[2048,1024]{1,0:T(8,128)(2,1)} %bitcast.402, bf16[2048,1024]{1,0:T(8,128)(2,1)} %bitcast.407, bf16[2048,1024]{1,0:T(8,128)(2,1)} %bitcast.403, ...), custom_call_target="tpu_custom_call" | custom-call | flops 4831838208 | bytes 17301504 | tf_op jit(solution)/shard_map/wgrad/pallas_call | solution.py:219
  499.0 3.6 fusion.58
  503.9 9.2 %fusion.136 = (bf16[4,2,256,1024]{3,2,1,0:T(8,128)(2,1)}, f32[4,2,256,1024]{3,2,1,0:T(8,128)S(1)}) fusion(f32[4,2,256,1024]{3,2,1,0:T(8,128)} %fusion.37, bf16[4,2,256,1024]{3,2,1,0:T(8,128)(2,1)S(1)} %copy-done.12, bf16[1024,1024]{1,0:T(8,128)(2,1)} %get-tuple-element.145), kind=kOutput, calls=%fused_computation.299 | convolution fusion | flops 4299161600 | bytes 27262976 | tf_op jit(solution)/shard_map/dot_general | solution.py:525
  513.1 3.8 slice_reduce_fusion.7
  516.9 4.8 collective-permute-done.40
  531.3 5.4 fusion.6
  539.4 4.8 concatenate.76
  546.1 3.4 fusion.32
  555.9 6.9 %fusion.138 = f32[512,1024]{1,0:T(8,128)S(1)} fusion(bf16[512,4096]{1,0:T(8,128)(2,1)S(1)} %copy-done.8, bf16[4096,1024]{1,0:T(8,128)(2,1)} %assemble.7), kind=kOutput, calls=%fused_computation.301 | convolution fusion | flops 4294967296 | bytes 14680064 | tf_op jit(solution)/shard_map/dot_general | solution.py:521
  591.1 4.7 collective-permute-done.54
  (402 shorter events, 213.2 us)
Async XLA Ops:
  9.8 16.9 %collective-permute-start.3 = (bf16[64,2176]{1,0:T(8,128)(2,1)S(1)}, bf16[64,2176]{1,0:T(8,128)(2,1)S(1)}, u32[]{:S(2)}, u32[]{:S(2)}) collective-permute-start(bf16[64,2176]{1,0:T(8,128)(2,1)S(1)} %get-tuple-element.291), channel_id=1, source_target_pairs={{0,16},{1,17},{2,18},{3,19},{4,20},{5,21},{6,22},{7,23},{8,24},{9,... | collective-permute-start | bytes 835592 | tf_op jit(solution)/shard_map/ppermute | solution.py:40
  36.6 30.9 %collective-permute-start.8 = (bf16[2,2,64,2176]{3,2,1,0:T(8,128)(2,1)S(1)}, bf16[2,2,64,2176]{3,2,1,0:T(8,128)(2,1)S(1)}, u32[]{:S(2)}, u32[]{:S(2)}) collective-permute-start(bf16[2,2,64,2176]{3,2,1,0:T(8,128)(2,1)S(1)} %get-tuple-element.278), channel_id=1, source_target_pairs={{0,8},{1,9},{2,10},{3,11},{4,12},{5,13},{6,14},{7,15},{8,0},{9,1},... | collective-permute-start | bytes 3342344 | tf_op jit(solution)/shard_map/ppermute | solution.py:40
  37.4 28.8 %collective-permute-start.4 = (bf16[64,2048]{1,0:T(8,128)(2,1)S(1)}, bf16[64,2048]{1,0:T(8,128)(2,1)S(1)}, u32[]{:S(2)}, u32[]{:S(2)}) collective-permute-start(bf16[64,2048]{1,0:T(8,128)(2,1)S(1)} %get-tuple-element.126), channel_id=1, source_target_pairs={{0,16},{1,17},{2,18},{3,19},{4,20},{5,21},{6,22},{7,23},{8,24},{9,... | collective-permute-start | bytes 786440 | tf_op jit(solution)/shard_map/ppermute | solution.py:40
  40.9 28.2 %collective-permute-start.1 = (bf16[2,256,1024]{2,1,0:T(8,128)(2,1)S(1)}, bf16[2,256,1024]{2,1,0:T(8,128)(2,1)S(1)}, u32[]{:S(2)}, u32[]{:S(2)}) collective-permute-start(bf16[2,256,1024]{2,1,0:T(8,128)(2,1)S(1)} %copy-done.6), channel_id=1, source_target_pairs={{0,2},{1,3},{2,0},{3,1},{4,6},{5,7},{6,4},{7,5},{8,10},{9,11},{10,... | collective-permute-start | bytes 3145736 | tf_op jit(solution)/shard_map/ppermute | solution.py:40
  67.7 33.2 %collective-permute-start.10 = (bf16[2,2,2,64,2176]{4,3,2,1,0:T(8,128)(2,1)S(1)}, bf16[2,2,2,64,2176]{4,3,2,1,0:T(8,128)(2,1)}, u32[]{:S(2)}, u32[]{:S(2)}) collective-permute-start(bf16[2,2,2,64,2176]{4,3,2,1,0:T(8,128)(2,1)S(1)} %pad_maximum_fusion.1.refs_1_), channel_id=1, source_target_pairs={{0,2},{1,5},{2,0},{3,7},{4,6},{5,1},{6,4},{7,3},{8,10},{9,13},{10,... | collective-permute-start | bytes 6684680 | tf_op jit(solution)/shard_map/ppermute | solution.py:40
  69.1 16.3 %collective-permute-start.6 = (bf16[2,256,1024]{2,1,0:T(8,128)(2,1)S(1)}, bf16[2,256,1024]{2,1,0:T(8,128)(2,1)S(1)}, u32[]{:S(2)}, u32[]{:S(2)}) collective-permute-start(bf16[2,256,1024]{2,1,0:T(8,128)(2,1)S(1)} %collective-permute-done.1), channel_id=1, source_target_pairs={{0,1},{1,0},{2,3},{3,2},{4,5},{5,4},{6,7},{7,6},{8,9},{9,8},{10,11... | collective-permute-start | bytes 3145736 | tf_op jit(solution)/shard_map/ppermute | solution.py:40
  69.1 16.3 %collective-permute-start = (bf16[2,256,1024]{2,1,0:T(8,128)(2,1)S(1)}, bf16[2,256,1024]{2,1,0:T(8,128)(2,1)S(1)}, u32[]{:S(2)}, u32[]{:S(2)}) collective-permute-start(bf16[2,256,1024]{2,1,0:T(8,128)(2,1)S(1)} %copy-done.6), channel_id=1, source_target_pairs={{0,1},{1,0},{2,3},{3,2},{4,5},{5,4},{6,7},{7,6},{8,9},{9,8},{10,11... | collective-permute-start | bytes 3145736 | tf_op jit(solution)/shard_map/ppermute | solution.py:40
  69.6 14.7 %collective-permute-start.7 = (bf16[64,2048]{1,0:T(8,128)(2,1)S(1)}, bf16[64,2048]{1,0:T(8,128)(2,1)S(1)}, u32[]{:S(2)}, u32[]{:S(2)}) collective-permute-start(bf16[64,2048]{1,0:T(8,128)(2,1)S(1)} %get-tuple-element.129), channel_id=1, source_target_pairs={{0,16},{1,17},{2,18},{3,19},{4,20},{5,21},{6,22},{7,23},{8,24},{9,... | collective-permute-start | bytes 786440 | tf_op jit(solution)/shard_map/ppermute | solution.py:40
  71.9 16.0 %collective-permute-start.11 = (bf16[2,64,2048]{2,1,0:T(8,128)(2,1)S(1)}, bf16[2,64,2048]{2,1,0:T(8,128)(2,1)S(1)}, u32[]{:S(2)}, u32[]{:S(2)}) collective-permute-start(bf16[2,64,2048]{2,1,0:T(8,128)(2,1)S(1)} %get-tuple-element.305), channel_id=1, source_target_pairs={{0,4},{1,3},{2,6},{3,1},{4,0},{5,7},{6,2},{7,5},{8,12},{9,11},{10,... | collective-permute-start | bytes 1572872 | tf_op jit(solution)/shard_map/ppermute | solution.py:40
  101.0 38.4 %collective-permute-start.12 = (bf16[2,2,2,64,2176]{4,3,2,1,0:T(8,128)(2,1)}, bf16[2,2,2,64,2176]{4,3,2,1,0:T(8,128)(2,1)}, u32[]{:S(2)}, u32[]{:S(2)}) collective-permute-start(bf16[2,2,2,64,2176]{4,3,2,1,0:T(8,128)(2,1)} %collective-permute-done.10.refs_2_), channel_id=1, source_target_pairs={{0,1},{1,0},{2,3},{3,2},{4,5},{5,4},{6,7},{7,6},{8,9},{9,8},{10,11... | collective-permute-start | bytes 6684680 | tf_op jit(solution)/shard_map/ppermute | solution.py:40
  101.0 38.4 %collective-permute-start.15 = (bf16[2,2,2,64,2176]{4,3,2,1,0:T(8,128)(2,1)S(1)}, bf16[2,2,2,64,2176]{4,3,2,1,0:T(8,128)(2,1)}, u32[]{:S(2)}, u32[]{:S(2)}) collective-permute-start(bf16[2,2,2,64,2176]{4,3,2,1,0:T(8,128)(2,1)S(1)} %pad_maximum_fusion.1.refs_1_), channel_id=1, source_target_pairs={{0,1},{1,0},{2,3},{3,2},{4,5},{5,4},{6,7},{7,6},{8,9},{9,8},{10,11... | collective-permute-start | bytes 6684680 | tf_op jit(solution)/shard_map/ppermute | solution.py:40
  101.5 32.1 %collective-permute-start.14 = (bf16[2,2,64,2048]{3,2,1,0:T(8,128)(2,1)}, bf16[2,2,64,2048]{3,2,1,0:T(8,128)(2,1)}, u32[]{:S(2)}, u32[]{:S(2)}) collective-permute-start(bf16[2,2,64,2048]{3,2,1,0:T(8,128)(2,1)} %get-tuple-element.285), channel_id=1, source_target_pairs={{0,8},{1,9},{2,10},{3,11},{4,12},{5,13},{6,14},{7,15},{8,0},{9,1},... | collective-permute-start | bytes 3145736 | tf_op jit(solution)/shard_map/ppermute | solution.py:40
  104.9 63.6 %collective-permute-start.16 = (bf16[256,512]{1,0:T(8,128)(2,1)S(1)}, bf16[256,512]{1,0:T(8,128)(2,1)S(1)}, u32[]{:S(2)}, u32[]{:S(2)}) collective-permute-start(bf16[256,512]{1,0:T(8,128)(2,1)S(1)} %maximum_select_fusion.1), channel_id=1, source_target_pairs={{0,16},{1,17},{2,18},{3,19},{4,20},{5,21},{6,22},{7,23},{8,24},{9,... | collective-permute-start | bytes 786440 | tf_op jit(solution)/shard_map/ppermute | solution.py:40
  106.6 31.3 %collective-permute-start.13 = (bf16[2,64,2048]{2,1,0:T(8,128)(2,1)}, bf16[2,64,2048]{2,1,0:T(8,128)(2,1)S(1)}, u32[]{:S(2)}, u32[]{:S(2)}) collective-permute-start(bf16[2,64,2048]{2,1,0:T(8,128)(2,1)} %get-tuple-element.303), channel_id=1, source_target_pairs={{0,4},{1,3},{2,6},{3,1},{4,0},{5,7},{6,2},{7,5},{8,12},{9,11},{10,... | collective-permute-start | bytes 1572872 | tf_op jit(solution)/shard_map/ppermute | solution.py:40
  136.4 32.3 %collective-permute-start.19 = (bf16[2,2,2,64,2048]{4,3,2,1,0:T(8,128)(2,1)}, bf16[2,2,2,64,2048]{4,3,2,1,0:T(8,128)(2,1)}, u32[]{:S(2)}, u32[]{:S(2)}) collective-permute-start(bf16[2,2,2,64,2048]{4,3,2,1,0:T(8,128)(2,1)} %pad_maximum_fusion.2.refs_1_), channel_id=1, source_target_pairs={{0,2},{1,5},{2,0},{3,7},{4,6},{5,1},{6,4},{7,3},{8,10},{9,13},{10,... | collective-permute-start | bytes 6291464 | tf_op jit(solution)/shard_map/ppermute | solution.py:40
  139.3 31.4 %collective-permute-start.18 = (bf16[2,2,64,2048]{3,2,1,0:T(8,128)(2,1)}, bf16[2,2,64,2048]{3,2,1,0:T(8,128)(2,1)}, u32[]{:S(2)}, u32[]{:S(2)}) collective-permute-start(bf16[2,2,64,2048]{3,2,1,0:T(8,128)(2,1)} %get-tuple-element.283), channel_id=1, source_target_pairs={{0,8},{1,9},{2,10},{3,11},{4,12},{5,13},{6,14},{7,15},{8,0},{9,1},... | collective-permute-start | bytes 3145736 | tf_op jit(solution)/shard_map/ppermute | solution.py:40
  168.6 41.4 %collective-permute-start.20 = (bf16[2,2,2,64,2048]{4,3,2,1,0:T(8,128)(2,1)}, bf16[2,2,2,64,2048]{4,3,2,1,0:T(8,128)(2,1)}, u32[]{:S(2)}, u32[]{:S(2)}) collective-permute-start(bf16[2,2,2,64,2048]{4,3,2,1,0:T(8,128)(2,1)} %collective-permute-done.19.refs_2_), channel_id=1, source_target_pairs={{0,1},{1,0},{2,3},{3,2},{4,5},{5,4},{6,7},{7,6},{8,9},{9,8},{10,11... | collective-permute-start | bytes 6291464 | tf_op jit(solution)/shard_map/ppermute | solution.py:40
  168.7 41.3 %collective-permute-start.22 = (bf16[2,2,2,64,2048]{4,3,2,1,0:T(8,128)(2,1)}, bf16[2,2,2,64,2048]{4,3,2,1,0:T(8,128)(2,1)}, u32[]{:S(2)}, u32[]{:S(2)}) collective-permute-start(bf16[2,2,2,64,2048]{4,3,2,1,0:T(8,128)(2,1)} %pad_maximum_fusion.2.refs_1_), channel_id=1, source_target_pairs={{0,1},{1,0},{2,3},{3,2},{4,5},{5,4},{6,7},{7,6},{8,9},{9,8},{10,11... | collective-permute-start | bytes 6291464 | tf_op jit(solution)/shard_map/ppermute | solution.py:40
  179.5 26.2 %collective-permute-start.21 = (bf16[2,2,256,512]{3,2,1,0:T(8,128)(2,1)}, bf16[2,2,256,512]{3,2,1,0:T(8,128)(2,1)}, u32[]{:S(2)}, u32[]{:S(2)}) collective-permute-start(bf16[2,2,256,512]{3,2,1,0:T(8,128)(2,1)} %get-tuple-element.281), channel_id=1, source_target_pairs={{0,8},{1,9},{2,10},{3,11},{4,12},{5,13},{6,14},{7,15},{8,0},{9,1},... | collective-permute-start | bytes 3145736 | tf_op jit(solution)/shard_map/ppermute | solution.py:40
  181.5 39.0 %collective-permute-start.23 = (bf16[2,2,2,64,2048]{4,3,2,1,0:T(8,128)(2,1)}, bf16[2,2,2,64,2048]{4,3,2,1,0:T(8,128)(2,1)}, u32[]{:S(2)}, u32[]{:S(2)}) collective-permute-start(bf16[2,2,2,64,2048]{4,3,2,1,0:T(8,128)(2,1)} %pad_maximum_fusion.3.refs_1_), channel_id=1, source_target_pairs={{0,2},{1,5},{2,0},{3,7},{4,6},{5,1},{6,4},{7,3},{8,10},{9,13},{10,... | collective-permute-start | bytes 6291464 | tf_op jit(solution)/shard_map/ppermute | solution.py:40
  182.6 55.5 %collective-permute-start.25 = (bf16[2,2,2,64,2048]{4,3,2,1,0:T(8,128)(2,1)}, bf16[2,2,2,64,2048]{4,3,2,1,0:T(8,128)(2,1)}, u32[]{:S(2)}, u32[]{:S(2)}) collective-permute-start(bf16[2,2,2,64,2048]{4,3,2,1,0:T(8,128)(2,1)} %pad_maximum_fusion.3.refs_1_), channel_id=1, source_target_pairs={{0,1},{1,0},{2,3},{3,2},{4,5},{5,4},{6,7},{7,6},{8,9},{9,8},{10,11... | collective-permute-start | bytes 6291464 | tf_op jit(solution)/shard_map/ppermute | solution.py:40
  208.5 56.8 %collective-permute-start.27 = (bf16[2,2,2,256,512]{4,3,2,1,0:T(8,128)(2,1)}, bf16[2,2,2,256,512]{4,3,2,1,0:T(8,128)(2,1)}, u32[]{:S(2)}, u32[]{:S(2)}) collective-permute-start(bf16[2,2,2,256,512]{4,3,2,1,0:T(8,128)(2,1)} %pad_maximum_fusion.4.refs_1_), channel_id=1, source_target_pairs={{0,2},{1,5},{2,0},{3,7},{4,6},{5,1},{6,4},{7,3},{8,10},{9,13},{10,... | collective-permute-start | bytes 6291464 | tf_op jit(solution)/shard_map/ppermute | solution.py:40
  220.6 17.6 %collective-permute-start.24 = (bf16[2,2,2,64,2048]{4,3,2,1,0:T(8,128)(2,1)}, bf16[2,2,2,64,2048]{4,3,2,1,0:T(8,128)(2,1)}, u32[]{:S(2)}, u32[]{:S(2)}) collective-permute-start(bf16[2,2,2,64,2048]{4,3,2,1,0:T(8,128)(2,1)} %collective-permute-done.23.refs_2_), channel_id=1, source_target_pairs={{0,1},{1,0},{2,3},{3,2},{4,5},{5,4},{6,7},{7,6},{8,9},{9,8},{10,11... | collective-permute-start | bytes 6291464 | tf_op jit(solution)/shard_map/ppermute | solution.py:40
  265.2 20.8 %collective-permute-start.26 = (bf16[2,2,2,2,256,512]{5,4,3,2,1,0:T(8,128)(2,1)}, bf16[2,2,2,2,256,512]{5,4,3,2,1,0:T(8,128)(2,1)}, u32[]{:S(2)}, u32[]{:S(2)}) collective-permute-start(bf16[2,2,2,2,256,512]{5,4,3,2,1,0:T(8,128)(2,1)} %wgrad.10), channel_id=1, source_target_pairs={{0,1},{1,0},{2,3},{3,2},{4,5},{5,4},{6,7},{7,6},{8,9},{9,8},{10,11... | collective-permute-start | bytes 12582920 | tf_op jit(solution)/shard_map/ppermute | solution.py:40
  265.7 13.0 %collective-permute-start.29 = (bf16[2,2,2,256,512]{4,3,2,1,0:T(8,128)(2,1)}, bf16[2,2,2,256,512]{4,3,2,1,0:T(8,128)(2,1)}, u32[]{:S(2)}, u32[]{:S(2)}) collective-permute-start(bf16[2,2,2,256,512]{4,3,2,1,0:T(8,128)(2,1)} %pad_maximum_fusion.4.refs_1_), channel_id=1, source_target_pairs={{0,1},{1,0},{2,3},{3,2},{4,5},{5,4},{6,7},{7,6},{8,9},{9,8},{10,11... | collective-permute-start | bytes 6291464 | tf_op jit(solution)/shard_map/ppermute | solution.py:40
  308.4 28.8 %collective-permute-start.32 = (bf16[2,2,2,256,512]{4,3,2,1,0:T(8,128)(2,1)}, bf16[2,2,2,256,512]{4,3,2,1,0:T(8,128)(2,1)}, u32[]{:S(2)}, u32[]{:S(2)}) collective-permute-start(bf16[2,2,2,256,512]{4,3,2,1,0:T(8,128)(2,1)} %fusion.29), channel_id=1, source_target_pairs={{0,2},{1,5},{2,0},{3,7},{4,6},{5,1},{6,4},{7,3},{8,10},{9,13},{10,... | collective-permute-start | bytes 6291464 | tf_op jit(solution)/shard_map/ppermute | solution.py:40
  321.8 45.8 %collective-permute-start.31 = (bf16[2,2,2,64,2048]{4,3,2,1,0:T(8,128)(2,1)}, bf16[2,2,2,64,2048]{4,3,2,1,0:T(8,128)(2,1)}, u32[]{:S(2)}, u32[]{:S(2)}) collective-permute-start(bf16[2,2,2,64,2048]{4,3,2,1,0:T(8,128)(2,1)} %fusion.30), channel_id=1, source_target_pairs={{0,2},{1,5},{2,0},{3,7},{4,6},{5,1},{6,4},{7,3},{8,10},{9,13},{10,... | collective-permute-start | bytes 6291464 | tf_op jit(solution)/shard_map/ppermute | solution.py:40
  340.9 25.0 %collective-permute-start.33 = (bf16[2,2,256,512]{3,2,1,0:T(8,128)(2,1)}, bf16[2,2,256,512]{3,2,1,0:T(8,128)(2,1)}, u32[]{:S(2)}, u32[]{:S(2)}) collective-permute-start(bf16[2,2,256,512]{3,2,1,0:T(8,128)(2,1)} %fusion.34), channel_id=1, source_target_pairs={{0,8},{1,9},{2,10},{3,11},{4,12},{5,13},{6,14},{7,15},{8,0},{9,1},... | collective-permute-start | bytes 3145736 | tf_op jit(solution)/shard_map/ppermute | solution.py:40
  377.8 17.9 %collective-permute-start.34 = (bf16[2,2,2,2,64,2560]{5,4,3,2,1,0:T(8,128)(2,1)}, bf16[2,2,2,2,64,2560]{5,4,3,2,1,0:T(8,128)(2,1)}, u32[]{:S(2)}, u32[]{:S(2)}) collective-permute-start(bf16[2,2,2,2,64,2560]{5,4,3,2,1,0:T(8,128)(2,1)} %wgrad.14), channel_id=1, source_target_pairs={{0,1},{1,0},{2,3},{3,2},{4,5},{5,4},{6,7},{7,6},{8,9},{9,8},{10,11... | collective-permute-start | bytes 15728648 | tf_op jit(solution)/shard_map/ppermute | solution.py:40
  381.6 31.2 %collective-permute-start.37 = (bf16[2,2,64,2048]{3,2,1,0:T(8,128)(2,1)}, bf16[2,2,64,2048]{3,2,1,0:T(8,128)(2,1)}, u32[]{:S(2)}, u32[]{:S(2)}) collective-permute-start(bf16[2,2,64,2048]{3,2,1,0:T(8,128)(2,1)} %fusion.33), channel_id=1, source_target_pairs={{0,8},{1,9},{2,10},{3,11},{4,12},{5,13},{6,14},{7,15},{8,0},{9,1},... | collective-permute-start | bytes 3145736 | tf_op jit(solution)/shard_map/ppermute | solution.py:40
  392.7 51.1 %collective-permute-start.39 = (bf16[256,512]{1,0:T(8,128)(2,1)}, bf16[256,512]{1,0:T(8,128)(2,1)S(1)}, u32[]{:S(2)}, u32[]{:S(2)}) collective-permute-start(bf16[256,512]{1,0:T(8,128)(2,1)} %slice_bitcast_fusion.21), channel_id=1, source_target_pairs={{0,16},{1,17},{2,18},{3,19},{4,20},{5,21},{6,22},{7,23},{8,24},{9,... | collective-permute-start | bytes 786440 | tf_op jit(solution)/shard_map/ppermute | solution.py:40
  400.5 48.4 %collective-permute-start.36 = (bf16[2,2,2,64,2560]{4,3,2,1,0:T(8,128)(2,1)}, bf16[2,2,2,64,2560]{4,3,2,1,0:T(8,128)(2,1)}, u32[]{:S(2)}, u32[]{:S(2)}) collective-permute-start(bf16[2,2,2,64,2560]{4,3,2,1,0:T(8,128)(2,1)} %fusion.12), channel_id=1, source_target_pairs={{0,2},{1,5},{2,0},{3,7},{4,6},{5,1},{6,4},{7,3},{8,10},{9,13},{10,... | collective-permute-start | bytes 7864328 | tf_op jit(solution)/shard_map/ppermute | solution.py:40
  414.6 31.2 %collective-permute-start.38 = (bf16[2,64,2048]{2,1,0:T(8,128)(2,1)S(1)}, bf16[2,64,2048]{2,1,0:T(8,128)(2,1)}, u32[]{:S(2)}, u32[]{:S(2)}) collective-permute-start(bf16[2,64,2048]{2,1,0:T(8,128)(2,1)S(1)} %fusion.87), channel_id=1, source_target_pairs={{0,4},{1,3},{2,6},{3,1},{4,0},{5,7},{6,2},{7,5},{8,12},{9,11},{10,... | collective-permute-start | bytes 1572872 | tf_op jit(solution)/shard_map/ppermute | solution.py:40
  464.1 34.9 %collective-permute-start.41 = (bf16[2,2,2,2,64,1536]{5,4,3,2,1,0:T(8,128)(2,1)}, bf16[2,2,2,2,64,1536]{5,4,3,2,1,0:T(8,128)(2,1)}, u32[]{:S(2)}, u32[]{:S(2)}) collective-permute-start(bf16[2,2,2,2,64,1536]{5,4,3,2,1,0:T(8,128)(2,1)} %wgrad.16), channel_id=1, source_target_pairs={{0,1},{1,0},{2,3},{3,2},{4,5},{5,4},{6,7},{7,6},{8,9},{9,8},{10,11... | collective-permute-start | bytes 9437192 | tf_op jit(solution)/shard_map/ppermute | solution.py:40
  472.1 58.1 %collective-permute-start.44 = (f32[128,512]{1,0:T(8,128)S(1)}, f32[128,512]{1,0:T(8,128)}, u32[]{:S(2)}, u32[]{:S(2)}) collective-permute-start(f32[128,512]{1,0:T(8,128)S(1)} %constant_dynamic-slice_fusion.4), channel_id=1, source_target_pairs={{0,1},{1,0},{2,3},{3,2},{4,5},{5,4},{6,7},{7,6},{8,9},{9,8},{10,11... | collective-permute-start | bytes 786440 | tf_op jit(solution)/shard_map/ppermute | solution.py:40
  484.2 83.8 %collective-permute-start.50 = (bf16[64,2048]{1,0:T(8,128)(2,1)}, bf16[64,2048]{1,0:T(8,128)(2,1)S(1)}, u32[]{:S(2)}, u32[]{:S(2)}) collective-permute-start(bf16[64,2048]{1,0:T(8,128)(2,1)} %slice_bitcast_fusion.20), channel_id=1, source_target_pairs={{0,16},{1,17},{2,18},{3,19},{4,20},{5,21},{6,22},{7,23},{8,24},{9,... | collective-permute-start | bytes 786440 | tf_op jit(solution)/shard_map/ppermute | solution.py:40
  485.0 36.7 %collective-permute-start.40 = (bf16[2,2,64,2560]{3,2,1,0:T(8,128)(2,1)S(1)}, bf16[2,2,64,2560]{3,2,1,0:T(8,128)(2,1)S(1)}, u32[]{:S(2)}, u32[]{:S(2)}) collective-permute-start(bf16[2,2,64,2560]{3,2,1,0:T(8,128)(2,1)S(1)} %copy-done.36), channel_id=1, source_target_pairs={{0,8},{1,9},{2,10},{3,11},{4,12},{5,13},{6,14},{7,15},{8,0},{9,1},... | collective-permute-start | bytes 3932168 | tf_op jit(solution)/shard_map/ppermute | solution.py:40
  502.6 47.4 %collective-permute-start.43 = (bf16[2,2,2,64,1536]{4,3,2,1,0:T(8,128)(2,1)}, bf16[2,2,2,64,1536]{4,3,2,1,0:T(8,128)(2,1)}, u32[]{:S(2)}, u32[]{:S(2)}) collective-permute-start(bf16[2,2,2,64,1536]{4,3,2,1,0:T(8,128)(2,1)} %fusion.58), channel_id=1, source_target_pairs={{0,2},{1,5},{2,0},{3,7},{4,6},{5,1},{6,4},{7,3},{8,10},{9,13},{10,... | collective-permute-start | bytes 4718600 | tf_op jit(solution)/shard_map/ppermute | solution.py:40
  523.3 22.8 %collective-permute-start.46 = (bf16[2,256,1024]{2,1,0:T(8,128)(2,1)}, bf16[2,256,1024]{2,1,0:T(8,128)(2,1)}, u32[]{:S(2)}, u32[]{:S(2)}) collective-permute-start(bf16[2,256,1024]{2,1,0:T(8,128)(2,1)} %get-tuple-element.276), channel_id=1, source_target_pairs={{0,1},{1,0},{2,3},{3,2},{4,5},{5,4},{6,7},{7,6},{8,9},{9,8},{10,11... | collective-permute-start | bytes 3145736 | tf_op jit(solution)/shard_map/ppermute | solution.py:40
  528.9 23.8 %collective-permute-start.42 = (bf16[2,64,2560]{2,1,0:T(8,128)(2,1)}, bf16[2,64,2560]{2,1,0:T(8,128)(2,1)}, u32[]{:S(2)}, u32[]{:S(2)}) collective-permute-start(bf16[2,64,2560]{2,1,0:T(8,128)(2,1)} %fusion.85), channel_id=1, source_target_pairs={{0,4},{1,3},{2,6},{3,1},{4,0},{5,7},{6,2},{7,5},{8,12},{9,11},{10,... | collective-permute-start | bytes 1966088 | tf_op jit(solution)/shard_map/ppermute | solution.py:40
  537.7 40.3 %collective-permute-start.45 = (bf16[2,256,1024]{2,1,0:T(8,128)(2,1)}, bf16[2,256,1024]{2,1,0:T(8,128)(2,1)}, u32[]{:S(2)}, u32[]{:S(2)}) collective-permute-start(bf16[2,256,1024]{2,1,0:T(8,128)(2,1)} %get-tuple-element.275), channel_id=1, source_target_pairs={{0,1},{1,0},{2,3},{3,2},{4,5},{5,4},{6,7},{7,6},{8,9},{9,8},{10,11... | collective-permute-start | bytes 3145736 | tf_op jit(solution)/shard_map/ppermute | solution.py:40
  549.5 30.3 %collective-permute-start.47 = (bf16[2,256,1024]{2,1,0:T(8,128)(2,1)}, bf16[2,256,1024]{2,1,0:T(8,128)(2,1)}, u32[]{:S(2)}, u32[]{:S(2)}) collective-permute-start(bf16[2,256,1024]{2,1,0:T(8,128)(2,1)} %fusion.32), channel_id=1, source_target_pairs={{0,2},{1,3},{2,0},{3,1},{4,6},{5,7},{6,4},{7,5},{8,10},{9,11},{10,... | collective-permute-start | bytes 3145736 | tf_op jit(solution)/shard_map/ppermute | solution.py:40
  552.6 33.0 %collective-permute-start.52 = (bf16[2,2,64,1536]{3,2,1,0:T(8,128)(2,1)}, bf16[2,2,64,1536]{3,2,1,0:T(8,128)(2,1)}, u32[]{:S(2)}, u32[]{:S(2)}) collective-permute-start(bf16[2,2,64,1536]{3,2,1,0:T(8,128)(2,1)} %fusion.59), channel_id=1, source_target_pairs={{0,8},{1,9},{2,10},{3,11},{4,12},{5,13},{6,14},{7,15},{8,0},{9,1},... | collective-permute-start | bytes 2359304 | tf_op jit(solution)/shard_map/ppermute | solution.py:40
  571.2 16.7 %collective-permute-start.51 = (bf16[2,2,2,2,64,128]{5,4,3,2,1,0:T(8,128)(2,1)}, bf16[2,2,2,2,64,128]{5,4,3,2,1,0:T(8,128)(2,1)}, u32[]{:S(2)}, u32[]{:S(2)}) collective-permute-start(bf16[2,2,2,2,64,128]{5,4,3,2,1,0:T(8,128)(2,1)} %wgrad.18), channel_id=1, source_target_pairs={{0,1},{1,0},{2,3},{3,2},{4,5},{5,4},{6,7},{7,6},{8,9},{9,8},{10,11... | collective-permute-start | bytes 786440 | tf_op jit(solution)/shard_map/ppermute | solution.py:40
  576.2 14.0 %collective-permute-start.55 = (f32[32,2048]{1,0:T(8,128)S(1)}, f32[32,2048]{1,0:T(8,128)S(1)}, u32[]{:S(2)}, u32[]{:S(2)}) collective-permute-start(f32[32,2048]{1,0:T(8,128)S(1)} %constant_dynamic-slice_fusion.3), channel_id=1, source_target_pairs={{0,1},{1,0},{2,3},{3,2},{4,5},{5,4},{6,7},{7,6},{8,9},{9,8},{10,11... | collective-permute-start | bytes 786440 | tf_op jit(solution)/shard_map/ppermute | solution.py:40
  578.0 17.8 %collective-permute-start.54 = (bf16[64,2560]{1,0:T(8,128)(2,1)S(1)}, bf16[64,2560]{1,0:T(8,128)(2,1)S(1)}, u32[]{:S(2)}, u32[]{:S(2)}) collective-permute-start(bf16[64,2560]{1,0:T(8,128)(2,1)S(1)} %slice_bitcast_fusion.19), channel_id=1, source_target_pairs={{0,16},{1,17},{2,18},{3,19},{4,20},{5,21},{6,22},{7,23},{8,24},{9,... | collective-permute-start | bytes 983048 | tf_op jit(solution)/shard_map/ppermute | solution.py:40
  579.8 19.4 %collective-permute-start.49 = (bf16[2,128,1024]{2,1,0:T(8,128)(2,1)S(1)}, bf16[2,128,1024]{2,1,0:T(8,128)(2,1)S(1)}, u32[]{:S(2)}, u32[]{:S(2)}) collective-permute-start(bf16[2,128,1024]{2,1,0:T(8,128)(2,1)S(1)} %add_convert_fusion.7), channel_id=1, source_target_pairs={{0,2},{1,3},{2,0},{3,1},{4,6},{5,7},{6,4},{7,5},{8,10},{9,11},{10,... | collective-permute-start | bytes 1572872 | tf_op jit(solution)/shard_map/ppermute | solution.py:40
  587.2 13.2 %collective-permute-start.57 = (bf16[2,64,1536]{2,1,0:T(8,128)(2,1)S(1)}, bf16[2,64,1536]{2,1,0:T(8,128)(2,1)S(1)}, u32[]{:S(2)}, u32[]{:S(2)}) collective-permute-start(bf16[2,64,1536]{2,1,0:T(8,128)(2,1)S(1)} %fusion.94), channel_id=1, source_target_pairs={{0,4},{1,3},{2,6},{3,1},{4,0},{5,7},{6,2},{7,5},{8,12},{9,11},{10,... | collective-permute-start | bytes 1179656 | tf_op jit(solution)/shard_map/ppermute | solution.py:40
  (80 other events, 598.5 us)

commit v3 on v2

v3 whole, which is shorter than its diff:
```python
import functools
import itertools

import jax
import jax.numpy as jnp
from jax import lax
from jax.experimental import pallas as pl
from jax.experimental.pallas import tpu as pltpu
from jax.sharding import PartitionSpec as P

HEADS = 16
AXES = ("dp", "seq")
BF = jnp.bfloat16
F32 = jnp.float32
epsilon = 1e-05
masked_score = -1e30
VMEM_LIMIT = 56 * 1024 * 1024


def device_count():
    return lax.axis_size("dp") * lax.axis_size("seq")


def place():
    index = lax.axis_index("dp") * lax.axis_size("seq") + lax.axis_index("seq")
    return index


def spots(core):
    index = place()
    c = index % 2
    half = c if core == "own" else 1 - c
    return jnp.stack(
        [half, (index // 4) % 2, (index // 2) % 2, (index // 8) % 2, index // 16]
    ).astype(jnp.int32)


def hop(values, change):
    count = device_count()
    pairs = [(i, change(i)) for i in range(count)]
    return lax.ppermute(values, AXES, pairs)


def hop_core(values):
    return hop(values, lambda i: i ^ 1)


def hop_first(values):
    return hop(values, lambda i: i ^ 4 if i % 2 == 0 else i ^ 2)


def hop_second(values):
    return hop(values, lambda i: i ^ 2 if i % 2 == 0 else i ^ 4)


def hop_z0(values):
    return hop(values, lambda i: i ^ 8)


def hop_z1(values, step):
    return hop(values, lambda i: i ^ (16 * step))


def far_count():
    return device_count() // 16


def column_half(values, half):
    width = values.shape[-1] // 2
    return lax.dynamic_slice_in_dim(values, half * width, width, values.ndim - 1)


def after(value, *others):
    return lax.optimization_barrier((value, *others))[0]


class Line:
    def __init__(self):
        self.last = ()

    def __call__(self, function, first, *rest):
        if self.last:
            first = after(first, *self.last)
        result = function(first, *rest)
        self.last = jax.tree.leaves(result)[:1]
        return result


class Gather:
    def __init__(self, shards):
        c = place() % 2
        self.mine = jnp.concatenate([column_half(s, c) for s in shards], axis=1)
        other = jnp.concatenate([column_half(s, 1 - c) for s in shards], axis=1)
        self.came = hop_core(other)

    def far(self, line):
        c = place() % 2
        self.sent = line(
            lambda came, mine: jnp.where(
                c == 0, jnp.concatenate([mine, came]), jnp.concatenate([came, mine])
            ),
            self.came,
            self.mine,
        )
        self.came = [hop_z1(self.sent, k) for k in range(1, far_count())]

    def first(self, line):
        self.sent = line(lambda c, s, *o: jnp.stack([s, *o, c]), self.came[-1], self.sent, *self.came[:-1])
        self.came = hop_first(self.sent)

    def near(self, line):
        self.sent = line(lambda c, s: jnp.stack([s, c]), self.came, self.sent)
        self.came = hop_z0(self.sent)

    def second(self, line):
        self.sent = line(lambda c, s: jnp.stack([s, c]), self.came, self.sent)
        self.came = hop_second(self.sent)
        self.sent_other = hop_core(self.sent)

    def pair(self, line):
        self.came = after(self.came, *line.last)
        self.came_other = hop_core(self.came)

    def pieces(self):
        return self.came_other, self.sent, self.came, self.sent_other


def fetch(spot_ref, pieces, targets, sems):
    far_other, near_own, far_own, near_other = pieces
    far, rows = near_own.shape[2], near_own.shape[3]
    c, mx, my, mz0, mz1 = (spot_ref[i] for i in range(5))
    started, start = [], 0
    for k, (target, first, both) in enumerate(targets):
        width = both // 2
        copies = []
        for half, sides in ((c, (near_own, far_own)), (1 - c, (near_other, far_other))):
            column = pl.multiple_of(first + half * width, 128)
            for d4, dz0, d2, dz1 in itertools.product(range(2), range(2), range(2), range(far)):
                x = jnp.where(half == 0, d2, d4) ^ mx
                y = jnp.where(half == 0, d4, d2) ^ my
                z = (dz1 ^ mz1) * 2 + (dz0 ^ mz0)
                row = pl.multiple_of(((z * 2 + x) * 2 + y) * rows, rows)
                copies.append(
                    pltpu.make_async_copy(
                        sides[d4].at[dz0, d2, dz1, :, pl.ds(start, width)],
                        target.at[pl.ds(row, rows), pl.ds(column, width)],
                        sems.at[k],
                    )
                )
        for copy in copies:
            copy.start()
        started.append(copies)
        start += width
    return started


def finish(copies):
    for copy in copies:
        copy.wait()


SHORT = pl.CostEstimate(flops=1, bytes_accessed=1, transcendentals=0)
ANY = pl.BlockSpec(memory_space=pl.ANY)
SMEM = pl.BlockSpec(memory_space=pltpu.SMEM)
VMEM = pl.BlockSpec(memory_space=pltpu.VMEM)


def call(kernel, name, outs, in_specs, out_specs, scratch, grid=()):
    return pl.pallas_call(
        kernel,
        out_shape=outs,
        grid=grid,
        in_specs=in_specs,
        out_specs=out_specs,
        scratch_shapes=scratch,
        compiler_params=pltpu.CompilerParams(vmem_limit_bytes=VMEM_LIMIT),
        cost_estimate=SHORT,
        name=name,
    )


def shaped(shape, dtype):
    return jax.ShapeDtypeStruct(tuple(shape), dtype)


def kdot(left, right):
    return jnp.dot(left, right, preferred_element_type=F32)


def kdot_t(left, right):
    return lax.dot_general(left, right, (((1,), (1,)), ((), ())), preferred_element_type=F32)


def unit_of(values):
    centered = values - jnp.mean(values, axis=-1, keepdims=True)
    inverse = lax.rsqrt(jnp.mean(centered * centered, axis=-1, keepdims=True) + epsilon)
    return centered * inverse, inverse


def unit_back(unit, inverse, grad_unit):
    return inverse * (
        grad_unit
        - jnp.mean(grad_unit, axis=-1, keepdims=True)
        - unit * jnp.mean(grad_unit * unit, axis=-1, keepdims=True)
    )


def project_kernel(
    spot_ref, token_ref, small_ref, p0, p1, p2, p3, p4, p5, p6, p7,
    a_ref, q_ref, k_ref, v_ref, w_ref, w, sems, out_sem,
):
    first = (pl.program_id(0) == 0) & (pl.program_id(1) == 0)
    last = (pl.program_id(0) == pl.num_programs(0) - 1) & (
        pl.program_id(1) == pl.num_programs(1) - 1
    )
    d = token_ref.shape[3]
    kept = pltpu.make_async_copy(w, w_ref, out_sem)

    @pl.when(first)
    def _():
        half = 3 * d // 2
        one = fetch(spot_ref, (p0, p1, p2, p3), [(w, 0, half)], sems)
        two = fetch(spot_ref, (p4, p5, p6, p7), [(w, half, half)], sems.at[pl.ds(1, 1)])
        finish(one[0])
        finish(two[0])
        kept.start()

    unit, _ = unit_of(token_ref[0, 0].astype(F32))
    normed = (unit * small_ref[0:1, :] + small_ref[1:2, :]).astype(BF)
    a_ref[0, 0] = normed
    k_ref[0, 0] = kdot(normed, w[:, d : 2 * d]).astype(BF)
    v_ref[0, 0] = kdot(normed, w[:, 2 * d :]).astype(BF)

    @pl.when(pl.program_id(0) == 0)
    def _():
        q_ref[0, 0] = kdot(normed, w[:, :d]).astype(BF)

    @pl.when(last)
    def _():
        kept.wait()


def project(tokens, small, pieces):
    blocks, items, count, d = tokens.shape
    block = pl.BlockSpec((1, 1, count, d), lambda b, i: (b, i, 0, 0))
    own = pl.BlockSpec(
        (1, 1, count, d), lambda b, i: (0, jnp.where(b == 0, i, items - 1), 0, 0)
    )
    big = shaped(tokens.shape, BF)
    return call(
        project_kernel,
        "project",
        [big, shaped((1, items, count, d), BF), big, big, shaped((d, 3 * d), BF)],
        [SMEM, block, pl.BlockSpec((16, d), lambda b, i: (0, 0))] + [ANY] * 8,
        [block, own, block, block, ANY],
        [pltpu.VMEM((d, 3 * d), BF), pltpu.SemaphoreType.DMA((2,)), pltpu.SemaphoreType.DMA],
        grid=(blocks, items),
    )(spots("own"), tokens, small, *pieces)


def mix_kernel(
    spot_ref, att_ref, token_ref, caption_ref, small_ref, p0, p1, p2, p3,
    r_ref, a_ref, cq_ref, memory_ref, wso_ref, wcq_ref, wcm_ref, wco_ref,
    wso, wcq, wcm, wco, sems, out_sems,
):
    weights = (wso, wcq, wcm, wco)
    targets = [(w, 0, w.shape[1]) for w in weights]
    groups = fetch(spot_ref, (p0, p1, p2, p3), targets, sems)
    kept = [
        pltpu.make_async_copy(w, out, out_sems.at[i])
        for i, (w, out) in enumerate(zip(weights, (wso_ref, wcq_ref, wcm_ref, wco_ref)))
    ]
    finish(groups[0])
    kept[0].start()
    residual = token_ref[...].astype(F32) + kdot(att_ref[...], wso[...])
    r_ref[...] = residual
    unit, _ = unit_of(residual)
    normed = (unit * small_ref[2:3, :] + small_ref[3:4, :]).astype(BF)
    a_ref[...] = normed
    finish(groups[1])
    kept[1].start()
    cq_ref[...] = kdot(normed, wcq[...]).astype(BF)
    finish(groups[2])
    kept[2].start()
    memory_ref[...] = kdot(caption_ref[...], wcm[...]).astype(BF)
    finish(groups[3])
    kept[3].start()
    finish(kept)


def mix(attended, tokens, captions, small, pieces):
    rows, d = tokens.shape
    weights = [(d, d), (d, d), (d, 2 * d), (d, d)]
    return call(
        mix_kernel,
        "mix",
        [shaped((rows, d), F32), shaped((rows, d), BF), shaped((rows, d), BF)]
        + [shaped((captions.shape[0], 2 * d), BF)]
        + [shaped(w, BF) for w in weights],
        [SMEM, VMEM, VMEM, VMEM, VMEM, ANY, ANY, ANY, ANY],
        [VMEM] * 4 + [ANY] * 4,
        [pltpu.VMEM(w, BF) for w in weights]
        + [pltpu.SemaphoreType.DMA((4,)), pltpu.SemaphoreType.DMA((4,))],
    )(spots("own"), attended, tokens, captions, small, *pieces)


def up_kernel(
    spot_ref, att_ref, r1_ref, wco_ref, small_ref, bias_ref, p0, p1, p2, p3,
    r2_ref, a_ref, act_ref, slope_ref, w_ref, w, sems, out_sem,
):
    n = pl.program_id(0)
    width = act_ref.shape[1]
    kept = pltpu.make_async_copy(w, w_ref, out_sem)

    @pl.when(n == 0)
    def _():
        (copies,) = fetch(spot_ref, (p0, p1, p2, p3), [(w, 0, w.shape[1])], sems)
        residual = r1_ref[...] + kdot(att_ref[...], wco_ref[...])
        r2_ref[...] = residual
        unit, _ = unit_of(residual)
        a_ref[...] = (unit * small_ref[4:5, :] + small_ref[5:6, :]).astype(BF)
        finish(copies)
        kept.start()

    part = w[:, pl.ds(pl.multiple_of(n * width, width), width)]
    before = kdot(a_ref[...], part) + bias_ref[...]
    phi = 0.5 + 0.5 * lax.erf(before * (0.5 ** 0.5))
    act_ref[...] = (before * phi).astype(BF)
    slope_ref[...] = (phi + before * (jnp.exp(-0.5 * before * before) * 0.3989422804014327)).astype(BF)

    @pl.when(n == pl.num_programs(0) - 1)
    def _():
        kept.wait()


def up_gelu(attended, residual, cross_out, small, bias, pieces, block=512):
    rows, d = residual.shape
    hidden = bias.shape[1]
    whole = pl.BlockSpec((rows, d), lambda n: (0, 0))
    column = pl.BlockSpec((rows, block), lambda n: (0, n))
    return call(
        up_kernel,
        "up_gelu",
        [shaped((rows, d), F32), shaped((rows, d), BF)]
        + [shaped((rows, hidden), BF)] * 2
        + [shaped((d, hidden), BF)],
        [
            SMEM, whole, whole, pl.BlockSpec((d, d), lambda n: (0, 0)),
            pl.BlockSpec((16, d), lambda n: (0, 0)), pl.BlockSpec((1, block), lambda n: (0, n)),
            ANY, ANY, ANY, ANY,
        ],
        [whole, whole, column, column, ANY],
        [pltpu.VMEM((d, hidden), BF), pltpu.SemaphoreType.DMA((1,)), pltpu.SemaphoreType.DMA],
        grid=(hidden // block,),
    )(spots("own"), attended, residual, cross_out, small, bias, *pieces)


def down_kernel(
    spot_ref, g_ref, slope_ref, act_ref, r2_ref, small_ref, p0, p1, p2, p3,
    out_ref, grad_ref, bias_ref, down_bias_ref, w, total, sems,
):
    n = pl.program_id(0)
    height = act_ref.shape[1]

    @pl.when(n == 0)
    def _():
        (copies,) = fetch(spot_ref, (p0, p1, p2, p3), [(w, 0, w.shape[1])], sems)
        total[...] = r2_ref[...] + small_ref[6:7, :]
        down_bias_ref[...] = jnp.sum(g_ref[...].astype(F32), axis=0, keepdims=True)
        finish(copies)

    part = w[pl.ds(pl.multiple_of(n * height, height), height), :]
    grad = (kdot_t(g_ref[...], part) * slope_ref[...].astype(F32)).astype(BF)
    grad_ref[...] = grad
    bias_ref[...] = jnp.sum(grad.astype(F32), axis=0, keepdims=True)
    total[...] += kdot(act_ref[...], part)

    @pl.when(n == pl.num_programs(0) - 1)
    def _():
        out_ref[...] = total[...].astype(BF)


def down_both(grad, slope, activated, residual, small, pieces, block=512):
    rows, d = residual.shape
    hidden = slope.shape[1]
    whole = pl.BlockSpec((rows, d), lambda n: (0, 0))
    column = pl.BlockSpec((rows, block), lambda n: (0, n))
    return call(
        down_kernel,
        "down",
        [shaped((rows, d), BF), shaped((rows, hidden), BF), shaped((1, hidden), F32), shaped((1, d), F32)],
        [SMEM, whole, column, column, whole, pl.BlockSpec((16, d), lambda n: (0, 0)), ANY, ANY, ANY, ANY],
        [whole, column, pl.BlockSpec((1, block), lambda n: (0, n)), pl.BlockSpec((1, d), lambda n: (0, 0))],
        [pltpu.VMEM((hidden, d), BF), pltpu.VMEM((rows, d), F32), pltpu.SemaphoreType.DMA((1,))],
        grid=(hidden // block,),
    )(spots("own"), grad, slope, activated, residual, small, *pieces)


def feed_back_kernel(
    g_ref, w_ref, r2_ref, cot_ref, small_ref, wco_ref, dr_ref, low_ref, datt_ref, vec_ref, total
):
    n = pl.program_id(0)

    @pl.when(n == 0)
    def _():
        total[...] = jnp.zeros_like(total)

    total[...] += kdot_t(g_ref[...], w_ref[...])

    @pl.when(n == pl.num_programs(0) - 1)
    def _():
        grad = total[...]
        unit, inverse = unit_of(r2_ref[...])
        vec_ref[0:1, :] = jnp.sum(grad * unit, axis=0, keepdims=True)
        vec_ref[1:2, :] = jnp.sum(grad, axis=0, keepdims=True)
        out = cot_ref[...].astype(F32) + unit_back(unit, inverse, grad * small_ref[4:5, :])
        dr_ref[...] = out
        low = out.astype(BF)
        low_ref[...] = low
        datt_ref[...] = kdot_t(low, wco_ref[...]).astype(BF)


def feed_back(grad, up, residual, cotangent, small, cross_out, block=1024):
    rows, d = residual.shape
    hidden = grad.shape[1]
    whole = pl.BlockSpec((rows, d), lambda n: (0, 0))
    return call(
        feed_back_kernel,
        "feed_back",
        [shaped((rows, d), F32), shaped((rows, d), BF), shaped((rows, d), BF), shaped((8, d), F32)],
        [
            pl.BlockSpec((rows, block), lambda n: (0, n)), pl.BlockSpec((d, block), lambda n: (0, n)),
            whole, whole, pl.BlockSpec((16, d), lambda n: (0, 0)), pl.BlockSpec((d, d), lambda n: (0, 0)),
        ],
        [whole, whole, whole, pl.BlockSpec((8, d), lambda n: (0, 0))],
        [pltpu.VMEM((rows, d), F32)],
        grid=(hidden // block,),
    )(grad, up, residual, cotangent, small, cross_out)


def cross_back_kernel(
    g_ref, wcq_ref, r1_ref, dr2_ref, small_ref, wso_ref, dr_ref, low_ref, datt_ref, vec_ref
):
    grad = kdot_t(g_ref[...], wcq_ref[...])
    unit, inverse = unit_of(r1_ref[...])
    vec_ref[0:1, :] = jnp.sum(grad * unit, axis=0, keepdims=True)
    vec_ref[1:2, :] = jnp.sum(grad, axis=0, keepdims=True)
    out = dr2_ref[...] + unit_back(unit, inverse, grad * small_ref[2:3, :])
    dr_ref[...] = out
    low = out.astype(BF)
    low_ref[...] = low
    datt_ref[...] = kdot_t(low, wso_ref[...]).astype(BF)


def cross_back(grad, cross_query, residual, grad_residual, small, self_out):
    rows, d = residual.shape
    return call(
        cross_back_kernel,
        "cross_back",
        [shaped((rows, d), F32), shaped((rows, d), BF), shaped((rows, d), BF), shaped((8, d), F32)],
        [VMEM] * 6,
        [VMEM] * 4,
        [],
    )(grad, cross_query, residual, grad_residual, small, self_out)


def self_back_kernel(
    dq0_ref, dk0_ref, dv0_ref, dq1_ref, dk1_ref, dv1_ref, token_ref, w_ref,
    cross_ref, feed_ref, down_ref, up_ref, *refs,
):
    *da_refs, vec_ref, own = refs
    first = (pl.program_id(0) == 0) & (pl.program_id(1) == 0)
    d = token_ref.shape[3]
    half = d // 2

    def back(ref, at):
        return kdot_t(ref[...].reshape(ref.shape[-2:]), w_ref[:, at : at + half])

    own[...] = (back(dk0_ref, d) + back(dk1_ref, d + half)) + (
        back(dv0_ref, 2 * d) + back(dv1_ref, 2 * d + half)
    )

    @pl.when(pl.program_id(0) == 0)
    def _():
        own[...] += back(dq0_ref, 0) + back(dq1_ref, half)

    grad = own[...]
    for b, da_ref in enumerate(da_refs):

        @pl.when(pl.program_id(0) == b)
        def _():
            da_ref[0] = grad.astype(BF)

    unit, _ = unit_of(token_ref[0, 0].astype(F32))
    gain = jnp.sum(grad * unit, axis=0, keepdims=True)
    shift = jnp.sum(grad, axis=0, keepdims=True)

    @pl.when(first)
    def _():
        vec_ref[0:1, :] = gain
        vec_ref[1:2, :] = shift
        vec_ref[2:4, :] = cross_ref[0:2, :]
        vec_ref[4:6, :] = feed_ref[0:2, :]
        vec_ref[6:7, :] = down_ref[...]
        for k in range(up_ref.shape[1] // d):
            vec_ref[7 + k : 8 + k, :] = up_ref[:, k * d : (k + 1) * d]

    @pl.when(jnp.logical_not(first))
    def _():
        vec_ref[0:1, :] += gain
        vec_ref[1:2, :] += shift


def self_back(grads, tokens, weight, cross, feed, down, up):
    blocks, items, count, d = tokens.shape
    block = pl.BlockSpec((1, 1, count, d), lambda b, i: (b, i, 0, 0))
    part = pl.BlockSpec((1, 1, count, d // 2), lambda b, i: (b, i, 0, 0))

    def only(at):
        return lambda b, i: (jnp.where(b == at, i, jnp.where(b < at, 0, items - 1)), 0, 0)

    def whole(array):
        return pl.BlockSpec(array.shape, lambda b, i: (0, 0))

    own = pl.BlockSpec((1, count, d // 2), only(0))
    height = 7 + up.shape[1] // d
    return call(
        self_back_kernel,
        "self_back",
        [shaped((items, count, d), BF)] * blocks + [shaped((height, d), F32)],
        [own, part, part, own, part, part, block]
        + [whole(a) for a in (weight, cross, feed, down, up)],
        [pl.BlockSpec((1, count, d), only(b)) for b in range(blocks)]
        + [pl.BlockSpec((height, d), lambda b, i: (0, 0))],
        [pltpu.VMEM((count, d), F32)],
        grid=(blocks, items),
    )(*grads, tokens, weight, cross, feed, down, up)


def wgrad_kernel(kinds, rows, side, spot_ref, *refs):
    half, mx, my, mz0 = (spot_ref[i] for i in range(4))
    scratch = refs[-1]
    outs = refs[-5:-1] if side == "other" else refs[-3:-1]
    at, start = 0, 0
    for kind in kinds:
        if kind == "dot":
            left, right = refs[at], refs[at + 1]
            at += 2
            block = lax.dot_general(
                left[...], right[...], (((0,), (0,)), ((), ())), preferred_element_type=F32
            )
        else:
            block = refs[at][...].astype(F32)
            at += 1
        scratch[:, start : start + block.shape[1]] = block
        start += block.shape[1]
    for d4, dz0, d2 in itertools.product(range(2), range(2), range(2)):
        x = jnp.where(half == 0, d2, d4) ^ mx
        y = jnp.where(half == 0, d4, d2) ^ my
        j = ((dz0 ^ mz0) * 2 + x) * 2 + y
        part = scratch[pl.ds(pl.multiple_of(j * rows, rows), rows), :]
        if side == "other":
            outs[d4 * 2 + dz0][d2, 0] = part.astype(BF)
        else:
            came = refs[at + d4 * 2 + dz0]
            outs[d4][dz0, d2, 0] = (part + came[d2, 0].astype(F32)).astype(BF)


def wgrad(terms, side, came=None):
    far = far_count()
    kinds = tuple("dot" if len(t) == 2 else "raw" for t in terms)
    height = terms[0][0].shape[1] if kinds[0] == "dot" else terms[0][0].shape[0]
    rows = height // (8 * far)
    specs, args, total = [], [], 0
    for term in terms:
        right = term[-1]
        width = right.shape[1] // 2
        if len(term) == 2:
            left = term[0]
            specs.append(pl.BlockSpec((left.shape[0], 8 * rows), lambda z, s: (0, z)))
            specs.append(pl.BlockSpec((right.shape[0], width), lambda z, s: (0, s[0])))
        else:
            specs.append(pl.BlockSpec((8 * rows, width), lambda z, s: (z, s[0])))
        args += list(term)
        total += width
    piece = pl.BlockSpec((2, 1, rows, total), lambda z, s: (0, z ^ s[4], 0, 0))
    part = pl.BlockSpec((2, 2, 1, rows, total), lambda z, s: (0, 0, z ^ s[4], 0, 0))
    if side == "other":
        out_shape, out_specs = [shaped((2, far, rows, total), BF)] * 4, [piece] * 4
    else:
        specs += [piece] * 4
        args += came
        out_shape, out_specs = [shaped((2, 2, far, rows, total), BF)] * 2, [part] * 2
    return pl.pallas_call(
        functools.partial(wgrad_kernel, kinds, rows, side),
        out_shape=out_shape,
        grid_spec=pltpu.PrefetchScalarGridSpec(
            num_scalar_prefetch=1,
            grid=(far,),
            in_specs=specs,
            out_specs=out_specs,
            scratch_shapes=[pltpu.VMEM((8 * rows, total), F32)],
        ),
        compiler_params=pltpu.CompilerParams(vmem_limit_bytes=VMEM_LIMIT),
        cost_estimate=SHORT,
        name="wgrad",
    )(spots(side), *args)


def wide(values):
    return values.astype(F32)


class Scatter:
    def __init__(self, line, terms):
        self.widths = [t[-1].shape[1] // 2 for t in terms]

        self.terms = terms
        sent = line(lambda f: wgrad([(f, *terms[0][1:]), *terms[1:]], "other"), terms[0][0])
        self.came0 = [hop_core(v) for v in sent]

    def second(self, line):
        self.own, sent = line(lambda *c: wgrad(self.terms, "own", c), *self.came0)
        self.came1 = hop_second(sent)

    def near(self, line):
        def add(c1, o):
            return (wide(o[1]) + wide(c1[1])).astype(BF)

        self.came2 = hop_z0(line(add, self.came1, self.own))

    def first(self, line):
        def add(c2, c1, o):
            return (wide(o[0, 1]) + wide(c1[0, 1]) + wide(c2[1])).astype(BF)

        self.came3 = hop_first(line(add, self.came2, self.came1, self.own))

    def far(self, line):
        def add(c3, c2, c1, o):
            kept = wide(o[0, 0]) + wide(c1[0, 0]) + wide(c2[0]) + wide(c3)
            return kept.astype(BF), kept[0]

        low, self.kept = line(add, self.came3, self.came2, self.came1, self.own)
        self.came4 = [hop_z1(low[k], k) for k in range(1, far_count())]

    def close(self, line):
        total = line(lambda c, t, *o: sum(map(wide, o), t + wide(c)), self.came4[-1], self.kept, *self.came4[:-1])
        rows = total.shape[0] // 2
        c = place() % 2
        self.mine = lax.dynamic_slice_in_dim(total, c * rows, rows, 0)
        self.theirs = hop_core(lax.dynamic_slice_in_dim(total, (1 - c) * rows, rows, 0))

    def result(self, line):
        c = place() % 2

        def join(came, mine):
            left = jnp.where(c == 0, mine, came)
            right = jnp.where(c == 0, came, mine)
            results, start = [], 0
            for width in self.widths:
                at = slice(start, start + width)
                results.append(jnp.concatenate([left[:, at], right[:, at]], axis=1))
                start += width
            return results

        return line(join, self.theirs, self.mine)


class SmallSum:
    def __init__(self, values):
        self.values, self.distance = values, 1
        self.send()

    def send(self):
        self.came = hop(self.values, lambda i: i ^ self.distance)

    def step(self, line):
        self.values = line(lambda c, v: c + v, self.came, self.values)
        self.distance *= 2
        if self.distance < device_count():
            self.send()

    def finish(self, line):
        while self.distance < device_count():
            self.step(line)
        return self.values


def small_rows(vectors, bias):
    n = device_count()
    part = vectors[0].shape[0]
    width = part * n
    rows = jnp.zeros((len(vectors), width), BF)
    rows = lax.dynamic_update_slice(rows, jnp.stack(vectors), (0, place() * part))
    long = jnp.zeros((bias.shape[0] * n,), BF)
    long = lax.dynamic_update_slice(long, bias, (place() * bias.shape[0],))
    return jnp.concatenate([rows, long.reshape(-1, width)])


def small_parts(rows, count):
    n = device_count()
    part = rows.shape[1] // n
    own = lax.dynamic_slice_in_dim(rows[:count], place() * part, part, 1)
    long = rows[count:].reshape(-1)
    share = long.shape[0] // n
    return [own[i] for i in range(count)], lax.dynamic_slice_in_dim(long, place() * share, share)


def shifts(info_ref, kind, block):
    if kind == "length" or block == 0:
        return None
    me = info_ref[0]
    return jnp.where((me ^ block) < me, 0.0, -masked_score).astype(F32)

def allowed_keys(info_ref, kind, item, span, count):
    shape = (span, count)
    row = lax.broadcasted_iota(jnp.int32, shape, 0)
    if kind == "length":
        return row < info_ref[item]
    return row <= lax.broadcasted_iota(jnp.int32, shape, 1)

def attend_kernel(kind, info_ref, q_ref, k_ref, v_ref, o_ref, lse_ref):
    blocks, _, span, wide_lanes = k_ref.shape
    count = q_ref.shape[2]
    lanes = 128
    head = lanes // 2
    low_lane = lax.broadcasted_iota(jnp.int32, (count, lanes), 1) < head
    allowed = allowed_keys(info_ref, kind, pl.program_id(0), span, count)
    outside = [shifts(info_ref, kind, j) for j in range(blocks)]
    for pair in range(wide_lanes // lanes):
        at = slice(pair * lanes, (pair + 1) * lanes)
        values_t = v_ref[:, :, :, at].reshape(blocks * span, lanes).T
        queries = q_ref[0, 0, :, at] * (head ** -0.5)
        outs = []
        for h in range(2):
            mine = jnp.where(low_lane if h == 0 else ~low_lane, queries, 0).astype(BF)
            scores = [
                lax.dot_general(k_ref[j, 0, :, at], mine, (((1,), (1,)), ((), ())), preferred_element_type=F32)
                for j in range(blocks)
            ]
            scores[0] = jnp.where(allowed, scores[0], masked_score)
            top = jnp.max(scores[0], axis=0, keepdims=True)
            for j in range(1, blocks):
                top = jnp.maximum(top, jnp.max(scores[j], axis=0, keepdims=True) - outside[j])
            soft = [jnp.exp(scores[0] - top)]
            soft += [jnp.exp(scores[j] - (top + outside[j])) for j in range(1, blocks)]
            total = sum(jnp.sum(s, axis=0, keepdims=True) for s in soft)
            lse_ref[0, pair, h : h + 1, :] = top + jnp.log(total)
            low = jnp.concatenate([s.astype(BF) for s in soft], axis=0)
            out = jnp.dot(values_t[h * head : (h + 1) * head], low, preferred_element_type=F32)
            outs.append(out / total)
        o_ref[0, :, at] = jnp.concatenate(outs, axis=0).T.astype(BF)

def attend(kind, info, queries, q_at, keyed, k_at, valued, v_at, group=1):
    blocks, items, span, _ = keyed.shape
    count = queries.shape[2]
    pairs = HEADS // 2
    lanes = 128 * group
    width = pairs * 128
    return pl.pallas_call(
        functools.partial(attend_kernel, kind),
        out_shape=[jax.ShapeDtypeStruct((items, count, width), BF), jax.ShapeDtypeStruct((items, pairs, 2, count), F32)],
        grid_spec=pltpu.PrefetchScalarGridSpec(
            num_scalar_prefetch=1, grid=(items, pairs // group),
            in_specs=[
                pl.BlockSpec((1, 1, count, lanes), lambda i, p, s: (0, i, 0, p + q_at // lanes)),
                pl.BlockSpec((blocks, 1, span, lanes), lambda i, p, s: (0, i, 0, p + k_at // lanes)),
                pl.BlockSpec((blocks, 1, span, lanes), lambda i, p, s: (0, i, 0, p + v_at // lanes)),
            ],
            out_specs=[
                pl.BlockSpec((1, count, lanes), lambda i, p, s: (i, 0, p)),
                pl.BlockSpec((1, group, 2, count), lambda i, p, s: (i, p, 0, 0)),
            ]),
        compiler_params=pltpu.CompilerParams(vmem_limit_bytes=VMEM_LIMIT),
        cost_estimate=SHORT,
        name="attend",
    )(info, queries, keyed, valued)

def attend_back_kernel(kind, info_ref, q_ref, k_ref, v_ref, o_ref, lse_ref, do_ref, dq_ref, dk_ref, dv_ref):
    blocks, _, span, wide_lanes = k_ref.shape
    count = q_ref.shape[2]
    lanes = 128
    head = lanes // 2
    scaling = head ** -0.5
    low_lane = lax.broadcasted_iota(jnp.int32, (count, lanes), 1) < head
    allowed = allowed_keys(info_ref, kind, pl.program_id(0), span, count)
    outside = [shifts(info_ref, kind, j) for j in range(blocks)]
    for pair in range(wide_lanes // lanes):
        at = slice(pair * lanes, (pair + 1) * lanes)
        keys_t = k_ref[:, :, :, at].reshape(blocks * span, lanes).T
        queries = q_ref[0, 0, :, at] * scaling
        grad = do_ref[0, :, at]
        product_t = (grad.astype(F32) * o_ref[0, :, at].astype(F32)).T
        grad_q, dk, dv = [], [0.0] * blocks, [0.0] * blocks
        for h in range(2):
            lane = low_lane if h == 0 else ~low_lane
            mine = jnp.where(lane, queries, 0).astype(BF)
            grad_mine = jnp.where(lane, grad, 0).astype(BF)
            lse = lse_ref[0, pair, h : h + 1, :]
            delta = jnp.sum(product_t[h * head : (h + 1) * head], axis=0, keepdims=True)
            grads = []
            for j in range(blocks):
                scores = lax.dot_general(k_ref[j, 0, :, at], mine, (((1,), (1,)), ((), ())), preferred_element_type=F32)
                if j == 0:
                    soft = jnp.where(allowed, jnp.exp(scores - lse), 0.0)
                else:
                    soft = jnp.exp(scores - (lse + outside[j]))
                grad_soft = lax.dot_general(v_ref[j, 0, :, at], grad_mine, (((1,), (1,)), ((), ())), preferred_element_type=F32)
                grads.append((soft * (grad_soft - delta)).astype(BF))
                dv[j] += jnp.dot(soft.astype(BF), grad_mine, preferred_element_type=F32)
                dk[j] += jnp.dot(grads[j], mine, preferred_element_type=F32)
            grad_scores = jnp.concatenate(grads, axis=0)
            grad_q.append(jnp.dot(keys_t[h * head : (h + 1) * head], grad_scores, preferred_element_type=F32))
        dq_ref[0, :, at] = (jnp.concatenate(grad_q, axis=0) * scaling).T.astype(BF)
        for j in range(blocks):
            dk_ref[j, 0, :, at] = dk[j].astype(BF)
            dv_ref[j, 0, :, at] = dv[j].astype(BF)

def attend_back(kind, info, queries, q_at, keyed, k_at, valued, v_at, attended, lse, grad, group=1, part=(0, 1)):
    blocks, items, span, _ = keyed.shape
    count = queries.shape[2]
    pairs = HEADS // 2 // part[1]
    skip = part[0] * pairs // group
    lanes = 128 * group
    width = pairs * 128
    row = pl.BlockSpec((1, count, lanes), lambda i, p, s: (i, 0, p + skip))
    out = pl.BlockSpec((1, count, lanes), lambda i, p, s: (i, 0, p))
    key = pl.BlockSpec((blocks, 1, span, lanes), lambda i, p, s: (0, i, 0, p))
    return pl.pallas_call(
        functools.partial(attend_back_kernel, kind),
        out_shape=[jax.ShapeDtypeStruct((items, count, width), BF)] + [jax.ShapeDtypeStruct((blocks, items, span, width), BF)]*2,
        grid_spec=pltpu.PrefetchScalarGridSpec(
            num_scalar_prefetch=1, grid=(items, pairs // group),
            in_specs=[
                pl.BlockSpec((1, 1, count, lanes), lambda i, p, s: (0, i, 0, p + skip + q_at // lanes)),
                pl.BlockSpec((blocks, 1, span, lanes), lambda i, p, s: (0, i, 0, p + skip + k_at // lanes)),
                pl.BlockSpec((blocks, 1, span, lanes), lambda i, p, s: (0, i, 0, p + skip + v_at // lanes)),
                row,
                pl.BlockSpec((1, group, 2, count), lambda i, p, s: (i, p + skip, 0, 0)),
                row,
            ],
            out_specs=[out, key, key]),
        compiler_params=pltpu.CompilerParams(vmem_limit_bytes=VMEM_LIMIT),
        cost_estimate=SHORT,
        name="attend_back",
    )(info, queries, keyed, valued, attended, lse, grad)

def flat(tensor):
    return tensor.reshape(-1, tensor.shape[-1])


def dot_t(left, right):
    return lax.dot_general(
        left, right, (((left.ndim - 1,), (1,)), ((), ())), preferred_element_type=F32
    )


def hop_seq(values, step):
    size = lax.axis_size("seq")
    return hop(values, lambda i: i // size * size + (i % size ^ step))


def body(
    tokens,
    captions,
    caption_lengths,
    cotangent,
    self_gain,
    self_shift,
    self_in_weight,
    self_out_weight,
    cross_gain,
    cross_shift,
    cross_query_weight,
    cross_memory_weight,
    cross_out_weight,
    feed_gain,
    feed_shift,
    up_weight,
    up_bias,
    down_weight,
    down_bias,
):
    features = tokens.shape[2]
    k_bias = up_weight.shape[1] // features
    half = 3 * features // 2
    ga = Gather([self_in_weight[:, :half]])
    line = Line()
    ga.far(line)
    tokens_y = hop_seq(tokens, 2)
    tokens_1 = hop_seq(tokens, 1)
    ge = Gather([self_in_weight[:, half:]])
    gb = Gather([self_out_weight, cross_query_weight, cross_memory_weight, cross_out_weight])
    gc = Gather([up_weight])
    gd = Gather([down_weight])
    small = SmallSum(
        small_rows(
            [self_gain, self_shift, cross_gain, cross_shift, feed_gain, feed_shift, down_bias],
            up_bias,
        )
    )
    ga.first(line)
    ge.far(line)
    ga.near(line)
    ge.first(line)
    ga.second(line)
    ge.near(line)
    small.step(line)
    gb.far(line)
    small.step(line)
    tokens_y = after(tokens_y, *line.last)
    tokens_3 = hop_seq(tokens_y, 1)
    ga.pair(line)
    ge.second(line)
    small.step(line)
    gb.first(line)
    small.step(line)
    small_low = small.finish(line)
    small_full = line(
        lambda v: jnp.pad(wide(v), ((0, 16 - v.shape[0]), (0, 0))), small_low
    )
    up_offset = wide(small_low[7:]).reshape(1, -1)
    all_tokens = line(lambda a, b, c, d: jnp.stack([d, b, c, a]), tokens_3, tokens_1, tokens_y, tokens)
    ge.pair(line)
    gb.near(line)
    gc.far(line)
    seq_place = lax.axis_index("seq").astype(jnp.int32)[None]

    normed1, queries, key_rows, value_rows, self_in = line(
        lambda t: project(t, small_full, ga.pieces() + ge.pieces()), all_tokens
    )
    gc.first(line)
    gb.second(line)
    gc.near(line)
    gd.far(line)
    attended1, lse1 = line(
        lambda q: attend("causal", seq_place, q, 0, key_rows, 0, value_rows, 0, 2), queries
    )
    gb.pair(line)
    gd.first(line)
    gc.second(line)
    gd.near(line)
    flat_tokens, flat_captions = flat(tokens), flat(captions)
    residual1, normed2, cross_queries, memory, self_out, cross_query, cross_memory, cross_out = line(
        lambda a: mix(flat(a), flat_tokens, flat_captions, small_full, gb.pieces()), attended1
    )
    cross_queries = cross_queries.reshape(1, *tokens.shape)
    memory = memory.reshape(1, *captions.shape[:2], -1)

    attended2, lse2 = line(
        lambda q: attend("length", caption_lengths, q, 0, memory, 0, memory, features, 8),
        cross_queries,
    )
    gc.pair(line)
    gd.second(line)

    residual2, normed3, activated, slope, up = line(
        lambda a: up_gelu(flat(a), residual1, cross_out, small_full, up_offset, gc.pieces()),
        attended2,
    )
    low3 = flat(cotangent)
    s1 = Scatter(line, [(activated, low3)])
    gd.pair(line)

    final, grad_before, grad_up_bias, grad_down_bias = line(
        lambda g: down_both(g, slope, activated, residual2, small_full, gd.pieces()), low3
    )
    s1.second(line)
    s2 = Scatter(line, [(normed3, grad_before)])
    grad_second, low2, grad_attended2, grad_feed = line(
        lambda g: feed_back(g, up, residual2, low3, small_full, cross_out), grad_before
    )
    s2.second(line)

    grad_attended2 = grad_attended2.reshape(tokens.shape)
    grad_cq, grad_mk, grad_mv = line(
        lambda g: attend_back(
            "length", caption_lengths, cross_queries, 0, memory, 0, memory, features,
            attended2, lse2, g, 8,
        ),
        grad_attended2,
    )
    s1.near(line)
    grad_cq = flat(grad_cq)
    grad_first, low1, grad_attended1, grad_cross = line(
        lambda g: cross_back(g, cross_query, residual1, grad_second, small_full, self_out), grad_cq
    )
    grad_memory = line(
        lambda k, v: jnp.concatenate([flat(k), flat(v)], axis=-1), grad_mk, grad_mv
    )
    caption_sum = line(lambda a: dot_t(a, cross_memory).astype(BF), grad_memory)
    caption_came = hop_seq(caption_sum, 1)
    s3 = Scatter(
        line,
        [
            (normed2, grad_cq),
            (flat_captions, grad_memory),
            (flat(attended2), low2),
            (flat(attended1), low1),
        ],
    )

    grad_attended1 = grad_attended1.reshape(tokens.shape)
    flat_normed1 = flat(normed1)

    def heads_back(i):
        return line(
            lambda g: attend_back(
                "causal", seq_place, queries, 0, key_rows, 0, value_rows, 0, attended1, lse1, g, 2,
                (i, 2),
            ),
            grad_attended1,
        )

    def heads_terms(grads):
        return [
            (flat_normed1[: low1.shape[0]], flat(grads[0])),
            (flat_normed1, flat(grads[1])),
            (flat_normed1, flat(grads[2])),
        ]

    s2.near(line)
    grads_a = heads_back(0)
    s1.first(line)
    s3.second(line)
    s4 = Scatter(line, heads_terms(grads_a))
    caption_sum = line(lambda c, v: (wide(c) + wide(v)).astype(BF), caption_came, caption_sum)
    caption_came = hop_seq(caption_sum, 2)
    s1.far(line)
    grads_b = heads_back(1)
    s2.first(line)
    s3.near(line)
    s5 = Scatter(line, heads_terms(grads_b))
    s4.second(line)
    s2.far(line)
    s1.close(line)
    s5.second(line)
    s4.near(line)
    *grad_blocks, small_grads = line(
        lambda g, *o: self_back(
            (g, *o, *grads_b), all_tokens, self_in, grad_cross, grad_feed, grad_down_bias, grad_up_bias
        ),
        *grads_a,
    )
    grad_ones = hop_seq(grad_blocks[1], 1)
    grad_threes = hop_seq(grad_blocks[3], 1)
    small = SmallSum(small_grads)
    s3.first(line)
    s5.near(line)
    grad_far = line(lambda a, b: (wide(a) + wide(b)).astype(BF), grad_threes, grad_blocks[2])
    grad_twos = hop_seq(grad_far, 2)
    s4.first(line)
    small.step(line)
    s2.close(line)
    small.step(line)
    s3.far(line)
    small.step(line)
    (grad_down,) = s1.result(line)
    s4.far(line)
    small.step(line)
    s5.first(line)
    small.step(line)
    (grad_up,) = s2.result(line)
    s3.close(line)
    grad_captions = line(lambda c, v: wide(c) + wide(v), caption_came, caption_sum)
    grad_captions = grad_captions.reshape(captions.shape)
    small_parts_out, grad_bias = small_parts(small.finish(line), 7)

    def last_norm(came, one, own):
        grad = wide(own) + wide(one) + wide(came)
        unit, inverse = unit_of(wide(tokens))
        return grad_first.reshape(tokens.shape) + unit_back(unit, inverse, grad * small_full[0])

    s5.far(line)
    grad_tokens = line(last_norm, grad_twos, grad_ones, grad_blocks[0])
    s4.close(line)
    results3 = s3.result(line)
    grad_cross_query, grad_cross_memory, grad_cross_out, grad_self_out = results3
    s5.close(line)
    grads_4 = s4.result(line)
    grads_5 = s5.result(line)
    return (
        final.reshape(tokens.shape),
        grad_tokens,
        grad_captions,
        small_parts_out[0],
        small_parts_out[1],
        jnp.concatenate([g for pair in zip(grads_4, grads_5) for g in pair], axis=1),
        grad_self_out,
        small_parts_out[2],
        small_parts_out[3],
        grad_cross_query,
        grad_cross_memory,
        grad_cross_out,
        small_parts_out[4],
        small_parts_out[5],
        grad_up,
        grad_bias,
        grad_down,
        small_parts_out[6],
    )


def solution(mesh):
    tokens_spec = P("dp", "seq", None)
    rows1, rows2 = P(AXES), P(AXES, None)
    return jax.shard_map(
        body,
        mesh=mesh,
        in_specs=(
            tokens_spec, P("dp", None, None), P("dp"), tokens_spec,
            rows1, rows1, rows2, rows2, rows1, rows1, rows2, rows2, rows2,
            rows1, rows1, rows2, rows1, rows2, rows1,
        ),
        out_specs=(
            tokens_spec, tokens_spec, P("dp", None, None),
            rows1, rows1, rows2, rows2, rows1, rows1, rows2, rows2, rows2,
            rows1, rows1, rows2, rows1, rows2, rows1,
        ),
        check_vma=False,
    )
```

time: 624 us -> 555 us (0.89)
  Pallas kernels: 181 us -> 264 us
  matrix products: 81.4 us -> 4.65 us
  other arithmetic: 123 us -> 50.1 us
  starting transfers between devices: 60.2 us -> 77.7 us
  local copies, waits for them, and re-layouts: 40.6 us -> 26.3 us
  waiting for transfers between devices: 131 us -> 122 us
    pallas_call x15 -> x17, Pallas kernels: 112 us -> 193 us  [the longest x10 80.8 us: wgrad(): pl.pallas_call(functools.partial(wgrad_kernel, kinds, rows, side), out_sh...]
    dot_general x9 -> x1, matrix products: 51.8 us -> 4.65 us  [dot_t(): lax.dot_general(left, right, (((left.ndim - 1,), (1,)), ((), ())), prefer...]
    convert_element_type x24 -> x12, other arithmetic: 59.2 us -> 15.6 us  [the longest x5 6.77 us: add(): return (wide(o[1]) + wide(c1[1])).astype(BF)]
    dot_general x8 -> x0, matrix products: 29.7 us -> none  [dot(): return jnp.dot(left, right, preferred_element_type=F32)]
    reduce_sum x15 -> x3, other arithmetic: 22.8 us -> 1.55 us  [the longest x1 0.93 us: unit_back(): jnp.mean(grad_unit, axis=-1, keepdims=True)]
    ppermute x64 -> x98, starting transfers between devices: 60.2 us -> 77.7 us  [hop(): return lax.ppermute(values, AXES, pairs)]
    ppermute x64 -> x98, waiting for transfers between devices: 131 us -> 122 us  [hop(): return lax.ppermute(values, AXES, pairs)]
    another operation x9 -> x1, local copies, waits for them, and re-layouts: 7.18 us -> 0.78 us  [small_rows(): jnp.stack(vectors)]
  transfers between devices with their start and end apart: 64 -> 98, of which waited for: 21 -> 28; matrix products, arithmetic and copies ran while one was open for 34% -> 12% of each run, Pallas kernels for 25% -> 44%
where the time goes in v3:
time: 555 us; the launch traced here: 547 us
  Pallas kernels  264 us (48%)
  waiting for transfers between devices  122 us (22%)
  starting transfers between devices  77.7 us (14%)
  other arithmetic  50.1 us (9%)
  local copies, waits for them, and re-layouts  26.3 us (5%)
    ppermute x98, waiting for transfers between devices, hop(): return lax.ppermute(values, AXES, pairs)  122 us
    pallas_call x10, Pallas kernels, wgrad(): pl.pallas_call(functools.partial(wgrad_kernel, kinds, rows, side), out_sh...  80.8 us
    ppermute x98, starting transfers between devices, hop(): return lax.ppermute(values, AXES, pairs)  77.7 us
    pallas_call x3, Pallas kernels, attend_back(): pl.pallas_call(functools.partial(attend_back_kernel, kind), out_shape=[ja...  41.6 us
    pallas_call x2, Pallas kernels, attend(): pl.pallas_call(functools.partial(attend_kernel, kind), out_shape=[jax.Sha...  29.5 us
    pallas_call x1, Pallas kernels, self_back(): call(self_back_kernel, 'self_back', [shaped((items, count, d), BF)] * blo...  22 us
    pallas_call x1, Pallas kernels, project(): call(project_kernel, 'project', [big, shaped((1, items, count, d), BF), b...  19.5 us
    pallas_call x1, Pallas kernels, up_gelu(): call(up_kernel, 'up_gelu', [shaped((rows, d), F32), shaped((rows, d), BF)...  18.5 us
  transfers between devices with their start and end apart: 98, of which 28 were waited for; matrix products, arithmetic and copies ran while one was open for 12% of the time, Pallas kernels for 44%

profile of v3, /device:TPU:0, one launch (start us, length us, event | category | flops | bytes accessed | tf_op | source)
XLA Modules:
  0.0 546.9 jit_solution(8201495961268790247)
XLA Ops:
  0.7 3.0 collective-permute-start.1
  11.1 2.7 collective-permute-start.5
  13.8 5.1 collective-permute-done.5
  21.2 3.5 collective-permute-done.7
  28.5 4.6 collective-permute-done.9
  33.1 3.6 collective-permute-start.11
  39.7 2.7 collective-permute-start.16
  44.1 10.7 %collective-permute-done.14 = bf16[2,2,64,768]{3,2,1,0:T(8,128)(2,1)S(1)} collective-permute-done((bf16[2,2,64,768]{3,2,1,0:T(8,128)(2,1)S(1)}, bf16[2,2,64,768]{3,2,1,0:T(8,128)(2,1)S(1)}, u32[]{:S(2)}, u32[]{:S(2)}) %collective-permute-start.14) | collective-permute-done | bytes 393248 | tf_op jit(solution)/shard_map/ppermute | solution.py:41
  59.7 3.4 collective-permute-done.15
  65.4 2.9 collective-permute-done.17
  69.0 3.6 pad_maximum_fusion.token_ref
  77.2 7.6 %collective-permute-done.23.p6 = bf16[2,2,2,64,768]{4,3,2,1,0:T(8,128)(2,1)} collective-permute-done((bf16[2,2,2,64,768]{4,3,2,1,0:T(8,128)(2,1)S(1)}, bf16[2,2,2,64,768]{4,3,2,1,0:T(8,128)(2,1)}, u32[]{:S(2)}, u32[]{:S(2)}) %collective-permute-start.23) | collective-permute-done | bytes 786464 | tf_op jit(solution)/shard_map/ppermute | solution.py:41
  89.0 19.5 %project.1 = (bf16[4,2,256,1024]{3,2,1,0:T(8,128)(2,1)}, bf16[1,2,256,1024]{3,2,1,0:T(8,128)(2,1)}, bf16[4,2,256,1024]{3,2,1,0:T(8,128)(2,1)}, bf16[4,2,256,1024]{3,2,1,0:T(8,128)(2,1)}, bf16[1024,3072]{1,0:T(8,128)(2,1)}) custom-call(s32[5]{0:T(128)} %stack.127.spot_ref, bf16[4,2,256,1024]{3,2,1,0:T(8,128)(2,1)} %pad_maximum_fusion.token_ref, ...), custom_call_target="tpu_custom_call" | custom-call | flops 1 | bytes 1 | tf_op jit(solution)/shard_map/project/pallas_call | solution.py:250
  115.3 13.6 %collective-permute-done.28 = bf16[2,64,2048]{2,1,0:T(8,128)(2,1)S(1)} collective-permute-done((bf16[2,64,2048]{2,1,0:T(8,128)(2,1)S(1)}, bf16[2,64,2048]{2,1,0:T(8,128)(2,1)S(1)}, u32[]{:S(2)}, u32[]{:S(2)}) %collective-permute-start.28) | collective-permute-done | bytes 524320 | tf_op jit(solution)/shard_map/ppermute | solution.py:41
  134.6 21.8 %attend.2 = (bf16[2,256,1024]{2,1,0:T(8,128)(2,1)}, f32[2,8,2,256]{3,2,1,0:T(2,128)}) custom-call(s32[1]{0:T(128)} %bitcast.7.info_ref, bf16[1,2,256,1024]{3,2,1,0:T(8,128)(2,1)} %get-tuple-element.213.q_ref, bf16[4,2,256,1024]{3,2,1,0:T(8,128)(2,1)} %get-tuple-element.214.k_ref, bf16[4,2,256,1024]{3,2,1,0:T(8,128)(2,1)} %get-tuple-element.215.v_ref), custom_call_target="tpu_custom_call" | custom-call | flops 1 | bytes 1 | tf_op jit(solution)/shard_map/attend/pallas_call | solution.py:760
  160.0 2.8 pad_maximum_fusion.2.p1
  163.3 14.5 %collective-permute-done.31 = bf16[2,256,512]{2,1,0:T(8,128)(2,1)S(1)} collective-permute-done((bf16[2,256,512]{2,1,0:T(8,128)(2,1)S(1)}, bf16[2,256,512]{2,1,0:T(8,128)(2,1)S(1)}, u32[]{:S(2)}, u32[]{:S(2)}) %collective-permute-start.31) | collective-permute-done | bytes 524320 | tf_op jit(solution)/shard_map/ppermute | solution.py:41
  181.7 11.4 %mix.1 = (f32[512,1024]{1,0:T(8,128)}, bf16[512,1024]{1,0:T(8,128)(2,1)}, bf16[512,1024]{1,0:T(8,128)(2,1)}, bf16[256,2048]{1,0:T(8,128)(2,1)}, bf16[1024,1024]{...) custom-call(s32[5]{0:T(128)} %stack.127.spot_ref, ...), custom_call_target="tpu_custom_call" | custom-call | flops 1 | bytes 1 | tf_op jit(solution)/shard_map/mix/pallas_call | solution.py:294
  193.1 7.8 %attend.3 = (bf16[2,256,1024]{2,1,0:T(8,128)(2,1)}, f32[2,8,2,256]{3,2,1,0:T(2,128)}) custom-call(s32[2]{0:T(128)} %info_ref.3, bf16[1,2,256,1024]{3,2,1,0:T(8,128)(2,1)} %bitcast.273, bf16[1,2,128,2048]{3,2,1,0:T(8,128)(2,1)} %bitcast.257, bf16[1,2,128,2048]{3,2,1,0:T(8,128)(2,1)} %bitcast.258), custom_call_target="tpu_custom_call" | custom-call | flops 1 | bytes 1 | tf_op jit(solution)/shard_map/attend/pallas_call | solution.py:760
  205.6 18.5 %up_gelu.1 = (f32[512,1024]{1,0:T(8,128)}, bf16[512,1024]{1,0:T(8,128)(2,1)}, bf16[512,4096]{1,0:T(8,128)(2,1)}, bf16[512,4096]{1,0:T(8,128)(2,1)}, bf16[1024,4096]{1,0:T(8,128)(2,1)}) custom-call(s32[5]{0:T(128)} %stack.127.spot_ref, bf16[512,1024]{1,0:T(8,128)(2,1)} %bitcast.254, f32[512,1024]{1,0:T(8,128)} %get-tuple-element.223.r1_ref, ...), custom_call_target="tpu_custom_call" | custom-call | flops 1 | bytes 1 | tf_op jit(solution)/shard_map/up_gelu/pallas_call | solution.py:341
  224.1 6.8 %wgrad.10 = (bf16[2,2,256,512]{3,2,1,0:T(8,128)(2,1)}, bf16[2,2,256,512]{3,2,1,0:T(8,128)(2,1)}, bf16[2,2,256,512]{3,2,1,0:T(8,128)(2,1)}, bf16[2,2,256,512]{3,2,1,0:T(8,128)(2,1)}) custom-call(s32[5]{0:T(128)} %stack.129.spot_ref, bf16[512,4096]{1,0:T(8,128)(2,1)} %get-tuple-element.233.refs_0_.act_ref, bf16[512,1024]{1,0:T(8,128)(2,1)} %bitcast.250), custom_call_target="tpu_custom_call" | custom-call | flops 1 | bytes 1 | tf_op jit(solution)/shard_map/wgrad/pallas_call | solution.py:594
  232.5 3.0 collective-permute-done.41.p0
  236.8 18.0 %down.1 = (bf16[512,1024]{1,0:T(8,128)(2,1)}, bf16[512,4096]{1,0:T(8,128)(2,1)}, f32[1,4096]{1,0:T(1,128)}, f32[1,1024]{1,0:T(1,128)}) custom-call(s32[5]{0:T(128)} %stack.127.spot_ref, bf16[512,1024]{1,0:T(8,128)(2,1)} %bitcast.251, bf16[512,4096]{1,0:T(8,128)(2,1)} %get-tuple-element.236.slope_ref, bf16[512,4096]{1,0:T(8,128)(2,1)} %get-tuple-element.233.refs_0_.act_ref, ...), custom_call_target="tpu_custom_call" | custom-call | flops 1 | bytes 1 | tf_op jit(solution)/shard_map/down/pallas_call | solution.py:388
  257.5 8.1 %wgrad.11 = (bf16[2,2,2,256,512]{4,3,2,1,0:T(8,128)(2,1)}, bf16[2,2,2,256,512]{4,3,2,1,0:T(8,128)(2,1)}) custom-call(s32[5]{0:T(128)} %stack.127.spot_ref, bf16[512,4096]{1,0:T(8,128)(2,1)} %get-tuple-element.233.refs_0_.act_ref, bf16[512,1024]{1,0:T(8,128)(2,1)} %bitcast.252, bf16[2,2,256,512]{3,2,1,0:T(8,128)(2,1)} %copy-done.17, ...), custom_call_target="tpu_custom_call" | custom-call | flops 1 | bytes 1 | tf_op jit(solution)/shard_map/wgrad/pallas_call | solution.py:594
  265.7 7.0 %wgrad.12 = (bf16[2,2,64,2048]{3,2,1,0:T(8,128)(2,1)}, bf16[2,2,64,2048]{3,2,1,0:T(8,128)(2,1)}, bf16[2,2,64,2048]{3,2,1,0:T(8,128)(2,1)}, bf16[2,2,64,2048]{3,2,1,0:T(8,128)(2,1)}) custom-call(s32[5]{0:T(128)} %stack.129.spot_ref, bf16[512,1024]{1,0:T(8,128)(2,1)} %get-tuple-element.247.refs_0_, bf16[512,4096]{1,0:T(8,128)(2,1)} %get-tuple-element.249.refs_1_.g_ref), custom_call_target="tpu_custom_call" | custom-call | flops 1 | bytes 1 | tf_op jit(solution)/shard_map/wgrad/pallas_call | solution.py:594
  275.1 14.3 %feed_back.1 = (f32[512,1024]{1,0:T(8,128)}, bf16[512,1024]{1,0:T(8,128)(2,1)}, bf16[512,1024]{1,0:T(8,128)(2,1)}, f32[8,1024]{1,0:T(8,128)}) custom-call(bf16[512,4096]{1,0:T(8,128)(2,1)} %get-tuple-element.249.refs_1_.g_ref, bf16[1024,4096]{1,0:T(8,128)(2,1)} %get-tuple-element.250.w_ref, f32[512,1024]{1,0:T(8,128)} %get-tuple-element.232.r2_ref, ...), custom_call_target="tpu_custom_call" | custom-call | flops 1 | bytes 1 | tf_op jit(solution)/shard_map/feed_back/pallas_call | solution.py:427
  292.0 8.3 %wgrad.13 = (bf16[2,2,2,64,2048]{4,3,2,1,0:T(8,128)(2,1)}, bf16[2,2,2,64,2048]{4,3,2,1,0:T(8,128)(2,1)}) custom-call(s32[5]{0:T(128)} %stack.127.spot_ref, bf16[512,1024]{1,0:T(8,128)(2,1)} %get-tuple-element.247.refs_0_, bf16[512,4096]{1,0:T(8,128)(2,1)} %get-tuple-element.249.refs_1_.g_ref, bf16[2,2,64,2048]{3,2,1,0:T(8,128)(2,1)} %copy-done.19, ...), custom_call_target="tpu_custom_call" | custom-call | flops 1 | bytes 1 | tf_op jit(solution)/shard_map/wgrad/pallas_call | solution.py:594
  300.9 10.6 %attend_back.3 = (bf16[2,256,1024]{2,1,0:T(8,128)(2,1)}, bf16[1,2,128,1024]{3,2,1,0:T(8,128)(2,1)}, bf16[1,2,128,1024]{3,2,1,0:T(8,128)(2,1)}) custom-call(s32[2]{0:T(128)} %info_ref.3, bf16[1,2,256,1024]{3,2,1,0:T(8,128)(2,1)} %bitcast.274, bf16[1,2,128,2048]{3,2,1,0:T(8,128)(2,1)} %bitcast.259, bf16[1,2,128,2048]{3,2,1,0:T(8,128)(2,1)} %bitcast.260, ...), custom_call_target="tpu_custom_call" | custom-call | flops 1 | bytes 1 | tf_op jit(solution)/shard_map/attend_back/pallas_call | solution.py:829
  314.1 8.3 %cross_back.1 = (f32[512,1024]{1,0:T(8,128)}, bf16[512,1024]{1,0:T(8,128)(2,1)}, bf16[512,1024]{1,0:T(8,128)(2,1)}, f32[8,1024]{1,0:T(8,128)}) custom-call(bf16[512,1024]{1,0:T(8,128)(2,1)} %bitcast.261, bf16[1024,1024]{1,0:T(8,128)(2,1)} %get-tuple-element.263.wcq_ref, f32[512,1024]{1,0:T(8,128)} %get-tuple-element.223.r1_ref, ...), custom_call_target="tpu_custom_call" | custom-call | flops 1 | bytes 1 | tf_op jit(solution)/shard_map/cross_back/pallas_call | solution.py:457
  323.5 4.6 convolution_convert_fusion
  328.2 7.8 %wgrad.14 = (bf16[2,2,64,2560]{3,2,1,0:T(8,128)(2,1)}, bf16[2,2,64,2560]{3,2,1,0:T(8,128)(2,1)}, bf16[2,2,64,2560]{3,2,1,0:T(8,128)(2,1)}, bf16[2,2,64,2560]{3,2,1,0:T(8,128)(2,1)}) custom-call(s32[5]{0:T(128)} %stack.129.spot_ref, bf16[512,1024]{1,0:T(8,128)(2,1)} %get-tuple-element.275.refs_0_, bf16[512,1024]{1,0:T(8,128)(2,1)} %bitcast.262, ...), custom_call_target="tpu_custom_call" | custom-call | flops 1 | bytes 1 | tf_op jit(solution)/shard_map/wgrad/pallas_call | solution.py:594
  338.3 15.5 %attend_back.4 = (bf16[2,256,512]{2,1,0:T(8,128)(2,1)}, bf16[4,2,256,512]{3,2,1,0:T(8,128)(2,1)}, bf16[4,2,256,512]{3,2,1,0:T(8,128)(2,1)}) custom-call(s32[1]{0:T(128)} %bitcast.7.info_ref, bf16[1,2,256,1024]{3,2,1,0:T(8,128)(2,1)} %get-tuple-element.213.q_ref, bf16[4,2,256,1024]{3,2,1,0:T(8,128)(2,1)} %get-tuple-element.214.k_ref, ...), custom_call_target="tpu_custom_call" | custom-call | flops 1 | bytes 1 | tf_op jit(solution)/shard_map/attend_back/pallas_call | solution.py:829
  356.1 9.5 %wgrad.15 = (bf16[2,2,2,64,2560]{4,3,2,1,0:T(8,128)(2,1)}, bf16[2,2,2,64,2560]{4,3,2,1,0:T(8,128)(2,1)}) custom-call(s32[5]{0:T(128)} %stack.127.spot_ref, bf16[512,1024]{1,0:T(8,128)(2,1)} %get-tuple-element.275.refs_0_, bf16[512,1024]{1,0:T(8,128)(2,1)} %bitcast.263, bf16[256,1024]{1,0:T(8,128)(2,1)} %bitcast.266, bf16[256,2048]{1,0:T(8,128)(2,1)} %copy-done.3, ...), custom_call_target="tpu_custom_call" | custom-call | flops 1 | bytes 1 | tf_op jit(solution)/shard_map/wgrad/pallas_call | solution.py:594
  373.0 8.4 %wgrad.16 = (bf16[2,2,64,768]{3,2,1,0:T(8,128)(2,1)}, bf16[2,2,64,768]{3,2,1,0:T(8,128)(2,1)}, bf16[2,2,64,768]{3,2,1,0:T(8,128)(2,1)}, bf16[2,2,64,768]{3,2,1,0:T(8,128)(2,1)}) custom-call(s32[5]{0:T(128)} %stack.129.spot_ref, bf16[512,1024]{1,0:T(8,128)(2,1)} %bitcast.238, bf16[512,512]{1,0:T(8,128)(2,1)} %bitcast.267, bf16[2048,1024]{1,0:T(8,128)(2,1)} %bitcast.225, ...), custom_call_target="tpu_custom_call" | custom-call | flops 1 | bytes 1 | tf_op jit(solution)/shard_map/wgrad/pallas_call | solution.py:594
  386.1 15.6 %attend_back.5 = (bf16[2,256,512]{2,1,0:T(8,128)(2,1)}, bf16[4,2,256,512]{3,2,1,0:T(8,128)(2,1)}, bf16[4,2,256,512]{3,2,1,0:T(8,128)(2,1)}) custom-call(s32[1]{0:T(128)} %bitcast.7.info_ref, bf16[1,2,256,1024]{3,2,1,0:T(8,128)(2,1)} %get-tuple-element.213.q_ref, bf16[4,2,256,1024]{3,2,1,0:T(8,128)(2,1)} %get-tuple-element.214.k_ref, ...), custom_call_target="tpu_custom_call" | custom-call | flops 1 | bytes 1 | tf_op jit(solution)/shard_map/attend_back/pallas_call | solution.py:829
  405.1 2.7 fusion.9
  407.8 8.4 %wgrad.17 = (bf16[2,2,64,768]{3,2,1,0:T(8,128)(2,1)}, bf16[2,2,64,768]{3,2,1,0:T(8,128)(2,1)}, bf16[2,2,64,768]{3,2,1,0:T(8,128)(2,1)}, bf16[2,2,64,768]{3,2,1,0:T(8,128)(2,1)}) custom-call(s32[5]{0:T(128)} %stack.129.spot_ref, bf16[512,1024]{1,0:T(8,128)(2,1)} %bitcast.239, bf16[512,512]{1,0:T(8,128)(2,1)} %bitcast.269, bf16[2048,1024]{1,0:T(8,128)(2,1)} %bitcast.227, ...), custom_call_target="tpu_custom_call" | custom-call | flops 1 | bytes 1 | tf_op jit(solution)/shard_map/wgrad/pallas_call | solution.py:594
  417.8 8.3 %wgrad.18 = (bf16[2,2,2,64,768]{4,3,2,1,0:T(8,128)(2,1)}, bf16[2,2,2,64,768]{4,3,2,1,0:T(8,128)(2,1)}) custom-call(s32[5]{0:T(128)} %stack.127.spot_ref, bf16[512,1024]{1,0:T(8,128)(2,1)} %bitcast.240, bf16[512,512]{1,0:T(8,128)(2,1)} %bitcast.268, bf16[2048,1024]{1,0:T(8,128)(2,1)} %bitcast.229, bf16[2048,512]{1,0:T(8,128)(2,1)} %bitcast.243, ...), custom_call_target="tpu_custom_call" | custom-call | flops 1 | bytes 1 | tf_op jit(solution)/shard_map/wgrad/pallas_call | solution.py:594
  436.3 8.3 %wgrad.19 = (bf16[2,2,2,64,768]{4,3,2,1,0:T(8,128)(2,1)}, bf16[2,2,2,64,768]{4,3,2,1,0:T(8,128)(2,1)}) custom-call(s32[5]{0:T(128)} %stack.127.spot_ref, bf16[512,1024]{1,0:T(8,128)(2,1)} %bitcast.241, bf16[512,512]{1,0:T(8,128)(2,1)} %bitcast.270, bf16[2048,1024]{1,0:T(8,128)(2,1)} %bitcast.231, bf16[2048,512]{1,0:T(8,128)(2,1)} %bitcast.247, ...), custom_call_target="tpu_custom_call" | custom-call | flops 1 | bytes 1 | tf_op jit(solution)/shard_map/wgrad/pallas_call | solution.py:594
  446.6 22.0 %self_back.1 = (bf16[2,256,1024]{2,1,0:T(8,128)(2,1)}, bf16[2,256,1024]{2,1,0:T(8,128)(2,1)}, bf16[2,256,1024]{2,1,0:T(8,128)(2,1)}, bf16[2,256,1024]{2,1,0:T(8,128)(2,1)}, f32[11,1024]{1,0:T(8,128)}) custom-call(bf16[2,256,512]{2,1,0:T(8,128)(2,1)} %get-tuple-element.317.dq0_ref, bf16[4,2,256,512]{3,2,1,0:T(8,128)(2,1)} %get-tuple-element.282.dk0_ref, ...), custom_call_target="tpu_custom_call" | custom-call | flops 1 | bytes 1 | tf_op jit(solution)/shard_map/self_back/pallas_call | solution.py:527
  472.9 9.1 %collective-permute-done.80 = bf16[2,2,64,768]{3,2,1,0:T(8,128)(2,1)S(1)} collective-permute-done((bf16[2,2,64,768]{3,2,1,0:T(8,128)(2,1)S(1)}, bf16[2,2,64,768]{3,2,1,0:T(8,128)(2,1)S(1)}, u32[]{:S(2)}, u32[]{:S(2)}) %collective-permute-start.80) | collective-permute-done | bytes 393248 | tf_op jit(solution)/shard_map/ppermute | solution.py:41
  486.2 3.1 collective-permute-done.81
  490.4 3.3 collective-permute-done.84
  500.9 2.7 collective-permute-done.86
  510.7 4.6 collective-permute-done.92
  519.6 13.1 %collective-permute-done.90 = bf16[64,2560]{1,0:T(8,128)(2,1)S(1)} collective-permute-done((bf16[64,2560]{1,0:T(8,128)(2,1)S(1)}, bf16[64,2560]{1,0:T(8,128)(2,1)S(1)}, u32[]{:S(2)}, u32[]{:S(2)}) %collective-permute-start.90) | collective-permute-done | bytes 327712 | tf_op jit(solution)/shard_map/ppermute | solution.py:41
  532.8 2.4 convert_add_fusion.6
  535.5 3.0 collective-permute-start.95
  (393 shorter events, 144.6 us)
Async XLA Ops:
  0.7 41.8 %collective-permute-start.1 = (bf16[2,256,1024]{2,1,0:T(8,128)(2,1)}, bf16[2,256,1024]{2,1,0:T(8,128)(2,1)}, u32[]{:S(2)}, u32[]{:S(2)}) collective-permute-start(bf16[2,256,1024]{2,1,0:T(8,128)(2,1)} %param.19), channel_id=1, source_target_pairs={{0,2},{1,3},{2,0},{3,1},{4,6},{5,7},{6,4},{7,5},{8,10},{9,11},{10,... | collective-permute-start | bytes 3145736 | tf_op jit(solution)/shard_map/ppermute | solution.py:41
  3.7 65.3 %collective-permute-start = (bf16[2,256,1024]{2,1,0:T(8,128)(2,1)}, bf16[2,256,1024]{2,1,0:T(8,128)(2,1)}, u32[]{:S(2)}, u32[]{:S(2)}) collective-permute-start(bf16[2,256,1024]{2,1,0:T(8,128)(2,1)} %param.19), channel_id=1, source_target_pairs={{0,1},{1,0},{2,3},{3,2},{4,5},{5,4},{6,7},{7,6},{8,9},{9,8},{10,11... | collective-permute-start | bytes 3145736 | tf_op jit(solution)/shard_map/ppermute | solution.py:41
  7.2 30.9 %collective-permute-start.2 = (bf16[11,1024]{1,0:T(8,128)(2,1)S(1)}, bf16[11,1024]{1,0:T(8,128)(2,1)S(1)}, u32[]{:S(2)}, u32[]{:S(2)}) collective-permute-start(bf16[11,1024]{1,0:T(8,128)(2,1)S(1)} %pad_maximum_fusion.24), channel_id=1, source_target_pairs={{0,1},{1,0},{2,3},{3,2},{4,5},{5,4},{6,7},{7,6},{8,9},{9,8},{10,11... | collective-permute-start | bytes 67592 | tf_op jit(solution)/shard_map/ppermute | solution.py:41
  36.8 18.0 %collective-permute-start.14 = (bf16[2,2,64,768]{3,2,1,0:T(8,128)(2,1)S(1)}, bf16[2,2,64,768]{3,2,1,0:T(8,128)(2,1)S(1)}, u32[]{:S(2)}, u32[]{:S(2)}) collective-permute-start(bf16[2,2,64,768]{3,2,1,0:T(8,128)(2,1)S(1)} %get-tuple-element.383), channel_id=1, source_target_pairs={{0,8},{1,9},{2,10},{3,11},{4,12},{5,13},{6,14},{7,15},{8,0},{9,1},... | collective-permute-start | bytes 1179656 | tf_op jit(solution)/shard_map/ppermute | solution.py:41
  39.7 17.1 %collective-permute-start.16 = (bf16[64,2560]{1,0:T(8,128)(2,1)S(1)}, bf16[64,2560]{1,0:T(8,128)(2,1)S(1)}, u32[]{:S(2)}, u32[]{:S(2)}) collective-permute-start(bf16[64,2560]{1,0:T(8,128)(2,1)S(1)} %maximum_select_fusion), channel_id=1, source_target_pairs={{0,16},{1,17},{2,18},{3,19},{4,20},{5,21},{6,22},{7,23},{8,24},{9,... | collective-permute-start | bytes 983048 | tf_op jit(solution)/shard_map/ppermute | solution.py:41
  42.4 26.6 %collective-permute-start.12 = (bf16[2,256,1024]{2,1,0:T(8,128)(2,1)}, bf16[2,256,1024]{2,1,0:T(8,128)(2,1)}, u32[]{:S(2)}, u32[]{:S(2)}) collective-permute-start(bf16[2,256,1024]{2,1,0:T(8,128)(2,1)} %collective-permute-done.1), channel_id=1, source_target_pairs={{0,1},{1,0},{2,3},{3,2},{4,5},{5,4},{6,7},{7,6},{8,9},{9,8},{10,11... | collective-permute-start | bytes 3145736 | tf_op jit(solution)/shard_map/ppermute | solution.py:41
  68.3 17.3 %collective-permute-start.22 = (bf16[2,2,2,64,768]{4,3,2,1,0:T(8,128)(2,1)S(1)}, bf16[2,2,2,64,768]{4,3,2,1,0:T(8,128)(2,1)S(1)}, u32[]{:S(2)}, u32[]{:S(2)}) collective-permute-start(bf16[2,2,2,64,768]{4,3,2,1,0:T(8,128)(2,1)S(1)} %pad_maximum_fusion.8.p1), channel_id=1, source_target_pairs={{0,1},{1,0},{2,3},{3,2},{4,5},{5,4},{6,7},{7,6},{8,9},{9,8},{10,11... | collective-permute-start | bytes 2359304 | tf_op jit(solution)/shard_map/ppermute | solution.py:41
  75.0 37.4 %collective-permute-start.29 = (bf16[2,2,64,2560]{3,2,1,0:T(8,128)(2,1)}, bf16[2,2,64,2560]{3,2,1,0:T(8,128)(2,1)}, u32[]{:S(2)}, u32[]{:S(2)}) collective-permute-start(bf16[2,2,64,2560]{3,2,1,0:T(8,128)(2,1)} %get-tuple-element.365), channel_id=1, source_target_pairs={{0,8},{1,9},{2,10},{3,11},{4,12},{5,13},{6,14},{7,15},{8,0},{9,1},... | collective-permute-start | bytes 3932168 | tf_op jit(solution)/shard_map/ppermute | solution.py:41
  86.6 23.5 %collective-permute-start.27 = (bf16[64,2048]{1,0:T(8,128)(2,1)S(1)}, bf16[64,2048]{1,0:T(8,128)(2,1)S(1)}, u32[]{:S(2)}, u32[]{:S(2)}) collective-permute-start(bf16[64,2048]{1,0:T(8,128)(2,1)S(1)} %maximum_select_fusion.2), channel_id=1, source_target_pairs={{0,16},{1,17},{2,18},{3,19},{4,20},{5,21},{6,22},{7,23},{8,24},{9,... | collective-permute-start | bytes 786440 | tf_op jit(solution)/shard_map/ppermute | solution.py:41
  114.0 42.4 %collective-permute-start.33 = (bf16[2,2,2,64,2560]{4,3,2,1,0:T(8,128)(2,1)S(1)}, bf16[2,2,2,64,2560]{4,3,2,1,0:T(8,128)(2,1)S(1)}, u32[]{:S(2)}, u32[]{:S(2)}) collective-permute-start(bf16[2,2,2,64,2560]{4,3,2,1,0:T(8,128)(2,1)S(1)} %pad_maximum_fusion.1.p1), channel_id=1, source_target_pairs={{0,2},{1,5},{2,0},{3,7},{4,6},{5,1},{6,4},{7,3},{8,10},{9,13},{10,... | collective-permute-start | bytes 7864328 | tf_op jit(solution)/shard_map/ppermute | solution.py:41
  129.1 30.9 %collective-permute-start.32 = (bf16[2,2,64,2048]{3,2,1,0:T(8,128)(2,1)S(1)}, bf16[2,2,64,2048]{3,2,1,0:T(8,128)(2,1)}, u32[]{:S(2)}, u32[]{:S(2)}) collective-permute-start(bf16[2,2,64,2048]{3,2,1,0:T(8,128)(2,1)S(1)} %get-tuple-element.369), channel_id=1, source_target_pairs={{0,8},{1,9},{2,10},{3,11},{4,12},{5,13},{6,14},{7,15},{8,0},{9,1},... | collective-permute-start | bytes 3145736 | tf_op jit(solution)/shard_map/ppermute | solution.py:41
  132.8 24.9 %collective-permute-start.30 = (bf16[256,512]{1,0:T(8,128)(2,1)S(1)}, bf16[256,512]{1,0:T(8,128)(2,1)S(1)}, u32[]{:S(2)}, u32[]{:S(2)}) collective-permute-start(bf16[256,512]{1,0:T(8,128)(2,1)S(1)} %maximum_select_fusion.4), channel_id=1, source_target_pairs={{0,16},{1,17},{2,18},{3,19},{4,20},{5,21},{6,22},{7,23},{8,24},{9,... | collective-permute-start | bytes 786440 | tf_op jit(solution)/shard_map/ppermute | solution.py:41
  134.6 45.6 %collective-permute-start.35 = (bf16[2,2,2,64,2560]{4,3,2,1,0:T(8,128)(2,1)S(1)}, bf16[2,2,2,64,2560]{4,3,2,1,0:T(8,128)(2,1)}, u32[]{:S(2)}, u32[]{:S(2)}) collective-permute-start(bf16[2,2,2,64,2560]{4,3,2,1,0:T(8,128)(2,1)S(1)} %pad_maximum_fusion.1.p1), channel_id=1, source_target_pairs={{0,1},{1,0},{2,3},{3,2},{4,5},{5,4},{6,7},{7,6},{8,9},{9,8},{10,11... | collective-permute-start | bytes 7864328 | tf_op jit(solution)/shard_map/ppermute | solution.py:41
  156.4 23.9 %collective-permute-start.34 = (bf16[2,2,2,64,2560]{4,3,2,1,0:T(8,128)(2,1)S(1)}, bf16[2,2,2,64,2560]{4,3,2,1,0:T(8,128)(2,1)S(1)}, u32[]{:S(2)}, u32[]{:S(2)}) collective-permute-start(bf16[2,2,2,64,2560]{4,3,2,1,0:T(8,128)(2,1)S(1)} %collective-permute-done.33.p2), channel_id=1, source_target_pairs={{0,1},{1,0},{2,3},{3,2},{4,5},{5,4},{6,7},{7,6},{8,9},{9,8},{10,11... | collective-permute-start | bytes 7864328 | tf_op jit(solution)/shard_map/ppermute | solution.py:41
  162.8 38.1 %collective-permute-start.37 = (bf16[2,2,2,64,2048]{4,3,2,1,0:T(8,128)(2,1)}, bf16[2,2,2,64,2048]{4,3,2,1,0:T(8,128)(2,1)}, u32[]{:S(2)}, u32[]{:S(2)}) collective-permute-start(bf16[2,2,2,64,2048]{4,3,2,1,0:T(8,128)(2,1)} %pad_maximum_fusion.2.p1), channel_id=1, source_target_pairs={{0,2},{1,5},{2,0},{3,7},{4,6},{5,1},{6,4},{7,3},{8,10},{9,13},{10,... | collective-permute-start | bytes 6291464 | tf_op jit(solution)/shard_map/ppermute | solution.py:41
  178.0 23.5 %collective-permute-start.36 = (bf16[2,2,256,512]{3,2,1,0:T(8,128)(2,1)S(1)}, bf16[2,2,256,512]{3,2,1,0:T(8,128)(2,1)}, u32[]{:S(2)}, u32[]{:S(2)}) collective-permute-start(bf16[2,2,256,512]{3,2,1,0:T(8,128)(2,1)S(1)} %get-tuple-element.367), channel_id=1, source_target_pairs={{0,8},{1,9},{2,10},{3,11},{4,12},{5,13},{6,14},{7,15},{8,0},{9,1},... | collective-permute-start | bytes 3145736 | tf_op jit(solution)/shard_map/ppermute | solution.py:41
  180.2 25.4 %collective-permute-start.39 = (bf16[2,2,2,64,2048]{4,3,2,1,0:T(8,128)(2,1)}, bf16[2,2,2,64,2048]{4,3,2,1,0:T(8,128)(2,1)}, u32[]{:S(2)}, u32[]{:S(2)}) collective-permute-start(bf16[2,2,2,64,2048]{4,3,2,1,0:T(8,128)(2,1)} %pad_maximum_fusion.2.p1), channel_id=1, source_target_pairs={{0,1},{1,0},{2,3},{3,2},{4,5},{5,4},{6,7},{7,6},{8,9},{9,8},{10,11... | collective-permute-start | bytes 6291464 | tf_op jit(solution)/shard_map/ppermute | solution.py:41
  202.9 28.0 %collective-permute-start.40 = (bf16[2,2,2,256,512]{4,3,2,1,0:T(8,128)(2,1)S(1)}, bf16[2,2,2,256,512]{4,3,2,1,0:T(8,128)(2,1)}, u32[]{:S(2)}, u32[]{:S(2)}) collective-permute-start(bf16[2,2,2,256,512]{4,3,2,1,0:T(8,128)(2,1)S(1)} %pad_maximum_fusion.3.p1), channel_id=1, source_target_pairs={{0,2},{1,5},{2,0},{3,7},{4,6},{5,1},{6,4},{7,3},{8,10},{9,13},{10,... | collective-permute-start | bytes 6291464 | tf_op jit(solution)/shard_map/ppermute | solution.py:41
  203.6 28.5 %collective-permute-start.42 = (bf16[2,2,2,256,512]{4,3,2,1,0:T(8,128)(2,1)S(1)}, bf16[2,2,2,256,512]{4,3,2,1,0:T(8,128)(2,1)}, u32[]{:S(2)}, u32[]{:S(2)}) collective-permute-start(bf16[2,2,2,256,512]{4,3,2,1,0:T(8,128)(2,1)S(1)} %pad_maximum_fusion.3.p1), channel_id=1, source_target_pairs={{0,1},{1,0},{2,3},{3,2},{4,5},{5,4},{6,7},{7,6},{8,9},{9,8},{10,11... | collective-permute-start | bytes 6291464 | tf_op jit(solution)/shard_map/ppermute | solution.py:41
  231.5 23.4 %collective-permute-start.43 = (bf16[2,2,256,512]{3,2,1,0:T(8,128)(2,1)}, bf16[2,2,256,512]{3,2,1,0:T(8,128)(2,1)S(1)}, u32[]{:S(2)}, u32[]{:S(2)}) collective-permute-start(bf16[2,2,256,512]{3,2,1,0:T(8,128)(2,1)} %get-tuple-element.234), channel_id=1, source_target_pairs={{0,1},{1,0},{2,3},{3,2},{4,5},{5,4},{6,7},{7,6},{8,9},{9,8},{10,11... | collective-permute-start | bytes 3145736 | tf_op jit(solution)/shard_map/ppermute | solution.py:41
  231.5 23.4 %collective-permute-start.44 = (bf16[2,2,256,512]{3,2,1,0:T(8,128)(2,1)}, bf16[2,2,256,512]{3,2,1,0:T(8,128)(2,1)S(1)}, u32[]{:S(2)}, u32[]{:S(2)}) collective-permute-start(bf16[2,2,256,512]{3,2,1,0:T(8,128)(2,1)} %get-tuple-element.243), channel_id=1, source_target_pairs={{0,1},{1,0},{2,3},{3,2},{4,5},{5,4},{6,7},{7,6},{8,9},{9,8},{10,11... | collective-permute-start | bytes 3145736 | tf_op jit(solution)/shard_map/ppermute | solution.py:41
  232.0 22.9 %collective-permute-start.45 = (bf16[2,2,256,512]{3,2,1,0:T(8,128)(2,1)}, bf16[2,2,256,512]{3,2,1,0:T(8,128)(2,1)S(1)}, u32[]{:S(2)}, u32[]{:S(2)}) collective-permute-start(bf16[2,2,256,512]{3,2,1,0:T(8,128)(2,1)} %get-tuple-element.244), channel_id=1, source_target_pairs={{0,1},{1,0},{2,3},{3,2},{4,5},{5,4},{6,7},{7,6},{8,9},{9,8},{10,11... | collective-permute-start | bytes 3145736 | tf_op jit(solution)/shard_map/ppermute | solution.py:41
  232.0 22.9 %collective-permute-start.46 = (bf16[2,2,256,512]{3,2,1,0:T(8,128)(2,1)}, bf16[2,2,256,512]{3,2,1,0:T(8,128)(2,1)S(1)}, u32[]{:S(2)}, u32[]{:S(2)}) collective-permute-start(bf16[2,2,256,512]{3,2,1,0:T(8,128)(2,1)} %get-tuple-element.245), channel_id=1, source_target_pairs={{0,1},{1,0},{2,3},{3,2},{4,5},{5,4},{6,7},{7,6},{8,9},{9,8},{10,11... | collective-permute-start | bytes 3145736 | tf_op jit(solution)/shard_map/ppermute | solution.py:41
  272.6 16.7 %collective-permute-start.47 = (bf16[2,2,64,2048]{3,2,1,0:T(8,128)(2,1)}, bf16[2,2,64,2048]{3,2,1,0:T(8,128)(2,1)S(1)}, u32[]{:S(2)}, u32[]{:S(2)}) collective-permute-start(bf16[2,2,64,2048]{3,2,1,0:T(8,128)(2,1)} %get-tuple-element.248), channel_id=1, source_target_pairs={{0,1},{1,0},{2,3},{3,2},{4,5},{5,4},{6,7},{7,6},{8,9},{9,8},{10,11... | collective-permute-start | bytes 3145736 | tf_op jit(solution)/shard_map/ppermute | solution.py:41
  273.7 37.8 %collective-permute-start.51 = (bf16[2,2,2,256,512]{4,3,2,1,0:T(8,128)(2,1)}, bf16[2,2,2,256,512]{4,3,2,1,0:T(8,128)(2,1)S(1)}, u32[]{:S(2)}, u32[]{:S(2)}) collective-permute-start(bf16[2,2,2,256,512]{4,3,2,1,0:T(8,128)(2,1)} %get-tuple-element.260), channel_id=1, source_target_pairs={{0,2},{1,5},{2,0},{3,7},{4,6},{5,1},{6,4},{7,3},{8,10},{9,13},{10,... | collective-permute-start | bytes 6291464 | tf_op jit(solution)/shard_map/ppermute | solution.py:41
  300.3 36.3 %collective-permute-start.52 = (bf16[2,2,2,64,2048]{4,3,2,1,0:T(8,128)(2,1)}, bf16[2,2,2,64,2048]{4,3,2,1,0:T(8,128)(2,1)S(1)}, u32[]{:S(2)}, u32[]{:S(2)}) collective-permute-start(bf16[2,2,2,64,2048]{4,3,2,1,0:T(8,128)(2,1)} %get-tuple-element.268), channel_id=1, source_target_pairs={{0,2},{1,5},{2,0},{3,7},{4,6},{5,1},{6,4},{7,3},{8,10},{9,13},{10,... | collective-permute-start | bytes 6291464 | tf_op jit(solution)/shard_map/ppermute | solution.py:41
  313.0 40.9 %collective-permute-start.54 = (bf16[2,2,256,512]{3,2,1,0:T(8,128)(2,1)}, bf16[2,2,256,512]{3,2,1,0:T(8,128)(2,1)}, u32[]{:S(2)}, u32[]{:S(2)}) collective-permute-start(bf16[2,2,256,512]{3,2,1,0:T(8,128)(2,1)} %fusion.12), channel_id=1, source_target_pairs={{0,8},{1,9},{2,10},{3,11},{4,12},{5,13},{6,14},{7,15},{8,0},{9,1},... | collective-permute-start | bytes 3145736 | tf_op jit(solution)/shard_map/ppermute | solution.py:41
  335.9 20.1 %collective-permute-start.53 = (bf16[2,2,64,2560]{3,2,1,0:T(8,128)(2,1)}, bf16[2,2,64,2560]{3,2,1,0:T(8,128)(2,1)}, u32[]{:S(2)}, u32[]{:S(2)}) collective-permute-start(bf16[2,2,64,2560]{3,2,1,0:T(8,128)(2,1)} %get-tuple-element.278), channel_id=1, source_target_pairs={{0,1},{1,0},{2,3},{3,2},{4,5},{5,4},{6,7},{7,6},{8,9},{9,8},{10,11... | collective-permute-start | bytes 3932168 | tf_op jit(solution)/shard_map/ppermute | solution.py:41
  336.0 20.1 %collective-permute-start.55 = (bf16[2,2,64,2560]{3,2,1,0:T(8,128)(2,1)}, bf16[2,2,64,2560]{3,2,1,0:T(8,128)(2,1)}, u32[]{:S(2)}, u32[]{:S(2)}) collective-permute-start(bf16[2,2,64,2560]{3,2,1,0:T(8,128)(2,1)} %get-tuple-element.286), channel_id=1, source_target_pairs={{0,1},{1,0},{2,3},{3,2},{4,5},{5,4},{6,7},{7,6},{8,9},{9,8},{10,11... | collective-permute-start | bytes 3932168 | tf_op jit(solution)/shard_map/ppermute | solution.py:41
  336.5 19.6 %collective-permute-start.56 = (bf16[2,2,64,2560]{3,2,1,0:T(8,128)(2,1)}, bf16[2,2,64,2560]{3,2,1,0:T(8,128)(2,1)}, u32[]{:S(2)}, u32[]{:S(2)}) collective-permute-start(bf16[2,2,64,2560]{3,2,1,0:T(8,128)(2,1)} %get-tuple-element.287), channel_id=1, source_target_pairs={{0,1},{1,0},{2,3},{3,2},{4,5},{5,4},{6,7},{7,6},{8,9},{9,8},{10,11... | collective-permute-start | bytes 3932168 | tf_op jit(solution)/shard_map/ppermute | solution.py:41
  336.5 19.5 %collective-permute-start.57 = (bf16[2,2,64,2560]{3,2,1,0:T(8,128)(2,1)}, bf16[2,2,64,2560]{3,2,1,0:T(8,128)(2,1)}, u32[]{:S(2)}, u32[]{:S(2)}) collective-permute-start(bf16[2,2,64,2560]{3,2,1,0:T(8,128)(2,1)} %get-tuple-element.288), channel_id=1, source_target_pairs={{0,1},{1,0},{2,3},{3,2},{4,5},{5,4},{6,7},{7,6},{8,9},{9,8},{10,11... | collective-permute-start | bytes 3932168 | tf_op jit(solution)/shard_map/ppermute | solution.py:41
  365.6 38.7 %collective-permute-start.59 = (bf16[2,2,2,64,2560]{4,3,2,1,0:T(8,128)(2,1)}, bf16[2,2,2,64,2560]{4,3,2,1,0:T(8,128)(2,1)}, u32[]{:S(2)}, u32[]{:S(2)}) collective-permute-start(bf16[2,2,2,64,2560]{4,3,2,1,0:T(8,128)(2,1)} %get-tuple-element.292), channel_id=1, source_target_pairs={{0,2},{1,5},{2,0},{3,7},{4,6},{5,1},{6,4},{7,3},{8,10},{9,13},{10,... | collective-permute-start | bytes 7864328 | tf_op jit(solution)/shard_map/ppermute | solution.py:41
  367.2 35.2 %collective-permute-start.60 = (bf16[2,2,64,2048]{3,2,1,0:T(8,128)(2,1)}, bf16[2,2,64,2048]{3,2,1,0:T(8,128)(2,1)}, u32[]{:S(2)}, u32[]{:S(2)}) collective-permute-start(bf16[2,2,64,2048]{3,2,1,0:T(8,128)(2,1)} %fusion.13), channel_id=1, source_target_pairs={{0,8},{1,9},{2,10},{3,11},{4,12},{5,13},{6,14},{7,15},{8,0},{9,1},... | collective-permute-start | bytes 3145736 | tf_op jit(solution)/shard_map/ppermute | solution.py:41
  381.4 34.8 %collective-permute-start.58 = (bf16[2,2,64,768]{3,2,1,0:T(8,128)(2,1)}, bf16[2,2,64,768]{3,2,1,0:T(8,128)(2,1)S(1)}, u32[]{:S(2)}, u32[]{:S(2)}) collective-permute-start(bf16[2,2,64,768]{3,2,1,0:T(8,128)(2,1)} %get-tuple-element.291), channel_id=1, source_target_pairs={{0,1},{1,0},{2,3},{3,2},{4,5},{5,4},{6,7},{7,6},{8,9},{9,8},{10,11... | collective-permute-start | bytes 1179656 | tf_op jit(solution)/shard_map/ppermute | solution.py:41
  381.5 35.2 %collective-permute-start.63 = (bf16[2,2,64,768]{3,2,1,0:T(8,128)(2,1)}, bf16[2,2,64,768]{3,2,1,0:T(8,128)(2,1)}, u32[]{:S(2)}, u32[]{:S(2)}) collective-permute-start(bf16[2,2,64,768]{3,2,1,0:T(8,128)(2,1)} %get-tuple-element.304), channel_id=1, source_target_pairs={{0,1},{1,0},{2,3},{3,2},{4,5},{5,4},{6,7},{7,6},{8,9},{9,8},{10,11... | collective-permute-start | bytes 1179656 | tf_op jit(solution)/shard_map/ppermute | solution.py:41
  384.2 32.5 %collective-permute-start.64 = (bf16[2,2,64,768]{3,2,1,0:T(8,128)(2,1)}, bf16[2,2,64,768]{3,2,1,0:T(8,128)(2,1)}, u32[]{:S(2)}, u32[]{:S(2)}) collective-permute-start(bf16[2,2,64,768]{3,2,1,0:T(8,128)(2,1)} %get-tuple-element.305), channel_id=1, source_target_pairs={{0,1},{1,0},{2,3},{3,2},{4,5},{5,4},{6,7},{7,6},{8,9},{9,8},{10,11... | collective-permute-start | bytes 1179656 | tf_op jit(solution)/shard_map/ppermute | solution.py:41
  404.3 21.9 %collective-permute-start.69 = (bf16[2,64,2048]{2,1,0:T(8,128)(2,1)S(1)}, bf16[2,64,2048]{2,1,0:T(8,128)(2,1)S(1)}, u32[]{:S(2)}, u32[]{:S(2)}) collective-permute-start(bf16[2,64,2048]{2,1,0:T(8,128)(2,1)S(1)} %fusion.15), channel_id=1, source_target_pairs={{0,4},{1,3},{2,6},{3,1},{4,0},{5,7},{6,2},{7,5},{8,12},{9,11},{10,... | collective-permute-start | bytes 1572872 | tf_op jit(solution)/shard_map/ppermute | solution.py:41
  416.7 52.1 %collective-permute-start.76 = (bf16[2,2,64,2560]{3,2,1,0:T(8,128)(2,1)}, bf16[2,2,64,2560]{3,2,1,0:T(8,128)(2,1)}, u32[]{:S(2)}, u32[]{:S(2)}) collective-permute-start(bf16[2,2,64,2560]{3,2,1,0:T(8,128)(2,1)} %fusion.9), channel_id=1, source_target_pairs={{0,8},{1,9},{2,10},{3,11},{4,12},{5,13},{6,14},{7,15},{8,0},{9,1},... | collective-permute-start | bytes 3932168 | tf_op jit(solution)/shard_map/ppermute | solution.py:41
  427.0 18.5 %collective-permute-start.66 = (bf16[2,2,2,64,768]{4,3,2,1,0:T(8,128)(2,1)}, bf16[2,2,2,64,768]{4,3,2,1,0:T(8,128)(2,1)}, u32[]{:S(2)}, u32[]{:S(2)}) collective-permute-start(bf16[2,2,2,64,768]{4,3,2,1,0:T(8,128)(2,1)} %get-tuple-element.308), channel_id=1, source_target_pairs={{0,2},{1,5},{2,0},{3,7},{4,6},{5,1},{6,4},{7,3},{8,10},{9,13},{10,... | collective-permute-start | bytes 2359304 | tf_op jit(solution)/shard_map/ppermute | solution.py:41
  433.7 99.2 %collective-permute-start.89 = (bf16[256,1024]{1,0:T(8,128)(2,1)}, bf16[256,1024]{1,0:T(8,128)(2,1)}, u32[]{:S(2)}, u32[]{:S(2)}) collective-permute-start(bf16[256,1024]{1,0:T(8,128)(2,1)} %add_convert_fusion.4), channel_id=1, source_target_pairs={{0,2},{1,3},{2,0},{3,1},{4,6},{5,7},{6,4},{7,5},{8,10},{9,11},{10,... | collective-permute-start | bytes 1572872 | tf_op jit(solution)/shard_map/ppermute | solution.py:41
  434.8 49.5 %collective-permute-start.82 = (bf16[64,2048]{1,0:T(8,128)(2,1)}, bf16[64,2048]{1,0:T(8,128)(2,1)}, u32[]{:S(2)}, u32[]{:S(2)}) collective-permute-start(bf16[64,2048]{1,0:T(8,128)(2,1)} %slice_bitcast_fusion.7), channel_id=1, source_target_pairs={{0,16},{1,17},{2,18},{3,19},{4,20},{5,21},{6,22},{7,23},{8,24},{9,... | collective-permute-start | bytes 786440 | tf_op jit(solution)/shard_map/ppermute | solution.py:41
  444.6 26.2 %collective-permute-start.75 = (bf16[2,2,2,64,768]{4,3,2,1,0:T(8,128)(2,1)}, bf16[2,2,2,64,768]{4,3,2,1,0:T(8,128)(2,1)S(1)}, u32[]{:S(2)}, u32[]{:S(2)}) collective-permute-start(bf16[2,2,2,64,768]{4,3,2,1,0:T(8,128)(2,1)} %get-tuple-element.326), channel_id=1, source_target_pairs={{0,2},{1,5},{2,0},{3,7},{4,6},{5,1},{6,4},{7,3},{8,10},{9,13},{10,... | collective-permute-start | bytes 2359304 | tf_op jit(solution)/shard_map/ppermute | solution.py:41
  468.8 30.3 %collective-permute-start.87 = (f32[128,512]{1,0:T(8,128)S(1)}, f32[128,512]{1,0:T(8,128)S(1)}, u32[]{:S(2)}, u32[]{:S(2)}) collective-permute-start(f32[128,512]{1,0:T(8,128)S(1)} %constant_dynamic-slice_fusion.5), channel_id=1, source_target_pairs={{0,1},{1,0},{2,3},{3,2},{4,5},{5,4},{6,7},{7,6},{8,9},{9,8},{10,11... | collective-permute-start | bytes 786440 | tf_op jit(solution)/shard_map/ppermute | solution.py:41
  482.0 56.5 %collective-permute-start.73 = (bf16[2,256,1024]{2,1,0:T(8,128)(2,1)S(1)}, bf16[2,256,1024]{2,1,0:T(8,128)(2,1)S(1)}, u32[]{:S(2)}, u32[]{:S(2)}) collective-permute-start(bf16[2,256,1024]{2,1,0:T(8,128)(2,1)S(1)} %copy-done.40), channel_id=1, source_target_pairs={{0,1},{1,0},{2,3},{3,2},{4,5},{5,4},{6,7},{7,6},{8,9},{9,8},{10,11... | collective-permute-start | bytes 3145736 | tf_op jit(solution)/shard_map/ppermute | solution.py:41
  489.4 19.3 %collective-permute-start.78 = (bf16[2,2,64,768]{3,2,1,0:T(8,128)(2,1)S(1)}, bf16[2,2,64,768]{3,2,1,0:T(8,128)(2,1)S(1)}, u32[]{:S(2)}, u32[]{:S(2)}) collective-permute-start(bf16[2,2,64,768]{3,2,1,0:T(8,128)(2,1)S(1)} %fusion.22), channel_id=1, source_target_pairs={{0,8},{1,9},{2,10},{3,11},{4,12},{5,13},{6,14},{7,15},{8,0},{9,1},... | collective-permute-start | bytes 1179656 | tf_op jit(solution)/shard_map/ppermute | solution.py:41
  499.1 39.4 %collective-permute-start.77 = (bf16[2,256,1024]{2,1,0:T(8,128)(2,1)S(1)}, bf16[2,256,1024]{2,1,0:T(8,128)(2,1)S(1)}, u32[]{:S(2)}, u32[]{:S(2)}) collective-permute-start(bf16[2,256,1024]{2,1,0:T(8,128)(2,1)S(1)} %add_convert_fusion.1), channel_id=1, source_target_pairs={{0,2},{1,3},{2,0},{3,1},{4,6},{5,7},{6,4},{7,5},{8,10},{9,11},{10,... | collective-permute-start | bytes 3145736 | tf_op jit(solution)/shard_map/ppermute | solution.py:41
  515.3 17.5 %collective-permute-start.90 = (bf16[64,2560]{1,0:T(8,128)(2,1)S(1)}, bf16[64,2560]{1,0:T(8,128)(2,1)S(1)}, u32[]{:S(2)}, u32[]{:S(2)}) collective-permute-start(bf16[64,2560]{1,0:T(8,128)(2,1)S(1)} %slice_bitcast_fusion.6), channel_id=1, source_target_pairs={{0,16},{1,17},{2,18},{3,19},{4,20},{5,21},{6,22},{7,23},{8,24},{9,... | collective-permute-start | bytes 983048 | tf_op jit(solution)/shard_map/ppermute | solution.py:41
  517.4 17.9 %collective-permute-start.88 = (bf16[2,64,768]{2,1,0:T(8,128)(2,1)S(1)}, bf16[2,64,768]{2,1,0:T(8,128)(2,1)S(1)}, u32[]{:S(2)}, u32[]{:S(2)}) collective-permute-start(bf16[2,64,768]{2,1,0:T(8,128)(2,1)S(1)} %fusion.23), channel_id=1, source_target_pairs={{0,4},{1,3},{2,6},{3,1},{4,0},{5,7},{6,2},{7,5},{8,12},{9,11},{10,... | collective-permute-start | bytes 589832 | tf_op jit(solution)/shard_map/ppermute | solution.py:41
  (94 other events, 744.8 us)

commit v4 on v3

--- a/solution.py
+++ b/solution.py
@@ -78,8 +78,10 @@
     def __init__(self):
         self.last = ()
 
-    def __call__(self, function, first, *rest):
-        if self.last:
+    def __call__(self, function, first, *rest, whole=False):
+        if self.last and whole:
+            first, *rest = lax.optimization_barrier((first, *rest, *self.last))[: 1 + len(rest)]
+        elif self.last:
             first = after(first, *self.last)
         result = function(first, *rest)
         self.last = jax.tree.leaves(result)[:1]
@@ -87,10 +89,16 @@
 
 
 class Gather:
-    def __init__(self, shards):
+    def __init__(self, line, shards):
         c = place() % 2
-        self.mine = jnp.concatenate([column_half(s, c) for s in shards], axis=1)
-        other = jnp.concatenate([column_half(s, 1 - c) for s in shards], axis=1)
+
+        def split(*parts):
+            return [
+                jnp.concatenate([column_half(p, half) for p in parts], axis=1)
+                for half in (1 - c, c)
+            ]
+
+        other, self.mine = line(split, *shards, whole=True)
         self.came = hop_core(other)
 
     def far(self, line):
@@ -118,7 +126,7 @@
         self.sent_other = hop_core(self.sent)
 
     def pair(self, line):
-        self.came = after(self.came, *line.last)
+        self.came = line(lambda v: v, self.came)
         self.came_other = hop_core(self.came)
 
     def pieces(self):
@@ -206,73 +214,79 @@
 
 
 def project_kernel(
-    spot_ref, token_ref, small_ref, p0, p1, p2, p3, p4, p5, p6, p7,
-    a_ref, q_ref, k_ref, v_ref, w_ref, w, sems, out_sem,
+    spot_ref, token_ref, p0, p1, p2, p3, p4, p5, p6, p7,
+    a_ref, q_ref, k_ref, v_ref, small_ref, w_ref, w, packed, vectors, sems, out_sem,
 ):
-    first = (pl.program_id(0) == 0) & (pl.program_id(1) == 0)
-    last = (pl.program_id(0) == pl.num_programs(0) - 1) & (
-        pl.program_id(1) == pl.num_programs(1) - 1
-    )
-    d = token_ref.shape[3]
+    _, items, count, d = token_ref.shape
     kept = pltpu.make_async_copy(w, w_ref, out_sem)
 
-    @pl.when(first)
+    @pl.when(pl.program_id(0) == 0)
     def _():
         half = 3 * d // 2
-        one = fetch(spot_ref, (p0, p1, p2, p3), [(w, 0, half)], sems)
-        two = fetch(spot_ref, (p4, p5, p6, p7), [(w, half, half)], sems.at[pl.ds(1, 1)])
+        one = fetch(spot_ref, (p0, p1, p2, p3), [(w, 0, half)], sems.at[pl.ds(0, 1)])
+        two = fetch(
+            spot_ref, (p4, p5, p6, p7), [(w, half, half), (packed, 0, 256)], sems.at[pl.ds(1, 2)]
+        )
+        finish(two[1])
+        vectors[...] = packed[...].astype(F32).T
+        small_ref[...] = vectors[0:16, :]
         finish(one[0])
         finish(two[0])
         kept.start()
 
-    unit, _ = unit_of(token_ref[0, 0].astype(F32))
-    normed = (unit * small_ref[0:1, :] + small_ref[1:2, :]).astype(BF)
-    a_ref[0, 0] = normed
-    k_ref[0, 0] = kdot(normed, w[:, d : 2 * d]).astype(BF)
-    v_ref[0, 0] = kdot(normed, w[:, 2 * d :]).astype(BF)
+    unit, _ = unit_of(token_ref[...].reshape(items * count, d).astype(F32))
+    normed = (unit * vectors[0:1, :] + vectors[1:2, :]).astype(BF)
+    a_ref[...] = normed.reshape(a_ref.shape)
+    k_ref[...] = kdot(normed, w[:, d : 2 * d]).astype(BF).reshape(k_ref.shape)
+    v_ref[...] = kdot(normed, w[:, 2 * d :]).astype(BF).reshape(v_ref.shape)
 
     @pl.when(pl.program_id(0) == 0)
     def _():
-        q_ref[0, 0] = kdot(normed, w[:, :d]).astype(BF)
-
-    @pl.when(last)
+        q_ref[...] = kdot(normed, w[:, :d]).astype(BF).reshape(q_ref.shape)
+
+    @pl.when(pl.program_id(0) == pl.num_programs(0) - 1)
     def _():
         kept.wait()
 
 
-def project(tokens, small, pieces):
+def project(tokens, pieces):
     blocks, items, count, d = tokens.shape
-    block = pl.BlockSpec((1, 1, count, d), lambda b, i: (b, i, 0, 0))
-    own = pl.BlockSpec(
-        (1, 1, count, d), lambda b, i: (0, jnp.where(b == 0, i, items - 1), 0, 0)
-    )
+    block = pl.BlockSpec((1, items, count, d), lambda b: (b, 0, 0, 0))
+    own = pl.BlockSpec((1, items, count, d), lambda b: (0, 0, 0, 0))
     big = shaped(tokens.shape, BF)
     return call(
         project_kernel,
         "project",
-        [big, shaped((1, items, count, d), BF), big, big, shaped((d, 3 * d), BF)],
-        [SMEM, block, pl.BlockSpec((16, d), lambda b, i: (0, 0))] + [ANY] * 8,
-        [block, own, block, block, ANY],
-        [pltpu.VMEM((d, 3 * d), BF), pltpu.SemaphoreType.DMA((2,)), pltpu.SemaphoreType.DMA],
-        grid=(blocks, items),
-    )(spots("own"), tokens, small, *pieces)
+        [big, shaped((1, items, count, d), BF), big, big, shaped((16, d), F32), shaped((d, 3 * d), BF)],
+        [SMEM, block] + [ANY] * 8,
+        [block, own, block, block, pl.BlockSpec((16, d), lambda b: (0, 0)), ANY],
+        [
+            pltpu.VMEM((d, 3 * d), BF),
+            pltpu.VMEM((d, 256), BF),
+            pltpu.VMEM((256, d), F32),
+            pltpu.SemaphoreType.DMA((3,)),
+            pltpu.SemaphoreType.DMA,
+        ],
+        grid=(blocks,),
+    )(spots("own"), tokens, *pieces)
 
 
 def mix_kernel(
-    spot_ref, att_ref, token_ref, caption_ref, small_ref, p0, p1, p2, p3,
-    r_ref, a_ref, cq_ref, memory_ref, wso_ref, wcq_ref, wcm_ref, wco_ref,
-    wso, wcq, wcm, wco, sems, out_sems,
+    spot_ref, att0_ref, att1_ref, token_ref, small_ref, p0, p1, p2, p3,
+    r_ref, a_ref, cq_ref, wso_ref, wcq_ref, wso, wcq, sems, out_sems,
 ):
-    weights = (wso, wcq, wcm, wco)
-    targets = [(w, 0, w.shape[1]) for w in weights]
-    groups = fetch(spot_ref, (p0, p1, p2, p3), targets, sems)
+    weights = (wso, wcq)
+    groups = fetch(spot_ref, (p0, p1, p2, p3), [(w, 0, w.shape[1]) for w in weights], sems)
     kept = [
         pltpu.make_async_copy(w, out, out_sems.at[i])
-        for i, (w, out) in enumerate(zip(weights, (wso_ref, wcq_ref, wcm_ref, wco_ref)))
+        for i, (w, out) in enumerate(zip(weights, (wso_ref, wcq_ref)))
     ]
     finish(groups[0])
     kept[0].start()
-    residual = token_ref[...].astype(F32) + kdot(att_ref[...], wso[...])
+    half = att0_ref.shape[1]
+    residual = token_ref[...].astype(F32) + (
+        kdot(att0_ref[...], wso[:half]) + kdot(att1_ref[...], wso[half:])
+    )
     r_ref[...] = residual
     unit, _ = unit_of(residual)
     normed = (unit * small_ref[2:3, :] + small_ref[3:4, :]).astype(BF)
@@ -280,28 +294,52 @@
     finish(groups[1])
     kept[1].start()
     cq_ref[...] = kdot(normed, wcq[...]).astype(BF)
-    finish(groups[2])
-    kept[2].start()
-    memory_ref[...] = kdot(caption_ref[...], wcm[...]).astype(BF)
-    finish(groups[3])
-    kept[3].start()
     finish(kept)
 
 
-def mix(attended, tokens, captions, small, pieces):
+def mix(attended0, attended1, tokens, small, pieces):
     rows, d = tokens.shape
-    weights = [(d, d), (d, d), (d, 2 * d), (d, d)]
     return call(
         mix_kernel,
         "mix",
         [shaped((rows, d), F32), shaped((rows, d), BF), shaped((rows, d), BF)]
-        + [shaped((captions.shape[0], 2 * d), BF)]
-        + [shaped(w, BF) for w in weights],
-        [SMEM, VMEM, VMEM, VMEM, VMEM, ANY, ANY, ANY, ANY],
-        [VMEM] * 4 + [ANY] * 4,
+        + [shaped((d, d), BF)] * 2,
+        [SMEM, VMEM, VMEM, VMEM, VMEM] + [ANY] * 4,
+        [VMEM] * 3 + [ANY] * 2,
+        [pltpu.VMEM((d, d), BF)] * 2
+        + [pltpu.SemaphoreType.DMA((2,)), pltpu.SemaphoreType.DMA((2,))],
+    )(spots("own"), attended0, attended1, tokens, small, *pieces)
+
+
+def memory_kernel(
+    spot_ref, caption_ref, p0, p1, p2, p3, memory_ref, wcm_ref, wco_ref, wcm, wco, sems, out_sems
+):
+    weights = (wcm, wco)
+    groups = fetch(spot_ref, (p0, p1, p2, p3), [(w, 0, w.shape[1]) for w in weights], sems)
+    kept = [
+        pltpu.make_async_copy(w, out, out_sems.at[i])
+        for i, (w, out) in enumerate(zip(weights, (wcm_ref, wco_ref)))
+    ]
+    finish(groups[0])
+    kept[0].start()
+    memory_ref[...] = kdot(caption_ref[...], wcm[...]).astype(BF)
+    finish(groups[1])
+    kept[1].start()
+    finish(kept)
+
+
+def remember(captions, pieces):
+    rows, d = captions.shape
+    weights = [(d, 2 * d), (d, d)]
+    return call(
+        memory_kernel,
+        "memory",
+        [shaped((rows, 2 * d), BF)] + [shaped(w, BF) for w in weights],
+        [SMEM, VMEM] + [ANY] * 4,
+        [VMEM] + [ANY] * 2,
         [pltpu.VMEM(w, BF) for w in weights]
-        + [pltpu.SemaphoreType.DMA((4,)), pltpu.SemaphoreType.DMA((4,))],
-    )(spots("own"), attended, tokens, captions, small, *pieces)
+        + [pltpu.SemaphoreType.DMA((2,)), pltpu.SemaphoreType.DMA((2,))],
+    )(spots("own"), captions, *pieces)
 
 
 def up_kernel(
@@ -469,71 +507,60 @@
     cross_ref, feed_ref, down_ref, up_ref, *refs,
 ):
     *da_refs, vec_ref, own = refs
-    first = (pl.program_id(0) == 0) & (pl.program_id(1) == 0)
-    d = token_ref.shape[3]
+    b = pl.program_id(0)
+    _, items, count, d = token_ref.shape
     half = d // 2
 
     def back(ref, at):
-        return kdot_t(ref[...].reshape(ref.shape[-2:]), w_ref[:, at : at + half])
+        return kdot_t(ref[...].reshape(items * count, half), w_ref[:, at : at + half])
 
     own[...] = (back(dk0_ref, d) + back(dk1_ref, d + half)) + (
         back(dv0_ref, 2 * d) + back(dv1_ref, 2 * d + half)
     )
 
-    @pl.when(pl.program_id(0) == 0)
+    @pl.when(b == 0)
     def _():
         own[...] += back(dq0_ref, 0) + back(dq1_ref, half)
-
-    grad = own[...]
-    for b, da_ref in enumerate(da_refs):
-
-        @pl.when(pl.program_id(0) == b)
-        def _():
-            da_ref[0] = grad.astype(BF)
-
-    unit, _ = unit_of(token_ref[0, 0].astype(F32))
-    gain = jnp.sum(grad * unit, axis=0, keepdims=True)
-    shift = jnp.sum(grad, axis=0, keepdims=True)
-
-    @pl.when(first)
-    def _():
-        vec_ref[0:1, :] = gain
-        vec_ref[1:2, :] = shift
+        vec_ref[0:2, :] = jnp.zeros((2, d), F32)
         vec_ref[2:4, :] = cross_ref[0:2, :]
         vec_ref[4:6, :] = feed_ref[0:2, :]
         vec_ref[6:7, :] = down_ref[...]
         for k in range(up_ref.shape[1] // d):
             vec_ref[7 + k : 8 + k, :] = up_ref[:, k * d : (k + 1) * d]
 
-    @pl.when(jnp.logical_not(first))
-    def _():
-        vec_ref[0:1, :] += gain
-        vec_ref[1:2, :] += shift
+    grad = own[...]
+    for k in range(len(da_refs) // items):
+
+        @pl.when(b == k)
+        def _():
+            for i in range(items):
+                da_refs[k * items + i][...] = grad[i * count : (i + 1) * count].astype(BF)
+
+    unit, _ = unit_of(token_ref[...].reshape(items * count, d).astype(F32))
+    vec_ref[0:1, :] += jnp.sum(grad * unit, axis=0, keepdims=True)
+    vec_ref[1:2, :] += jnp.sum(grad, axis=0, keepdims=True)
 
 
 def self_back(grads, tokens, weight, cross, feed, down, up):
     blocks, items, count, d = tokens.shape
-    block = pl.BlockSpec((1, 1, count, d), lambda b, i: (b, i, 0, 0))
-    part = pl.BlockSpec((1, 1, count, d // 2), lambda b, i: (b, i, 0, 0))
-
-    def only(at):
-        return lambda b, i: (jnp.where(b == at, i, jnp.where(b < at, 0, items - 1)), 0, 0)
+    block = pl.BlockSpec((1, items, count, d), lambda b: (b, 0, 0, 0))
+    part = pl.BlockSpec((1, items, count, d // 2), lambda b: (b, 0, 0, 0))
+
+    height = 7 + up.shape[1] // d
 
     def whole(array):
-        return pl.BlockSpec(array.shape, lambda b, i: (0, 0))
-
-    own = pl.BlockSpec((1, count, d // 2), only(0))
-    height = 7 + up.shape[1] // d
+        return pl.BlockSpec(array.shape, lambda b: (0,) * array.ndim)
+
     return call(
         self_back_kernel,
         "self_back",
-        [shaped((items, count, d), BF)] * blocks + [shaped((height, d), F32)],
-        [own, part, part, own, part, part, block]
+        [shaped((count, d), BF)] * (blocks * items) + [shaped((height, d), F32)],
+        [whole(grads[0]), part, part, whole(grads[3]), part, part, block]
         + [whole(a) for a in (weight, cross, feed, down, up)],
-        [pl.BlockSpec((1, count, d), only(b)) for b in range(blocks)]
-        + [pl.BlockSpec((height, d), lambda b, i: (0, 0))],
-        [pltpu.VMEM((count, d), F32)],
-        grid=(blocks, items),
+        [pl.BlockSpec((count, d), lambda b: (0, 0))] * (blocks * items)
+        + [pl.BlockSpec((height, d), lambda b: (0, 0))],
+        [pltpu.VMEM((items * count, d), F32)],
+        grid=(blocks,),
     )(*grads, tokens, weight, cross, feed, down, up)
 
 
@@ -666,44 +693,51 @@
         return line(join, self.theirs, self.mine)
 
 
+def pack_small(vectors, bias):
+    r = vectors[0].shape[0]
+    k = bias.shape[0] // r
+    rows = jnp.concatenate([jnp.stack(vectors), bias.reshape(k, r)])
+    return jnp.pad(rows.T, ((0, 0), (0, 256 - rows.shape[0])))
+
+
+def offset_rows(rows):
+    k, d = rows.shape
+    n = device_count()
+    return rows.reshape(k, n, d // n).transpose(1, 0, 2).reshape(1, k * d)
+
+
 class SmallSum:
     def __init__(self, values):
-        self.values, self.distance = values, 1
+        self.values = values
+        far = 16
+        self.distances = [1, 4]
+        while far < device_count():
+            self.distances.append(far)
+            far *= 2
+        self.distances += [8, 2]
         self.send()
 
     def send(self):
-        self.came = hop(self.values, lambda i: i ^ self.distance)
+        distance = self.distances.pop(0)
+        self.came = hop(self.values, lambda i: i ^ distance)
 
     def step(self, line):
         self.values = line(lambda c, v: c + v, self.came, self.values)
-        self.distance *= 2
-        if self.distance < device_count():
+        if self.distances:
             self.send()
-
-    def finish(self, line):
-        while self.distance < device_count():
-            self.step(line)
-        return self.values
-
-
-def small_rows(vectors, bias):
-    n = device_count()
-    part = vectors[0].shape[0]
-    width = part * n
-    rows = jnp.zeros((len(vectors), width), BF)
-    rows = lax.dynamic_update_slice(rows, jnp.stack(vectors), (0, place() * part))
-    long = jnp.zeros((bias.shape[0] * n,), BF)
-    long = lax.dynamic_update_slice(long, bias, (place() * bias.shape[0],))
-    return jnp.concatenate([rows, long.reshape(-1, width)])
-
-
-def small_parts(rows, count):
-    n = device_count()
-    part = rows.shape[1] // n
-    own = lax.dynamic_slice_in_dim(rows[:count], place() * part, part, 1)
-    long = rows[count:].reshape(-1)
-    share = long.shape[0] // n
-    return [own[i] for i in range(count)], lax.dynamic_slice_in_dim(long, place() * share, share)
+            return True
+        return False
+
+    def parts(self, line, count):
+        while self.step(line):
+            pass
+        rows = self.values
+        n = device_count()
+        part = rows.shape[1] // n
+        own = lax.dynamic_slice_in_dim(rows[:count], place() * part, part, 1)
+        long = rows[count:].reshape(-1)
+        share = long.shape[0] // n
+        return own, lax.dynamic_slice_in_dim(long, place() * share, share)
 
 
 def shifts(info_ref, kind, block):
@@ -751,10 +785,11 @@
             outs.append(out / total)
         o_ref[0, :, at] = jnp.concatenate(outs, axis=0).T.astype(BF)
 
-def attend(kind, info, queries, q_at, keyed, k_at, valued, v_at, group=1):
+def attend(kind, info, queries, q_at, keyed, k_at, valued, v_at, group=1, part=(0, 1)):
     blocks, items, span, _ = keyed.shape
     count = queries.shape[2]
-    pairs = HEADS // 2
+    pairs = HEADS // 2 // part[1]
+    skip = part[0] * pairs // group
     lanes = 128 * group
     width = pairs * 128
     return pl.pallas_call(
@@ -763,9 +798,9 @@
         grid_spec=pltpu.PrefetchScalarGridSpec(
             num_scalar_prefetch=1, grid=(items, pairs // group),
             in_specs=[
-                pl.BlockSpec((1, 1, count, lanes), lambda i, p, s: (0, i, 0, p + q_at // lanes)),
-                pl.BlockSpec((blocks, 1, span, lanes), lambda i, p, s: (0, i, 0, p + k_at // lanes)),
-                pl.BlockSpec((blocks, 1, span, lanes), lambda i, p, s: (0, i, 0, p + v_at // lanes)),
+                pl.BlockSpec((1, 1, count, lanes), lambda i, p, s: (0, i, 0, p + skip + q_at // lanes)),
+                pl.BlockSpec((blocks, 1, span, lanes), lambda i, p, s: (0, i, 0, p + skip + k_at // lanes)),
+                pl.BlockSpec((blocks, 1, span, lanes), lambda i, p, s: (0, i, 0, p + skip + v_at // lanes)),
             ],
             out_specs=[
                 pl.BlockSpec((1, count, lanes), lambda i, p, s: (i, 0, p)),
@@ -884,75 +919,83 @@
     features = tokens.shape[2]
     k_bias = up_weight.shape[1] // features
     half = 3 * features // 2
-    ga = Gather([self_in_weight[:, :half]])
     line = Line()
+    tokens_y = hop_seq(tokens, 2)
+    ga = Gather(line, [self_in_weight[:, :half]])
     ga.far(line)
-    tokens_y = hop_seq(tokens, 2)
-    tokens_1 = hop_seq(tokens, 1)
-    ge = Gather([self_in_weight[:, half:]])
-    gb = Gather([self_out_weight, cross_query_weight, cross_memory_weight, cross_out_weight])
-    gc = Gather([up_weight])
-    gd = Gather([down_weight])
-    small = SmallSum(
-        small_rows(
-            [self_gain, self_shift, cross_gain, cross_shift, feed_gain, feed_shift, down_bias],
-            up_bias,
-        )
-    )
+    small = line(
+        lambda *v: pack_small(list(v[:-1]), v[-1]),
+        self_gain, self_shift, cross_gain, cross_shift, feed_gain, feed_shift, down_bias, up_bias,
+        whole=True,
+    )
+    ge = Gather(line, [self_in_weight[:, half:], small])
     ga.first(line)
     ge.far(line)
     ga.near(line)
     ge.first(line)
+    tokens_y = line(lambda v: v, tokens_y)
+    tokens_3 = hop_seq(tokens_y, 1)
+    gb = Gather(line, [self_out_weight, cross_query_weight])
     ga.second(line)
     ge.near(line)
-    small.step(line)
     gb.far(line)
-    small.step(line)
-    tokens_y = after(tokens_y, *line.last)
-    tokens_3 = hop_seq(tokens_y, 1)
+    gf = Gather(line, [cross_memory_weight, cross_out_weight])
+    gc = Gather(line, [up_weight])
     ga.pair(line)
     ge.second(line)
-    small.step(line)
     gb.first(line)
-    small.step(line)
-    small_low = small.finish(line)
-    small_full = line(
-        lambda v: jnp.pad(wide(v), ((0, 16 - v.shape[0]), (0, 0))), small_low
-    )
-    up_offset = wide(small_low[7:]).reshape(1, -1)
+    gf.far(line)
+    tokens_1 = hop_seq(tokens, 1)
     all_tokens = line(lambda a, b, c, d: jnp.stack([d, b, c, a]), tokens_3, tokens_1, tokens_y, tokens)
+    gd = Gather(line, [down_weight])
     ge.pair(line)
+    gf.first(line)
     gb.near(line)
     gc.far(line)
     seq_place = lax.axis_index("seq").astype(jnp.int32)[None]
 
-    normed1, queries, key_rows, value_rows, self_in = line(
-        lambda t: project(t, small_full, ga.pieces() + ge.pieces()), all_tokens
-    )
+    normed1, queries, key_rows, value_rows, small_full, self_in = line(
+        lambda t: project(t, ga.pieces() + ge.pieces()), all_tokens
+    )
+    up_offset = offset_rows(small_full[7 : 7 + k_bias])
+    gd.far(line)
     gc.first(line)
+    gf.near(line)
     gb.second(line)
-    gc.near(line)
-    gd.far(line)
-    attended1, lse1 = line(
-        lambda q: attend("causal", seq_place, q, 0, key_rows, 0, value_rows, 0, 2), queries
-    )
-    gb.pair(line)
-    gd.first(line)
+    halves = []
+    for i in range(2):
+        halves.append(
+            line(
+                lambda q: attend("causal", seq_place, q, 0, key_rows, 0, value_rows, 0, 2, (i, 2)),
+                queries,
+            )
+        )
+        if i == 0:
+            gd.first(line)
+            gc.near(line)
+            gf.second(line)
+            gb.pair(line)
+    flat_tokens, flat_captions = flat(tokens), flat(captions)
+    residual1, normed2, cross_queries, self_out, cross_query = line(
+        lambda b, a: mix(flat(a), flat(b), flat_tokens, small_full, gb.pieces()),
+        halves[1][0],
+        halves[0][0],
+    )
+    cross_queries = cross_queries.reshape(1, *tokens.shape)
+    gd.near(line)
     gc.second(line)
-    gd.near(line)
-    flat_tokens, flat_captions = flat(tokens), flat(captions)
-    residual1, normed2, cross_queries, memory, self_out, cross_query, cross_memory, cross_out = line(
-        lambda a: mix(flat(a), flat_tokens, flat_captions, small_full, gb.pieces()), attended1
-    )
-    cross_queries = cross_queries.reshape(1, *tokens.shape)
+    gf.pair(line)
+    attended1 = jnp.concatenate([h[0] for h in halves], axis=2)
+    lse1 = jnp.concatenate([h[1] for h in halves], axis=1)
+
+    memory, cross_memory, cross_out = line(lambda c: remember(c, gf.pieces()), flat_captions)
     memory = memory.reshape(1, *captions.shape[:2], -1)
-
     attended2, lse2 = line(
         lambda q: attend("length", caption_lengths, q, 0, memory, 0, memory, features, 8),
         cross_queries,
     )
+    gd.second(line)
     gc.pair(line)
-    gd.second(line)
 
     residual2, normed3, activated, slope, up = line(
         lambda a: up_gelu(flat(a), residual1, cross_out, small_full, up_offset, gc.pieces()),
@@ -1019,85 +1062,95 @@
             (flat_normed1, flat(grads[2])),
         ]
 
+    caption_sum = line(lambda c, v: (wide(c) + wide(v)).astype(BF), caption_came, caption_sum)
+    caption_came = hop_seq(caption_sum, 2)
     s2.near(line)
     grads_a = heads_back(0)
     s1.first(line)
     s3.second(line)
     s4 = Scatter(line, heads_terms(grads_a))
-    caption_sum = line(lambda c, v: (wide(c) + wide(v)).astype(BF), caption_came, caption_sum)
-    caption_came = hop_seq(caption_sum, 2)
     s1.far(line)
     grads_b = heads_back(1)
+    s4.second(line)
+    s5 = Scatter(line, heads_terms(grads_b))
     s2.first(line)
     s3.near(line)
-    s5 = Scatter(line, heads_terms(grads_b))
-    s4.second(line)
-    s2.far(line)
-    s1.close(line)
+    grad_captions = line(lambda c, v: wide(c) + wide(v), caption_came, caption_sum)
+    grad_captions = grad_captions.reshape(captions.shape)
     s5.second(line)
     s4.near(line)
     *grad_blocks, small_grads = line(
         lambda g, *o: self_back(
-            (g, *o, *grads_b), all_tokens, self_in, grad_cross, grad_feed, grad_down_bias, grad_up_bias
+            (g, *o, *grads_b), all_tokens, self_in, grad_cross, grad_feed, grad_down_bias,
+            grad_up_bias,
         ),
         *grads_a,
     )
-    grad_ones = hop_seq(grad_blocks[1], 1)
-    grad_threes = hop_seq(grad_blocks[3], 1)
+    items = tokens.shape[0]
+    grad_blocks = [grad_blocks[k * items : (k + 1) * items] for k in range(4)]
     small = SmallSum(small_grads)
+    grad_threes = [hop_seq(v, 1) for v in grad_blocks[3]]
+    grad_ones = [hop_seq(v, 1) for v in grad_blocks[1]]
+    s5.near(line)
     s3.first(line)
-    s5.near(line)
-    grad_far = line(lambda a, b: (wide(a) + wide(b)).astype(BF), grad_threes, grad_blocks[2])
-    grad_twos = hop_seq(grad_far, 2)
+    grad_twos = [
+        hop_seq(line(lambda a, b: (wide(a) + wide(b)).astype(BF), came, own), 2)
+        for came, own in zip(grad_threes, grad_blocks[2])
+    ]
+    s2.far(line)
+    small.step(line)
     s4.first(line)
+    s3.far(line)
+    small.step(line)
+    s5.first(line)
+    s4.far(line)
+    small.step(line)
+    s1.close(line)
+    s5.far(line)
+
+    def last_norm(came, one, own, token, residual):
+        grad = wide(own) + wide(one) + wide(came)
+        unit, inverse = unit_of(wide(token))
+        return residual + unit_back(unit, inverse, grad * small_full[0])
+
+    grad_first = grad_first.reshape(tokens.shape)
+    grad_tokens = jnp.stack(
+        [
+            line(last_norm, grad_twos[i], grad_ones[i], grad_blocks[0][i], tokens[i], grad_first[i])
+            for i in range(items)
+        ]
+    )
     small.step(line)
     s2.close(line)
-    small.step(line)
-    s3.far(line)
-    small.step(line)
+    s3.close(line)
+    s4.close(line)
+    s5.close(line)
+    small_out, grad_bias = small.parts(line, 7)
     (grad_down,) = s1.result(line)
-    s4.far(line)
-    small.step(line)
-    s5.first(line)
-    small.step(line)
     (grad_up,) = s2.result(line)
-    s3.close(line)
-    grad_captions = line(lambda c, v: wide(c) + wide(v), caption_came, caption_sum)
-    grad_captions = grad_captions.reshape(captions.shape)
-    small_parts_out, grad_bias = small_parts(small.finish(line), 7)
-
-    def last_norm(came, one, own):
-        grad = wide(own) + wide(one) + wide(came)
-        unit, inverse = unit_of(wide(tokens))
-        return grad_first.reshape(tokens.shape) + unit_back(unit, inverse, grad * small_full[0])
-
-    s5.far(line)
-    grad_tokens = line(last_norm, grad_twos, grad_ones, grad_blocks[0])
-    s4.close(line)
     results3 = s3.result(line)
     grad_cross_query, grad_cross_memory, grad_cross_out, grad_self_out = results3
-    s5.close(line)
     grads_4 = s4.result(line)
     grads_5 = s5.result(line)
     return (
         final.reshape(tokens.shape),
         grad_tokens,
         grad_captions,
-        small_parts_out[0],
-        small_parts_out[1],
+        small_out[0],
+        small_out[1],
         jnp.concatenate([g for pair in zip(grads_4, grads_5) for g in pair], axis=1),
         grad_self_out,
-        small_parts_out[2],
-        small_parts_out[3],
+        small_out[2],
+        small_out[3],
         grad_cross_query,
         grad_cross_memory,
         grad_cross_out,
-        small_parts_out[4],
-        small_parts_out[5],
+        small_out[4],
+        small_out[5],
         grad_up,
         grad_bias,
         grad_down,
-        small_parts_out[6],
+        small_out[6],
     )
 
 

time: 555 us -> 543 us (0.978)
  waiting for transfers between devices: 122 us -> 91.7 us
  starting transfers between devices: 77.7 us -> 93.1 us
    ppermute x98 -> x103, waiting for transfers between devices: 122 us -> 91.7 us  [hop(): return lax.ppermute(values, AXES, pairs)]
    ppermute x98 -> x103, starting transfers between devices: 77.7 us -> 93.1 us  [hop(): return lax.ppermute(values, AXES, pairs)]
    pallas_call x1 -> x2, Pallas kernels: 22 us -> 28.5 us  [the longest x1 21.6 us: self_back(): call(self_back_kernel, 'self_back', [shaped((count, d), BF)] * (blocks *...]
    pallas_call x2 -> x3, Pallas kernels: 29.5 us -> 31.5 us  [attend(): pl.pallas_call(functools.partial(attend_kernel, kind), out_shape=[jax.Sha...]
    unnamed x102 -> x155, local copies, waits for them, and re-layouts: 12.6 us -> 12 us
  transfers between devices with their start and end apart: 98 -> 103, of which waited for: 28 -> 26; matrix products, arithmetic and copies ran while one was open for 12% -> 13% of each run, Pallas kernels for 44% -> 47%
where the time goes in v4:
time: 543 us; the launch traced here: 539 us
  Pallas kernels  269 us (50%)
  starting transfers between devices  93.1 us (17%)
  waiting for transfers between devices  91.7 us (17%)
  other arithmetic  50.8 us (9%)
  local copies, waits for them, and re-layouts  27.5 us (5%)
    ppermute x103, starting transfers between devices, hop(): return lax.ppermute(values, AXES, pairs)  93.1 us
    ppermute x103, waiting for transfers between devices, hop(): return lax.ppermute(values, AXES, pairs)  91.7 us
    pallas_call x10, Pallas kernels, wgrad(): pl.pallas_call(functools.partial(wgrad_kernel, kinds, rows, side), out_sh...  80.9 us
    pallas_call x3, Pallas kernels, attend_back(): pl.pallas_call(functools.partial(attend_back_kernel, kind), out_shape=[ja...  41.6 us
    pallas_call x3, Pallas kernels, attend(): pl.pallas_call(functools.partial(attend_kernel, kind), out_shape=[jax.Sha...  31.5 us
    pallas_call x1, Pallas kernels, self_back(): call(self_back_kernel, 'self_back', [shaped((count, d), BF)] * (blocks *...  21.6 us
    pallas_call x1, Pallas kernels, project(): call(project_kernel, 'project', [big, shaped((1, items, count, d), BF), b...  19.1 us
    pallas_call x1, Pallas kernels, up_gelu(): call(up_kernel, 'up_gelu', [shaped((rows, d), F32), shaped((rows, d), BF)...  18.4 us
  transfers between devices with their start and end apart: 103, of which 26 were waited for; matrix products, arithmetic and copies ran while one was open for 13% of the time, Pallas kernels for 47%

profile of v4, /device:TPU:0, one launch (start us, length us, event | category | flops | bytes accessed | tf_op | source)
XLA Modules:
  0.0 538.6 jit_solution(3584269166142748942)
XLA Ops:
  2.2 2.6 collective-permute-start.1
  5.6 2.7 collective-permute-start.4
  16.7 3.7 collective-permute-done.6
  26.1 2.9 collective-permute-done.1
  29.0 4.7 collective-permute-start.7
  34.5 4.8 collective-permute-start.21
  41.3 4.8 collective-permute-done.14.p2
  48.6 6.0 %collective-permute-done.13 = bf16[2,2,64,896]{3,2,1,0:T(8,128)(2,1)S(1)} collective-permute-done((bf16[2,2,64,896]{3,2,1,0:T(8,128)(2,1)S(1)}, bf16[2,2,64,896]{3,2,1,0:T(8,128)(2,1)S(1)}, u32[]{:S(2)}, u32[]{:S(2)}) %collective-permute-start.13) | collective-permute-done | bytes 458784 | tf_op jit(solution)/shard_map/ppermute | solution.py:41
  59.6 2.8 pad_maximum_fusion.token_ref
  62.4 8.6 %collective-permute-done.19.p6 = bf16[2,2,2,64,896]{4,3,2,1,0:T(8,128)(2,1)S(1)} collective-permute-done((bf16[2,2,2,64,896]{4,3,2,1,0:T(8,128)(2,1)S(1)}, bf16[2,2,2,64,896]{4,3,2,1,0:T(8,128)(2,1)S(1)}, u32[]{:S(2)}, u32[]{:S(2)}) %collective-permute-start.19) | collective-permute-done | bytes 917536 | tf_op jit(solution)/shard_map/ppermute | solution.py:41
  72.1 2.7 collective-permute-done.16
  79.6 19.1 %project.1 = (bf16[4,2,256,1024]{3,2,1,0:T(8,128)(2,1)}, bf16[1,2,256,1024]{3,2,1,0:T(8,128)(2,1)}, bf16[4,2,256,1024]{3,2,1,0:T(8,128)(2,1)}, bf16[4,2,256,1024...) custom-call(s32[5]{0:T(128)} %stack.147.spot_ref, ...), custom_call_target="tpu_custom_call" | custom-call | flops 1 | bytes 1 | tf_op jit(solution)/shard_map/project/pallas_call | solution.py:257
  105.9 11.8 %attend.3 = (bf16[2,256,512]{2,1,0:T(8,128)(2,1)}, f32[2,4,2,256]{3,2,1,0:T(2,128)}) custom-call(s32[1]{0:T(128)} %bitcast.42.info_ref, bf16[1,2,256,1024]{3,2,1,0:T(8,128)(2,1)} %get-tuple-element.261.q_ref, bf16[4,2,256,1024]{3,2,1,0:T(8,128)(2,1)} %get-tuple-element.254.k_ref, bf16[4,2,256,1024]{3,2,1,0:T(8,128)(2,1)} %get-tuple-element.255.v_ref), custom_call_target="tpu_custom_call" | custom-call | flops 1 | bytes 1 | tf_op jit(solution)/shard_map/attend/pallas_call | solution.py:795
  117.8 6.4 %collective-permute-done.24 = bf16[256,512]{1,0:T(8,128)(2,1)S(1)} collective-permute-done((bf16[256,512]{1,0:T(8,128)(2,1)S(1)}, bf16[256,512]{1,0:T(8,128)(2,1)S(1)}, u32[]{:S(2)}, u32[]{:S(2)}) %collective-permute-start.24) | collective-permute-done | bytes 262176 | tf_op jit(solution)/shard_map/ppermute | solution.py:41
  131.5 11.9 %attend.4 = (bf16[2,256,512]{2,1,0:T(8,128)(2,1)}, f32[2,4,2,256]{3,2,1,0:T(2,128)}) custom-call(s32[1]{0:T(128)} %bitcast.42.info_ref, bf16[1,2,256,1024]{3,2,1,0:T(8,128)(2,1)} %get-tuple-element.261.q_ref, bf16[4,2,256,1024]{3,2,1,0:T(8,128)(2,1)} %get-tuple-element.254.k_ref, bf16[4,2,256,1024]{3,2,1,0:T(8,128)(2,1)} %get-tuple-element.255.v_ref), custom_call_target="tpu_custom_call" | custom-call | flops 1 | bytes 1 | tf_op jit(solution)/shard_map/attend/pallas_call | solution.py:795
  143.5 8.4 %mix.1 = (f32[512,1024]{1,0:T(8,128)}, bf16[512,1024]{1,0:T(8,128)(2,1)}, bf16[512,1024]{1,0:T(8,128)(2,1)}, bf16[1024,1024]{1,0:T(8,128)(2,1)}, bf16[1024,1024]{1,0:T(8,128)(2,1)}) custom-call(s32[5]{0:T(128)} %stack.147.spot_ref, bf16[512,512]{1,0:T(8,128)(2,1)} %bitcast.333, bf16[512,512]{1,0:T(8,128)(2,1)} %bitcast.334, bf16[512,1024]{1,0:T(8,128)(2,1)} %bitcast.290, ...), custom_call_target="tpu_custom_call" | custom-call | flops 1 | bytes 1 | tf_op jit(solution)/shard_map/mix/pallas_call | solution.py:302
  154.1 2.7 pad_maximum_fusion.1.p1
  165.1 6.9 %memory.1 = (bf16[256,2048]{1,0:T(8,128)(2,1)}, bf16[1024,2048]{1,0:T(8,128)(2,1)}, bf16[1024,1024]{1,0:T(8,128)(2,1)}) custom-call(s32[5]{0:T(128)} %stack.147.spot_ref, bf16[256,1024]{1,0:T(8,128)(2,1)} %bitcast.324, bf16[2,2,2,64,1536]{4,3,2,1,0:T(8,128)(2,1)} %copy-done.24, bf16[2,2,2,64,1536]{4,3,2,1,0:T(8,128)(2,1)} %copy-done.5, ...), custom_call_target="tpu_custom_call" | custom-call | flops 1 | bytes 1 | tf_op jit(solution)/shard_map/memory/pallas_call | solution.py:334
  172.0 7.8 %attend.5 = (bf16[2,256,1024]{2,1,0:T(8,128)(2,1)}, f32[2,8,2,256]{3,2,1,0:T(2,128)}) custom-call(s32[2]{0:T(128)} %info_ref.3, bf16[1,2,256,1024]{3,2,1,0:T(8,128)(2,1)} %bitcast.329, bf16[1,2,128,2048]{3,2,1,0:T(8,128)(2,1)} %bitcast.313, bf16[1,2,128,2048]{3,2,1,0:T(8,128)(2,1)} %bitcast.314), custom_call_target="tpu_custom_call" | custom-call | flops 1 | bytes 1 | tf_op jit(solution)/shard_map/attend/pallas_call | solution.py:795
  179.8 4.4 collective-permute-done.34
  190.3 18.4 %up_gelu.1 = (f32[512,1024]{1,0:T(8,128)}, bf16[512,1024]{1,0:T(8,128)(2,1)}, bf16[512,4096]{1,0:T(8,128)(2,1)}, bf16[512,4096]{1,0:T(8,128)(2,1)}, bf16[1024,4096]{1,0:T(8,128)(2,1)}) custom-call(s32[5]{0:T(128)} %stack.147.spot_ref, bf16[512,1024]{1,0:T(8,128)(2,1)} %bitcast.310, f32[512,1024]{1,0:T(8,128)} %get-tuple-element.265.r1_ref, ...), custom_call_target="tpu_custom_call" | custom-call | flops 1 | bytes 1 | tf_op jit(solution)/shard_map/up_gelu/pallas_call | solution.py:379
  208.7 6.8 %wgrad.10 = (bf16[2,2,256,512]{3,2,1,0:T(8,128)(2,1)}, bf16[2,2,256,512]{3,2,1,0:T(8,128)(2,1)}, bf16[2,2,256,512]{3,2,1,0:T(8,128)(2,1)}, bf16[2,2,256,512]{3,2,1,0:T(8,128)(2,1)}) custom-call(s32[5]{0:T(128)} %stack.368.spot_ref, bf16[512,4096]{1,0:T(8,128)(2,1)} %get-tuple-element.280.refs_0_.act_ref, bf16[512,1024]{1,0:T(8,128)(2,1)} %bitcast.306), custom_call_target="tpu_custom_call" | custom-call | flops 1 | bytes 1 | tf_op jit(solution)/shard_map/wgrad/pallas_call | solution.py:621
  216.7 3.2 collective-permute-done.43.p0
  221.2 18.1 %down.1 = (bf16[512,1024]{1,0:T(8,128)(2,1)}, bf16[512,4096]{1,0:T(8,128)(2,1)}, f32[1,4096]{1,0:T(1,128)}, f32[1,1024]{1,0:T(1,128)}) custom-call(s32[5]{0:T(128)} %stack.147.spot_ref, bf16[512,1024]{1,0:T(8,128)(2,1)} %bitcast.307, bf16[512,4096]{1,0:T(8,128)(2,1)} %get-tuple-element.284.slope_ref, bf16[512,4096]{1,0:T(8,128)(2,1)} %get-tuple-element.280.refs_0_.act_ref, ...), custom_call_target="tpu_custom_call" | custom-call | flops 1 | bytes 1 | tf_op jit(solution)/shard_map/down/pallas_call | solution.py:426
  241.9 8.2 %wgrad.11 = (bf16[2,2,2,256,512]{4,3,2,1,0:T(8,128)(2,1)}, bf16[2,2,2,256,512]{4,3,2,1,0:T(8,128)(2,1)}) custom-call(s32[5]{0:T(128)} %stack.147.spot_ref, bf16[512,4096]{1,0:T(8,128)(2,1)} %get-tuple-element.280.refs_0_.act_ref, bf16[512,1024]{1,0:T(8,128)(2,1)} %bitcast.308, bf16[2,2,256,512]{3,2,1,0:T(8,128)(2,1)} %copy-done.27, ...), custom_call_target="tpu_custom_call" | custom-call | flops 1 | bytes 1 | tf_op jit(solution)/shard_map/wgrad/pallas_call | solution.py:621
  250.6 6.9 %wgrad.12 = (bf16[2,2,64,2048]{3,2,1,0:T(8,128)(2,1)}, bf16[2,2,64,2048]{3,2,1,0:T(8,128)(2,1)}, bf16[2,2,64,2048]{3,2,1,0:T(8,128)(2,1)}, bf16[2,2,64,2048]{3,2,1,0:T(8,128)(2,1)}) custom-call(s32[5]{0:T(128)} %stack.368.spot_ref, bf16[512,1024]{1,0:T(8,128)(2,1)} %get-tuple-element.294.refs_0_, bf16[512,4096]{1,0:T(8,128)(2,1)} %get-tuple-element.296.refs_1_.g_ref), custom_call_target="tpu_custom_call" | custom-call | flops 1 | bytes 1 | tf_op jit(solution)/shard_map/wgrad/pallas_call | solution.py:621
  258.5 14.2 %feed_back.1 = (f32[512,1024]{1,0:T(8,128)}, bf16[512,1024]{1,0:T(8,128)(2,1)}, bf16[512,1024]{1,0:T(8,128)(2,1)}, f32[8,1024]{1,0:T(8,128)}) custom-call(bf16[512,4096]{1,0:T(8,128)(2,1)} %get-tuple-element.296.refs_1_.g_ref, bf16[1024,4096]{1,0:T(8,128)(2,1)} %get-tuple-element.297.w_ref, f32[512,1024]{1,0:T(8,128)} %get-tuple-element.279.r2_ref, ...), custom_call_target="tpu_custom_call" | custom-call | flops 1 | bytes 1 | tf_op jit(solution)/shard_map/feed_back/pallas_call | solution.py:465
  275.3 8.2 %wgrad.13 = (bf16[2,2,2,64,2048]{4,3,2,1,0:T(8,128)(2,1)}, bf16[2,2,2,64,2048]{4,3,2,1,0:T(8,128)(2,1)}) custom-call(s32[5]{0:T(128)} %stack.147.spot_ref, bf16[512,1024]{1,0:T(8,128)(2,1)} %get-tuple-element.294.refs_0_, bf16[512,4096]{1,0:T(8,128)(2,1)} %get-tuple-element.296.refs_1_.g_ref, bf16[2,2,64,2048]{3,2,1,0:T(8,128)(2,1)} %copy-done.30, ...), custom_call_target="tpu_custom_call" | custom-call | flops 1 | bytes 1 | tf_op jit(solution)/shard_map/wgrad/pallas_call | solution.py:621
  285.0 10.6 %attend_back.3 = (bf16[2,256,1024]{2,1,0:T(8,128)(2,1)}, bf16[1,2,128,1024]{3,2,1,0:T(8,128)(2,1)}, bf16[1,2,128,1024]{3,2,1,0:T(8,128)(2,1)}) custom-call(s32[2]{0:T(128)} %info_ref.3, bf16[1,2,256,1024]{3,2,1,0:T(8,128)(2,1)} %bitcast.330, bf16[1,2,128,2048]{3,2,1,0:T(8,128)(2,1)} %bitcast.315, bf16[1,2,128,2048]{3,2,1,0:T(8,128)(2,1)} %bitcast.316, ...), custom_call_target="tpu_custom_call" | custom-call | flops 1 | bytes 1 | tf_op jit(solution)/shard_map/attend_back/pallas_call | solution.py:864
  297.1 8.3 %cross_back.1 = (f32[512,1024]{1,0:T(8,128)}, bf16[512,1024]{1,0:T(8,128)(2,1)}, bf16[512,1024]{1,0:T(8,128)(2,1)}, f32[8,1024]{1,0:T(8,128)}) custom-call(bf16[512,1024]{1,0:T(8,128)(2,1)} %bitcast.317, bf16[1024,1024]{1,0:T(8,128)(2,1)} %get-tuple-element.310.wcq_ref, f32[512,1024]{1,0:T(8,128)} %get-tuple-element.265.r1_ref, ...), custom_call_target="tpu_custom_call" | custom-call | flops 1 | bytes 1 | tf_op jit(solution)/shard_map/cross_back/pallas_call | solution.py:495
  305.5 4.0 convolution_convert_fusion
  312.6 7.7 %wgrad.14 = (bf16[2,2,64,2560]{3,2,1,0:T(8,128)(2,1)}, bf16[2,2,64,2560]{3,2,1,0:T(8,128)(2,1)}, bf16[2,2,64,2560]{3,2,1,0:T(8,128)(2,1)}, bf16[2,2,64,2560]{3,2,1,0:T(8,128)(2,1)}) custom-call(s32[5]{0:T(128)} %stack.368.spot_ref, bf16[512,1024]{1,0:T(8,128)(2,1)} %get-tuple-element.323.refs_0_, bf16[512,1024]{1,0:T(8,128)(2,1)} %bitcast.318, ...), custom_call_target="tpu_custom_call" | custom-call | flops 1 | bytes 1 | tf_op jit(solution)/shard_map/wgrad/pallas_call | solution.py:621
  324.6 15.6 %attend_back.4 = (bf16[2,256,512]{2,1,0:T(8,128)(2,1)}, bf16[4,2,256,512]{3,2,1,0:T(8,128)(2,1)}, bf16[4,2,256,512]{3,2,1,0:T(8,128)(2,1)}) custom-call(s32[1]{0:T(128)} %bitcast.42.info_ref, bf16[1,2,256,1024]{3,2,1,0:T(8,128)(2,1)} %get-tuple-element.261.q_ref, bf16[4,2,256,1024]{3,2,1,0:T(8,128)(2,1)} %get-tuple-element.254.k_ref, ...), custom_call_target="tpu_custom_call" | custom-call | flops 1 | bytes 1 | tf_op jit(solution)/shard_map/attend_back/pallas_call | solution.py:864
  342.2 9.4 %wgrad.15 = (bf16[2,2,2,64,2560]{4,3,2,1,0:T(8,128)(2,1)}, bf16[2,2,2,64,2560]{4,3,2,1,0:T(8,128)(2,1)}) custom-call(s32[5]{0:T(128)} %stack.147.spot_ref, bf16[512,1024]{1,0:T(8,128)(2,1)} %get-tuple-element.323.refs_0_, bf16[512,1024]{1,0:T(8,128)(2,1)} %bitcast.319, bf16[256,1024]{1,0:T(8,128)(2,1)} %bitcast.326, bf16[256,2048]{1,0:T(8,128)(2,1)} %copy-done.3, ...), custom_call_target="tpu_custom_call" | custom-call | flops 1 | bytes 1 | tf_op jit(solution)/shard_map/wgrad/pallas_call | solution.py:621
  355.9 8.5 %wgrad.16 = (bf16[2,2,64,768]{3,2,1,0:T(8,128)(2,1)}, bf16[2,2,64,768]{3,2,1,0:T(8,128)(2,1)}, bf16[2,2,64,768]{3,2,1,0:T(8,128)(2,1)}, bf16[2,2,64,768]{3,2,1,0:T(8,128)(2,1)}) custom-call(s32[5]{0:T(128)} %stack.368.spot_ref, bf16[512,1024]{1,0:T(8,128)(2,1)} %bitcast.292, bf16[512,512]{1,0:T(8,128)(2,1)} %bitcast.320, bf16[2048,1024]{1,0:T(8,128)(2,1)} %bitcast.282, ...), custom_call_target="tpu_custom_call" | custom-call | flops 1 | bytes 1 | tf_op jit(solution)/shard_map/wgrad/pallas_call | solution.py:621
  370.7 15.4 %attend_back.5 = (bf16[2,256,512]{2,1,0:T(8,128)(2,1)}, bf16[4,2,256,512]{3,2,1,0:T(8,128)(2,1)}, bf16[4,2,256,512]{3,2,1,0:T(8,128)(2,1)}) custom-call(s32[1]{0:T(128)} %bitcast.42.info_ref, bf16[1,2,256,1024]{3,2,1,0:T(8,128)(2,1)} %get-tuple-element.261.q_ref, bf16[4,2,256,1024]{3,2,1,0:T(8,128)(2,1)} %get-tuple-element.254.k_ref, ...), custom_call_target="tpu_custom_call" | custom-call | flops 1 | bytes 1 | tf_op jit(solution)/shard_map/attend_back/pallas_call | solution.py:864
  387.8 8.5 %wgrad.17 = (bf16[2,2,2,64,768]{4,3,2,1,0:T(8,128)(2,1)}, bf16[2,2,2,64,768]{4,3,2,1,0:T(8,128)(2,1)}) custom-call(s32[5]{0:T(128)} %stack.147.spot_ref, bf16[512,1024]{1,0:T(8,128)(2,1)} %bitcast.293, bf16[512,512]{1,0:T(8,128)(2,1)} %bitcast.321, bf16[2048,1024]{1,0:T(8,128)(2,1)} %bitcast.284, bf16[2048,512]{1,0:T(8,128)(2,1)} %bitcast.299, ...), custom_call_target="tpu_custom_call" | custom-call | flops 1 | bytes 1 | tf_op jit(solution)/shard_map/wgrad/pallas_call | solution.py:621
  396.2 8.5 %wgrad.18 = (bf16[2,2,64,768]{3,2,1,0:T(8,128)(2,1)}, bf16[2,2,64,768]{3,2,1,0:T(8,128)(2,1)}, bf16[2,2,64,768]{3,2,1,0:T(8,128)(2,1)}, bf16[2,2,64,768]{3,2,1,0:T(8,128)(2,1)}) custom-call(s32[5]{0:T(128)} %stack.368.spot_ref, bf16[512,1024]{1,0:T(8,128)(2,1)} %bitcast.294, bf16[512,512]{1,0:T(8,128)(2,1)} %bitcast.322, bf16[2048,1024]{1,0:T(8,128)(2,1)} %bitcast.286, ...), custom_call_target="tpu_custom_call" | custom-call | flops 1 | bytes 1 | tf_op jit(solution)/shard_map/wgrad/pallas_call | solution.py:621
  408.0 2.7 fusion
  416.1 8.2 %wgrad.19 = (bf16[2,2,2,64,768]{4,3,2,1,0:T(8,128)(2,1)}, bf16[2,2,2,64,768]{4,3,2,1,0:T(8,128)(2,1)}) custom-call(s32[5]{0:T(128)} %stack.147.spot_ref, bf16[512,1024]{1,0:T(8,128)(2,1)} %bitcast.295, bf16[512,512]{1,0:T(8,128)(2,1)} %bitcast.323, bf16[2048,1024]{1,0:T(8,128)(2,1)} %bitcast.288, bf16[2048,512]{1,0:T(8,128)(2,1)} %bitcast.303, ...), custom_call_target="tpu_custom_call" | custom-call | flops 1 | bytes 1 | tf_op jit(solution)/shard_map/wgrad/pallas_call | solution.py:621
  432.6 21.6 %self_back.1 = (bf16[256,1024]{1,0:T(8,128)(2,1)}, bf16[256,1024]{1,0:T(8,128)(2,1)}, bf16[256,1024]{1,0:T(8,128)(2,1)}, bf16[256,1024]{1,0:T(8,128)(2,1)}, bf16...) custom-call(bf16[2,256,512]{2,1,0:T(8,128)(2,1)} %get-tuple-element., ...), custom_call_target="tpu_custom_call" | custom-call | flops 1 | bytes 1 | tf_op jit(solution)/shard_map/self_back/pallas_call | solution.py:554
  464.3 7.9 %collective-permute-done.84 = bf16[2,64,2560]{2,1,0:T(8,128)(2,1)S(1)} collective-permute-done((bf16[2,64,2560]{2,1,0:T(8,128)(2,1)S(1)}, bf16[2,64,2560]{2,1,0:T(8,128)(2,1)S(1)}, u32[]{:S(2)}, u32[]{:S(2)}) %collective-permute-start.84) | collective-permute-done | bytes 655392 | tf_op jit(solution)/shard_map/ppermute | solution.py:41
  484.0 3.2 collective-permute-done.88
  490.7 3.5 collective-permute-done.86
  500.5 3.3 collective-permute-done.91
  505.1 4.3 collective-permute-start.101
  512.2 5.8 %collective-permute-done.97 = bf16[64,2048]{1,0:T(8,128)(2,1)S(1)} collective-permute-done((bf16[64,2048]{1,0:T(8,128)(2,1)S(1)}, bf16[64,2048]{1,0:T(8,128)(2,1)S(1)}, u32[]{:S(2)}, u32[]{:S(2)}) %collective-permute-start.97) | collective-permute-done | bytes 262176 | tf_op jit(solution)/shard_map/ppermute | solution.py:41
  519.6 7.6 %collective-permute-done.96 = bf16[64,2560]{1,0:T(8,128)(2,1)S(1)} collective-permute-done((bf16[64,2560]{1,0:T(8,128)(2,1)S(1)}, bf16[64,2560]{1,0:T(8,128)(2,1)S(1)}, u32[]{:S(2)}, u32[]{:S(2)}) %collective-permute-start.96) | collective-permute-done | bytes 327712 | tf_op jit(solution)/shard_map/ppermute | solution.py:41
  (479 shorter events, 161.8 us)
Async XLA Ops:
  2.2 26.8 %collective-permute-start.1 = (bf16[2,256,1024]{2,1,0:T(8,128)(2,1)}, bf16[2,256,1024]{2,1,0:T(8,128)(2,1)S(1)}, u32[]{:S(2)}, u32[]{:S(2)}) collective-permute-start(bf16[2,256,1024]{2,1,0:T(8,128)(2,1)} %param.19), channel_id=1, source_target_pairs={{0,2},{1,3},{2,0},{3,1},{4,6},{5,7},{6,4},{7,5},{8,10},{9,11},{10,... | collective-permute-start | bytes 3145736 | tf_op jit(solution)/shard_map/ppermute | solution.py:41
  4.8 54.6 %collective-permute-start = (bf16[2,256,1024]{2,1,0:T(8,128)(2,1)}, bf16[2,256,1024]{2,1,0:T(8,128)(2,1)S(1)}, u32[]{:S(2)}, u32[]{:S(2)}) collective-permute-start(bf16[2,256,1024]{2,1,0:T(8,128)(2,1)} %param.19), channel_id=1, source_target_pairs={{0,1},{1,0},{2,3},{3,2},{4,5},{5,4},{6,7},{7,6},{8,9},{9,8},{10,11... | collective-permute-start | bytes 3145736 | tf_op jit(solution)/shard_map/ppermute | solution.py:41
  29.0 30.2 %collective-permute-start.7 = (bf16[2,256,1024]{2,1,0:T(8,128)(2,1)S(1)}, bf16[2,256,1024]{2,1,0:T(8,128)(2,1)S(1)}, u32[]{:S(2)}, u32[]{:S(2)}) collective-permute-start(bf16[2,256,1024]{2,1,0:T(8,128)(2,1)S(1)} %collective-permute-done.1), channel_id=1, source_target_pairs={{0,1},{1,0},{2,3},{3,2},{4,5},{5,4},{6,7},{7,6},{8,9},{9,8},{10,11... | collective-permute-start | bytes 3145736 | tf_op jit(solution)/shard_map/ppermute | solution.py:41
  34.5 40.5 %collective-permute-start.21 = (bf16[2,2,2,64,768]{4,3,2,1,0:T(8,128)(2,1)S(1)}, bf16[2,2,2,64,768]{4,3,2,1,0:T(8,128)(2,1)S(1)}, u32[]{:S(2)}, u32[]{:S(2)}) collective-permute-start(bf16[2,2,2,64,768]{4,3,2,1,0:T(8,128)(2,1)S(1)} %pad_maximum_fusion.10.p1), channel_id=1, source_target_pairs={{0,1},{1,0},{2,3},{3,2},{4,5},{5,4},{6,7},{7,6},{8,9},{9,8},{10,11... | collective-permute-start | bytes 2359304 | tf_op jit(solution)/shard_map/ppermute | solution.py:41
  74.8 23.8 %collective-permute-start.15 = (bf16[128,512]{1,0:T(8,128)(2,1)S(1)}, bf16[128,512]{1,0:T(8,128)(2,1)S(1)}, u32[]{:S(2)}, u32[]{:S(2)}) collective-permute-start(bf16[128,512]{1,0:T(8,128)(2,1)S(1)} %get-tuple-element.458), channel_id=1, source_target_pairs={{0,1},{1,0},{2,3},{3,2},{4,5},{5,4},{6,7},{7,6},{8,9},{9,8},{10,11... | collective-permute-start | bytes 393224 | tf_op jit(solution)/shard_map/ppermute | solution.py:41
  75.0 26.0 %collective-permute-start.26 = (bf16[2,64,1536]{2,1,0:T(8,128)(2,1)S(1)}, bf16[2,64,1536]{2,1,0:T(8,128)(2,1)S(1)}, u32[]{:S(2)}, u32[]{:S(2)}) collective-permute-start(bf16[2,64,1536]{2,1,0:T(8,128)(2,1)S(1)} %get-tuple-element.444), channel_id=1, source_target_pairs={{0,4},{1,3},{2,6},{3,1},{4,0},{5,7},{6,2},{7,5},{8,12},{9,11},{10,... | collective-permute-start | bytes 1179656 | tf_op jit(solution)/shard_map/ppermute | solution.py:41
  75.2 23.5 %collective-permute-start.27 = (bf16[64,2048]{1,0:T(8,128)(2,1)S(1)}, bf16[64,2048]{1,0:T(8,128)(2,1)S(1)}, u32[]{:S(2)}, u32[]{:S(2)}) collective-permute-start(bf16[64,2048]{1,0:T(8,128)(2,1)S(1)} %maximum_select_fusion), channel_id=1, source_target_pairs={{0,16},{1,17},{2,18},{3,19},{4,20},{5,21},{6,22},{7,23},{8,24},{9,... | collective-permute-start | bytes 786440 | tf_op jit(solution)/shard_map/ppermute | solution.py:41
  76.1 26.0 %collective-permute-start.25 = (bf16[2,2,64,1024]{3,2,1,0:T(8,128)(2,1)S(1)}, bf16[2,2,64,1024]{3,2,1,0:T(8,128)(2,1)}, u32[]{:S(2)}, u32[]{:S(2)}) collective-permute-start(bf16[2,2,64,1024]{3,2,1,0:T(8,128)(2,1)S(1)} %get-tuple-element.440), channel_id=1, source_target_pairs={{0,8},{1,9},{2,10},{3,11},{4,12},{5,13},{6,14},{7,15},{8,0},{9,1},... | collective-permute-start | bytes 1572872 | tf_op jit(solution)/shard_map/ppermute | solution.py:41
  99.4 24.8 %collective-permute-start.31 = (bf16[2,64,2048]{2,1,0:T(8,128)(2,1)S(1)}, bf16[2,64,2048]{2,1,0:T(8,128)(2,1)S(1)}, u32[]{:S(2)}, u32[]{:S(2)}) collective-permute-start(bf16[2,64,2048]{2,1,0:T(8,128)(2,1)S(1)} %get-tuple-element.438), channel_id=1, source_target_pairs={{0,4},{1,3},{2,6},{3,1},{4,0},{5,7},{6,2},{7,5},{8,12},{9,11},{10,... | collective-permute-start | bytes 1572872 | tf_op jit(solution)/shard_map/ppermute | solution.py:41
  101.1 26.1 %collective-permute-start.30 = (bf16[2,2,64,1536]{3,2,1,0:T(8,128)(2,1)S(1)}, bf16[2,2,64,1536]{3,2,1,0:T(8,128)(2,1)S(1)}, u32[]{:S(2)}, u32[]{:S(2)}) collective-permute-start(bf16[2,2,64,1536]{3,2,1,0:T(8,128)(2,1)S(1)} %get-tuple-element.434), channel_id=1, source_target_pairs={{0,8},{1,9},{2,10},{3,11},{4,12},{5,13},{6,14},{7,15},{8,0},{9,1},... | collective-permute-start | bytes 2359304 | tf_op jit(solution)/shard_map/ppermute | solution.py:41
  103.2 24.2 %collective-permute-start.29 = (bf16[2,2,2,64,1024]{4,3,2,1,0:T(8,128)(2,1)S(1)}, bf16[2,2,2,64,1024]{4,3,2,1,0:T(8,128)(2,1)S(1)}, u32[]{:S(2)}, u32[]{:S(2)}) collective-permute-start(bf16[2,2,2,64,1024]{4,3,2,1,0:T(8,128)(2,1)S(1)} %pad_maximum_fusion.5.p1), channel_id=1, source_target_pairs={{0,2},{1,5},{2,0},{3,7},{4,6},{5,1},{6,4},{7,3},{8,10},{9,13},{10,... | collective-permute-start | bytes 3145736 | tf_op jit(solution)/shard_map/ppermute | solution.py:41
  105.9 37.5 %collective-permute-start.33 = (bf16[2,2,2,64,1024]{4,3,2,1,0:T(8,128)(2,1)S(1)}, bf16[2,2,2,64,1024]{4,3,2,1,0:T(8,128)(2,1)}, u32[]{:S(2)}, u32[]{:S(2)}) collective-permute-start(bf16[2,2,2,64,1024]{4,3,2,1,0:T(8,128)(2,1)S(1)} %pad_maximum_fusion.5.p1), channel_id=1, source_target_pairs={{0,1},{1,0},{2,3},{3,2},{4,5},{5,4},{6,7},{7,6},{8,9},{9,8},{10,11... | collective-permute-start | bytes 3145736 | tf_op jit(solution)/shard_map/ppermute | solution.py:41
  127.5 26.6 %collective-permute-start.36 = (bf16[2,2,64,2048]{3,2,1,0:T(8,128)(2,1)}, bf16[2,2,64,2048]{3,2,1,0:T(8,128)(2,1)}, u32[]{:S(2)}, u32[]{:S(2)}) collective-permute-start(bf16[2,2,64,2048]{3,2,1,0:T(8,128)(2,1)} %get-tuple-element.426), channel_id=1, source_target_pairs={{0,8},{1,9},{2,10},{3,11},{4,12},{5,13},{6,14},{7,15},{8,0},{9,1},... | collective-permute-start | bytes 3145736 | tf_op jit(solution)/shard_map/ppermute | solution.py:41
  130.0 28.3 %collective-permute-start.35 = (bf16[2,2,2,64,1536]{4,3,2,1,0:T(8,128)(2,1)S(1)}, bf16[2,2,2,64,1536]{4,3,2,1,0:T(8,128)(2,1)S(1)}, u32[]{:S(2)}, u32[]{:S(2)}) collective-permute-start(bf16[2,2,2,64,1536]{4,3,2,1,0:T(8,128)(2,1)S(1)} %pad_maximum_fusion.4.p1), channel_id=1, source_target_pairs={{0,2},{1,5},{2,0},{3,7},{4,6},{5,1},{6,4},{7,3},{8,10},{9,13},{10,... | collective-permute-start | bytes 4718600 | tf_op jit(solution)/shard_map/ppermute | solution.py:41
  131.5 20.4 %collective-permute-start.28 = (bf16[2,256,512]{2,1,0:T(8,128)(2,1)S(1)}, bf16[2,256,512]{2,1,0:T(8,128)(2,1)S(1)}, u32[]{:S(2)}, u32[]{:S(2)}) collective-permute-start(bf16[2,256,512]{2,1,0:T(8,128)(2,1)S(1)} %get-tuple-element.436), channel_id=1, source_target_pairs={{0,4},{1,3},{2,6},{3,1},{4,0},{5,7},{6,2},{7,5},{8,12},{9,11},{10,... | collective-permute-start | bytes 1572872 | tf_op jit(solution)/shard_map/ppermute | solution.py:41
  156.8 28.9 %collective-permute-start.40 = (bf16[2,2,2,64,2048]{4,3,2,1,0:T(8,128)(2,1)}, bf16[2,2,2,64,2048]{4,3,2,1,0:T(8,128)(2,1)}, u32[]{:S(2)}, u32[]{:S(2)}) collective-permute-start(bf16[2,2,2,64,2048]{4,3,2,1,0:T(8,128)(2,1)} %pad_maximum_fusion.1.p1), channel_id=1, source_target_pairs={{0,2},{1,5},{2,0},{3,7},{4,6},{5,1},{6,4},{7,3},{8,10},{9,13},{10,... | collective-permute-start | bytes 6291464 | tf_op jit(solution)/shard_map/ppermute | solution.py:41
  158.8 25.5 %collective-permute-start.34 = (bf16[2,2,256,512]{3,2,1,0:T(8,128)(2,1)}, bf16[2,2,256,512]{3,2,1,0:T(8,128)(2,1)}, u32[]{:S(2)}, u32[]{:S(2)}) collective-permute-start(bf16[2,2,256,512]{3,2,1,0:T(8,128)(2,1)} %get-tuple-element.424), channel_id=1, source_target_pairs={{0,8},{1,9},{2,10},{3,11},{4,12},{5,13},{6,14},{7,15},{8,0},{9,1},... | collective-permute-start | bytes 3145736 | tf_op jit(solution)/shard_map/ppermute | solution.py:41
  160.6 28.2 %collective-permute-start.42 = (bf16[2,2,2,64,2048]{4,3,2,1,0:T(8,128)(2,1)}, bf16[2,2,2,64,2048]{4,3,2,1,0:T(8,128)(2,1)}, u32[]{:S(2)}, u32[]{:S(2)}) collective-permute-start(bf16[2,2,2,64,2048]{4,3,2,1,0:T(8,128)(2,1)} %pad_maximum_fusion.1.p1), channel_id=1, source_target_pairs={{0,1},{1,0},{2,3},{3,2},{4,5},{5,4},{6,7},{7,6},{8,9},{9,8},{10,11... | collective-permute-start | bytes 6291464 | tf_op jit(solution)/shard_map/ppermute | solution.py:41
  185.8 29.7 %collective-permute-start.39 = (bf16[2,2,2,256,512]{4,3,2,1,0:T(8,128)(2,1)S(1)}, bf16[2,2,2,256,512]{4,3,2,1,0:T(8,128)(2,1)}, u32[]{:S(2)}, u32[]{:S(2)}) collective-permute-start(bf16[2,2,2,256,512]{4,3,2,1,0:T(8,128)(2,1)S(1)} %pad_maximum_fusion.2.p1), channel_id=1, source_target_pairs={{0,2},{1,5},{2,0},{3,7},{4,6},{5,1},{6,4},{7,3},{8,10},{9,13},{10,... | collective-permute-start | bytes 6291464 | tf_op jit(solution)/shard_map/ppermute | solution.py:41
  186.4 30.1 %collective-permute-start.44 = (bf16[2,2,2,256,512]{4,3,2,1,0:T(8,128)(2,1)S(1)}, bf16[2,2,2,256,512]{4,3,2,1,0:T(8,128)(2,1)}, u32[]{:S(2)}, u32[]{:S(2)}) collective-permute-start(bf16[2,2,2,256,512]{4,3,2,1,0:T(8,128)(2,1)S(1)} %pad_maximum_fusion.2.p1), channel_id=1, source_target_pairs={{0,1},{1,0},{2,3},{3,2},{4,5},{5,4},{6,7},{7,6},{8,9},{9,8},{10,11... | collective-permute-start | bytes 6291464 | tf_op jit(solution)/shard_map/ppermute | solution.py:41
  215.7 23.6 %collective-permute-start.45 = (bf16[2,2,256,512]{3,2,1,0:T(8,128)(2,1)}, bf16[2,2,256,512]{3,2,1,0:T(8,128)(2,1)S(1)}, u32[]{:S(2)}, u32[]{:S(2)}) collective-permute-start(bf16[2,2,256,512]{3,2,1,0:T(8,128)(2,1)} %get-tuple-element.281), channel_id=1, source_target_pairs={{0,1},{1,0},{2,3},{3,2},{4,5},{5,4},{6,7},{7,6},{8,9},{9,8},{10,11... | collective-permute-start | bytes 3145736 | tf_op jit(solution)/shard_map/ppermute | solution.py:41
  216.0 23.3 %collective-permute-start.46 = (bf16[2,2,256,512]{3,2,1,0:T(8,128)(2,1)}, bf16[2,2,256,512]{3,2,1,0:T(8,128)(2,1)S(1)}, u32[]{:S(2)}, u32[]{:S(2)}) collective-permute-start(bf16[2,2,256,512]{3,2,1,0:T(8,128)(2,1)} %get-tuple-element.290), channel_id=1, source_target_pairs={{0,1},{1,0},{2,3},{3,2},{4,5},{5,4},{6,7},{7,6},{8,9},{9,8},{10,11... | collective-permute-start | bytes 3145736 | tf_op jit(solution)/shard_map/ppermute | solution.py:41
  216.2 23.1 %collective-permute-start.47 = (bf16[2,2,256,512]{3,2,1,0:T(8,128)(2,1)}, bf16[2,2,256,512]{3,2,1,0:T(8,128)(2,1)S(1)}, u32[]{:S(2)}, u32[]{:S(2)}) collective-permute-start(bf16[2,2,256,512]{3,2,1,0:T(8,128)(2,1)} %get-tuple-element.291), channel_id=1, source_target_pairs={{0,1},{1,0},{2,3},{3,2},{4,5},{5,4},{6,7},{7,6},{8,9},{9,8},{10,11... | collective-permute-start | bytes 3145736 | tf_op jit(solution)/shard_map/ppermute | solution.py:41
  216.6 22.8 %collective-permute-start.48 = (bf16[2,2,256,512]{3,2,1,0:T(8,128)(2,1)}, bf16[2,2,256,512]{3,2,1,0:T(8,128)(2,1)S(1)}, u32[]{:S(2)}, u32[]{:S(2)}) collective-permute-start(bf16[2,2,256,512]{3,2,1,0:T(8,128)(2,1)} %get-tuple-element.292), channel_id=1, source_target_pairs={{0,1},{1,0},{2,3},{3,2},{4,5},{5,4},{6,7},{7,6},{8,9},{9,8},{10,11... | collective-permute-start | bytes 3145736 | tf_op jit(solution)/shard_map/ppermute | solution.py:41
  250.1 45.5 %collective-permute-start.53 = (bf16[2,2,2,256,512]{4,3,2,1,0:T(8,128)(2,1)}, bf16[2,2,2,256,512]{4,3,2,1,0:T(8,128)(2,1)S(1)}, u32[]{:S(2)}, u32[]{:S(2)}) collective-permute-start(bf16[2,2,2,256,512]{4,3,2,1,0:T(8,128)(2,1)} %get-tuple-element.307), channel_id=1, source_target_pairs={{0,2},{1,5},{2,0},{3,7},{4,6},{5,1},{6,4},{7,3},{8,10},{9,13},{10,... | collective-permute-start | bytes 6291464 | tf_op jit(solution)/shard_map/ppermute | solution.py:41
  283.5 37.5 %collective-permute-start.54 = (bf16[2,2,2,64,2048]{4,3,2,1,0:T(8,128)(2,1)}, bf16[2,2,2,64,2048]{4,3,2,1,0:T(8,128)(2,1)S(1)}, u32[]{:S(2)}, u32[]{:S(2)}) collective-permute-start(bf16[2,2,2,64,2048]{4,3,2,1,0:T(8,128)(2,1)} %get-tuple-element.316), channel_id=1, source_target_pairs={{0,2},{1,5},{2,0},{3,7},{4,6},{5,1},{6,4},{7,3},{8,10},{9,13},{10,... | collective-permute-start | bytes 6291464 | tf_op jit(solution)/shard_map/ppermute | solution.py:41
  309.7 30.5 %collective-permute-start.57 = (bf16[2,2,256,512]{3,2,1,0:T(8,128)(2,1)}, bf16[2,2,256,512]{3,2,1,0:T(8,128)(2,1)}, u32[]{:S(2)}, u32[]{:S(2)}) collective-permute-start(bf16[2,2,256,512]{3,2,1,0:T(8,128)(2,1)} %fusion.23), channel_id=1, source_target_pairs={{0,8},{1,9},{2,10},{3,11},{4,12},{5,13},{6,14},{7,15},{8,0},{9,1},... | collective-permute-start | bytes 3145736 | tf_op jit(solution)/shard_map/ppermute | solution.py:41
  320.3 21.9 %collective-permute-start.56 = (bf16[2,2,64,2560]{3,2,1,0:T(8,128)(2,1)}, bf16[2,2,64,2560]{3,2,1,0:T(8,128)(2,1)}, u32[]{:S(2)}, u32[]{:S(2)}) collective-permute-start(bf16[2,2,64,2560]{3,2,1,0:T(8,128)(2,1)} %get-tuple-element.326), channel_id=1, source_target_pairs={{0,1},{1,0},{2,3},{3,2},{4,5},{5,4},{6,7},{7,6},{8,9},{9,8},{10,11... | collective-permute-start | bytes 3932168 | tf_op jit(solution)/shard_map/ppermute | solution.py:41
  320.5 21.7 %collective-permute-start.58 = (bf16[2,2,64,2560]{3,2,1,0:T(8,128)(2,1)}, bf16[2,2,64,2560]{3,2,1,0:T(8,128)(2,1)}, u32[]{:S(2)}, u32[]{:S(2)}) collective-permute-start(bf16[2,2,64,2560]{3,2,1,0:T(8,128)(2,1)} %get-tuple-element.335), channel_id=1, source_target_pairs={{0,1},{1,0},{2,3},{3,2},{4,5},{5,4},{6,7},{7,6},{8,9},{9,8},{10,11... | collective-permute-start | bytes 3932168 | tf_op jit(solution)/shard_map/ppermute | solution.py:41
  320.8 21.4 %collective-permute-start.59 = (bf16[2,2,64,2560]{3,2,1,0:T(8,128)(2,1)}, bf16[2,2,64,2560]{3,2,1,0:T(8,128)(2,1)}, u32[]{:S(2)}, u32[]{:S(2)}) collective-permute-start(bf16[2,2,64,2560]{3,2,1,0:T(8,128)(2,1)} %get-tuple-element.336), channel_id=1, source_target_pairs={{0,1},{1,0},{2,3},{3,2},{4,5},{5,4},{6,7},{7,6},{8,9},{9,8},{10,11... | collective-permute-start | bytes 3932168 | tf_op jit(solution)/shard_map/ppermute | solution.py:41
  321.0 21.2 %collective-permute-start.60 = (bf16[2,2,64,2560]{3,2,1,0:T(8,128)(2,1)}, bf16[2,2,64,2560]{3,2,1,0:T(8,128)(2,1)}, u32[]{:S(2)}, u32[]{:S(2)}) collective-permute-start(bf16[2,2,64,2560]{3,2,1,0:T(8,128)(2,1)} %get-tuple-element.337), channel_id=1, source_target_pairs={{0,1},{1,0},{2,3},{3,2},{4,5},{5,4},{6,7},{7,6},{8,9},{9,8},{10,11... | collective-permute-start | bytes 3932168 | tf_op jit(solution)/shard_map/ppermute | solution.py:41
  351.7 56.0 %collective-permute-start.69 = (bf16[2,2,2,64,2560]{4,3,2,1,0:T(8,128)(2,1)}, bf16[2,2,2,64,2560]{4,3,2,1,0:T(8,128)(2,1)}, u32[]{:S(2)}, u32[]{:S(2)}) collective-permute-start(bf16[2,2,2,64,2560]{4,3,2,1,0:T(8,128)(2,1)} %get-tuple-element.354), channel_id=1, source_target_pairs={{0,2},{1,5},{2,0},{3,7},{4,6},{5,1},{6,4},{7,3},{8,10},{9,13},{10,... | collective-permute-start | bytes 7864328 | tf_op jit(solution)/shard_map/ppermute | solution.py:41
  352.3 53.0 %collective-permute-start.70 = (bf16[2,2,64,2048]{3,2,1,0:T(8,128)(2,1)}, bf16[2,2,64,2048]{3,2,1,0:T(8,128)(2,1)}, u32[]{:S(2)}, u32[]{:S(2)}) collective-permute-start(bf16[2,2,64,2048]{3,2,1,0:T(8,128)(2,1)} %fusion.24), channel_id=1, source_target_pairs={{0,8},{1,9},{2,10},{3,11},{4,12},{5,13},{6,14},{7,15},{8,0},{9,1},... | collective-permute-start | bytes 3145736 | tf_op jit(solution)/shard_map/ppermute | solution.py:41
  364.7 21.5 %collective-permute-start.63 = (bf16[2,2,64,768]{3,2,1,0:T(8,128)(2,1)}, bf16[2,2,64,768]{3,2,1,0:T(8,128)(2,1)S(1)}, u32[]{:S(2)}, u32[]{:S(2)}) collective-permute-start(bf16[2,2,64,768]{3,2,1,0:T(8,128)(2,1)} %get-tuple-element.345), channel_id=1, source_target_pairs={{0,1},{1,0},{2,3},{3,2},{4,5},{5,4},{6,7},{7,6},{8,9},{9,8},{10,11... | collective-permute-start | bytes 1179656 | tf_op jit(solution)/shard_map/ppermute | solution.py:41
  367.6 20.1 %collective-permute-start.64 = (bf16[2,2,64,768]{3,2,1,0:T(8,128)(2,1)}, bf16[2,2,64,768]{3,2,1,0:T(8,128)(2,1)}, u32[]{:S(2)}, u32[]{:S(2)}) collective-permute-start(bf16[2,2,64,768]{3,2,1,0:T(8,128)(2,1)} %get-tuple-element.346), channel_id=1, source_target_pairs={{0,1},{1,0},{2,3},{3,2},{4,5},{5,4},{6,7},{7,6},{8,9},{9,8},{10,11... | collective-permute-start | bytes 1179656 | tf_op jit(solution)/shard_map/ppermute | solution.py:41
  386.2 24.5 %collective-permute-start.68 = (bf16[256,1024]{1,0:T(8,128)(2,1)S(1)}, bf16[256,1024]{1,0:T(8,128)(2,1)}, u32[]{:S(2)}, u32[]{:S(2)}) collective-permute-start(bf16[256,1024]{1,0:T(8,128)(2,1)S(1)} %add_convert_fusion.5), channel_id=1, source_target_pairs={{0,2},{1,3},{2,0},{3,1},{4,6},{5,7},{6,4},{7,5},{8,10},{9,11},{10,... | collective-permute-start | bytes 1572872 | tf_op jit(solution)/shard_map/ppermute | solution.py:41
  411.4 44.2 %collective-permute-start.76 = (bf16[2,2,64,2560]{3,2,1,0:T(8,128)(2,1)}, bf16[2,2,64,2560]{3,2,1,0:T(8,128)(2,1)}, u32[]{:S(2)}, u32[]{:S(2)}) collective-permute-start(bf16[2,2,64,2560]{3,2,1,0:T(8,128)(2,1)} %fusion), channel_id=1, source_target_pairs={{0,8},{1,9},{2,10},{3,11},{4,12},{5,13},{6,14},{7,15},{8,0},{9,1},... | collective-permute-start | bytes 3932168 | tf_op jit(solution)/shard_map/ppermute | solution.py:41
  424.3 30.1 %collective-permute-start.77 = (bf16[2,2,2,64,768]{4,3,2,1,0:T(8,128)(2,1)}, bf16[2,2,2,64,768]{4,3,2,1,0:T(8,128)(2,1)}, u32[]{:S(2)}, u32[]{:S(2)}) collective-permute-start(bf16[2,2,2,64,768]{4,3,2,1,0:T(8,128)(2,1)} %get-tuple-element.373), channel_id=1, source_target_pairs={{0,2},{1,5},{2,0},{3,7},{4,6},{5,1},{6,4},{7,3},{8,10},{9,13},{10,... | collective-permute-start | bytes 2359304 | tf_op jit(solution)/shard_map/ppermute | solution.py:41
  427.1 61.3 %collective-permute-start.87 = (bf16[256,512]{1,0:T(8,128)(2,1)}, bf16[256,512]{1,0:T(8,128)(2,1)}, u32[]{:S(2)}, u32[]{:S(2)}) collective-permute-start(bf16[256,512]{1,0:T(8,128)(2,1)} %slice_bitcast_fusion.8), channel_id=1, source_target_pairs={{0,16},{1,17},{2,18},{3,19},{4,20},{5,21},{6,22},{7,23},{8,24},{9,... | collective-permute-start | bytes 786440 | tf_op jit(solution)/shard_map/ppermute | solution.py:41
  429.0 29.7 %collective-permute-start.81 = (bf16[2,64,2048]{2,1,0:T(8,128)(2,1)}, bf16[2,64,2048]{2,1,0:T(8,128)(2,1)S(1)}, u32[]{:S(2)}, u32[]{:S(2)}) collective-permute-start(bf16[2,64,2048]{2,1,0:T(8,128)(2,1)} %fusion.26), channel_id=1, source_target_pairs={{0,4},{1,3},{2,6},{3,1},{4,0},{5,7},{6,2},{7,5},{8,12},{9,11},{10,... | collective-permute-start | bytes 1572872 | tf_op jit(solution)/shard_map/ppermute | solution.py:41
  431.4 30.2 %collective-permute-start.85 = (bf16[2,2,64,768]{3,2,1,0:T(8,128)(2,1)}, bf16[2,2,64,768]{3,2,1,0:T(8,128)(2,1)}, u32[]{:S(2)}, u32[]{:S(2)}) collective-permute-start(bf16[2,2,64,768]{3,2,1,0:T(8,128)(2,1)} %fusion.32), channel_id=1, source_target_pairs={{0,8},{1,9},{2,10},{3,11},{4,12},{5,13},{6,14},{7,15},{8,0},{9,1},... | collective-permute-start | bytes 1179656 | tf_op jit(solution)/shard_map/ppermute | solution.py:41
  458.1 40.1 %collective-permute-start.74 = (bf16[256,1024]{1,0:T(8,128)(2,1)S(1)}, bf16[256,1024]{1,0:T(8,128)(2,1)S(1)}, u32[]{:S(2)}, u32[]{:S(2)}) collective-permute-start(bf16[256,1024]{1,0:T(8,128)(2,1)S(1)} %copy-done.68), channel_id=1, source_target_pairs={{0,1},{1,0},{2,3},{3,2},{4,5},{5,4},{6,7},{7,6},{8,9},{9,8},{10,11... | collective-permute-start | bytes 1572872 | tf_op jit(solution)/shard_map/ppermute | solution.py:41
  458.7 46.3 %collective-permute-start.90 = (bf16[256,1024]{1,0:T(8,128)(2,1)S(1)}, bf16[256,1024]{1,0:T(8,128)(2,1)S(1)}, u32[]{:S(2)}, u32[]{:S(2)}) collective-permute-start(bf16[256,1024]{1,0:T(8,128)(2,1)S(1)} %copy-done.67), channel_id=1, source_target_pairs={{0,1},{1,0},{2,3},{3,2},{4,5},{5,4},{6,7},{7,6},{8,9},{9,8},{10,11... | collective-permute-start | bytes 1572872 | tf_op jit(solution)/shard_map/ppermute | solution.py:41
  494.2 23.8 %collective-permute-start.97 = (bf16[64,2048]{1,0:T(8,128)(2,1)S(1)}, bf16[64,2048]{1,0:T(8,128)(2,1)S(1)}, u32[]{:S(2)}, u32[]{:S(2)}) collective-permute-start(bf16[64,2048]{1,0:T(8,128)(2,1)S(1)} %slice_bitcast_fusion.7), channel_id=1, source_target_pairs={{0,16},{1,17},{2,18},{3,19},{4,20},{5,21},{6,22},{7,23},{8,24},{9,... | collective-permute-start | bytes 786440 | tf_op jit(solution)/shard_map/ppermute | solution.py:41
  496.2 30.9 %collective-permute-start.96 = (bf16[64,2560]{1,0:T(8,128)(2,1)S(1)}, bf16[64,2560]{1,0:T(8,128)(2,1)S(1)}, u32[]{:S(2)}, u32[]{:S(2)}) collective-permute-start(bf16[64,2560]{1,0:T(8,128)(2,1)S(1)} %slice_bitcast_fusion.6), channel_id=1, source_target_pairs={{0,16},{1,17},{2,18},{3,19},{4,20},{5,21},{6,22},{7,23},{8,24},{9,... | collective-permute-start | bytes 983048 | tf_op jit(solution)/shard_map/ppermute | solution.py:41
  498.2 31.1 %collective-permute-start.95 = (bf16[64,768]{1,0:T(8,128)(2,1)S(1)}, bf16[64,768]{1,0:T(8,128)(2,1)S(1)}, u32[]{:S(2)}, u32[]{:S(2)}) collective-permute-start(bf16[64,768]{1,0:T(8,128)(2,1)S(1)} %slice_bitcast_fusion.13), channel_id=1, source_target_pairs={{0,16},{1,17},{2,18},{3,19},{4,20},{5,21},{6,22},{7,23},{8,24},{9,... | collective-permute-start | bytes 294920 | tf_op jit(solution)/shard_map/ppermute | solution.py:41
  505.1 26.4 %collective-permute-start.101 = (f32[128,512]{1,0:T(8,128)S(1)}, f32[128,512]{1,0:T(8,128)S(1)}, u32[]{:S(2)}, u32[]{:S(2)}) collective-permute-start(f32[128,512]{1,0:T(8,128)S(1)} %constant_dynamic-slice_fusion.1), channel_id=1, source_target_pairs={{0,1},{1,0},{2,3},{3,2},{4,5},{5,4},{6,7},{7,6},{8,9},{9,8},{10,11... | collective-permute-start | bytes 786440 | tf_op jit(solution)/shard_map/ppermute | solution.py:41
  510.5 20.9 %collective-permute-start.93 = (f32[11,1024]{1,0:T(8,128)S(1)}, f32[11,1024]{1,0:T(8,128)S(1)}, u32[]{:S(2)}, u32[]{:S(2)}) collective-permute-start(f32[11,1024]{1,0:T(8,128)S(1)} %add.468), channel_id=1, source_target_pairs={{0,2},{1,3},{2,0},{3,1},{4,6},{5,7},{6,4},{7,5},{8,10},{9,11},{10,... | collective-permute-start | bytes 135176 | tf_op jit(solution)/shard_map/ppermute | solution.py:41
  (125 other events, 1100.4 us)

commit v5 on v4

--- a/solution.py
+++ b/solution.py
@@ -14,7 +14,7 @@
 F32 = jnp.float32
 epsilon = 1e-05
 masked_score = -1e30
-VMEM_LIMIT = 56 * 1024 * 1024
+VMEM_LIMIT = 34 * 1024 * 1024
 
 
 def device_count():
@@ -1055,30 +1055,28 @@
             grad_attended1,
         )
 
-    def heads_terms(grads):
-        return [
-            (flat_normed1[: low1.shape[0]], flat(grads[0])),
-            (flat_normed1, flat(grads[1])),
-            (flat_normed1, flat(grads[2])),
-        ]
-
     caption_sum = line(lambda c, v: (wide(c) + wide(v)).astype(BF), caption_came, caption_sum)
     caption_came = hop_seq(caption_sum, 2)
     s2.near(line)
     grads_a = heads_back(0)
     s1.first(line)
     s3.second(line)
-    s4 = Scatter(line, heads_terms(grads_a))
+    grads_b = heads_back(1)
+    own1 = flat_normed1[: low1.shape[0]]
+    s4 = Scatter(
+        line,
+        [
+            (own1 if k == 0 else flat_normed1, flat(g))
+            for k, pair in enumerate(zip(grads_a, grads_b))
+            for g in pair
+        ],
+    )
     s1.far(line)
-    grads_b = heads_back(1)
-    s4.second(line)
-    s5 = Scatter(line, heads_terms(grads_b))
     s2.first(line)
     s3.near(line)
     grad_captions = line(lambda c, v: wide(c) + wide(v), caption_came, caption_sum)
     grad_captions = grad_captions.reshape(captions.shape)
-    s5.second(line)
-    s4.near(line)
+    s4.second(line)
     *grad_blocks, small_grads = line(
         lambda g, *o: self_back(
             (g, *o, *grads_b), all_tokens, self_in, grad_cross, grad_feed, grad_down_bias,
@@ -1091,54 +1089,51 @@
     small = SmallSum(small_grads)
     grad_threes = [hop_seq(v, 1) for v in grad_blocks[3]]
     grad_ones = [hop_seq(v, 1) for v in grad_blocks[1]]
-    s5.near(line)
     s3.first(line)
+    s4.near(line)
+    small.step(line)
     grad_twos = [
         hop_seq(line(lambda a, b: (wide(a) + wide(b)).astype(BF), came, own), 2)
         for came, own in zip(grad_threes, grad_blocks[2])
     ]
     s2.far(line)
     small.step(line)
+
+    def last_norm(i):
+        def run(came, one, own, token, residual):
+            grad = wide(own) + wide(one) + wide(came)
+            unit, inverse = unit_of(wide(token))
+            return residual + unit_back(unit, inverse, grad * small_full[0])
+
+        return line(
+            run, grad_twos[i], grad_ones[i], grad_blocks[0][i], tokens[i],
+            grad_first.reshape(tokens.shape)[i],
+        )
+
+    grad_tokens = [last_norm(0)]
+    s3.far(line)
     s4.first(line)
-    s3.far(line)
     small.step(line)
-    s5.first(line)
+    grad_tokens += [last_norm(i) for i in range(1, items)]
+    grad_tokens = jnp.stack(grad_tokens)
     s4.far(line)
-    small.step(line)
-    s1.close(line)
-    s5.far(line)
-
-    def last_norm(came, one, own, token, residual):
-        grad = wide(own) + wide(one) + wide(came)
-        unit, inverse = unit_of(wide(token))
-        return residual + unit_back(unit, inverse, grad * small_full[0])
-
-    grad_first = grad_first.reshape(tokens.shape)
-    grad_tokens = jnp.stack(
-        [
-            line(last_norm, grad_twos[i], grad_ones[i], grad_blocks[0][i], tokens[i], grad_first[i])
-            for i in range(items)
-        ]
-    )
-    small.step(line)
     s2.close(line)
     s3.close(line)
+    s1.close(line)
+    small_out, grad_bias = small.parts(line, 7)
     s4.close(line)
-    s5.close(line)
-    small_out, grad_bias = small.parts(line, 7)
     (grad_down,) = s1.result(line)
     (grad_up,) = s2.result(line)
     results3 = s3.result(line)
     grad_cross_query, grad_cross_memory, grad_cross_out, grad_self_out = results3
     grads_4 = s4.result(line)
-    grads_5 = s5.result(line)
     return (
         final.reshape(tokens.shape),
         grad_tokens,
         grad_captions,
         small_out[0],
         small_out[1],
-        jnp.concatenate([g for pair in zip(grads_4, grads_5) for g in pair], axis=1),
+        jnp.concatenate(grads_4, axis=1),
         grad_self_out,
         small_out[2],
         small_out[3],

time: 543 us -> 501 us (0.923)
  Pallas kernels: 269 us -> 208 us
  waiting for transfers between devices: 91.7 us -> 126 us
  starting transfers between devices: 93.1 us -> 74.6 us
  local copies, waits for them, and re-layouts: 27.5 us -> 40.2 us
  other arithmetic: 50.8 us -> 41.9 us
    ppermute x103 -> x94, waiting for transfers between devices: 91.7 us -> 126 us  [hop(): return lax.ppermute(values, AXES, pairs)]
    pallas_call x10 -> x8, Pallas kernels: 80.9 us -> 54.5 us  [wgrad(): pl.pallas_call(functools.partial(wgrad_kernel, kinds, rows, side), out_sh...]
    ppermute x103 -> x94, starting transfers between devices: 93.1 us -> 74.6 us  [hop(): return lax.ppermute(values, AXES, pairs)]
    unnamed x155 -> x167, local copies, waits for them, and re-layouts: 12 us -> 29.6 us
    pallas_call x3, Pallas kernels: 41.6 us -> 36.1 us  [attend_back(): pl.pallas_call(functools.partial(attend_back_kernel, kind), out_shape=[ja...]
  transfers between devices with their start and end apart: 103 -> 94, of which waited for: 26 -> 30; matrix products, arithmetic and copies ran while one was open for 13% -> 11% of each run, Pallas kernels for 47% -> 39%
where the time goes in v5:
time: 501 us; the launch traced here: 497 us
  Pallas kernels  208 us (42%)
  waiting for transfers between devices  126 us (25%)
  starting transfers between devices  74.6 us (15%)
  other arithmetic  41.9 us (8%)
  local copies, waits for them, and re-layouts  40.2 us (8%)
    ppermute x94, waiting for transfers between devices, hop(): return lax.ppermute(values, AXES, pairs)  126 us
    ppermute x94, starting transfers between devices, hop(): return lax.ppermute(values, AXES, pairs)  74.6 us
    pallas_call x8, Pallas kernels, wgrad(): pl.pallas_call(functools.partial(wgrad_kernel, kinds, rows, side), out_sh...  54.5 us
    pallas_call x3, Pallas kernels, attend_back(): pl.pallas_call(functools.partial(attend_back_kernel, kind), out_shape=[ja...  36.1 us
    unnamed x167, local copies, waits for them, and re-layouts  29.6 us
    pallas_call x3, Pallas kernels, attend(): pl.pallas_call(functools.partial(attend_kernel, kind), out_shape=[jax.Sha...  27 us
    pallas_call x1, Pallas kernels, self_back(): call(self_back_kernel, 'self_back', [shaped((count, d), BF)] * (blocks *...  18 us
    pallas_call x1, Pallas kernels, up_gelu(): call(up_kernel, 'up_gelu', [shaped((rows, d), F32), shaped((rows, d), BF)...  17 us
  transfers between devices with their start and end apart: 94, of which 30 were waited for; matrix products, arithmetic and copies ran while one was open for 11% of the time, Pallas kernels for 39%

profile of v5, /device:TPU:0, one launch (start us, length us, event | category | flops | bytes accessed | tf_op | source)
XLA Modules:
  0.0 497.0 jit_solution(12294925640846773425)
XLA Ops:
  5.1 2.7 collective-permute-start.4
  16.2 3.7 collective-permute-done.6
  25.6 3.5 collective-permute-done.1
  29.1 4.6 collective-permute-start.7
  34.5 4.8 collective-permute-start.21
  41.2 4.8 collective-permute-done.14.p2
  48.6 6.0 %collective-permute-done.13 = bf16[2,2,64,896]{3,2,1,0:T(8,128)(2,1)S(1)} collective-permute-done((bf16[2,2,64,896]{3,2,1,0:T(8,128)(2,1)S(1)}, bf16[2,2,64,896]{3,2,1,0:T(8,128)(2,1)S(1)}, u32[]{:S(2)}, u32[]{:S(2)}) %collective-permute-start.13) | collective-permute-done | bytes 458784 | tf_op jit(solution)/shard_map/ppermute | solution.py:41
  59.6 3.6 pad_maximum_fusion.token_ref
  63.2 7.8 %collective-permute-done.19.p6 = bf16[2,2,2,64,896]{4,3,2,1,0:T(8,128)(2,1)S(1)} collective-permute-done((bf16[2,2,2,64,896]{4,3,2,1,0:T(8,128)(2,1)S(1)}, bf16[2,2,2,64,896]{4,3,2,1,0:T(8,128)(2,1)S(1)}, u32[]{:S(2)}, u32[]{:S(2)}) %collective-permute-start.19) | collective-permute-done | bytes 917536 | tf_op jit(solution)/shard_map/ppermute | solution.py:41
  72.1 2.7 collective-permute-done.16
  78.6 15.9 %project.1 = (bf16[4,2,256,1024]{3,2,1,0:T(8,128)(2,1)S(1)}, bf16[1,2,256,1024]{3,2,1,0:T(8,128)(2,1)S(1)}, bf16[4,2,256,1024]{3,2,1,0:T(8,128)(2,1)S(1)}, bf16[...) custom-call(s32[5]{0:T(128)S(1)} %stack.294.spot_ref, ...), custom_call_target="tpu_custom_call" | custom-call | flops 1 | bytes 1 | tf_op jit(solution)/shard_map/project/pallas_call | solution.py:257
  100.2 10.6 %attend.3 = (bf16[2,256,512]{2,1,0:T(8,128)(2,1)S(1)}, f32[2,4,2,256]{3,2,1,0:T(2,128)S(1)}) custom-call(s32[1]{0:T(128)} %bitcast.42.info_ref, bf16[1,2,256,1024]{3,2,1,0:T(8,128)(2,1)S(1)} %get-tuple-element.249.q_ref, bf16[4,2,256,1024]{3,2,1,0:T(8,128)(2,1)S(1)} %get-tuple-element.242.k_ref, bf16[4,2,256,1024]{3,2,1,0:T(8,128)(2,1)S(1)} %get-tuple-element.243.v_ref), custom_call_target="tpu_custom_call" | custom-call | flops 1 | bytes 1 | tf_op jit(solution)/shard_map/attend/pallas_call | solution.py:795
  110.9 9.1 %collective-permute-done.24 = bf16[256,512]{1,0:T(8,128)(2,1)S(1)} collective-permute-done((bf16[256,512]{1,0:T(8,128)(2,1)S(1)}, bf16[256,512]{1,0:T(8,128)(2,1)S(1)}, u32[]{:S(2)}, u32[]{:S(2)}) %collective-permute-start.24) | collective-permute-done | bytes 262176 | tf_op jit(solution)/shard_map/ppermute | solution.py:41
  124.0 10.7 %attend.4 = (bf16[2,256,512]{2,1,0:T(8,128)(2,1)S(1)}, f32[2,4,2,256]{3,2,1,0:T(2,128)S(1)}) custom-call(s32[1]{0:T(128)} %bitcast.42.info_ref, bf16[1,2,256,1024]{3,2,1,0:T(8,128)(2,1)S(1)} %get-tuple-element.249.q_ref, bf16[4,2,256,1024]{3,2,1,0:T(8,128)(2,1)S(1)} %get-tuple-element.242.k_ref, bf16[4,2,256,1024]{3,2,1,0:T(8,128)(2,1)S(1)} %get-tuple-element.243.v_ref), custom_call_target="tpu_custom_call" | custom-call | flops 1 | bytes 1 | tf_op jit(solution)/shard_map/attend/pallas_call | solution.py:795
  134.7 5.2 %mix.1 = (f32[512,1024]{1,0:T(8,128)S(1)}, bf16[512,1024]{1,0:T(8,128)(2,1)S(1)}, bf16[512,1024]{1,0:T(8,128)(2,1)S(1)}, bf16[1024,1024]{1,0:T(8,128)(2,1)S(1)}, bf16[1024,1024]{1,0:T(8,128)(2,1)S(1)}) custom-call(s32[5]{0:T(128)S(1)} %stack.294.spot_ref, bf16[512,512]{1,0:T(8,128)(2,1)S(1)} %bitcast.309, bf16[512,512]{1,0:T(8,128)(2,1)S(1)} %bitcast.310, ...), custom_call_target="tpu_custom_call" | custom-call | flops 1 | bytes 1 | tf_op jit(solution)/shard_map/mix/pallas_call | solution.py:302
  141.4 6.6 %collective-permute-done.36 = bf16[2,2,64,2048]{3,2,1,0:T(8,128)(2,1)S(1)} collective-permute-done((bf16[2,2,64,2048]{3,2,1,0:T(8,128)(2,1)S(1)}, bf16[2,2,64,2048]{3,2,1,0:T(8,128)(2,1)S(1)}, u32[]{:S(2)}, u32[]{:S(2)}) %collective-permute-start.36) | collective-permute-done | bytes 1048608 | tf_op jit(solution)/shard_map/ppermute | solution.py:41
  153.5 4.5 collective-permute-done.37.p0
  158.0 3.7 memory.1
  163.8 5.8 %attend.5 = (bf16[2,256,1024]{2,1,0:T(8,128)(2,1)S(1)}, f32[2,8,2,256]{3,2,1,0:T(2,128)S(1)}) custom-call(s32[2]{0:T(128)S(1)} %copy-done.67, bf16[1,2,256,1024]{3,2,1,0:T(8,128)(2,1)S(1)} %bitcast.307, bf16[1,2,128,2048]{3,2,1,0:T(8,128)(2,1)S(1)} %bitcast.291, bf16[1,2,128,2048]{3,2,1,0:T(8,128)(2,1)S(1)} %bitcast.292), custom_call_target="tpu_custom_call" | custom-call | flops 1 | bytes 1 | tf_op jit(solution)/shard_map/attend/pallas_call | solution.py:795
  169.5 6.1 %collective-permute-done.34 = bf16[2,2,256,512]{3,2,1,0:T(8,128)(2,1)S(1)} collective-permute-done((bf16[2,2,256,512]{3,2,1,0:T(8,128)(2,1)S(1)}, bf16[2,2,256,512]{3,2,1,0:T(8,128)(2,1)S(1)}, u32[]{:S(2)}, u32[]{:S(2)}) %collective-permute-start.34) | collective-permute-done | bytes 1048608 | tf_op jit(solution)/shard_map/ppermute | solution.py:41
  186.2 17.0 %up_gelu.1 = (f32[512,1024]{1,0:T(8,128)S(1)}, bf16[512,1024]{1,0:T(8,128)(2,1)S(1)}, bf16[512,4096]{1,0:T(8,128)(2,1)}, bf16[512,4096]{1,0:T(8,128)(2,1)}, bf16[1024,4096]{1,0:T(8,128)(2,1)}) custom-call(s32[5]{0:T(128)S(1)} %stack.294.spot_ref, bf16[512,1024]{1,0:T(8,128)(2,1)S(1)} %bitcast.288, f32[512,1024]{1,0:T(8,128)S(1)} %copy-done.36, ...), custom_call_target="tpu_custom_call" | custom-call | flops 1 | bytes 1 | tf_op jit(solution)/shard_map/up_gelu/pallas_call | solution.py:379
  203.2 2.9 copy-done.9
  206.1 5.3 %wgrad.8 = (bf16[2,2,256,512]{3,2,1,0:T(8,128)(2,1)}, bf16[2,2,256,512]{3,2,1,0:T(8,128)(2,1)}, bf16[2,2,256,512]{3,2,1,0:T(8,128)(2,1)}, bf16[2,2,256,512]{3,2,1,0:T(8,128)(2,1)}) custom-call(s32[5]{0:T(128)S(1)} %stack.356.spot_ref, bf16[512,4096]{1,0:T(8,128)(2,1)S(1)} %copy-done.9, bf16[512,1024]{1,0:T(8,128)(2,1)S(1)} %bitcast.284), custom_call_target="tpu_custom_call" | custom-call | flops 1 | bytes 1 | tf_op jit(solution)/shard_map/wgrad/pallas_call | solution.py:621
  212.7 3.2 collective-permute-done.43.p0
  219.6 16.8 %down.1 = (bf16[512,1024]{1,0:T(8,128)(2,1)}, bf16[512,4096]{1,0:T(8,128)(2,1)S(1)}, f32[1,4096]{1,0:T(1,128)S(1)}, f32[1,1024]{1,0:T(1,128)S(1)}) custom-call(s32[5]{0:T(128)S(1)} %stack.294.spot_ref, bf16[512,1024]{1,0:T(8,128)(2,1)S(1)} %bitcast.285, bf16[512,4096]{1,0:T(8,128)(2,1)S(1)} %copy-done.47, ...), custom_call_target="tpu_custom_call" | custom-call | flops 1 | bytes 1 | tf_op jit(solution)/shard_map/down/pallas_call | solution.py:426
  236.6 6.1 %wgrad.9 = (bf16[2,2,2,256,512]{4,3,2,1,0:T(8,128)(2,1)S(1)}, bf16[2,2,2,256,512]{4,3,2,1,0:T(8,128)(2,1)}) custom-call(s32[5]{0:T(128)S(1)} %stack.294.spot_ref, bf16[512,4096]{1,0:T(8,128)(2,1)S(1)} %copy-done.10, bf16[512,1024]{1,0:T(8,128)(2,1)S(1)} %bitcast.286, bf16[2,2,256,512]{3,2,1,0:T(8,128)(2,1)S(1)} %collective-permute-done.45.refs_2_, ...), custom_call_target="tpu_custom_call" | custom-call | flops 1 | bytes 1 | tf_op jit(solution)/shard_map/wgrad/pallas_call | solution.py:621
  244.2 4.1 wgrad.10
  249.4 10.0 %feed_back.1 = (f32[512,1024]{1,0:T(8,128)S(1)}, bf16[512,1024]{1,0:T(8,128)(2,1)S(1)}, bf16[512,1024]{1,0:T(8,128)(2,1)S(1)}, f32[8,1024]{1,0:T(8,128)S(1)}) custom-call(bf16[512,4096]{1,0:T(8,128)(2,1)S(1)} %get-tuple-element.284.refs_1_.g_ref, bf16[1024,4096]{1,0:T(8,128)(2,1)} %get-tuple-element.285.w_ref, f32[512,1024]{1,0:T(8,128)S(1)} %copy-done.31, ...), custom_call_target="tpu_custom_call" | custom-call | flops 1 | bytes 1 | tf_op jit(solution)/shard_map/feed_back/pallas_call | solution.py:465
  259.5 6.0 %wgrad.11 = (bf16[2,2,2,64,2048]{4,3,2,1,0:T(8,128)(2,1)S(1)}, bf16[2,2,2,64,2048]{4,3,2,1,0:T(8,128)(2,1)}) custom-call(s32[5]{0:T(128)S(1)} %stack.294.spot_ref, bf16[512,1024]{1,0:T(8,128)(2,1)S(1)} %get-tuple-element.282.refs_0_, bf16[512,4096]{1,0:T(8,128)(2,1)S(1)} %get-tuple-element.284.refs_1_.g_ref, ...), custom_call_target="tpu_custom_call" | custom-call | flops 1 | bytes 1 | tf_op jit(solution)/shard_map/wgrad/pallas_call | solution.py:621
  267.4 7.8 %attend_back.3 = (bf16[2,256,1024]{2,1,0:T(8,128)(2,1)S(1)}, bf16[1,2,128,1024]{3,2,1,0:T(8,128)(2,1)S(1)}, bf16[1,2,128,1024]{3,2,1,0:T(8,128)(2,1)S(1)}) custom-call(s32[2]{0:T(128)S(1)} %copy-done.67, bf16[1,2,256,1024]{3,2,1,0:T(8,128)(2,1)S(1)} %bitcast.308, bf16[1,2,128,2048]{3,2,1,0:T(8,128)(2,1)S(1)} %bitcast.293, ...), custom_call_target="tpu_custom_call" | custom-call | flops 1 | bytes 1 | tf_op jit(solution)/shard_map/attend_back/pallas_call | solution.py:864
  277.9 3.3 cross_back.1
  281.3 4.5 convolution_convert_fusion
  287.1 5.8 %wgrad.12 = (bf16[2,2,64,2560]{3,2,1,0:T(8,128)(2,1)}, bf16[2,2,64,2560]{3,2,1,0:T(8,128)(2,1)}, bf16[2,2,64,2560]{3,2,1,0:T(8,128)(2,1)}, bf16[2,2,64,2560]{3,2,1,0:T(8,128)(2,1)}) custom-call(s32[5]{0:T(128)S(1)} %stack.356.spot_ref, bf16[512,1024]{1,0:T(8,128)(2,1)S(1)} %copy-done.40, bf16[512,1024]{1,0:T(8,128)(2,1)S(1)} %bitcast.296, ...), custom_call_target="tpu_custom_call" | custom-call | flops 1 | bytes 1 | tf_op jit(solution)/shard_map/wgrad/pallas_call | solution.py:621
  294.9 3.1 fusion.24
  298.0 14.3 %attend_back.4 = (bf16[2,256,512]{2,1,0:T(8,128)(2,1)S(1)}, bf16[4,2,256,512]{3,2,1,0:T(8,128)(2,1)S(1)}, bf16[4,2,256,512]{3,2,1,0:T(8,128)(2,1)S(1)}) custom-call(s32[1]{0:T(128)} %bitcast.42.info_ref, bf16[1,2,256,1024]{3,2,1,0:T(8,128)(2,1)S(1)} %copy-done.21, bf16[4,2,256,1024]{3,2,1,0:T(8,128)(2,1)S(1)} %copy-done.3, ...), custom_call_target="tpu_custom_call" | custom-call | flops 1 | bytes 1 | tf_op jit(solution)/shard_map/attend_back/pallas_call | solution.py:864
  319.8 7.6 %wgrad.13 = (bf16[2,2,2,64,2560]{4,3,2,1,0:T(8,128)(2,1)S(1)}, bf16[2,2,2,64,2560]{4,3,2,1,0:T(8,128)(2,1)}) custom-call(s32[5]{0:T(128)S(1)} %stack.294.spot_ref, bf16[512,1024]{1,0:T(8,128)(2,1)S(1)} %copy-done.40, bf16[512,1024]{1,0:T(8,128)(2,1)S(1)} %bitcast.297, bf16[256,1024]{1,0:T(8,128)(2,1)S(1)} %bitcast.304, ...), custom_call_target="tpu_custom_call" | custom-call | flops 1 | bytes 1 | tf_op jit(solution)/shard_map/wgrad/pallas_call | solution.py:621
  340.8 14.0 %attend_back.5 = (bf16[2,256,512]{2,1,0:T(8,128)(2,1)S(1)}, bf16[4,2,256,512]{3,2,1,0:T(8,128)(2,1)S(1)}, bf16[4,2,256,512]{3,2,1,0:T(8,128)(2,1)S(1)}) custom-call(s32[1]{0:T(128)} %bitcast.42.info_ref, bf16[1,2,256,1024]{3,2,1,0:T(8,128)(2,1)S(1)} %copy-done.22, bf16[4,2,256,1024]{3,2,1,0:T(8,128)(2,1)S(1)} %copy-done.4, ...), custom_call_target="tpu_custom_call" | custom-call | flops 1 | bytes 1 | tf_op jit(solution)/shard_map/attend_back/pallas_call | solution.py:864
  354.9 8.6 %wgrad.14 = (bf16[2,2,64,1536]{3,2,1,0:T(8,128)(2,1)S(1)}, bf16[2,2,64,1536]{3,2,1,0:T(8,128)(2,1)S(1)}, bf16[2,2,64,1536]{3,2,1,0:T(8,128)(2,1)S(1)}, bf16[2,2,64,1536]{3,2,1,0:T(8,128)(2,1)S(1)}) custom-call(s32[5]{0:T(128)S(1)} %stack.356.spot_ref, bf16[512,1024]{1,0:T(8,128)(2,1)S(1)} %bitcast.270, bf16[512,512]{1,0:T(8,128)(2,1)S(1)} %bitcast.298, ...), custom_call_target="tpu_custom_call" | custom-call | flops 1 | bytes 1 | tf_op jit(solution)/shard_map/wgrad/pallas_call | solution.py:621
  368.6 3.6 collective-permute-done.63
  372.2 2.9 fusion
  381.1 11.0 %wgrad.15 = (bf16[2,2,2,64,1536]{4,3,2,1,0:T(8,128)(2,1)S(1)}, bf16[2,2,2,64,1536]{4,3,2,1,0:T(8,128)(2,1)S(1)}) custom-call(s32[5]{0:T(128)S(1)} %stack.294.spot_ref, bf16[512,1024]{1,0:T(8,128)(2,1)S(1)} %bitcast.272, bf16[512,512]{1,0:T(8,128)(2,1)S(1)} %bitcast.299, bf16[512,1024]{1,0:T(8,128)(2,1)S(1)} %bitcast.273, bf16[512,512]{1,0:T(8,128)(2,1)S(1)} %bitcast.301, ...), custom_call_target="tpu_custom_call" | custom-call | flops 1 | bytes 1 | tf_op jit(solution)/shard_map/wgrad/pallas_call | solution.py:621
  396.1 18.0 %self_back.1 = (bf16[256,1024]{1,0:T(8,128)(2,1)S(1)}, bf16[256,1024]{1,0:T(8,128)(2,1)S(1)}, bf16[256,1024]{1,0:T(8,128)(2,1)S(1)}, bf16[256,1024]{1,0:T(8,128)...) custom-call(bf16[2,256,512]{2,1,0:T(8,128)(2,1)S(1)} %get-tuple-elem, ...), custom_call_target="tpu_custom_call" | custom-call | flops 1 | bytes 1 | tf_op jit(solution)/shard_map/self_back/pallas_call | solution.py:554
  424.4 10.8 %collective-permute-done.74 = bf16[256,1024]{1,0:T(8,128)(2,1)S(1)} collective-permute-done((bf16[256,1024]{1,0:T(8,128)(2,1)S(1)}, bf16[256,1024]{1,0:T(8,128)(2,1)S(1)}, u32[]{:S(2)}, u32[]{:S(2)}) %collective-permute-start.74) | collective-permute-done | bytes 524320 | tf_op jit(solution)/shard_map/ppermute | solution.py:41
  442.0 16.1 %collective-permute-done.81 = bf16[2,2,64,1536]{3,2,1,0:T(8,128)(2,1)S(1)} collective-permute-done((bf16[2,2,64,1536]{3,2,1,0:T(8,128)(2,1)S(1)}, bf16[2,2,64,1536]{3,2,1,0:T(8,128)(2,1)S(1)}, u32[]{:S(2)}, u32[]{:S(2)}) %collective-permute-start.81) | collective-permute-done | bytes 786464 | tf_op jit(solution)/shard_map/ppermute | solution.py:41
  458.3 8.8 %collective-permute-done.80 = f32[11,1024]{1,0:T(8,128)S(1)} collective-permute-done((f32[11,1024]{1,0:T(8,128)S(1)}, f32[11,1024]{1,0:T(8,128)S(1)}, u32[]{:S(2)}, u32[]{:S(2)}) %collective-permute-start.80) | collective-permute-done | bytes 45088 | tf_op jit(solution)/shard_map/ppermute | solution.py:41
  467.2 5.1 %collective-permute-start.87 = (bf16[2,64,1536]{2,1,0:T(8,128)(2,1)S(1)}, bf16[2,64,1536]{2,1,0:T(8,128)(2,1)S(1)}, u32[]{:S(2)}, u32[]{:S(2)}) collective-permute-start(bf16[2,64,1536]{2,1,0:T(8,128)(2,1)S(1)} %fusion.31), channel_id=1, source_target_pairs={{0,4},{1,3},{2,6},{3,1},{4,0},{5,7},{6,2},{7,5},{8,12},{9,11},{10,... | collective-permute-start | bytes 1179656 | tf_op jit(solution)/shard_map/ppermute | solution.py:41
  474.9 3.2 collective-permute-done.87
  486.8 4.3 collective-permute-done.89
  (465 shorter events, 147.7 us)
Async XLA Ops:
  2.2 26.9 %collective-permute-start.1 = (bf16[2,256,1024]{2,1,0:T(8,128)(2,1)}, bf16[2,256,1024]{2,1,0:T(8,128)(2,1)}, u32[]{:S(2)}, u32[]{:S(2)}) collective-permute-start(bf16[2,256,1024]{2,1,0:T(8,128)(2,1)} %param.19), channel_id=1, source_target_pairs={{0,2},{1,3},{2,0},{3,1},{4,6},{5,7},{6,4},{7,5},{8,10},{9,11},{10,... | collective-permute-start | bytes 3145736 | tf_op jit(solution)/shard_map/ppermute | solution.py:41
  4.8 54.5 %collective-permute-start = (bf16[2,256,1024]{2,1,0:T(8,128)(2,1)}, bf16[2,256,1024]{2,1,0:T(8,128)(2,1)}, u32[]{:S(2)}, u32[]{:S(2)}) collective-permute-start(bf16[2,256,1024]{2,1,0:T(8,128)(2,1)} %param.19), channel_id=1, source_target_pairs={{0,1},{1,0},{2,3},{3,2},{4,5},{5,4},{6,7},{7,6},{8,9},{9,8},{10,11... | collective-permute-start | bytes 3145736 | tf_op jit(solution)/shard_map/ppermute | solution.py:41
  29.1 30.1 %collective-permute-start.7 = (bf16[2,256,1024]{2,1,0:T(8,128)(2,1)}, bf16[2,256,1024]{2,1,0:T(8,128)(2,1)S(1)}, u32[]{:S(2)}, u32[]{:S(2)}) collective-permute-start(bf16[2,256,1024]{2,1,0:T(8,128)(2,1)} %collective-permute-done.1), channel_id=1, source_target_pairs={{0,1},{1,0},{2,3},{3,2},{4,5},{5,4},{6,7},{7,6},{8,9},{9,8},{10,11... | collective-permute-start | bytes 3145736 | tf_op jit(solution)/shard_map/ppermute | solution.py:41
  34.5 40.4 %collective-permute-start.21 = (bf16[2,2,2,64,768]{4,3,2,1,0:T(8,128)(2,1)S(1)}, bf16[2,2,2,64,768]{4,3,2,1,0:T(8,128)(2,1)S(1)}, u32[]{:S(2)}, u32[]{:S(2)}) collective-permute-start(bf16[2,2,2,64,768]{4,3,2,1,0:T(8,128)(2,1)S(1)} %pad_maximum_fusion.10.p1), channel_id=1, source_target_pairs={{0,1},{1,0},{2,3},{3,2},{4,5},{5,4},{6,7},{7,6},{8,9},{9,8},{10,11... | collective-permute-start | bytes 2359304 | tf_op jit(solution)/shard_map/ppermute | solution.py:41
  59.3 16.7 %collective-permute-start.23 = (bf16[2,2,2,64,896]{4,3,2,1,0:T(8,128)(2,1)S(1)}, bf16[2,2,2,64,896]{4,3,2,1,0:T(8,128)(2,1)S(1)}, u32[]{:S(2)}, u32[]{:S(2)}) collective-permute-start(bf16[2,2,2,64,896]{4,3,2,1,0:T(8,128)(2,1)S(1)} %pad_maximum_fusion.9.p5), channel_id=1, source_target_pairs={{0,1},{1,0},{2,3},{3,2},{4,5},{5,4},{6,7},{7,6},{8,9},{9,8},{10,11... | collective-permute-start | bytes 2752520 | tf_op jit(solution)/shard_map/ppermute | solution.py:41
  74.8 19.7 %collective-permute-start.15 = (bf16[128,512]{1,0:T(8,128)(2,1)S(1)}, bf16[128,512]{1,0:T(8,128)(2,1)S(1)}, u32[]{:S(2)}, u32[]{:S(2)}) collective-permute-start(bf16[128,512]{1,0:T(8,128)(2,1)S(1)} %get-tuple-element.430), channel_id=1, source_target_pairs={{0,1},{1,0},{2,3},{3,2},{4,5},{5,4},{6,7},{7,6},{8,9},{9,8},{10,11... | collective-permute-start | bytes 393224 | tf_op jit(solution)/shard_map/ppermute | solution.py:41
  75.0 21.3 %collective-permute-start.26 = (bf16[2,64,1536]{2,1,0:T(8,128)(2,1)S(1)}, bf16[2,64,1536]{2,1,0:T(8,128)(2,1)S(1)}, u32[]{:S(2)}, u32[]{:S(2)}) collective-permute-start(bf16[2,64,1536]{2,1,0:T(8,128)(2,1)S(1)} %get-tuple-element.420), channel_id=1, source_target_pairs={{0,4},{1,3},{2,6},{3,1},{4,0},{5,7},{6,2},{7,5},{8,12},{9,11},{10,... | collective-permute-start | bytes 1179656 | tf_op jit(solution)/shard_map/ppermute | solution.py:41
  75.2 19.4 %collective-permute-start.27 = (bf16[64,2048]{1,0:T(8,128)(2,1)S(1)}, bf16[64,2048]{1,0:T(8,128)(2,1)S(1)}, u32[]{:S(2)}, u32[]{:S(2)}) collective-permute-start(bf16[64,2048]{1,0:T(8,128)(2,1)S(1)} %maximum_select_fusion), channel_id=1, source_target_pairs={{0,16},{1,17},{2,18},{3,19},{4,20},{5,21},{6,22},{7,23},{8,24},{9,... | collective-permute-start | bytes 786440 | tf_op jit(solution)/shard_map/ppermute | solution.py:41
  76.0 20.7 %collective-permute-start.25 = (bf16[2,2,64,1024]{3,2,1,0:T(8,128)(2,1)S(1)}, bf16[2,2,64,1024]{3,2,1,0:T(8,128)(2,1)S(1)}, u32[]{:S(2)}, u32[]{:S(2)}) collective-permute-start(bf16[2,2,64,1024]{3,2,1,0:T(8,128)(2,1)S(1)} %get-tuple-element.416), channel_id=1, source_target_pairs={{0,8},{1,9},{2,10},{3,11},{4,12},{5,13},{6,14},{7,15},{8,0},{9,1},... | collective-permute-start | bytes 1572872 | tf_op jit(solution)/shard_map/ppermute | solution.py:41
  94.7 25.4 %collective-permute-start.31 = (bf16[2,64,2048]{2,1,0:T(8,128)(2,1)S(1)}, bf16[2,64,2048]{2,1,0:T(8,128)(2,1)S(1)}, u32[]{:S(2)}, u32[]{:S(2)}) collective-permute-start(bf16[2,64,2048]{2,1,0:T(8,128)(2,1)S(1)} %get-tuple-element.414), channel_id=1, source_target_pairs={{0,4},{1,3},{2,6},{3,1},{4,0},{5,7},{6,2},{7,5},{8,12},{9,11},{10,... | collective-permute-start | bytes 1572872 | tf_op jit(solution)/shard_map/ppermute | solution.py:41
  96.5 25.6 %collective-permute-start.30 = (bf16[2,2,64,1536]{3,2,1,0:T(8,128)(2,1)S(1)}, bf16[2,2,64,1536]{3,2,1,0:T(8,128)(2,1)S(1)}, u32[]{:S(2)}, u32[]{:S(2)}) collective-permute-start(bf16[2,2,64,1536]{3,2,1,0:T(8,128)(2,1)S(1)} %get-tuple-element.408), channel_id=1, source_target_pairs={{0,8},{1,9},{2,10},{3,11},{4,12},{5,13},{6,14},{7,15},{8,0},{9,1},... | collective-permute-start | bytes 2359304 | tf_op jit(solution)/shard_map/ppermute | solution.py:41
  96.9 25.4 %collective-permute-start.29 = (bf16[2,2,2,64,1024]{4,3,2,1,0:T(8,128)(2,1)S(1)}, bf16[2,2,2,64,1024]{4,3,2,1,0:T(8,128)(2,1)S(1)}, u32[]{:S(2)}, u32[]{:S(2)}) collective-permute-start(bf16[2,2,2,64,1024]{4,3,2,1,0:T(8,128)(2,1)S(1)} %pad_maximum_fusion.5.p1), channel_id=1, source_target_pairs={{0,2},{1,5},{2,0},{3,7},{4,6},{5,1},{6,4},{7,3},{8,10},{9,13},{10,... | collective-permute-start | bytes 3145736 | tf_op jit(solution)/shard_map/ppermute | solution.py:41
  98.2 21.7 %collective-permute-start.24 = (bf16[256,512]{1,0:T(8,128)(2,1)S(1)}, bf16[256,512]{1,0:T(8,128)(2,1)S(1)}, u32[]{:S(2)}, u32[]{:S(2)}) collective-permute-start(bf16[256,512]{1,0:T(8,128)(2,1)S(1)} %maximum_select_fusion.2), channel_id=1, source_target_pairs={{0,16},{1,17},{2,18},{3,19},{4,20},{5,21},{6,22},{7,23},{8,24},{9,... | collective-permute-start | bytes 786440 | tf_op jit(solution)/shard_map/ppermute | solution.py:41
  100.2 34.5 %collective-permute-start.33 = (bf16[2,2,2,64,1024]{4,3,2,1,0:T(8,128)(2,1)S(1)}, bf16[2,2,2,64,1024]{4,3,2,1,0:T(8,128)(2,1)S(1)}, u32[]{:S(2)}, u32[]{:S(2)}) collective-permute-start(bf16[2,2,2,64,1024]{4,3,2,1,0:T(8,128)(2,1)S(1)} %pad_maximum_fusion.5.p1), channel_id=1, source_target_pairs={{0,1},{1,0},{2,3},{3,2},{4,5},{5,4},{6,7},{7,6},{8,9},{9,8},{10,11... | collective-permute-start | bytes 3145736 | tf_op jit(solution)/shard_map/ppermute | solution.py:41
  122.4 25.6 %collective-permute-start.36 = (bf16[2,2,64,2048]{3,2,1,0:T(8,128)(2,1)S(1)}, bf16[2,2,64,2048]{3,2,1,0:T(8,128)(2,1)S(1)}, u32[]{:S(2)}, u32[]{:S(2)}) collective-permute-start(bf16[2,2,64,2048]{3,2,1,0:T(8,128)(2,1)S(1)} %get-tuple-element.400), channel_id=1, source_target_pairs={{0,8},{1,9},{2,10},{3,11},{4,12},{5,13},{6,14},{7,15},{8,0},{9,1},... | collective-permute-start | bytes 3145736 | tf_op jit(solution)/shard_map/ppermute | solution.py:41
  123.0 27.1 %collective-permute-start.35 = (bf16[2,2,2,64,1536]{4,3,2,1,0:T(8,128)(2,1)S(1)}, bf16[2,2,2,64,1536]{4,3,2,1,0:T(8,128)(2,1)S(1)}, u32[]{:S(2)}, u32[]{:S(2)}) collective-permute-start(bf16[2,2,2,64,1536]{4,3,2,1,0:T(8,128)(2,1)S(1)} %pad_maximum_fusion.4.p1), channel_id=1, source_target_pairs={{0,2},{1,5},{2,0},{3,7},{4,6},{5,1},{6,4},{7,3},{8,10},{9,13},{10,... | collective-permute-start | bytes 4718600 | tf_op jit(solution)/shard_map/ppermute | solution.py:41
  123.5 17.7 %collective-permute-start.28 = (bf16[2,256,512]{2,1,0:T(8,128)(2,1)S(1)}, bf16[2,256,512]{2,1,0:T(8,128)(2,1)S(1)}, u32[]{:S(2)}, u32[]{:S(2)}) collective-permute-start(bf16[2,256,512]{2,1,0:T(8,128)(2,1)S(1)} %get-tuple-element.412), channel_id=1, source_target_pairs={{0,4},{1,3},{2,6},{3,1},{4,0},{5,7},{6,2},{7,5},{8,12},{9,11},{10,... | collective-permute-start | bytes 1572872 | tf_op jit(solution)/shard_map/ppermute | solution.py:41
  149.5 27.7 %collective-permute-start.40 = (bf16[2,2,2,64,2048]{4,3,2,1,0:T(8,128)(2,1)}, bf16[2,2,2,64,2048]{4,3,2,1,0:T(8,128)(2,1)}, u32[]{:S(2)}, u32[]{:S(2)}) collective-permute-start(bf16[2,2,2,64,2048]{4,3,2,1,0:T(8,128)(2,1)} %pad_maximum_fusion.1.p1), channel_id=1, source_target_pairs={{0,2},{1,5},{2,0},{3,7},{4,6},{5,1},{6,4},{7,3},{8,10},{9,13},{10,... | collective-permute-start | bytes 6291464 | tf_op jit(solution)/shard_map/ppermute | solution.py:41
  150.6 25.1 %collective-permute-start.34 = (bf16[2,2,256,512]{3,2,1,0:T(8,128)(2,1)S(1)}, bf16[2,2,256,512]{3,2,1,0:T(8,128)(2,1)S(1)}, u32[]{:S(2)}, u32[]{:S(2)}) collective-permute-start(bf16[2,2,256,512]{3,2,1,0:T(8,128)(2,1)S(1)} %get-tuple-element.398), channel_id=1, source_target_pairs={{0,8},{1,9},{2,10},{3,11},{4,12},{5,13},{6,14},{7,15},{8,0},{9,1},... | collective-permute-start | bytes 3145736 | tf_op jit(solution)/shard_map/ppermute | solution.py:41
  151.2 28.0 %collective-permute-start.42 = (bf16[2,2,2,64,2048]{4,3,2,1,0:T(8,128)(2,1)}, bf16[2,2,2,64,2048]{4,3,2,1,0:T(8,128)(2,1)}, u32[]{:S(2)}, u32[]{:S(2)}) collective-permute-start(bf16[2,2,2,64,2048]{4,3,2,1,0:T(8,128)(2,1)} %pad_maximum_fusion.1.p1), channel_id=1, source_target_pairs={{0,1},{1,0},{2,3},{3,2},{4,5},{5,4},{6,7},{7,6},{8,9},{9,8},{10,11... | collective-permute-start | bytes 6291464 | tf_op jit(solution)/shard_map/ppermute | solution.py:41
  177.3 34.2 %collective-permute-start.39 = (bf16[2,2,2,256,512]{4,3,2,1,0:T(8,128)(2,1)}, bf16[2,2,2,256,512]{4,3,2,1,0:T(8,128)(2,1)}, u32[]{:S(2)}, u32[]{:S(2)}) collective-permute-start(bf16[2,2,2,256,512]{4,3,2,1,0:T(8,128)(2,1)} %pad_maximum_fusion.2.p1), channel_id=1, source_target_pairs={{0,2},{1,5},{2,0},{3,7},{4,6},{5,1},{6,4},{7,3},{8,10},{9,13},{10,... | collective-permute-start | bytes 6291464 | tf_op jit(solution)/shard_map/ppermute | solution.py:41
  178.9 33.7 %collective-permute-start.44 = (bf16[2,2,2,256,512]{4,3,2,1,0:T(8,128)(2,1)}, bf16[2,2,2,256,512]{4,3,2,1,0:T(8,128)(2,1)}, u32[]{:S(2)}, u32[]{:S(2)}) collective-permute-start(bf16[2,2,2,256,512]{4,3,2,1,0:T(8,128)(2,1)} %pad_maximum_fusion.2.p1), channel_id=1, source_target_pairs={{0,1},{1,0},{2,3},{3,2},{4,5},{5,4},{6,7},{7,6},{8,9},{9,8},{10,11... | collective-permute-start | bytes 6291464 | tf_op jit(solution)/shard_map/ppermute | solution.py:41
  211.6 24.9 %collective-permute-start.45 = (bf16[2,2,256,512]{3,2,1,0:T(8,128)(2,1)}, bf16[2,2,256,512]{3,2,1,0:T(8,128)(2,1)S(1)}, u32[]{:S(2)}, u32[]{:S(2)}) collective-permute-start(bf16[2,2,256,512]{3,2,1,0:T(8,128)(2,1)} %get-tuple-element.269), channel_id=1, source_target_pairs={{0,1},{1,0},{2,3},{3,2},{4,5},{5,4},{6,7},{7,6},{8,9},{9,8},{10,11... | collective-permute-start | bytes 3145736 | tf_op jit(solution)/shard_map/ppermute | solution.py:41
  212.0 24.5 %collective-permute-start.46 = (bf16[2,2,256,512]{3,2,1,0:T(8,128)(2,1)}, bf16[2,2,256,512]{3,2,1,0:T(8,128)(2,1)S(1)}, u32[]{:S(2)}, u32[]{:S(2)}) collective-permute-start(bf16[2,2,256,512]{3,2,1,0:T(8,128)(2,1)} %get-tuple-element.278), channel_id=1, source_target_pairs={{0,1},{1,0},{2,3},{3,2},{4,5},{5,4},{6,7},{7,6},{8,9},{9,8},{10,11... | collective-permute-start | bytes 3145736 | tf_op jit(solution)/shard_map/ppermute | solution.py:41
  212.1 24.4 %collective-permute-start.47 = (bf16[2,2,256,512]{3,2,1,0:T(8,128)(2,1)}, bf16[2,2,256,512]{3,2,1,0:T(8,128)(2,1)S(1)}, u32[]{:S(2)}, u32[]{:S(2)}) collective-permute-start(bf16[2,2,256,512]{3,2,1,0:T(8,128)(2,1)} %get-tuple-element.279), channel_id=1, source_target_pairs={{0,1},{1,0},{2,3},{3,2},{4,5},{5,4},{6,7},{7,6},{8,9},{9,8},{10,11... | collective-permute-start | bytes 3145736 | tf_op jit(solution)/shard_map/ppermute | solution.py:41
  212.5 24.0 %collective-permute-start.48 = (bf16[2,2,256,512]{3,2,1,0:T(8,128)(2,1)}, bf16[2,2,256,512]{3,2,1,0:T(8,128)(2,1)S(1)}, u32[]{:S(2)}, u32[]{:S(2)}) collective-permute-start(bf16[2,2,256,512]{3,2,1,0:T(8,128)(2,1)} %get-tuple-element.280), channel_id=1, source_target_pairs={{0,1},{1,0},{2,3},{3,2},{4,5},{5,4},{6,7},{7,6},{8,9},{9,8},{10,11... | collective-permute-start | bytes 3145736 | tf_op jit(solution)/shard_map/ppermute | solution.py:41
  242.6 32.6 %collective-permute-start.53 = (bf16[2,2,2,256,512]{4,3,2,1,0:T(8,128)(2,1)}, bf16[2,2,2,256,512]{4,3,2,1,0:T(8,128)(2,1)}, u32[]{:S(2)}, u32[]{:S(2)}) collective-permute-start(bf16[2,2,2,256,512]{4,3,2,1,0:T(8,128)(2,1)} %get-tuple-element.295), channel_id=1, source_target_pairs={{0,2},{1,5},{2,0},{3,7},{4,6},{5,1},{6,4},{7,3},{8,10},{9,13},{10,... | collective-permute-start | bytes 6291464 | tf_op jit(solution)/shard_map/ppermute | solution.py:41
  266.9 26.5 %collective-permute-start.54 = (bf16[2,2,2,64,2048]{4,3,2,1,0:T(8,128)(2,1)}, bf16[2,2,2,64,2048]{4,3,2,1,0:T(8,128)(2,1)}, u32[]{:S(2)}, u32[]{:S(2)}) collective-permute-start(bf16[2,2,2,64,2048]{4,3,2,1,0:T(8,128)(2,1)} %get-tuple-element.304), channel_id=1, source_target_pairs={{0,2},{1,5},{2,0},{3,7},{4,6},{5,1},{6,4},{7,3},{8,10},{9,13},{10,... | collective-permute-start | bytes 6291464 | tf_op jit(solution)/shard_map/ppermute | solution.py:41
  286.0 29.0 %collective-permute-start.57 = (bf16[2,2,256,512]{3,2,1,0:T(8,128)(2,1)}, bf16[2,2,256,512]{3,2,1,0:T(8,128)(2,1)}, u32[]{:S(2)}, u32[]{:S(2)}) collective-permute-start(bf16[2,2,256,512]{3,2,1,0:T(8,128)(2,1)} %fusion.23), channel_id=1, source_target_pairs={{0,8},{1,9},{2,10},{3,11},{4,12},{5,13},{6,14},{7,15},{8,0},{9,1},... | collective-permute-start | bytes 3145736 | tf_op jit(solution)/shard_map/ppermute | solution.py:41
  292.9 24.6 %collective-permute-start.56 = (bf16[2,2,64,2560]{3,2,1,0:T(8,128)(2,1)}, bf16[2,2,64,2560]{3,2,1,0:T(8,128)(2,1)S(1)}, u32[]{:S(2)}, u32[]{:S(2)}) collective-permute-start(bf16[2,2,64,2560]{3,2,1,0:T(8,128)(2,1)} %get-tuple-element.314), channel_id=1, source_target_pairs={{0,1},{1,0},{2,3},{3,2},{4,5},{5,4},{6,7},{7,6},{8,9},{9,8},{10,11... | collective-permute-start | bytes 3932168 | tf_op jit(solution)/shard_map/ppermute | solution.py:41
  292.9 24.6 %collective-permute-start.58 = (bf16[2,2,64,2560]{3,2,1,0:T(8,128)(2,1)}, bf16[2,2,64,2560]{3,2,1,0:T(8,128)(2,1)S(1)}, u32[]{:S(2)}, u32[]{:S(2)}) collective-permute-start(bf16[2,2,64,2560]{3,2,1,0:T(8,128)(2,1)} %get-tuple-element.321), channel_id=1, source_target_pairs={{0,1},{1,0},{2,3},{3,2},{4,5},{5,4},{6,7},{7,6},{8,9},{9,8},{10,11... | collective-permute-start | bytes 3932168 | tf_op jit(solution)/shard_map/ppermute | solution.py:41
  293.4 25.1 %collective-permute-start.59 = (bf16[2,2,64,2560]{3,2,1,0:T(8,128)(2,1)}, bf16[2,2,64,2560]{3,2,1,0:T(8,128)(2,1)}, u32[]{:S(2)}, u32[]{:S(2)}) collective-permute-start(bf16[2,2,64,2560]{3,2,1,0:T(8,128)(2,1)} %get-tuple-element.322), channel_id=1, source_target_pairs={{0,1},{1,0},{2,3},{3,2},{4,5},{5,4},{6,7},{7,6},{8,9},{9,8},{10,11... | collective-permute-start | bytes 3932168 | tf_op jit(solution)/shard_map/ppermute | solution.py:41
  293.4 25.1 %collective-permute-start.60 = (bf16[2,2,64,2560]{3,2,1,0:T(8,128)(2,1)}, bf16[2,2,64,2560]{3,2,1,0:T(8,128)(2,1)}, u32[]{:S(2)}, u32[]{:S(2)}) collective-permute-start(bf16[2,2,64,2560]{3,2,1,0:T(8,128)(2,1)} %get-tuple-element.323), channel_id=1, source_target_pairs={{0,1},{1,0},{2,3},{3,2},{4,5},{5,4},{6,7},{7,6},{8,9},{9,8},{10,11... | collective-permute-start | bytes 3932168 | tf_op jit(solution)/shard_map/ppermute | solution.py:41
  329.0 43.2 %collective-permute-start.63 = (bf16[2,2,2,64,2560]{4,3,2,1,0:T(8,128)(2,1)}, bf16[2,2,2,64,2560]{4,3,2,1,0:T(8,128)(2,1)}, u32[]{:S(2)}, u32[]{:S(2)}) collective-permute-start(bf16[2,2,2,64,2560]{4,3,2,1,0:T(8,128)(2,1)} %get-tuple-element.333), channel_id=1, source_target_pairs={{0,2},{1,5},{2,0},{3,7},{4,6},{5,1},{6,4},{7,3},{8,10},{9,13},{10,... | collective-permute-start | bytes 7864328 | tf_op jit(solution)/shard_map/ppermute | solution.py:41
  330.5 35.6 %collective-permute-start.64 = (bf16[2,2,64,2048]{3,2,1,0:T(8,128)(2,1)}, bf16[2,2,64,2048]{3,2,1,0:T(8,128)(2,1)}, u32[]{:S(2)}, u32[]{:S(2)}) collective-permute-start(bf16[2,2,64,2048]{3,2,1,0:T(8,128)(2,1)} %fusion.24), channel_id=1, source_target_pairs={{0,8},{1,9},{2,10},{3,11},{4,12},{5,13},{6,14},{7,15},{8,0},{9,1},... | collective-permute-start | bytes 3145736 | tf_op jit(solution)/shard_map/ppermute | solution.py:41
  331.7 31.9 %collective-permute-start.65 = (bf16[2,256,512]{2,1,0:T(8,128)(2,1)}, bf16[2,256,512]{2,1,0:T(8,128)(2,1)}, u32[]{:S(2)}, u32[]{:S(2)}) collective-permute-start(bf16[2,256,512]{2,1,0:T(8,128)(2,1)} %fusion.28), channel_id=1, source_target_pairs={{0,4},{1,3},{2,6},{3,1},{4,0},{5,7},{6,2},{7,5},{8,12},{9,11},{10,... | collective-permute-start | bytes 1572872 | tf_op jit(solution)/shard_map/ppermute | solution.py:41
  333.8 44.0 %collective-permute-start.62 = (bf16[256,1024]{1,0:T(8,128)(2,1)}, bf16[256,1024]{1,0:T(8,128)(2,1)S(1)}, u32[]{:S(2)}, u32[]{:S(2)}) collective-permute-start(bf16[256,1024]{1,0:T(8,128)(2,1)} %add_convert_fusion.6), channel_id=1, source_target_pairs={{0,2},{1,3},{2,0},{3,1},{4,6},{5,7},{6,4},{7,5},{8,10},{9,11},{10,... | collective-permute-start | bytes 1572872 | tf_op jit(solution)/shard_map/ppermute | solution.py:41
  363.5 17.6 %collective-permute-start.61 = (bf16[2,2,64,1536]{3,2,1,0:T(8,128)(2,1)S(1)}, bf16[2,2,64,1536]{3,2,1,0:T(8,128)(2,1)S(1)}, u32[]{:S(2)}, u32[]{:S(2)}) collective-permute-start(bf16[2,2,64,1536]{3,2,1,0:T(8,128)(2,1)S(1)} %get-tuple-element.332), channel_id=1, source_target_pairs={{0,1},{1,0},{2,3},{3,2},{4,5},{5,4},{6,7},{7,6},{8,9},{9,8},{10,11... | collective-permute-start | bytes 2359304 | tf_op jit(solution)/shard_map/ppermute | solution.py:41
  363.6 17.5 %collective-permute-start.66 = (bf16[2,2,64,1536]{3,2,1,0:T(8,128)(2,1)S(1)}, bf16[2,2,64,1536]{3,2,1,0:T(8,128)(2,1)S(1)}, u32[]{:S(2)}, u32[]{:S(2)}) collective-permute-start(bf16[2,2,64,1536]{3,2,1,0:T(8,128)(2,1)S(1)} %get-tuple-element.339), channel_id=1, source_target_pairs={{0,1},{1,0},{2,3},{3,2},{4,5},{5,4},{6,7},{7,6},{8,9},{9,8},{10,11... | collective-permute-start | bytes 2359304 | tf_op jit(solution)/shard_map/ppermute | solution.py:41
  377.7 36.4 %collective-permute-start.73 = (bf16[2,2,64,2560]{3,2,1,0:T(8,128)(2,1)}, bf16[2,2,64,2560]{3,2,1,0:T(8,128)(2,1)}, u32[]{:S(2)}, u32[]{:S(2)}) collective-permute-start(bf16[2,2,64,2560]{3,2,1,0:T(8,128)(2,1)} %fusion), channel_id=1, source_target_pairs={{0,8},{1,9},{2,10},{3,11},{4,12},{5,13},{6,14},{7,15},{8,0},{9,1},... | collective-permute-start | bytes 3932168 | tf_op jit(solution)/shard_map/ppermute | solution.py:41
  392.1 25.4 %collective-permute-start.72 = (bf16[2,2,2,64,1536]{4,3,2,1,0:T(8,128)(2,1)S(1)}, bf16[2,2,2,64,1536]{4,3,2,1,0:T(8,128)(2,1)S(1)}, u32[]{:S(2)}, u32[]{:S(2)}) collective-permute-start(bf16[2,2,2,64,1536]{4,3,2,1,0:T(8,128)(2,1)S(1)} %get-tuple-element.353), channel_id=1, source_target_pairs={{0,2},{1,5},{2,0},{3,7},{4,6},{5,1},{6,4},{7,3},{8,10},{9,13},{10,... | collective-permute-start | bytes 4718600 | tf_op jit(solution)/shard_map/ppermute | solution.py:41
  393.9 87.1 %collective-permute-start.84 = (bf16[256,512]{1,0:T(8,128)(2,1)S(1)}, bf16[256,512]{1,0:T(8,128)(2,1)S(1)}, u32[]{:S(2)}, u32[]{:S(2)}) collective-permute-start(bf16[256,512]{1,0:T(8,128)(2,1)S(1)} %slice_bitcast_fusion.10), channel_id=1, source_target_pairs={{0,16},{1,17},{2,18},{3,19},{4,20},{5,21},{6,22},{7,23},{8,24},{9,... | collective-permute-start | bytes 786440 | tf_op jit(solution)/shard_map/ppermute | solution.py:41
  395.5 24.9 %collective-permute-start.76 = (bf16[2,64,2048]{2,1,0:T(8,128)(2,1)}, bf16[2,64,2048]{2,1,0:T(8,128)(2,1)S(1)}, u32[]{:S(2)}, u32[]{:S(2)}) collective-permute-start(bf16[2,64,2048]{2,1,0:T(8,128)(2,1)} %fusion.26), channel_id=1, source_target_pairs={{0,4},{1,3},{2,6},{3,1},{4,0},{5,7},{6,2},{7,5},{8,12},{9,11},{10,... | collective-permute-start | bytes 1572872 | tf_op jit(solution)/shard_map/ppermute | solution.py:41
  417.7 18.4 %collective-permute-start.69 = (bf16[256,1024]{1,0:T(8,128)(2,1)S(1)}, bf16[256,1024]{1,0:T(8,128)(2,1)S(1)}, u32[]{:S(2)}, u32[]{:S(2)}) collective-permute-start(bf16[256,1024]{1,0:T(8,128)(2,1)S(1)} %get-tuple-element.350), channel_id=1, source_target_pairs={{0,1},{1,0},{2,3},{3,2},{4,5},{5,4},{6,7},{7,6},{8,9},{9,8},{10,11... | collective-permute-start | bytes 1572872 | tf_op jit(solution)/shard_map/ppermute | solution.py:41
  418.3 54.0 %collective-permute-start.78 = (bf16[256,1024]{1,0:T(8,128)(2,1)S(1)}, bf16[256,1024]{1,0:T(8,128)(2,1)S(1)}, u32[]{:S(2)}, u32[]{:S(2)}) collective-permute-start(bf16[256,1024]{1,0:T(8,128)(2,1)S(1)} %get-tuple-element.366), channel_id=1, source_target_pairs={{0,1},{1,0},{2,3},{3,2},{4,5},{5,4},{6,7},{7,6},{8,9},{9,8},{10,11... | collective-permute-start | bytes 1572872 | tf_op jit(solution)/shard_map/ppermute | solution.py:41
  435.2 22.9 %collective-permute-start.81 = (bf16[2,2,64,1536]{3,2,1,0:T(8,128)(2,1)S(1)}, bf16[2,2,64,1536]{3,2,1,0:T(8,128)(2,1)S(1)}, u32[]{:S(2)}, u32[]{:S(2)}) collective-permute-start(bf16[2,2,64,1536]{3,2,1,0:T(8,128)(2,1)S(1)} %fusion.29), channel_id=1, source_target_pairs={{0,8},{1,9},{2,10},{3,11},{4,12},{5,13},{6,14},{7,15},{8,0},{9,1},... | collective-permute-start | bytes 2359304 | tf_op jit(solution)/shard_map/ppermute | solution.py:41
  436.1 31.1 %collective-permute-start.79 = (bf16[256,1024]{1,0:T(8,128)(2,1)S(1)}, bf16[256,1024]{1,0:T(8,128)(2,1)S(1)}, u32[]{:S(2)}, u32[]{:S(2)}) collective-permute-start(bf16[256,1024]{1,0:T(8,128)(2,1)S(1)} %add_convert_fusion.4), channel_id=1, source_target_pairs={{0,2},{1,3},{2,0},{3,1},{4,6},{5,7},{6,4},{7,5},{8,10},{9,11},{10,... | collective-permute-start | bytes 1572872 | tf_op jit(solution)/shard_map/ppermute | solution.py:41
  438.9 39.4 %collective-permute-start.86 = (bf16[64,2048]{1,0:T(8,128)(2,1)S(1)}, bf16[64,2048]{1,0:T(8,128)(2,1)S(1)}, u32[]{:S(2)}, u32[]{:S(2)}) collective-permute-start(bf16[64,2048]{1,0:T(8,128)(2,1)S(1)} %slice_bitcast_fusion.9), channel_id=1, source_target_pairs={{0,16},{1,17},{2,18},{3,19},{4,20},{5,21},{6,22},{7,23},{8,24},{9,... | collective-permute-start | bytes 786440 | tf_op jit(solution)/shard_map/ppermute | solution.py:41
  (122 other events, 1137.6 us)

commit v6 on v5

--- a/solution.py
+++ b/solution.py
@@ -181,7 +181,7 @@
         in_specs=in_specs,
         out_specs=out_specs,
         scratch_shapes=scratch,
-        compiler_params=pltpu.CompilerParams(vmem_limit_bytes=VMEM_LIMIT),
+        compiler_params=pltpu.CompilerParams(vmem_limit_bytes=VMEM_LIMIT - 6 * 1024 * 1024),
         cost_estimate=SHORT,
         name=name,
     )
@@ -806,7 +806,7 @@
                 pl.BlockSpec((1, count, lanes), lambda i, p, s: (i, 0, p)),
                 pl.BlockSpec((1, group, 2, count), lambda i, p, s: (i, p, 0, 0)),
             ]),
-        compiler_params=pltpu.CompilerParams(vmem_limit_bytes=VMEM_LIMIT),
+        compiler_params=pltpu.CompilerParams(vmem_limit_bytes=VMEM_LIMIT - 12 * 1024 * 1024),
         cost_estimate=SHORT,
         name="attend",
     )(info, queries, keyed, valued)
@@ -875,7 +875,7 @@
                 row,
             ],
             out_specs=[out, key, key]),
-        compiler_params=pltpu.CompilerParams(vmem_limit_bytes=VMEM_LIMIT),
+        compiler_params=pltpu.CompilerParams(vmem_limit_bytes=VMEM_LIMIT - 12 * 1024 * 1024),
         cost_estimate=SHORT,
         name="attend_back",
     )(info, queries, keyed, valued, attended, lse, grad)

time: 501 us -> 491 us (0.980)
  Pallas kernels: 208 us -> 200 us
  waiting for transfers between devices: 126 us -> 119 us
    ppermute x94, waiting for transfers between devices: 126 us -> 119 us  [hop(): return lax.ppermute(values, AXES, pairs)]
    unnamed x167 -> x173, local copies, waits for them, and re-layouts: 29.6 us -> 33.4 us
  transfers between devices with their start and end apart: 94 -> 94, of which waited for: 30 -> 29; matrix products, arithmetic and copies ran while one was open for 11% -> 10% of each run, Pallas kernels for 39% -> 38%
where the time goes in v6:
time: 491 us; the launch traced here: 485 us
  Pallas kernels  200 us (41%)
  waiting for transfers between devices  119 us (24%)
  starting transfers between devices  78.7 us (16%)
  local copies, waits for them, and re-layouts  44.7 us (9%)
  other arithmetic  38.9 us (8%)
    ppermute x94, waiting for transfers between devices, hop(): return lax.ppermute(values, AXES, pairs)  119 us
    ppermute x94, starting transfers between devices, hop(): return lax.ppermute(values, AXES, pairs)  78.7 us
    pallas_call x8, Pallas kernels, wgrad(): pl.pallas_call(functools.partial(wgrad_kernel, kinds, rows, side), out_sh...  53.9 us
    pallas_call x3, Pallas kernels, attend_back(): pl.pallas_call(functools.partial(attend_back_kernel, kind), out_shape=[ja...  36.1 us
    unnamed x173, local copies, waits for them, and re-layouts  33.4 us
    pallas_call x3, Pallas kernels, attend(): pl.pallas_call(functools.partial(attend_kernel, kind), out_shape=[jax.Sha...  27 us
    pallas_call x1, Pallas kernels, down_both(): call(down_kernel, 'down', [shaped((rows, d), BF), shaped((rows, hidden),...  16.4 us
    pallas_call x1, Pallas kernels, self_back(): call(self_back_kernel, 'self_back', [shaped((count, d), BF)] * (blocks *...  15.3 us
  transfers between devices with their start and end apart: 94, of which 29 were waited for; matrix products, arithmetic and copies ran while one was open for 10% of the time, Pallas kernels for 38%

profile of v6, /device:TPU:0, one launch (start us, length us, event | category | flops | bytes accessed | tf_op | source)
XLA Modules:
  0.0 485.5 jit_solution(14416123311851215432)
XLA Ops:
  5.1 2.7 collective-permute-start.4
  16.2 3.7 collective-permute-done.6
  25.6 3.4 collective-permute-done.1
  29.0 4.7 collective-permute-start.7
  34.5 4.8 collective-permute-start.21
  41.2 4.8 collective-permute-done.14.p2
  48.6 6.0 %collective-permute-done.13 = bf16[2,2,64,896]{3,2,1,0:T(8,128)(2,1)S(1)} collective-permute-done((bf16[2,2,64,896]{3,2,1,0:T(8,128)(2,1)S(1)}, bf16[2,2,64,896]{3,2,1,0:T(8,128)(2,1)S(1)}, u32[]{:S(2)}, u32[]{:S(2)}) %collective-permute-start.13) | collective-permute-done | bytes 458784 | tf_op jit(solution)/shard_map/ppermute | solution.py:41
  61.4 9.6 %collective-permute-done.19.p6 = bf16[2,2,2,64,896]{4,3,2,1,0:T(8,128)(2,1)S(1)} collective-permute-done((bf16[2,2,2,64,896]{4,3,2,1,0:T(8,128)(2,1)S(1)}, bf16[2,2,2,64,896]{4,3,2,1,0:T(8,128)(2,1)S(1)}, u32[]{:S(2)}, u32[]{:S(2)}) %collective-permute-start.19) | collective-permute-done | bytes 917536 | tf_op jit(solution)/shard_map/ppermute | solution.py:41
  72.1 2.7 collective-permute-done.16
  78.6 15.2 %project.1 = (bf16[4,2,256,1024]{3,2,1,0:T(8,128)(2,1)S(1)}, bf16[1,2,256,1024]{3,2,1,0:T(8,128)(2,1)S(1)}, bf16[4,2,256,1024]{3,2,1,0:T(8,128)(2,1)S(1)}, bf16[...) custom-call(s32[5]{0:T(128)S(1)} %stack.294.spot_ref, ...), custom_call_target="tpu_custom_call" | custom-call | flops 1 | bytes 1 | tf_op jit(solution)/shard_map/project/pallas_call | solution.py:257
  99.4 10.6 %attend.3 = (bf16[2,256,512]{2,1,0:T(8,128)(2,1)S(1)}, f32[2,4,2,256]{3,2,1,0:T(2,128)S(1)}) custom-call(s32[1]{0:T(128)} %bitcast.42.info_ref, bf16[1,2,256,1024]{3,2,1,0:T(8,128)(2,1)S(1)} %get-tuple-element.249.q_ref, bf16[4,2,256,1024]{3,2,1,0:T(8,128)(2,1)S(1)} %get-tuple-element.242.k_ref, bf16[4,2,256,1024]{3,2,1,0:T(8,128)(2,1)S(1)} %get-tuple-element.243.v_ref), custom_call_target="tpu_custom_call" | custom-call | flops 1 | bytes 1 | tf_op jit(solution)/shard_map/attend/pallas_call | solution.py:795
  110.1 9.2 %collective-permute-done.24 = bf16[256,512]{1,0:T(8,128)(2,1)S(1)} collective-permute-done((bf16[256,512]{1,0:T(8,128)(2,1)S(1)}, bf16[256,512]{1,0:T(8,128)(2,1)S(1)}, u32[]{:S(2)}, u32[]{:S(2)}) %collective-permute-start.24) | collective-permute-done | bytes 262176 | tf_op jit(solution)/shard_map/ppermute | solution.py:41
  123.3 10.6 %attend.4 = (bf16[2,256,512]{2,1,0:T(8,128)(2,1)S(1)}, f32[2,4,2,256]{3,2,1,0:T(2,128)S(1)}) custom-call(s32[1]{0:T(128)} %bitcast.42.info_ref, bf16[1,2,256,1024]{3,2,1,0:T(8,128)(2,1)S(1)} %get-tuple-element.249.q_ref, bf16[4,2,256,1024]{3,2,1,0:T(8,128)(2,1)S(1)} %get-tuple-element.242.k_ref, bf16[4,2,256,1024]{3,2,1,0:T(8,128)(2,1)S(1)} %get-tuple-element.243.v_ref), custom_call_target="tpu_custom_call" | custom-call | flops 1 | bytes 1 | tf_op jit(solution)/shard_map/attend/pallas_call | solution.py:795
  134.0 5.2 %mix.1 = (f32[512,1024]{1,0:T(8,128)S(1)}, bf16[512,1024]{1,0:T(8,128)(2,1)S(1)}, bf16[512,1024]{1,0:T(8,128)(2,1)S(1)}, bf16[1024,1024]{1,0:T(8,128)(2,1)S(1)}, bf16[1024,1024]{1,0:T(8,128)(2,1)S(1)}) custom-call(s32[5]{0:T(128)S(1)} %stack.294.spot_ref, bf16[512,512]{1,0:T(8,128)(2,1)S(1)} %bitcast.309, bf16[512,512]{1,0:T(8,128)(2,1)S(1)} %bitcast.310, ...), custom_call_target="tpu_custom_call" | custom-call | flops 1 | bytes 1 | tf_op jit(solution)/shard_map/mix/pallas_call | solution.py:302
  140.6 6.6 %collective-permute-done.36 = bf16[2,2,64,2048]{3,2,1,0:T(8,128)(2,1)S(1)} collective-permute-done((bf16[2,2,64,2048]{3,2,1,0:T(8,128)(2,1)S(1)}, bf16[2,2,64,2048]{3,2,1,0:T(8,128)(2,1)S(1)}, u32[]{:S(2)}, u32[]{:S(2)}) %collective-permute-start.36) | collective-permute-done | bytes 1048608 | tf_op jit(solution)/shard_map/ppermute | solution.py:41
  152.8 4.5 collective-permute-done.37.p0
  157.3 3.7 memory.1
  163.1 5.8 %attend.5 = (bf16[2,256,1024]{2,1,0:T(8,128)(2,1)S(1)}, f32[2,8,2,256]{3,2,1,0:T(2,128)S(1)}) custom-call(s32[2]{0:T(128)S(1)} %copy-done.63, bf16[1,2,256,1024]{3,2,1,0:T(8,128)(2,1)S(1)} %bitcast.307, bf16[1,2,128,2048]{3,2,1,0:T(8,128)(2,1)S(1)} %bitcast.291, bf16[1,2,128,2048]{3,2,1,0:T(8,128)(2,1)S(1)} %bitcast.292), custom_call_target="tpu_custom_call" | custom-call | flops 1 | bytes 1 | tf_op jit(solution)/shard_map/attend/pallas_call | solution.py:795
  168.8 6.1 %collective-permute-done.34 = bf16[2,2,256,512]{3,2,1,0:T(8,128)(2,1)S(1)} collective-permute-done((bf16[2,2,256,512]{3,2,1,0:T(8,128)(2,1)S(1)}, bf16[2,2,256,512]{3,2,1,0:T(8,128)(2,1)S(1)}, u32[]{:S(2)}, u32[]{:S(2)}) %collective-permute-start.34) | collective-permute-done | bytes 1048608 | tf_op jit(solution)/shard_map/ppermute | solution.py:41
  185.5 15.0 %up_gelu.1 = (f32[512,1024]{1,0:T(8,128)S(1)}, bf16[512,1024]{1,0:T(8,128)(2,1)S(1)}, bf16[512,4096]{1,0:T(8,128)(2,1)S(1)}, bf16[512,4096]{1,0:T(8,128)(2,1)S(1)}, bf16[1024,4096]{1,0:T(8,128)(2,1)}) custom-call(s32[5]{0:T(128)S(1)} %stack.294.spot_ref, bf16[512,1024]{1,0:T(8,128)(2,1)S(1)} %bitcast.288, f32[512,1024]{1,0:T(8,128)S(1)} %copy-done.29, ...), custom_call_target="tpu_custom_call" | custom-call | flops 1 | bytes 1 | tf_op jit(solution)/shard_map/up_gelu/pallas_call | solution.py:379
  202.5 5.1 %wgrad.8 = (bf16[2,2,256,512]{3,2,1,0:T(8,128)(2,1)}, bf16[2,2,256,512]{3,2,1,0:T(8,128)(2,1)S(1)}, bf16[2,2,256,512]{3,2,1,0:T(8,128)(2,1)S(1)}, bf16[2,2,256,512]{3,2,1,0:T(8,128)(2,1)}) custom-call(s32[5]{0:T(128)S(1)} %stack.356.spot_ref, bf16[512,4096]{1,0:T(8,128)(2,1)S(1)} %get-tuple-element.268.refs_0_.act_ref, bf16[512,1024]{1,0:T(8,128)(2,1)S(1)} %bitcast.284), custom_call_target="tpu_custom_call" | custom-call | flops 1 | bytes 1 | tf_op jit(solution)/shard_map/wgrad/pallas_call | solution.py:621
  208.7 3.2 collective-permute-done.43.p0
  213.5 16.4 %down.1 = (bf16[512,1024]{1,0:T(8,128)(2,1)}, bf16[512,4096]{1,0:T(8,128)(2,1)S(1)}, f32[1,4096]{1,0:T(1,128)S(1)}, f32[1,1024]{1,0:T(1,128)S(1)}) custom-call(s32[5]{0:T(128)S(1)} %stack.294.spot_ref, bf16[512,1024]{1,0:T(8,128)(2,1)S(1)} %bitcast.285, bf16[512,4096]{1,0:T(8,128)(2,1)S(1)} %copy-done.43, ...), custom_call_target="tpu_custom_call" | custom-call | flops 1 | bytes 1 | tf_op jit(solution)/shard_map/down/pallas_call | solution.py:426
  230.0 6.1 %wgrad.9 = (bf16[2,2,2,256,512]{4,3,2,1,0:T(8,128)(2,1)S(1)}, bf16[2,2,2,256,512]{4,3,2,1,0:T(8,128)(2,1)}) custom-call(s32[5]{0:T(128)S(1)} %stack.294.spot_ref, bf16[512,4096]{1,0:T(8,128)(2,1)S(1)} %get-tuple-element.268.refs_0_.act_ref, bf16[512,1024]{1,0:T(8,128)(2,1)S(1)} %bitcast.286, bf16[2,2,256,512]{3,2,1,0:T(8,128)(2,1)S(1)} %collective-permute-done.45.refs_2_, ...), custom_call_target="tpu_custom_call" | custom-call | flops 1 | bytes 1 | tf_op jit(solution)/shard_map/wgrad/pallas_call | solution.py:621
  237.6 4.9 %wgrad.10 = (bf16[2,2,64,2048]{3,2,1,0:T(8,128)(2,1)}, bf16[2,2,64,2048]{3,2,1,0:T(8,128)(2,1)S(1)}, bf16[2,2,64,2048]{3,2,1,0:T(8,128)(2,1)S(1)}, bf16[2,2,64,2048]{3,2,1,0:T(8,128)(2,1)}) custom-call(s32[5]{0:T(128)S(1)} %stack.356.spot_ref, bf16[512,1024]{1,0:T(8,128)(2,1)S(1)} %get-tuple-element.282.refs_0_, ...), custom_call_target="tpu_custom_call" | custom-call | flops 1 | bytes 1 | tf_op jit(solution)/shard_map/wgrad/pallas_call | solution.py:621
  243.5 3.4 copy-done.24
  246.9 8.7 %feed_back.1 = (f32[512,1024]{1,0:T(8,128)S(1)}, bf16[512,1024]{1,0:T(8,128)(2,1)S(1)}, bf16[512,1024]{1,0:T(8,128)(2,1)S(1)}, f32[8,1024]{1,0:T(8,128)S(1)}) custom-call(bf16[512,4096]{1,0:T(8,128)(2,1)S(1)} %get-tuple-element.284.refs_1_.g_ref, bf16[1024,4096]{1,0:T(8,128)(2,1)S(1)} %copy-done.24, f32[512,1024]{1,0:T(8,128)S(1)} %copy-done.23, ...), custom_call_target="tpu_custom_call" | custom-call | flops 1 | bytes 1 | tf_op jit(solution)/shard_map/feed_back/pallas_call | solution.py:465
  255.7 6.0 %wgrad.11 = (bf16[2,2,2,64,2048]{4,3,2,1,0:T(8,128)(2,1)S(1)}, bf16[2,2,2,64,2048]{4,3,2,1,0:T(8,128)(2,1)}) custom-call(s32[5]{0:T(128)S(1)} %stack.294.spot_ref, bf16[512,1024]{1,0:T(8,128)(2,1)S(1)} %get-tuple-element.282.refs_0_, bf16[512,4096]{1,0:T(8,128)(2,1)S(1)} %get-tuple-element.284.refs_1_.g_ref, ...), custom_call_target="tpu_custom_call" | custom-call | flops 1 | bytes 1 | tf_op jit(solution)/shard_map/wgrad/pallas_call | solution.py:621
  262.3 7.7 %attend_back.3 = (bf16[2,256,1024]{2,1,0:T(8,128)(2,1)S(1)}, bf16[1,2,128,1024]{3,2,1,0:T(8,128)(2,1)S(1)}, bf16[1,2,128,1024]{3,2,1,0:T(8,128)(2,1)S(1)}) custom-call(s32[2]{0:T(128)S(1)} %copy-done.63, bf16[1,2,256,1024]{3,2,1,0:T(8,128)(2,1)S(1)} %bitcast.308, bf16[1,2,128,2048]{3,2,1,0:T(8,128)(2,1)S(1)} %bitcast.293, ...), custom_call_target="tpu_custom_call" | custom-call | flops 1 | bytes 1 | tf_op jit(solution)/shard_map/attend_back/pallas_call | solution.py:864
  271.9 3.2 cross_back.1
  278.4 5.3 %wgrad.12 = (bf16[2,2,64,2560]{3,2,1,0:T(8,128)(2,1)S(1)}, bf16[2,2,64,2560]{3,2,1,0:T(8,128)(2,1)S(1)}, bf16[2,2,64,2560]{3,2,1,0:T(8,128)(2,1)}, bf16[2,2,64,2560]{3,2,1,0:T(8,128)(2,1)S(1)}) custom-call(s32[5]{0:T(128)S(1)} %stack.356.spot_ref, bf16[512,1024]{1,0:T(8,128)(2,1)S(1)} %copy-done.37, bf16[512,1024]{1,0:T(8,128)(2,1)S(1)} %bitcast.296, ...), custom_call_target="tpu_custom_call" | custom-call | flops 1 | bytes 1 | tf_op jit(solution)/shard_map/wgrad/pallas_call | solution.py:621
  285.3 2.8 collective-permute-done.54
  289.1 3.0 fusion.24
  292.1 14.3 %attend_back.4 = (bf16[2,256,512]{2,1,0:T(8,128)(2,1)S(1)}, bf16[4,2,256,512]{3,2,1,0:T(8,128)(2,1)S(1)}, bf16[4,2,256,512]{3,2,1,0:T(8,128)(2,1)S(1)}) custom-call(s32[1]{0:T(128)} %bitcast.42.info_ref, bf16[1,2,256,1024]{3,2,1,0:T(8,128)(2,1)S(1)} %get-tuple-element.249.q_ref, bf16[4,2,256,1024]{3,2,1,0:T(8,128)(2,1)S(1)} %copy-done.3, ...), custom_call_target="tpu_custom_call" | custom-call | flops 1 | bytes 1 | tf_op jit(solution)/shard_map/attend_back/pallas_call | solution.py:864
  314.8 6.9 %wgrad.13 = (bf16[2,2,2,64,2560]{4,3,2,1,0:T(8,128)(2,1)S(1)}, bf16[2,2,2,64,2560]{4,3,2,1,0:T(8,128)(2,1)}) custom-call(s32[5]{0:T(128)S(1)} %stack.294.spot_ref, bf16[512,1024]{1,0:T(8,128)(2,1)S(1)} %copy-done.37, bf16[512,1024]{1,0:T(8,128)(2,1)S(1)} %bitcast.297, bf16[256,1024]{1,0:T(8,128)(2,1)S(1)} %bitcast.304, ...), custom_call_target="tpu_custom_call" | custom-call | flops 1 | bytes 1 | tf_op jit(solution)/shard_map/wgrad/pallas_call | solution.py:621
  332.4 14.1 %attend_back.5 = (bf16[2,256,512]{2,1,0:T(8,128)(2,1)S(1)}, bf16[4,2,256,512]{3,2,1,0:T(8,128)(2,1)S(1)}, bf16[4,2,256,512]{3,2,1,0:T(8,128)(2,1)S(1)}) custom-call(s32[1]{0:T(128)} %bitcast.42.info_ref, bf16[1,2,256,1024]{3,2,1,0:T(8,128)(2,1)S(1)} %get-tuple-element.249.q_ref, bf16[4,2,256,1024]{3,2,1,0:T(8,128)(2,1)S(1)} %copy-done.4, ...), custom_call_target="tpu_custom_call" | custom-call | flops 1 | bytes 1 | tf_op jit(solution)/shard_map/attend_back/pallas_call | solution.py:864
  346.5 8.6 %wgrad.14 = (bf16[2,2,64,1536]{3,2,1,0:T(8,128)(2,1)S(1)}, bf16[2,2,64,1536]{3,2,1,0:T(8,128)(2,1)S(1)}, bf16[2,2,64,1536]{3,2,1,0:T(8,128)(2,1)S(1)}, bf16[2,2,64,1536]{3,2,1,0:T(8,128)(2,1)S(1)}) custom-call(s32[5]{0:T(128)S(1)} %stack.356.spot_ref, bf16[512,1024]{1,0:T(8,128)(2,1)S(1)} %bitcast.270, bf16[512,512]{1,0:T(8,128)(2,1)S(1)} %bitcast.298, ...), custom_call_target="tpu_custom_call" | custom-call | flops 1 | bytes 1 | tf_op jit(solution)/shard_map/wgrad/pallas_call | solution.py:621
  355.7 3.1 fusion.56
  361.1 5.4 %collective-permute-done.63 = bf16[2,2,2,64,2560]{4,3,2,1,0:T(8,128)(2,1)} collective-permute-done((bf16[2,2,2,64,2560]{4,3,2,1,0:T(8,128)(2,1)}, bf16[2,2,2,64,2560]{4,3,2,1,0:T(8,128)(2,1)}, u32[]{:S(2)}, u32[]{:S(2)}) %collective-permute-start.63) | collective-permute-done | bytes 2621472 | tf_op jit(solution)/shard_map/ppermute | solution.py:41
  366.5 2.7 fusion
  369.2 2.8 collective-permute-done.62
  373.7 11.0 %wgrad.15 = (bf16[2,2,2,64,1536]{4,3,2,1,0:T(8,128)(2,1)S(1)}, bf16[2,2,2,64,1536]{4,3,2,1,0:T(8,128)(2,1)S(1)}) custom-call(s32[5]{0:T(128)S(1)} %stack.294.spot_ref, bf16[512,1024]{1,0:T(8,128)(2,1)S(1)} %bitcast.272, bf16[512,512]{1,0:T(8,128)(2,1)S(1)} %bitcast.299, bf16[512,1024]{1,0:T(8,128)(2,1)S(1)} %bitcast.273, bf16[512,512]{1,0:T(8,128)(2,1)S(1)} %bitcast.301, ...), custom_call_target="tpu_custom_call" | custom-call | flops 1 | bytes 1 | tf_op jit(solution)/shard_map/wgrad/pallas_call | solution.py:621
  388.7 2.8 copy-done.31
  391.5 15.3 %self_back.1 = (bf16[256,1024]{1,0:T(8,128)(2,1)S(1)}, bf16[256,1024]{1,0:T(8,128)(2,1)S(1)}, bf16[256,1024]{1,0:T(8,128)(2,1)S(1)}, bf16[256,1024]{1,0:T(8,128)...) custom-call(bf16[2,256,512]{2,1,0:T(8,128)(2,1)S(1)} %copy-done.33, ...), custom_call_target="tpu_custom_call" | custom-call | flops 1 | bytes 1 | tf_op jit(solution)/shard_map/self_back/pallas_call | solution.py:554
  417.4 10.8 %collective-permute-done.74 = bf16[256,1024]{1,0:T(8,128)(2,1)S(1)} collective-permute-done((bf16[256,1024]{1,0:T(8,128)(2,1)S(1)}, bf16[256,1024]{1,0:T(8,128)(2,1)S(1)}, u32[]{:S(2)}, u32[]{:S(2)}) %collective-permute-start.74) | collective-permute-done | bytes 524320 | tf_op jit(solution)/shard_map/ppermute | solution.py:41
  434.9 16.3 %collective-permute-done.81 = bf16[2,2,64,1536]{3,2,1,0:T(8,128)(2,1)S(1)} collective-permute-done((bf16[2,2,64,1536]{3,2,1,0:T(8,128)(2,1)S(1)}, bf16[2,2,64,1536]{3,2,1,0:T(8,128)(2,1)S(1)}, u32[]{:S(2)}, u32[]{:S(2)}) %collective-permute-start.81) | collective-permute-done | bytes 786464 | tf_op jit(solution)/shard_map/ppermute | solution.py:41
  451.9 4.7 collective-permute-done.80
  457.6 10.1 %collective-permute-start.83 = (f32[11,1024]{1,0:T(8,128)S(1)}, f32[11,1024]{1,0:T(8,128)S(1)}, u32[]{:S(2)}, u32[]{:S(2)}) collective-permute-start(f32[11,1024]{1,0:T(8,128)S(1)} %add.408), channel_id=1, source_target_pairs={{0,8},{1,9},{2,10},{3,11},{4,12},{5,13},{6,14},{7,15},{8,0},{9,1},... | collective-permute-start | bytes 135176 | tf_op jit(solution)/shard_map/ppermute | solution.py:41
  (471 shorter events, 143.4 us)
Async XLA Ops:
  2.2 26.8 %collective-permute-start.1 = (bf16[2,256,1024]{2,1,0:T(8,128)(2,1)}, bf16[2,256,1024]{2,1,0:T(8,128)(2,1)S(1)}, u32[]{:S(2)}, u32[]{:S(2)}) collective-permute-start(bf16[2,256,1024]{2,1,0:T(8,128)(2,1)} %param.19), channel_id=1, source_target_pairs={{0,2},{1,3},{2,0},{3,1},{4,6},{5,7},{6,4},{7,5},{8,10},{9,11},{10,... | collective-permute-start | bytes 3145736 | tf_op jit(solution)/shard_map/ppermute | solution.py:41
  4.8 54.5 %collective-permute-start = (bf16[2,256,1024]{2,1,0:T(8,128)(2,1)}, bf16[2,256,1024]{2,1,0:T(8,128)(2,1)}, u32[]{:S(2)}, u32[]{:S(2)}) collective-permute-start(bf16[2,256,1024]{2,1,0:T(8,128)(2,1)} %param.19), channel_id=1, source_target_pairs={{0,1},{1,0},{2,3},{3,2},{4,5},{5,4},{6,7},{7,6},{8,9},{9,8},{10,11... | collective-permute-start | bytes 3145736 | tf_op jit(solution)/shard_map/ppermute | solution.py:41
  29.0 30.2 %collective-permute-start.7 = (bf16[2,256,1024]{2,1,0:T(8,128)(2,1)S(1)}, bf16[2,256,1024]{2,1,0:T(8,128)(2,1)S(1)}, u32[]{:S(2)}, u32[]{:S(2)}) collective-permute-start(bf16[2,256,1024]{2,1,0:T(8,128)(2,1)S(1)} %collective-permute-done.1), channel_id=1, source_target_pairs={{0,1},{1,0},{2,3},{3,2},{4,5},{5,4},{6,7},{7,6},{8,9},{9,8},{10,11... | collective-permute-start | bytes 3145736 | tf_op jit(solution)/shard_map/ppermute | solution.py:41
  34.5 40.4 %collective-permute-start.21 = (bf16[2,2,2,64,768]{4,3,2,1,0:T(8,128)(2,1)S(1)}, bf16[2,2,2,64,768]{4,3,2,1,0:T(8,128)(2,1)S(1)}, u32[]{:S(2)}, u32[]{:S(2)}) collective-permute-start(bf16[2,2,2,64,768]{4,3,2,1,0:T(8,128)(2,1)S(1)} %pad_maximum_fusion.10.p1), channel_id=1, source_target_pairs={{0,1},{1,0},{2,3},{3,2},{4,5},{5,4},{6,7},{7,6},{8,9},{9,8},{10,11... | collective-permute-start | bytes 2359304 | tf_op jit(solution)/shard_map/ppermute | solution.py:41
  59.3 16.7 %collective-permute-start.23 = (bf16[2,2,2,64,896]{4,3,2,1,0:T(8,128)(2,1)S(1)}, bf16[2,2,2,64,896]{4,3,2,1,0:T(8,128)(2,1)S(1)}, u32[]{:S(2)}, u32[]{:S(2)}) collective-permute-start(bf16[2,2,2,64,896]{4,3,2,1,0:T(8,128)(2,1)S(1)} %pad_maximum_fusion.9.p5), channel_id=1, source_target_pairs={{0,1},{1,0},{2,3},{3,2},{4,5},{5,4},{6,7},{7,6},{8,9},{9,8},{10,11... | collective-permute-start | bytes 2752520 | tf_op jit(solution)/shard_map/ppermute | solution.py:41
  74.8 19.0 %collective-permute-start.15 = (bf16[128,512]{1,0:T(8,128)(2,1)S(1)}, bf16[128,512]{1,0:T(8,128)(2,1)S(1)}, u32[]{:S(2)}, u32[]{:S(2)}) collective-permute-start(bf16[128,512]{1,0:T(8,128)(2,1)S(1)} %get-tuple-element.430), channel_id=1, source_target_pairs={{0,1},{1,0},{2,3},{3,2},{4,5},{5,4},{6,7},{7,6},{8,9},{9,8},{10,11... | collective-permute-start | bytes 393224 | tf_op jit(solution)/shard_map/ppermute | solution.py:41
  75.0 20.6 %collective-permute-start.26 = (bf16[2,64,1536]{2,1,0:T(8,128)(2,1)S(1)}, bf16[2,64,1536]{2,1,0:T(8,128)(2,1)S(1)}, u32[]{:S(2)}, u32[]{:S(2)}) collective-permute-start(bf16[2,64,1536]{2,1,0:T(8,128)(2,1)S(1)} %get-tuple-element.420), channel_id=1, source_target_pairs={{0,4},{1,3},{2,6},{3,1},{4,0},{5,7},{6,2},{7,5},{8,12},{9,11},{10,... | collective-permute-start | bytes 1179656 | tf_op jit(solution)/shard_map/ppermute | solution.py:41
  75.2 18.7 %collective-permute-start.27 = (bf16[64,2048]{1,0:T(8,128)(2,1)S(1)}, bf16[64,2048]{1,0:T(8,128)(2,1)S(1)}, u32[]{:S(2)}, u32[]{:S(2)}) collective-permute-start(bf16[64,2048]{1,0:T(8,128)(2,1)S(1)} %maximum_select_fusion), channel_id=1, source_target_pairs={{0,16},{1,17},{2,18},{3,19},{4,20},{5,21},{6,22},{7,23},{8,24},{9,... | collective-permute-start | bytes 786440 | tf_op jit(solution)/shard_map/ppermute | solution.py:41
  76.0 20.7 %collective-permute-start.25 = (bf16[2,2,64,1024]{3,2,1,0:T(8,128)(2,1)S(1)}, bf16[2,2,64,1024]{3,2,1,0:T(8,128)(2,1)S(1)}, u32[]{:S(2)}, u32[]{:S(2)}) collective-permute-start(bf16[2,2,64,1024]{3,2,1,0:T(8,128)(2,1)S(1)} %get-tuple-element.416), channel_id=1, source_target_pairs={{0,8},{1,9},{2,10},{3,11},{4,12},{5,13},{6,14},{7,15},{8,0},{9,1},... | collective-permute-start | bytes 1572872 | tf_op jit(solution)/shard_map/ppermute | solution.py:41
  93.9 25.4 %collective-permute-start.31 = (bf16[2,64,2048]{2,1,0:T(8,128)(2,1)S(1)}, bf16[2,64,2048]{2,1,0:T(8,128)(2,1)S(1)}, u32[]{:S(2)}, u32[]{:S(2)}) collective-permute-start(bf16[2,64,2048]{2,1,0:T(8,128)(2,1)S(1)} %get-tuple-element.414), channel_id=1, source_target_pairs={{0,4},{1,3},{2,6},{3,1},{4,0},{5,7},{6,2},{7,5},{8,12},{9,11},{10,... | collective-permute-start | bytes 1572872 | tf_op jit(solution)/shard_map/ppermute | solution.py:41
  95.8 25.6 %collective-permute-start.30 = (bf16[2,2,64,1536]{3,2,1,0:T(8,128)(2,1)S(1)}, bf16[2,2,64,1536]{3,2,1,0:T(8,128)(2,1)S(1)}, u32[]{:S(2)}, u32[]{:S(2)}) collective-permute-start(bf16[2,2,64,1536]{3,2,1,0:T(8,128)(2,1)S(1)} %get-tuple-element.408), channel_id=1, source_target_pairs={{0,8},{1,9},{2,10},{3,11},{4,12},{5,13},{6,14},{7,15},{8,0},{9,1},... | collective-permute-start | bytes 2359304 | tf_op jit(solution)/shard_map/ppermute | solution.py:41
  96.9 24.7 %collective-permute-start.29 = (bf16[2,2,2,64,1024]{4,3,2,1,0:T(8,128)(2,1)S(1)}, bf16[2,2,2,64,1024]{4,3,2,1,0:T(8,128)(2,1)S(1)}, u32[]{:S(2)}, u32[]{:S(2)}) collective-permute-start(bf16[2,2,2,64,1024]{4,3,2,1,0:T(8,128)(2,1)S(1)} %pad_maximum_fusion.5.p1), channel_id=1, source_target_pairs={{0,2},{1,5},{2,0},{3,7},{4,6},{5,1},{6,4},{7,3},{8,10},{9,13},{10,... | collective-permute-start | bytes 3145736 | tf_op jit(solution)/shard_map/ppermute | solution.py:41
  97.8 21.5 %collective-permute-start.24 = (bf16[256,512]{1,0:T(8,128)(2,1)S(1)}, bf16[256,512]{1,0:T(8,128)(2,1)S(1)}, u32[]{:S(2)}, u32[]{:S(2)}) collective-permute-start(bf16[256,512]{1,0:T(8,128)(2,1)S(1)} %maximum_select_fusion.2), channel_id=1, source_target_pairs={{0,16},{1,17},{2,18},{3,19},{4,20},{5,21},{6,22},{7,23},{8,24},{9,... | collective-permute-start | bytes 786440 | tf_op jit(solution)/shard_map/ppermute | solution.py:41
  99.4 34.5 %collective-permute-start.33 = (bf16[2,2,2,64,1024]{4,3,2,1,0:T(8,128)(2,1)S(1)}, bf16[2,2,2,64,1024]{4,3,2,1,0:T(8,128)(2,1)S(1)}, u32[]{:S(2)}, u32[]{:S(2)}) collective-permute-start(bf16[2,2,2,64,1024]{4,3,2,1,0:T(8,128)(2,1)S(1)} %pad_maximum_fusion.5.p1), channel_id=1, source_target_pairs={{0,1},{1,0},{2,3},{3,2},{4,5},{5,4},{6,7},{7,6},{8,9},{9,8},{10,11... | collective-permute-start | bytes 3145736 | tf_op jit(solution)/shard_map/ppermute | solution.py:41
  121.7 25.6 %collective-permute-start.36 = (bf16[2,2,64,2048]{3,2,1,0:T(8,128)(2,1)S(1)}, bf16[2,2,64,2048]{3,2,1,0:T(8,128)(2,1)S(1)}, u32[]{:S(2)}, u32[]{:S(2)}) collective-permute-start(bf16[2,2,64,2048]{3,2,1,0:T(8,128)(2,1)S(1)} %get-tuple-element.400), channel_id=1, source_target_pairs={{0,8},{1,9},{2,10},{3,11},{4,12},{5,13},{6,14},{7,15},{8,0},{9,1},... | collective-permute-start | bytes 3145736 | tf_op jit(solution)/shard_map/ppermute | solution.py:41
  122.3 27.1 %collective-permute-start.35 = (bf16[2,2,2,64,1536]{4,3,2,1,0:T(8,128)(2,1)S(1)}, bf16[2,2,2,64,1536]{4,3,2,1,0:T(8,128)(2,1)S(1)}, u32[]{:S(2)}, u32[]{:S(2)}) collective-permute-start(bf16[2,2,2,64,1536]{4,3,2,1,0:T(8,128)(2,1)S(1)} %pad_maximum_fusion.4.p1), channel_id=1, source_target_pairs={{0,2},{1,5},{2,0},{3,7},{4,6},{5,1},{6,4},{7,3},{8,10},{9,13},{10,... | collective-permute-start | bytes 4718600 | tf_op jit(solution)/shard_map/ppermute | solution.py:41
  122.8 17.6 %collective-permute-start.28 = (bf16[2,256,512]{2,1,0:T(8,128)(2,1)S(1)}, bf16[2,256,512]{2,1,0:T(8,128)(2,1)S(1)}, u32[]{:S(2)}, u32[]{:S(2)}) collective-permute-start(bf16[2,256,512]{2,1,0:T(8,128)(2,1)S(1)} %get-tuple-element.412), channel_id=1, source_target_pairs={{0,4},{1,3},{2,6},{3,1},{4,0},{5,7},{6,2},{7,5},{8,12},{9,11},{10,... | collective-permute-start | bytes 1572872 | tf_op jit(solution)/shard_map/ppermute | solution.py:41
  148.8 27.7 %collective-permute-start.40 = (bf16[2,2,2,64,2048]{4,3,2,1,0:T(8,128)(2,1)}, bf16[2,2,2,64,2048]{4,3,2,1,0:T(8,128)(2,1)}, u32[]{:S(2)}, u32[]{:S(2)}) collective-permute-start(bf16[2,2,2,64,2048]{4,3,2,1,0:T(8,128)(2,1)} %pad_maximum_fusion.1.p1), channel_id=1, source_target_pairs={{0,2},{1,5},{2,0},{3,7},{4,6},{5,1},{6,4},{7,3},{8,10},{9,13},{10,... | collective-permute-start | bytes 6291464 | tf_op jit(solution)/shard_map/ppermute | solution.py:41
  149.9 25.1 %collective-permute-start.34 = (bf16[2,2,256,512]{3,2,1,0:T(8,128)(2,1)S(1)}, bf16[2,2,256,512]{3,2,1,0:T(8,128)(2,1)S(1)}, u32[]{:S(2)}, u32[]{:S(2)}) collective-permute-start(bf16[2,2,256,512]{3,2,1,0:T(8,128)(2,1)S(1)} %get-tuple-element.398), channel_id=1, source_target_pairs={{0,8},{1,9},{2,10},{3,11},{4,12},{5,13},{6,14},{7,15},{8,0},{9,1},... | collective-permute-start | bytes 3145736 | tf_op jit(solution)/shard_map/ppermute | solution.py:41
  150.5 28.1 %collective-permute-start.42 = (bf16[2,2,2,64,2048]{4,3,2,1,0:T(8,128)(2,1)}, bf16[2,2,2,64,2048]{4,3,2,1,0:T(8,128)(2,1)}, u32[]{:S(2)}, u32[]{:S(2)}) collective-permute-start(bf16[2,2,2,64,2048]{4,3,2,1,0:T(8,128)(2,1)} %pad_maximum_fusion.1.p1), channel_id=1, source_target_pairs={{0,1},{1,0},{2,3},{3,2},{4,5},{5,4},{6,7},{7,6},{8,9},{9,8},{10,11... | collective-permute-start | bytes 6291464 | tf_op jit(solution)/shard_map/ppermute | solution.py:41
  176.6 30.9 %collective-permute-start.39 = (bf16[2,2,2,256,512]{4,3,2,1,0:T(8,128)(2,1)}, bf16[2,2,2,256,512]{4,3,2,1,0:T(8,128)(2,1)}, u32[]{:S(2)}, u32[]{:S(2)}) collective-permute-start(bf16[2,2,2,256,512]{4,3,2,1,0:T(8,128)(2,1)} %pad_maximum_fusion.2.p1), channel_id=1, source_target_pairs={{0,2},{1,5},{2,0},{3,7},{4,6},{5,1},{6,4},{7,3},{8,10},{9,13},{10,... | collective-permute-start | bytes 6291464 | tf_op jit(solution)/shard_map/ppermute | solution.py:41
  178.2 30.4 %collective-permute-start.44 = (bf16[2,2,2,256,512]{4,3,2,1,0:T(8,128)(2,1)}, bf16[2,2,2,256,512]{4,3,2,1,0:T(8,128)(2,1)}, u32[]{:S(2)}, u32[]{:S(2)}) collective-permute-start(bf16[2,2,2,256,512]{4,3,2,1,0:T(8,128)(2,1)} %pad_maximum_fusion.2.p1), channel_id=1, source_target_pairs={{0,1},{1,0},{2,3},{3,2},{4,5},{5,4},{6,7},{7,6},{8,9},{9,8},{10,11... | collective-permute-start | bytes 6291464 | tf_op jit(solution)/shard_map/ppermute | solution.py:41
  207.7 22.2 %collective-permute-start.45 = (bf16[2,2,256,512]{3,2,1,0:T(8,128)(2,1)}, bf16[2,2,256,512]{3,2,1,0:T(8,128)(2,1)S(1)}, u32[]{:S(2)}, u32[]{:S(2)}) collective-permute-start(bf16[2,2,256,512]{3,2,1,0:T(8,128)(2,1)} %get-tuple-element.269), channel_id=1, source_target_pairs={{0,1},{1,0},{2,3},{3,2},{4,5},{5,4},{6,7},{7,6},{8,9},{9,8},{10,11... | collective-permute-start | bytes 3145736 | tf_op jit(solution)/shard_map/ppermute | solution.py:41
  208.1 21.8 %collective-permute-start.46 = (bf16[2,2,256,512]{3,2,1,0:T(8,128)(2,1)S(1)}, bf16[2,2,256,512]{3,2,1,0:T(8,128)(2,1)S(1)}, u32[]{:S(2)}, u32[]{:S(2)}) collective-permute-start(bf16[2,2,256,512]{3,2,1,0:T(8,128)(2,1)S(1)} %get-tuple-element.278), channel_id=1, source_target_pairs={{0,1},{1,0},{2,3},{3,2},{4,5},{5,4},{6,7},{7,6},{8,9},{9,8},{10,11... | collective-permute-start | bytes 3145736 | tf_op jit(solution)/shard_map/ppermute | solution.py:41
  208.2 21.7 %collective-permute-start.47 = (bf16[2,2,256,512]{3,2,1,0:T(8,128)(2,1)S(1)}, bf16[2,2,256,512]{3,2,1,0:T(8,128)(2,1)S(1)}, u32[]{:S(2)}, u32[]{:S(2)}) collective-permute-start(bf16[2,2,256,512]{3,2,1,0:T(8,128)(2,1)S(1)} %get-tuple-element.279), channel_id=1, source_target_pairs={{0,1},{1,0},{2,3},{3,2},{4,5},{5,4},{6,7},{7,6},{8,9},{9,8},{10,11... | collective-permute-start | bytes 3145736 | tf_op jit(solution)/shard_map/ppermute | solution.py:41
  208.6 21.4 %collective-permute-start.48 = (bf16[2,2,256,512]{3,2,1,0:T(8,128)(2,1)}, bf16[2,2,256,512]{3,2,1,0:T(8,128)(2,1)S(1)}, u32[]{:S(2)}, u32[]{:S(2)}) collective-permute-start(bf16[2,2,256,512]{3,2,1,0:T(8,128)(2,1)} %get-tuple-element.280), channel_id=1, source_target_pairs={{0,1},{1,0},{2,3},{3,2},{4,5},{5,4},{6,7},{7,6},{8,9},{9,8},{10,11... | collective-permute-start | bytes 3145736 | tf_op jit(solution)/shard_map/ppermute | solution.py:41
  236.1 34.0 %collective-permute-start.53 = (bf16[2,2,2,256,512]{4,3,2,1,0:T(8,128)(2,1)}, bf16[2,2,2,256,512]{4,3,2,1,0:T(8,128)(2,1)}, u32[]{:S(2)}, u32[]{:S(2)}) collective-permute-start(bf16[2,2,2,256,512]{4,3,2,1,0:T(8,128)(2,1)} %get-tuple-element.295), channel_id=1, source_target_pairs={{0,2},{1,5},{2,0},{3,7},{4,6},{5,1},{6,4},{7,3},{8,10},{9,13},{10,... | collective-permute-start | bytes 6291464 | tf_op jit(solution)/shard_map/ppermute | solution.py:41
  261.7 26.4 %collective-permute-start.54 = (bf16[2,2,2,64,2048]{4,3,2,1,0:T(8,128)(2,1)}, bf16[2,2,2,64,2048]{4,3,2,1,0:T(8,128)(2,1)}, u32[]{:S(2)}, u32[]{:S(2)}) collective-permute-start(bf16[2,2,2,64,2048]{4,3,2,1,0:T(8,128)(2,1)} %get-tuple-element.304), channel_id=1, source_target_pairs={{0,2},{1,5},{2,0},{3,7},{4,6},{5,1},{6,4},{7,3},{8,10},{9,13},{10,... | collective-permute-start | bytes 6291464 | tf_op jit(solution)/shard_map/ppermute | solution.py:41
  276.9 32.9 %collective-permute-start.57 = (bf16[2,2,256,512]{3,2,1,0:T(8,128)(2,1)S(1)}, bf16[2,2,256,512]{3,2,1,0:T(8,128)(2,1)S(1)}, u32[]{:S(2)}, u32[]{:S(2)}) collective-permute-start(bf16[2,2,256,512]{3,2,1,0:T(8,128)(2,1)S(1)} %fusion.23), channel_id=1, source_target_pairs={{0,8},{1,9},{2,10},{3,11},{4,12},{5,13},{6,14},{7,15},{8,0},{9,1},... | collective-permute-start | bytes 3145736 | tf_op jit(solution)/shard_map/ppermute | solution.py:41
  284.8 27.7 %collective-permute-start.56 = (bf16[2,2,64,2560]{3,2,1,0:T(8,128)(2,1)S(1)}, bf16[2,2,64,2560]{3,2,1,0:T(8,128)(2,1)S(1)}, u32[]{:S(2)}, u32[]{:S(2)}) collective-permute-start(bf16[2,2,64,2560]{3,2,1,0:T(8,128)(2,1)S(1)} %get-tuple-element.314), channel_id=1, source_target_pairs={{0,1},{1,0},{2,3},{3,2},{4,5},{5,4},{6,7},{7,6},{8,9},{9,8},{10,11... | collective-permute-start | bytes 3932168 | tf_op jit(solution)/shard_map/ppermute | solution.py:41
  284.8 27.7 %collective-permute-start.58 = (bf16[2,2,64,2560]{3,2,1,0:T(8,128)(2,1)S(1)}, bf16[2,2,64,2560]{3,2,1,0:T(8,128)(2,1)S(1)}, u32[]{:S(2)}, u32[]{:S(2)}) collective-permute-start(bf16[2,2,64,2560]{3,2,1,0:T(8,128)(2,1)S(1)} %get-tuple-element.321), channel_id=1, source_target_pairs={{0,1},{1,0},{2,3},{3,2},{4,5},{5,4},{6,7},{7,6},{8,9},{9,8},{10,11... | collective-permute-start | bytes 3932168 | tf_op jit(solution)/shard_map/ppermute | solution.py:41
  285.3 28.2 %collective-permute-start.59 = (bf16[2,2,64,2560]{3,2,1,0:T(8,128)(2,1)}, bf16[2,2,64,2560]{3,2,1,0:T(8,128)(2,1)S(1)}, u32[]{:S(2)}, u32[]{:S(2)}) collective-permute-start(bf16[2,2,64,2560]{3,2,1,0:T(8,128)(2,1)} %get-tuple-element.322), channel_id=1, source_target_pairs={{0,1},{1,0},{2,3},{3,2},{4,5},{5,4},{6,7},{7,6},{8,9},{9,8},{10,11... | collective-permute-start | bytes 3932168 | tf_op jit(solution)/shard_map/ppermute | solution.py:41
  288.1 25.4 %collective-permute-start.60 = (bf16[2,2,64,2560]{3,2,1,0:T(8,128)(2,1)}, bf16[2,2,64,2560]{3,2,1,0:T(8,128)(2,1)S(1)}, u32[]{:S(2)}, u32[]{:S(2)}) collective-permute-start(bf16[2,2,64,2560]{3,2,1,0:T(8,128)(2,1)} %copy-done.66), channel_id=1, source_target_pairs={{0,1},{1,0},{2,3},{3,2},{4,5},{5,4},{6,7},{7,6},{8,9},{9,8},{10,11... | collective-permute-start | bytes 3932168 | tf_op jit(solution)/shard_map/ppermute | solution.py:41
  323.3 43.2 %collective-permute-start.63 = (bf16[2,2,2,64,2560]{4,3,2,1,0:T(8,128)(2,1)}, bf16[2,2,2,64,2560]{4,3,2,1,0:T(8,128)(2,1)}, u32[]{:S(2)}, u32[]{:S(2)}) collective-permute-start(bf16[2,2,2,64,2560]{4,3,2,1,0:T(8,128)(2,1)} %get-tuple-element.333), channel_id=1, source_target_pairs={{0,2},{1,5},{2,0},{3,7},{4,6},{5,1},{6,4},{7,3},{8,10},{9,13},{10,... | collective-permute-start | bytes 7864328 | tf_op jit(solution)/shard_map/ppermute | solution.py:41
  323.8 35.0 %collective-permute-start.64 = (bf16[2,2,64,2048]{3,2,1,0:T(8,128)(2,1)}, bf16[2,2,64,2048]{3,2,1,0:T(8,128)(2,1)}, u32[]{:S(2)}, u32[]{:S(2)}) collective-permute-start(bf16[2,2,64,2048]{3,2,1,0:T(8,128)(2,1)} %fusion.24), channel_id=1, source_target_pairs={{0,8},{1,9},{2,10},{3,11},{4,12},{5,13},{6,14},{7,15},{8,0},{9,1},... | collective-permute-start | bytes 3145736 | tf_op jit(solution)/shard_map/ppermute | solution.py:41
  324.4 30.8 %collective-permute-start.65 = (bf16[2,256,512]{2,1,0:T(8,128)(2,1)}, bf16[2,256,512]{2,1,0:T(8,128)(2,1)}, u32[]{:S(2)}, u32[]{:S(2)}) collective-permute-start(bf16[2,256,512]{2,1,0:T(8,128)(2,1)} %fusion.28), channel_id=1, source_target_pairs={{0,4},{1,3},{2,6},{3,1},{4,0},{5,7},{6,2},{7,5},{8,12},{9,11},{10,... | collective-permute-start | bytes 1572872 | tf_op jit(solution)/shard_map/ppermute | solution.py:41
  326.9 45.1 %collective-permute-start.62 = (bf16[256,1024]{1,0:T(8,128)(2,1)S(1)}, bf16[256,1024]{1,0:T(8,128)(2,1)S(1)}, u32[]{:S(2)}, u32[]{:S(2)}) collective-permute-start(bf16[256,1024]{1,0:T(8,128)(2,1)S(1)} %copy-done.68), channel_id=1, source_target_pairs={{0,2},{1,3},{2,0},{3,1},{4,6},{5,7},{6,4},{7,5},{8,10},{9,11},{10,... | collective-permute-start | bytes 1572872 | tf_op jit(solution)/shard_map/ppermute | solution.py:41
  355.1 18.6 %collective-permute-start.61 = (bf16[2,2,64,1536]{3,2,1,0:T(8,128)(2,1)S(1)}, bf16[2,2,64,1536]{3,2,1,0:T(8,128)(2,1)S(1)}, u32[]{:S(2)}, u32[]{:S(2)}) collective-permute-start(bf16[2,2,64,1536]{3,2,1,0:T(8,128)(2,1)S(1)} %get-tuple-element.332), channel_id=1, source_target_pairs={{0,1},{1,0},{2,3},{3,2},{4,5},{5,4},{6,7},{7,6},{8,9},{9,8},{10,11... | collective-permute-start | bytes 2359304 | tf_op jit(solution)/shard_map/ppermute | solution.py:41
  355.2 18.5 %collective-permute-start.66 = (bf16[2,2,64,1536]{3,2,1,0:T(8,128)(2,1)S(1)}, bf16[2,2,64,1536]{3,2,1,0:T(8,128)(2,1)S(1)}, u32[]{:S(2)}, u32[]{:S(2)}) collective-permute-start(bf16[2,2,64,1536]{3,2,1,0:T(8,128)(2,1)S(1)} %get-tuple-element.339), channel_id=1, source_target_pairs={{0,1},{1,0},{2,3},{3,2},{4,5},{5,4},{6,7},{7,6},{8,9},{9,8},{10,11... | collective-permute-start | bytes 2359304 | tf_op jit(solution)/shard_map/ppermute | solution.py:41
  372.0 34.9 %collective-permute-start.73 = (bf16[2,2,64,2560]{3,2,1,0:T(8,128)(2,1)}, bf16[2,2,64,2560]{3,2,1,0:T(8,128)(2,1)}, u32[]{:S(2)}, u32[]{:S(2)}) collective-permute-start(bf16[2,2,64,2560]{3,2,1,0:T(8,128)(2,1)} %fusion), channel_id=1, source_target_pairs={{0,8},{1,9},{2,10},{3,11},{4,12},{5,13},{6,14},{7,15},{8,0},{9,1},... | collective-permute-start | bytes 3932168 | tf_op jit(solution)/shard_map/ppermute | solution.py:41
  384.7 25.1 %collective-permute-start.72 = (bf16[2,2,2,64,1536]{4,3,2,1,0:T(8,128)(2,1)S(1)}, bf16[2,2,2,64,1536]{4,3,2,1,0:T(8,128)(2,1)S(1)}, u32[]{:S(2)}, u32[]{:S(2)}) collective-permute-start(bf16[2,2,2,64,1536]{4,3,2,1,0:T(8,128)(2,1)S(1)} %get-tuple-element.353), channel_id=1, source_target_pairs={{0,2},{1,5},{2,0},{3,7},{4,6},{5,1},{6,4},{7,3},{8,10},{9,13},{10,... | collective-permute-start | bytes 4718600 | tf_op jit(solution)/shard_map/ppermute | solution.py:41
  386.4 84.3 %collective-permute-start.84 = (bf16[256,512]{1,0:T(8,128)(2,1)}, bf16[256,512]{1,0:T(8,128)(2,1)S(1)}, u32[]{:S(2)}, u32[]{:S(2)}) collective-permute-start(bf16[256,512]{1,0:T(8,128)(2,1)} %slice_bitcast_fusion.10), channel_id=1, source_target_pairs={{0,16},{1,17},{2,18},{3,19},{4,20},{5,21},{6,22},{7,23},{8,24},{9,... | collective-permute-start | bytes 786440 | tf_op jit(solution)/shard_map/ppermute | solution.py:41
  387.9 25.5 %collective-permute-start.76 = (bf16[2,64,2048]{2,1,0:T(8,128)(2,1)}, bf16[2,64,2048]{2,1,0:T(8,128)(2,1)S(1)}, u32[]{:S(2)}, u32[]{:S(2)}) collective-permute-start(bf16[2,64,2048]{2,1,0:T(8,128)(2,1)} %fusion.26), channel_id=1, source_target_pairs={{0,4},{1,3},{2,6},{3,1},{4,0},{5,7},{6,2},{7,5},{8,12},{9,11},{10,... | collective-permute-start | bytes 1572872 | tf_op jit(solution)/shard_map/ppermute | solution.py:41
  410.0 19.8 %collective-permute-start.69 = (bf16[256,1024]{1,0:T(8,128)(2,1)S(1)}, bf16[256,1024]{1,0:T(8,128)(2,1)S(1)}, u32[]{:S(2)}, u32[]{:S(2)}) collective-permute-start(bf16[256,1024]{1,0:T(8,128)(2,1)S(1)} %get-tuple-element.350), channel_id=1, source_target_pairs={{0,1},{1,0},{2,3},{3,2},{4,5},{5,4},{6,7},{7,6},{8,9},{9,8},{10,11... | collective-permute-start | bytes 1572872 | tf_op jit(solution)/shard_map/ppermute | solution.py:41
  410.6 47.0 %collective-permute-start.78 = (bf16[256,1024]{1,0:T(8,128)(2,1)S(1)}, bf16[256,1024]{1,0:T(8,128)(2,1)S(1)}, u32[]{:S(2)}, u32[]{:S(2)}) collective-permute-start(bf16[256,1024]{1,0:T(8,128)(2,1)S(1)} %get-tuple-element.366), channel_id=1, source_target_pairs={{0,1},{1,0},{2,3},{3,2},{4,5},{5,4},{6,7},{7,6},{8,9},{9,8},{10,11... | collective-permute-start | bytes 1572872 | tf_op jit(solution)/shard_map/ppermute | solution.py:41
  428.2 22.9 %collective-permute-start.81 = (bf16[2,2,64,1536]{3,2,1,0:T(8,128)(2,1)S(1)}, bf16[2,2,64,1536]{3,2,1,0:T(8,128)(2,1)S(1)}, u32[]{:S(2)}, u32[]{:S(2)}) collective-permute-start(bf16[2,2,64,1536]{3,2,1,0:T(8,128)(2,1)S(1)} %fusion.29), channel_id=1, source_target_pairs={{0,8},{1,9},{2,10},{3,11},{4,12},{5,13},{6,14},{7,15},{8,0},{9,1},... | collective-permute-start | bytes 2359304 | tf_op jit(solution)/shard_map/ppermute | solution.py:41
  429.8 27.1 %collective-permute-start.79 = (bf16[256,1024]{1,0:T(8,128)(2,1)S(1)}, bf16[256,1024]{1,0:T(8,128)(2,1)S(1)}, u32[]{:S(2)}, u32[]{:S(2)}) collective-permute-start(bf16[256,1024]{1,0:T(8,128)(2,1)S(1)} %add_convert_fusion.4), channel_id=1, source_target_pairs={{0,2},{1,3},{2,0},{3,1},{4,6},{5,7},{6,4},{7,5},{8,10},{9,11},{10,... | collective-permute-start | bytes 1572872 | tf_op jit(solution)/shard_map/ppermute | solution.py:41
  431.8 38.8 %collective-permute-start.86 = (bf16[64,2048]{1,0:T(8,128)(2,1)S(1)}, bf16[64,2048]{1,0:T(8,128)(2,1)S(1)}, u32[]{:S(2)}, u32[]{:S(2)}) collective-permute-start(bf16[64,2048]{1,0:T(8,128)(2,1)S(1)} %slice_bitcast_fusion.9), channel_id=1, source_target_pairs={{0,16},{1,17},{2,18},{3,19},{4,20},{5,21},{6,22},{7,23},{8,24},{9,... | collective-permute-start | bytes 786440 | tf_op jit(solution)/shard_map/ppermute | solution.py:41
  (125 other events, 1048.8 us)
